TPU v7x, 32 devices: a whole 2x2x4 slice. The times are simulated.
32 devices in a mesh: blk: 8 (over z, y), pair: 4 (over x, core).
Axes of the slice: x: 2, y: 2, z: 4, core: 2. Of those that a mesh axis runs over, the one named last changes fastest.
Arguments:
- basis: float32 [8, 64, 510, 128], P(None, ('blk', 'pair'))
- mie_coeffs: float32 [64, 510, 128], P(('blk', 'pair')), may hold values from -8 to 8
- rot_table: bfloat16 [8, 510, 510], replicated, may hold values from -0.25 to 0.25
- axial_table: bfloat16 [8, 2, 510, 510], replicated, may hold values from -0.1875 to 0.1875
- pair_table: int32 [8, 128, 3], P('blk'), may hold values from 0 to 23, as said below
- pair_count: int32 [8], P('blk'), may hold values from 32 to 128, as said below
Outputs:
- projections: float32 [2, 8], replicated
- next_basis: float32 [64, 510, 128], P(('blk', 'pair'))
Inputs may be any that keep to these rules, and one draw needn't show every extreme that they name: `pair_table`: row p of blk index i is (a, b, g): a names one of the 8 blocks of blk index i; b counts from the first block of blk index i - 1 and is never a + 8; on blk index 0, b >= 8; on the last, b < 16; g < 8. Rows from pair_count on are ignored. `pair_count`: some blk index lists all 128 rows.
All inputs are finite; a program needn't handle non-finite values.
Results may differ from a plain program's by a relative error of at most 0.0003.
Values may be sent and summed in bfloat16 or wider, within the bound.
No kernel may reach another device: no remote copies, remote signals or barrier semaphores. Data moves between devices by JAX's collectives and lax.ppermute only.
A program may use at most 128 MiB of HBM per device.

v0:
```python
import jax
import jax.numpy as jnp
from jax import lax
from jax.sharding import PartitionSpec as P

batch_pairs = 8


def extended(value, sides, width):
    for axis, dim in sides:
        count, length = (lax.axis_size(axis), value.shape[dim])
        up = [(i, (i + 1) % count) for i in range(count - 1)]
        down = [(j, i) for i, j in up]
        last = lax.slice_in_dim(value, length - width, length, axis=dim)
        leading = lax.slice_in_dim(value, 0, width, axis=dim)
        before = lax.ppermute(last, axis, up)
        after = lax.ppermute(leading, axis, down)
        value = jnp.concatenate([before, value, after], axis=dim)
    return value


def shifted(value, axis, steps):
    count = lax.axis_size(axis)
    leading, last = (max(0, -steps), min(count, count - steps))
    return lax.ppermute(value, axis, [(source, source + steps) for source in range(leading, last)])


def swap_parts(packed):
    half_width = packed.shape[-1] // 2
    return jnp.concatenate([-packed[..., half_width:], packed[..., :half_width]], axis=-1)


def complex_product(left, right):
    half_width = left.shape[-1] // 2
    left_real, left_imag = (left[..., :half_width], left[..., half_width:])
    right_real, right_imag = (right[..., :half_width], right[..., half_width:])
    return jnp.concatenate(
        [
            left_real * right_real - left_imag * right_imag,
            left_real * right_imag + left_imag * right_real,
        ],
        axis=-1,
    )


def translate(rotation, axial_pair, source, transposed):
    turned = jnp.einsum(
        "pij,pjk->pik", rotation, source, preferred_element_type=jnp.float32
    ).astype(jnp.bfloat16)
    stacked = jnp.stack([turned, swap_parts(turned)], axis=1)
    if transposed:
        moved = jnp.einsum(
            "pcji,pcjk->pik", axial_pair, stacked, preferred_element_type=jnp.float32
        )
    else:
        moved = jnp.einsum(
            "pcij,pcjk->pik", axial_pair, stacked, preferred_element_type=jnp.float32
        )
    moved = moved.astype(jnp.bfloat16)
    return jnp.einsum("pji,pjk->pik", rotation, moved, preferred_element_type=jnp.float32)


def shards(basis, mie_coeffs, rot_table, axial_table, pair_table, pair_count):
    vector_count = basis.shape[0]
    quarter = basis.shape[1]
    mode_count = basis.shape[2]
    column_count = basis.shape[3]
    pair_ways = lax.axis_size("pair")
    blk_ways = lax.axis_size("blk")
    own_count = quarter * pair_ways
    current = basis[vector_count - 1].astype(jnp.bfloat16)
    own_coeff = lax.all_gather(current, "pair", axis=0, tiled=True)
    window = extended(own_coeff, (("blk", 0),), own_count)
    pair_rows = pair_table[0]
    live_total = pair_count[0]
    slot_total = pair_rows.shape[0]
    share = slot_total // pair_ways
    member = lax.axis_index("pair")
    live_here = jnp.clip(live_total - member * share, 0, share)
    first_slot = member * share
    stride_length = 1
    group_total = (live_here + batch_pairs - 1) // batch_pairs

    def accumulate(group_index, scattered):
        ordinal = group_index * batch_pairs + jnp.arange(batch_pairs, dtype=jnp.int32)
        active = ordinal < live_here
        chosen = pair_rows[jnp.minimum(first_slot + stride_length * ordinal, slot_total - 1)]
        target_rows = chosen[:, 0] + own_count
        source_rows = chosen[:, 1]
        table_rows = chosen[:, 2]
        rotation = rot_table[table_rows]
        axial_pair = axial_table[table_rows]
        forward = translate(rotation, axial_pair, window[source_rows], False)
        backward = translate(rotation, axial_pair, window[target_rows], True)
        forward = jnp.where(active[:, None, None], forward, jnp.float32(0.0))
        backward = jnp.where(active[:, None, None], backward, jnp.float32(0.0))
        return scattered.at[target_rows].add(forward).at[source_rows].add(backward)

    start_field = jnp.zeros((3 * own_count, mode_count, own_coeff.shape[2]), jnp.float32)
    scattered = lax.fori_loop(0, group_total, accumulate, start_field)
    lower_part = shifted(scattered[:own_count].astype(jnp.bfloat16), "blk", -1).astype(jnp.float32)
    upper_part = shifted(scattered[2 * own_count :].astype(jnp.bfloat16), "blk", 1).astype(
        jnp.float32
    )
    middle = scattered[own_count : 2 * own_count] + lower_part + upper_part
    field_here = lax.psum_scatter(
        middle.astype(jnp.bfloat16), "pair", scatter_dimension=0, tiled=True
    ).astype(jnp.float32)
    image = basis[vector_count - 1] - complex_product(mie_coeffs, field_here)
    mean_scale = 1.0 / (own_count * blk_ways * mode_count * column_count)
    highest = lax.Precision.HIGHEST
    real_local = jnp.einsum("kbcs,bcs->k", basis, image, precision=highest)
    imag_local = -jnp.einsum("kbcs,bcs->k", basis, swap_parts(image), precision=highest)
    dots = lax.psum(jnp.stack([real_local, imag_local]), ("blk", "pair")) * mean_scale
    real_part, imag_part = (dots[0], dots[1])
    remainder = image - jnp.einsum("k,kbcs->bcs", real_part, basis, precision=highest)
    remainder = remainder - jnp.einsum(
        "k,kbcs->bcs", imag_part, swap_parts(basis), precision=highest
    )
    norm_square = lax.psum(jnp.sum(remainder * remainder), ("blk", "pair")) * mean_scale
    next_basis = remainder * lax.rsqrt(norm_square)
    return (dots, next_basis)


def solution(mesh):
    placed = (
        P(None, ("blk", "pair"), None, None),
        P(("blk", "pair"), None, None),
        P(),
        P(),
        P("blk", None, None),
        P("blk"),
    )
    return jax.shard_map(
        shards,
        mesh=mesh,
        in_specs=placed,
        out_specs=(P(), P(("blk", "pair"), None, None)),
        check_vma=False,
    )
```

profile of v0, /device:TPU:0, one launch (start us, length us, event | category | flops | bytes accessed | tf_op | source)
XLA Modules:
  0.0 651.3 jit_solution(9012484402192539858)
XLA Ops:
  9.1 11.5 %all_gather.3 = bf16[8,510,128]{2,1,0:T(8,128)(2,1)S(1)} all-gather(bf16[2,510,128]{2,1,0:T(8,128)(2,1)S(1)} %bitcast.112), channel_id=1, replica_groups=mesh['blk'=8,'pair'=4] {'pair'}, dimensions={0}, use_global_device_ids=true | all-gather | bytes 1305600 | tf_op jit(solution)/shard_map/all_gather | solution.py:72
  22.5 4.6 collective-permute-start
  27.9 5.6 copy.56
  33.6 15.0 %collective-permute-done.1 = bf16[8,510,128]{2,0,1:T(8,128)(2,1)} collective-permute-done((bf16[8,510,128]{2,0,1:T(8,128)(2,1)S(1)}, bf16[8,510,128]{2,0,1:T(8,128)(2,1)}, u32[]{:S(2)}, u32[]{:S(2)}) %collective-permute-start.1) | collective-permute-done | bytes 1044512 | tf_op jit(solution)/shard_map/ppermute | solution.py:17
  49.9 20.9 %collective-permute-done = bf16[8,510,128]{2,0,1:T(8,128)(2,1)S(1)} collective-permute-done((bf16[8,510,128]{2,0,1:T(8,128)(2,1)S(1)}, bf16[8,510,128]{2,0,1:T(8,128)(2,1)S(1)}, u32[]{:S(2)}, u32[]{:S(2)}) %collective-permute-start) | collective-permute-done | bytes 1044512 | tf_op jit(solution)/shard_map/ppermute | solution.py:16
  76.3 364.6 %while.12 = (s32[]{:T(128)}, f32[24,510,128]{2,1,0:T(8,128)}, s32[]{:T(128)}, s32[]{:T(128)}, s32[128,3]{1,0:T(8,128)S(1)}, /*index=5*/s32[]{:T(128)}, bf16[8,51...) while((s32[]{:T(128)}, f32[24,510,128]{2,1,0:T(8,128)}, ...), condition=%wide.region_3.4_spmd, body=%wide.region_0.3_spmd.sunk | while | flops 4272449536 | bytes 112527400 | solution.py:100
  77.4 5.1 gather_fusion.1
  82.5 21.4 %gather_fusion.2 = bf16[8,2,510,510]{3,1,2,0:T(2,128)(2,1)} fusion(bf16[8,2,510,510]{3,1,2,0:T(2,128)(2,1)} %get-tuple-element.299, s32[1024]{0:T(1024)S(1)} %pad_clamp_fusion.8), kind=kCustom, calls=%fused_computation.2.clone.1 | custom fusion | bytes 16646432 | tf_op jit(solution)/shard_map/while/body/gather | solution.py:92
  103.8 21.3 %copy.139 = bf16[8,2,510,510]{2,3,1,0:T(8,128)(2,1)} copy(bf16[8,2,510,510]{3,1,2,0:T(2,128)(2,1)} %gather_fusion.2) | data formatting | bytes 16646400 | tf_op jit(solution)/shard_map/while/body/gather | solution.py:92
  127.8 3.7 convolution_convert_fusion.4
  131.7 9.9 %convolution_select_fusion.4 = f32[8,510,128]{2,1,0:T(8,128)} fusion(bf16[8,510,510]{2,1,0:T(8,128)(2,1)} %gather_fusion.1, pred[8]{0:T(512)(128)(4,1)S(1)} %add_compare_fusion.2, bf16[8,2,510,510]{2,3,1,0:T(8,128)(2,1)} %copy.139, bf16[8,1,510,128]{2,3,0,1:T(8,128)(2,1)S(1)} %maximum_bitcast_fusion.5, bf16[8,1,510,128]{2,3,0,1:T(8,128)(2,1)S(1)} %bitcast.110), kind=kOutput, calls=%fused_computation.16.clone.1 | convolution fusion | flops 1600143360 | bytes 16662728 | tf_op jit(solution)/shard_map/while/body/pji,pjk->pik/dot_general | solution.py:60
  141.6 4.9 scatter_fusion
  153.0 9.5 %convolution_select_fusion.5 = f32[8,510,128]{2,1,0:T(8,128)} fusion(bf16[8,510,510]{2,1,0:T(8,128)(2,1)} %gather_fusion.1, pred[8]{0:T(512)(128)(4,1)S(1)} %add_compare_fusion.2, bf16[8,2,510,510]{2,3,1,0:T(8,128)(2,1)} %copy.139, bf16[8,1,510,128]{2,3,0,1:T(8,128)(2,1)S(1)} %maximum_bitcast_fusion.6, bf16[8,1,510,128]{2,3,0,1:T(8,128)(2,1)S(1)} %bitcast.109), kind=kOutput, calls=%fused_computation.15.clone.1 | convolution fusion | flops 1600143360 | bytes 16662728 | tf_op jit(solution)/shard_map/while/body/pji,pjk->pik/dot_general | solution.py:60
  162.5 5.2 scatter_fusion.1
  168.6 5.1 gather_fusion.1
  173.7 21.4 %gather_fusion.2 = bf16[8,2,510,510]{3,1,2,0:T(2,128)(2,1)} fusion(bf16[8,2,510,510]{3,1,2,0:T(2,128)(2,1)} %get-tuple-element.299, s32[1024]{0:T(1024)S(1)} %pad_clamp_fusion.8), kind=kCustom, calls=%fused_computation.2.clone.1 | custom fusion | bytes 16646432 | tf_op jit(solution)/shard_map/while/body/gather | solution.py:92
  195.0 21.3 %copy.139 = bf16[8,2,510,510]{2,3,1,0:T(8,128)(2,1)} copy(bf16[8,2,510,510]{3,1,2,0:T(2,128)(2,1)} %gather_fusion.2) | data formatting | bytes 16646400 | tf_op jit(solution)/shard_map/while/body/gather | solution.py:92
  218.9 3.7 convolution_convert_fusion.4
  222.9 9.9 %convolution_select_fusion.4 = f32[8,510,128]{2,1,0:T(8,128)} fusion(bf16[8,510,510]{2,1,0:T(8,128)(2,1)} %gather_fusion.1, pred[8]{0:T(512)(128)(4,1)S(1)} %add_compare_fusion.2, bf16[8,2,510,510]{2,3,1,0:T(8,128)(2,1)} %copy.139, bf16[8,1,510,128]{2,3,0,1:T(8,128)(2,1)S(1)} %maximum_bitcast_fusion.5, bf16[8,1,510,128]{2,3,0,1:T(8,128)(2,1)S(1)} %bitcast.110), kind=kOutput, calls=%fused_computation.16.clone.1 | convolution fusion | flops 1600143360 | bytes 16662728 | tf_op jit(solution)/shard_map/while/body/pji,pjk->pik/dot_general | solution.py:60
  232.7 4.8 scatter_fusion
  244.1 9.5 %convolution_select_fusion.5 = f32[8,510,128]{2,1,0:T(8,128)} fusion(bf16[8,510,510]{2,1,0:T(8,128)(2,1)} %gather_fusion.1, pred[8]{0:T(512)(128)(4,1)S(1)} %add_compare_fusion.2, bf16[8,2,510,510]{2,3,1,0:T(8,128)(2,1)} %copy.139, bf16[8,1,510,128]{2,3,0,1:T(8,128)(2,1)S(1)} %maximum_bitcast_fusion.6, bf16[8,1,510,128]{2,3,0,1:T(8,128)(2,1)S(1)} %bitcast.109), kind=kOutput, calls=%fused_computation.15.clone.1 | convolution fusion | flops 1600143360 | bytes 16662728 | tf_op jit(solution)/shard_map/while/body/pji,pjk->pik/dot_general | solution.py:60
  253.6 5.1 scatter_fusion.1
  259.6 5.1 gather_fusion.1
  264.7 21.3 %gather_fusion.2 = bf16[8,2,510,510]{3,1,2,0:T(2,128)(2,1)} fusion(bf16[8,2,510,510]{3,1,2,0:T(2,128)(2,1)} %get-tuple-element.299, s32[1024]{0:T(1024)S(1)} %pad_clamp_fusion.8), kind=kCustom, calls=%fused_computation.2.clone.1 | custom fusion | bytes 16646432 | tf_op jit(solution)/shard_map/while/body/gather | solution.py:92
  286.0 21.3 %copy.139 = bf16[8,2,510,510]{2,3,1,0:T(8,128)(2,1)} copy(bf16[8,2,510,510]{3,1,2,0:T(2,128)(2,1)} %gather_fusion.2) | data formatting | bytes 16646400 | tf_op jit(solution)/shard_map/while/body/gather | solution.py:92
  313.8 9.9 %convolution_select_fusion.4 = f32[8,510,128]{2,1,0:T(8,128)} fusion(bf16[8,510,510]{2,1,0:T(8,128)(2,1)} %gather_fusion.1, pred[8]{0:T(512)(128)(4,1)S(1)} %add_compare_fusion.2, bf16[8,2,510,510]{2,3,1,0:T(8,128)(2,1)} %copy.139, bf16[8,1,510,128]{2,3,0,1:T(8,128)(2,1)S(1)} %maximum_bitcast_fusion.5, bf16[8,1,510,128]{2,3,0,1:T(8,128)(2,1)S(1)} %bitcast.110), kind=kOutput, calls=%fused_computation.16.clone.1 | convolution fusion | flops 1600143360 | bytes 16662728 | tf_op jit(solution)/shard_map/while/body/pji,pjk->pik/dot_general | solution.py:60
  323.7 4.9 scatter_fusion
  331.3 3.7 convolution_convert_fusion.5
  335.2 9.5 %convolution_select_fusion.5 = f32[8,510,128]{2,1,0:T(8,128)} fusion(bf16[8,510,510]{2,1,0:T(8,128)(2,1)} %gather_fusion.1, pred[8]{0:T(512)(128)(4,1)S(1)} %add_compare_fusion.2, bf16[8,2,510,510]{2,3,1,0:T(8,128)(2,1)} %copy.139, bf16[8,1,510,128]{2,3,0,1:T(8,128)(2,1)S(1)} %maximum_bitcast_fusion.6, bf16[8,1,510,128]{2,3,0,1:T(8,128)(2,1)S(1)} %bitcast.109), kind=kOutput, calls=%fused_computation.15.clone.1 | convolution fusion | flops 1600143360 | bytes 16662728 | tf_op jit(solution)/shard_map/while/body/pji,pjk->pik/dot_general | solution.py:60
  344.7 5.0 scatter_fusion.1
  350.6 5.1 gather_fusion.1
  355.7 21.4 %gather_fusion.2 = bf16[8,2,510,510]{3,1,2,0:T(2,128)(2,1)} fusion(bf16[8,2,510,510]{3,1,2,0:T(2,128)(2,1)} %get-tuple-element.299, s32[1024]{0:T(1024)S(1)} %pad_clamp_fusion.8), kind=kCustom, calls=%fused_computation.2.clone.1 | custom fusion | bytes 16646432 | tf_op jit(solution)/shard_map/while/body/gather | solution.py:92
  377.1 21.3 %copy.139 = bf16[8,2,510,510]{2,3,1,0:T(8,128)(2,1)} copy(bf16[8,2,510,510]{3,1,2,0:T(2,128)(2,1)} %gather_fusion.2) | data formatting | bytes 16646400 | tf_op jit(solution)/shard_map/while/body/gather | solution.py:92
  401.0 3.7 convolution_convert_fusion.4
  404.9 9.9 %convolution_select_fusion.4 = f32[8,510,128]{2,1,0:T(8,128)} fusion(bf16[8,510,510]{2,1,0:T(8,128)(2,1)} %gather_fusion.1, pred[8]{0:T(512)(128)(4,1)S(1)} %add_compare_fusion.2, bf16[8,2,510,510]{2,3,1,0:T(8,128)(2,1)} %copy.139, bf16[8,1,510,128]{2,3,0,1:T(8,128)(2,1)S(1)} %maximum_bitcast_fusion.5, bf16[8,1,510,128]{2,3,0,1:T(8,128)(2,1)S(1)} %bitcast.110), kind=kOutput, calls=%fused_computation.16.clone.1 | convolution fusion | flops 1600143360 | bytes 16662728 | tf_op jit(solution)/shard_map/while/body/pji,pjk->pik/dot_general | solution.py:60
  414.8 4.7 scatter_fusion
  426.0 9.5 %convolution_select_fusion.5 = f32[8,510,128]{2,1,0:T(8,128)} fusion(bf16[8,510,510]{2,1,0:T(8,128)(2,1)} %gather_fusion.1, pred[8]{0:T(512)(128)(4,1)S(1)} %add_compare_fusion.2, bf16[8,2,510,510]{2,3,1,0:T(8,128)(2,1)} %copy.139, bf16[8,1,510,128]{2,3,0,1:T(8,128)(2,1)S(1)} %maximum_bitcast_fusion.6, bf16[8,1,510,128]{2,3,0,1:T(8,128)(2,1)S(1)} %bitcast.109), kind=kOutput, calls=%fused_computation.15.clone.1 | convolution fusion | flops 1600143360 | bytes 16662728 | tf_op jit(solution)/shard_map/while/body/pji,pjk->pik/dot_general | solution.py:60
  435.5 5.0 scatter_fusion.1
  444.5 4.9 collective-permute-start.3
  450.7 33.4 %collective-permute-done.3 = bf16[8,510,128]{2,1,0:T(8,128)(2,1)S(1)} collective-permute-done((bf16[8,510,128]{2,1,0:T(8,128)(2,1)S(1)}, bf16[8,510,128]{2,1,0:T(8,128)(2,1)S(1)}, u32[]{:S(2)}, u32[]{:S(2)}) %collective-permute-start.3) | collective-permute-done | bytes 1044512 | tf_op jit(solution)/shard_map/ppermute | solution.py:25
  487.8 11.1 %slice_negate_fusion.2 = (f32[8,2,510,64]{3,1,2,0:T(2,128)}, f32[8,2,510,64]{3,1,2,0:T(2,128)}) fusion(f32[8,2,510,128]{3,1,2,0:T(2,128)} %param.8), kind=kLoop, calls=%fused_computation.39 | loop fusion | flops 522240 | bytes 8355840 | tf_op jit(solution)/shard_map/neg | solution.py:30
  498.9 23.6 %reduce-scatter.2.cloned.1.call-done = bf16[2,510,128]{2,1,0:T(8,128)(2,1)} async-done(((bf16[8,510,128]{2,1,0:T(8,128)(2,1)}), bf16[2,510,128]{2,1,0:T(8,128)(2,1)}) %reduce-scatter.2.cloned.1.call-update) | async-done | bytes 261136 | tf_op jit(solution)/shard_map/reduce_scatter | solution.py:106
  525.6 9.6 %fusion.33 = f32[1,8]{1,0:T(1,128)S(1)} fusion(f32[8,2,510,128]{3,1,2,0:T(2,128)S(1)} %copy-done, f32[2,510,128,1]{2,1,0,3:T(8,128)S(1)} %maximum_bitcast_fusion.2), kind=kOutput, calls=%fused_computation.51 | convolution fusion | flops 12533768 | bytes 4700192 | tf_op jit(solution)/shard_map/kbcs,bcs->k/dot_general | solution.py:113
  535.2 9.4 %fusion.24 = f32[1,8]{1,0:T(1,128)S(1)} fusion(f32[8,2,510,128]{3,1,2,0:T(2,128)S(1)} %copy-done, f32[2,510,128,1]{2,1,0,3:T(8,128)S(1)} %bitcast.111), kind=kOutput, calls=%fused_computation.48 | convolution fusion | flops 12533760 | bytes 4700192 | tf_op jit(solution)/shard_map/kbcs,bcs->k/dot_general | solution.py:112
  544.7 6.5 pad_maximum_fusion.2
  551.2 39.3 %psum.14 = f32[2,8]{1,0:T(2,128)S(1)} all-reduce(f32[2,8]{1,0:T(2,128)S(1)} %pad_maximum_fusion.4), channel_id=1, replica_groups=mesh['blk'=8,'pair'=4] {'blk','pair'}, use_global_device_ids=true, to_apply=%region_5.6 | all-reduce | flops 16 | bytes 128 | tf_op jit(solution)/shard_map/psum | solution.py:114
  590.5 6.2 fusion.18
  601.1 41.2 %psum.15 = f32[]{:T(128)} all-reduce(f32[]{:T(128)} %multiply_reduce_fusion), channel_id=1, replica_groups=mesh['blk'=8,'pair'=4] {'blk','pair'}, use_global_device_ids=true, to_apply=%region_7.8 | all-reduce | flops 1 | bytes 8 | tf_op jit(solution)/shard_map/psum | solution.py:120
  (102 shorter events, 69.4 us)
Async XLA Ops:
  7.2 20.7 %copy-start.8 = (s32[1,128,3]{1,0,2:T(1,128)S(1)}, s32[1,128,3]{1,0,2:T(1,128)}, u32[]{:S(2)}) copy-start(s32[1,128,3]{1,0,2:T(1,128)} %param.12) | copy-start | bytes 4612
  7.2 515.3 %reduce-scatter.2.cloned.1.call-start = ((), (), s32[]{:S(2)}) async-start(), calls=%async_computation.1 | async-start | bytes 1310720 | tf_op jit(solution)/shard_map/reduce_scatter | solution.py:106
  8.3 0.8 copy-start.4
  21.2 27.3 %collective-permute-start.1 = (bf16[8,510,128]{2,0,1:T(8,128)(2,1)S(1)}, bf16[8,510,128]{2,0,1:T(8,128)(2,1)}, u32[]{:S(2)}, u32[]{:S(2)}) collective-permute-start(bf16[8,510,128]{2,0,1:T(8,128)(2,1)S(1)} %copy.52), channel_id=1, source_target_pairs={{4,0},{8,4},{12,8},{16,12},{20,16},{24,20},{28,24},{5,1},{9,5},{13... | collective-permute-start | bytes 3133448 | tf_op jit(solution)/shard_map/ppermute | solution.py:17
  22.5 48.2 %collective-permute-start = (bf16[8,510,128]{2,0,1:T(8,128)(2,1)S(1)}, bf16[8,510,128]{2,0,1:T(8,128)(2,1)S(1)}, u32[]{:S(2)}, u32[]{:S(2)}) collective-permute-start(bf16[8,510,128]{2,0,1:T(8,128)(2,1)S(1)} %copy.52), channel_id=1, source_target_pairs={{0,4},{4,8},{8,12},{12,16},{16,20},{20,24},{24,28},{1,5},{5,9},{9,... | collective-permute-start | bytes 3133448 | tf_op jit(solution)/shard_map/ppermute | solution.py:16
  444.5 42.7 %copy-start.6 = (f32[2,510,128]{2,0,1:T(2,128)S(1)}, f32[2,510,128]{2,0,1:T(2,128)}, u32[]{:S(2)}) copy-start(f32[2,510,128]{2,0,1:T(2,128)} %param.9) | copy-start | bytes 1566724
  444.5 39.6 %collective-permute-start.3 = (bf16[8,510,128]{2,1,0:T(8,128)(2,1)S(1)}, bf16[8,510,128]{2,1,0:T(8,128)(2,1)S(1)}, u32[]{:S(2)}, u32[]{:S(2)}) collective-permute-start(bf16[8,510,128]{2,1,0:T(8,128)(2,1)S(1)} %get-tuple-element.189), channel_id=1, source_target_pairs={{0,4},{4,8},{8,12},{12,16},{16,20},{20,24},{24,28},{1,5},{5,9},{9,... | collective-permute-start | bytes 3133448 | tf_op jit(solution)/shard_map/ppermute | solution.py:25
  449.4 34.7 %collective-permute-start.2 = (bf16[8,510,128]{2,1,0:T(8,128)(2,1)S(1)}, bf16[8,510,128]{2,1,0:T(8,128)(2,1)S(1)}, u32[]{:S(2)}, u32[]{:S(2)}) collective-permute-start(bf16[8,510,128]{2,1,0:T(8,128)(2,1)S(1)} %get-tuple-element.188), channel_id=1, source_target_pairs={{4,0},{8,4},{12,8},{16,12},{20,16},{24,20},{28,24},{5,1},{9,5},{13... | collective-permute-start | bytes 3133448 | tf_op jit(solution)/shard_map/ppermute | solution.py:25
  498.9 24.9 %copy-start.5 = (f32[1,2,510,128]{3,1,2,0:T(2,128)S(1)}, f32[1,2,510,128]{3,1,2,0:T(2,128)}, u32[]{:S(2)}) copy-start(f32[1,2,510,128]{3,1,2,0:T(2,128)} %copy-done.4) | copy-start | bytes 1566724
  523.4 2.2 copy-start
  525.6 19.0 %copy-start.2 = (f32[8,2,510,64]{3,1,2,0:T(2,128)S(1)}, f32[8,2,510,64]{3,1,2,0:T(2,128)}, u32[]{:S(2)}) copy-start(f32[8,2,510,64]{3,1,2,0:T(2,128)} %get-tuple-element.186) | copy-start | bytes 6266884
  525.6 19.0 %copy-start.3 = (f32[8,2,510,64]{3,1,2,0:T(2,128)S(1)}, f32[8,2,510,64]{3,1,2,0:T(2,128)}, u32[]{:S(2)}) copy-start(f32[8,2,510,64]{3,1,2,0:T(2,128)} %get-tuple-element.187) | copy-start | bytes 6266884
  590.4 6.2 copy-start.1
  590.5 9.9 %copy-start.7 = (f32[2,8]{1,0:T(2,128)}, f32[2,8]{1,0:T(2,128)S(1)}, u32[]{:S(2)}) copy-start(f32[2,8]{1,0:T(2,128)S(1)} %broadcast_multiply_fusion.1) | copy-start | bytes 196
Sparse Core Ops, SparseCore 0:
  487.3 35.0 reduce-scatter.1
where the time goes:
time: 659 us; the launch traced here: 651 us
  local copies, waits for them, and re-layouts  230 us (35%)
  matrix products  136 us (21%)
  waiting for transfers between devices  92.9 us (14%)
  blocking collectives  91.9 us (14%)
  other arithmetic  71.5 us (11%)
  between operations  15.8 us (2%)
  starting transfers between devices  12.1 us (2%)
    gather x8, local copies, waits for them, and re-layouts, accumulate(): axial_pair = axial_table[table_rows]  170 us
    dot_general x8, matrix products, translate(): jnp.einsum('pji,pjk->pik', rotation, moved, preferred_element_type=jnp.fl...  77.4 us
    psum x1, blocking collectives, shards(): lax.psum(jnp.sum(remainder * remainder), ('blk', 'pair')) * mean_scale  41.2 us
    scatter-add x8, other arithmetic, accumulate(): return scattered.at[target_rows].add(forward).at[source_rows].add(backward)  39.7 us
    psum x1, blocking collectives, shards(): lax.psum(jnp.stack([real_local, imag_local]), ('blk', 'pair')) * mean_scale  39.3 us
    ppermute x2, waiting for transfers between devices, shifted(): lax.ppermute(value, axis, [(source, source + steps) for source in range(l...  33.4 us
    dot_general x8, matrix products, translate(): jnp.einsum('pij,pjk->pik', rotation, source, preferred_element_type=jnp.f...  29.5 us
    reduce_scatter x1, waiting for transfers between devices, shards(): lax.psum_scatter(middle.astype(jnp.bfloat16), 'pair', scatter_dimension=0...  23.6 us
  transfers between devices with their start and end apart: 5, of which 4 were waited for; matrix products, arithmetic and copies ran while one was open for 3% of the time, Pallas kernels for 0%

commit v1 on v0

v1 whole, which is shorter than its diff:
```python
import functools

import jax
import jax.numpy as jnp
from jax import lax
from jax.experimental import pallas as pl
from jax.experimental.pallas import tpu as pltpu
from jax.sharding import PartitionSpec as P

MIB = 1024 * 1024
F32 = jnp.float32
BF16 = jnp.bfloat16


def params(mib):
    return pltpu.CompilerParams(vmem_limit_bytes=mib * MIB)


def whole():
    return pl.BlockSpec(memory_space=pltpu.VMEM)


def rounded_up(value, unit):
    return (value + unit - 1) // unit * unit


def iota(shape, dim):
    return lax.broadcasted_iota(jnp.int32, shape, dim)


def dot_nn(left, right):
    return lax.dot_general(left, right, (((1,), (0,)), ((), ())), preferred_element_type=F32)


def dot_nt(left, right):
    return lax.dot_general(left, right, (((1,), (1,)), ((), ())), preferred_element_type=F32)


def pack_kernel(quarter, modes, ways, pair_rows_ref, count_ref, basis_ref, out_ref, codes_ref, pad_ref):
    columns = pad_ref.shape[1]
    part = columns // 2 // ways
    first = basis_ref.shape[1] - quarter * modes
    pad_ref[...] = jnp.zeros_like(pad_ref)
    for j in range(quarter):
        pad_ref[0:modes, :] = basis_ref[0, pl.ds(first + j, modes, quarter), :]
        turned = jnp.transpose(pad_ref[...]).astype(BF16)
        for p in range(ways):
            for c in range(2):
                row = c * (columns // 2) + p * part
                out_ref[p, c, j] = turned[row : row + part]
    slots = pair_rows_ref.shape[2]
    live = iota((1, slots), 1) < count_ref[0]
    zero = jnp.zeros((1, slots), jnp.int32)
    codes_ref[...] = jnp.zeros_like(codes_ref)
    codes_ref[0:1, :] = jnp.where(live, pair_rows_ref[0], zero)
    codes_ref[1:2, :] = jnp.where(live, pair_rows_ref[1], zero)
    codes_ref[2:3, :] = jnp.where(live, pair_rows_ref[2] + 1, zero)


def tables_kernel(modes, tables, axial_ref, rot_ref, rot_out_ref, axial_out_ref, lines_ref):
    step = pl.program_id(0)
    size = rot_out_ref.shape[1]
    chunk = 256

    @pl.when(step == 0)
    def _():
        rot_out_ref[...] = jnp.zeros_like(rot_out_ref)
        lines_ref[...] = jnp.zeros_like(lines_ref)

    out_row, in_row = iota((chunk, chunk), 0), iota((chunk, chunk), 1)
    each = chunk // 2
    halves = (in_row == 2 * lax.rem(out_row, each) + lax.div(out_row, each)).astype(F32).astype(BF16)
    lines_ref[0 : 2 * modes, 0:modes] = axial_ref[0].reshape(2 * modes, modes)
    for q in range(2 * size // chunk):
        sorted_rows = dot_nn(halves, lines_ref[q * chunk : (q + 1) * chunk, :]).astype(BF16)
        for c in range(2):
            axial_out_ref[0, c * size + q * each : c * size + (q + 1) * each, :] = sorted_rows[c * each : (c + 1) * each]
    each = chunk // tables
    entries = (in_row == tables * lax.rem(out_row, each) + lax.div(out_row, each)).astype(F32).astype(BF16)
    block = rot_ref.shape[0]
    left = tables * modes - step * block
    rows = jnp.where(iota((block, modes), 0) < left, rot_ref[...], jnp.zeros((), BF16))
    for q in range(block // chunk):
        sorted_rows = dot_nn(entries, rows[q * chunk : (q + 1) * chunk]).astype(BF16)
        start = pl.multiple_of(step * (block // tables) + q * each, each)
        for g in range(tables):
            rot_out_ref[g, pl.ds(start, each), 0:modes] = sorted_rows[g * each : (g + 1) * each]


def weights_kernel(own, part, codes_ref, below_ref, above_ref, out_ref):
    tables = out_ref.shape[0]
    group = own * part
    slots = codes_ref.shape[1]
    stacked = jnp.concatenate([below_ref[...], codes_ref[...], above_ref[...]], axis=0).astype(F32)
    filler = jnp.zeros((slots - stacked.shape[0], slots), F32)
    columns = jnp.transpose(jnp.concatenate([stacked, filler], axis=0)).astype(jnp.int32)
    row = iota((tables * group, slots), 0)
    entry = lax.div(row, group) + 1
    block = lax.rem(lax.div(row, part), own)

    def chosen(codes, line, shift):
        hit = (codes[2:3, :] == entry) & (codes[line : line + 1, :] - shift == block)
        return jnp.where(hit, 1.0, 0.0).astype(BF16)

    def spread(column, blocks):
        lane = lax.div(iota((slots, blocks * part), 1), part)
        return jnp.where(column == lane, 1.0, 0.0).astype(BF16)

    def store(direction, first, counts):
        lanes = counts.shape[1]
        same = lax.rem(iota(counts.shape, 0), part) == lax.rem(iota(counts.shape, 1), part)
        kept = jnp.where(same, counts, 0.0).astype(BF16)
        for g in range(tables):
            out_ref[g, direction * group : (direction + 1) * group, first : first + lanes] = kept[g * group : (g + 1) * group]

    store(0, 0, dot_nn(chosen(codes_ref[...], 0, 0), spread(columns[:, 9:10], 3 * own)))
    for window, ref in enumerate((below_ref, codes_ref, above_ref)):
        shift = (2 - window) * own
        counts = dot_nn(chosen(ref[...], 1, shift), spread(columns[:, 8 * window : 8 * window + 1], own))
        store(1, window * group, counts)


def swapped(value):
    half = value.shape[0] // 2
    return jnp.concatenate([-value[half:], value[:half]], axis=0)


def field_kernel(weights_ref, rot_ref, axial_ref, below_ref, own_ref, above_ref, out_ref, window_ref, total_ref):
    step = pl.program_id(0)
    group = weights_ref.shape[1] // 2
    size = window_ref.shape[2]

    @pl.when(step == 0)
    def _():
        for w, ref in enumerate((below_ref, own_ref, above_ref)):
            for c in range(2):
                window_ref[c, w * group : (w + 1) * group, :] = ref[:, c].reshape(group, size)
        total_ref[...] = jnp.zeros_like(total_ref)

    weights = weights_ref[0]
    real = dot_nn(weights, window_ref[0]).astype(BF16)
    imag = dot_nn(weights, window_ref[1]).astype(BF16)
    sums = jnp.concatenate([real[:group], imag[:group], real[group:], imag[group:]], axis=0)
    rotation = rot_ref[0]
    turned = dot_nt(sums, rotation).astype(BF16)
    forward, backward = turned[: 2 * group], turned[2 * group :]
    moved = dot_nt(forward, axial_ref[0, :size]) + dot_nt(swapped(forward), axial_ref[0, size:])
    moved += dot_nn(jnp.concatenate([backward, swapped(backward)], axis=1), axial_ref[0])
    total_ref[...] += dot_nn(moved.astype(BF16), rotation)

    @pl.when(step == pl.num_programs(0) - 1)
    def _():
        for c in range(2):
            out_ref[:, c] = total_ref[c * group : (c + 1) * group].astype(BF16).reshape(out_ref[:, c].shape)


def lane_swap(value):
    half = value.shape[1] // 2
    rolled = pltpu.roll(value, half, axis=1)
    return jnp.where(iota(value.shape, 1) < half, -rolled, rolled)


def folded(value):
    return jnp.sum(value.reshape(value.shape[0] // 8, 8, value.shape[1]), axis=0)


def image_kernel(quarter, modes, basis_ref, mie_ref, pieces_ref, image_ref, sums_ref, lines_ref, kept_ref):
    step = pl.program_id(0)
    rows = quarter * modes
    full = kept_ref.shape[1]
    gap = full - rows
    blocks = pl.num_programs(0)

    @pl.when(step == 0)
    def _():
        ways, _, _, part, size = pieces_ref.shape
        for j in range(quarter):
            turned = jnp.concatenate([pieces_ref[:, c, j].reshape(ways * part, size) for c in range(2)], axis=0)
            lines_ref[pl.ds(j, modes, quarter), :] = jnp.transpose(turned.astype(F32))[:modes]
        field = lines_ref[0:rows, :]
        mie = mie_ref[...]
        half = mie.shape[1] // 2
        left = iota(mie.shape, 1) < half
        other = pltpu.roll(mie, half, axis=1)
        product = jnp.where(left, mie, other) * field + jnp.where(left, -other, mie) * pltpu.roll(field, half, axis=1)
        image = basis_ref[0, rows : 2 * rows, :] - product
        kept_ref[...] = jnp.zeros_like(kept_ref)
        kept_ref[0, 0:rows, :] = image
        kept_ref[1, gap:full, :] = image
        image_ref[...] = kept_ref[0]
        kept_ref[2] = lane_swap(kept_ref[0])
        kept_ref[3] = lane_swap(kept_ref[1])
        sums_ref[...] = jnp.zeros_like(sums_ref)

    tile = iota(sums_ref.shape, 0), iota(sums_ref.shape, 1)
    update = jnp.zeros(sums_ref.shape, F32)
    for side in range(2):
        first = side * (2 * rows - full)
        values = basis_ref[0, first : first + full, :]
        k = 2 * (blocks - 1 - step) + side
        real = jnp.sum(folded(values * kept_ref[side]), axis=(0, 1), keepdims=True)
        imag = -jnp.sum(folded(values * kept_ref[2 + side]), axis=(0, 1), keepdims=True)
        update += jnp.where((tile[0] == k) & (tile[1] == 0), real, 0.0)
        update += jnp.where((tile[0] == k) & (tile[1] == 1), imag, 0.0)
    sums_ref[...] += update


def remainder_kernel(quarter, modes, dots_ref, basis_ref, image_ref, out_ref, squares_ref, kept_ref):
    step = pl.program_id(0)
    rows = quarter * modes
    full = kept_ref.shape[1]
    gap = full - rows
    for side in range(2):
        first = side * (2 * rows - full)
        values = basis_ref[0, first : first + full, :]
        k = 2 * step + side
        real, imag = dots_ref[k, 0] * values, dots_ref[k, 1] * values

        @pl.when(step == 0)
        def _():
            kept_ref[side] = real
            kept_ref[2 + side] = imag

        @pl.when(step > 0)
        def _():
            kept_ref[side] += real
            kept_ref[2 + side] += imag

    @pl.when(step == pl.num_programs(0) - 1)
    def _():
        real = kept_ref[0, 0:rows, :] + kept_ref[1, gap:full, :]
        imag = kept_ref[2, 0:rows, :] + kept_ref[3, gap:full, :]
        remainder = image_ref[0:rows, :] - real - lane_swap(imag)
        out_ref[...] = remainder
        squares = jnp.sum(remainder * remainder, axis=(0, 1), keepdims=True)
        squares_ref[...] = jnp.broadcast_to(squares, squares_ref.shape)


def butterfly(value, axis):
    count = lax.axis_size(axis)
    if count & (count - 1):
        return lax.psum(value, axis)
    distance = 1
    while distance < count:
        value = value + lax.ppermute(value, axis, [(i, i ^ distance) for i in range(count)])
        distance *= 2
    return value


def exchanged(value):
    return lax.all_to_all(value, "pair", split_axis=0, concat_axis=0, tiled=True)


def neighbours(value):
    count = lax.axis_size("blk")
    up = [(i, i + 1) for i in range(count - 1)]
    down = [(j, i) for i, j in up]
    return lax.ppermute(value, "blk", up), lax.ppermute(value, "blk", down)


def shards(basis, mie_coeffs, rot_table, axial_table, pair_table, pair_count):
    vectors, quarter, modes, columns = basis.shape
    ways = lax.axis_size("pair")
    blk_ways = lax.axis_size("blk")
    tables = rot_table.shape[0]
    slots = pair_table.shape[1]
    own = quarter * ways
    part = columns // 2 // ways
    group = own * part
    size = rounded_up(modes, 128)
    rows = quarter * modes
    full = rounded_up(rows, 8)
    pairs_of_vectors = vectors // 2

    basis_rows = basis.transpose(0, 2, 1, 3).reshape(pairs_of_vectors, 2 * rows, columns)
    mie_rows = mie_coeffs.transpose(1, 0, 2).reshape(rows, columns)
    rot_rows = rot_table.transpose(1, 0, 2).reshape(modes * tables, modes)
    axial_rows = axial_table.transpose(0, 2, 1, 3)
    pair_rows = pair_table.transpose(2, 0, 1)

    pieces_shape = (ways, 2, quarter, part, size)
    pieces, codes = pl.pallas_call(
        functools.partial(pack_kernel, quarter, modes, ways),
        grid=(1,),
        in_specs=[
            whole(),
            pl.BlockSpec(memory_space=pltpu.SMEM),
            pl.BlockSpec((1, 2 * rows, columns), lambda i: (pairs_of_vectors - 1, 0, 0)),
        ],
        out_specs=[whole(), whole()],
        out_shape=[jax.ShapeDtypeStruct(pieces_shape, BF16), jax.ShapeDtypeStruct((8, slots), jnp.int32)],
        scratch_shapes=[pltpu.VMEM((size, columns), F32)],
        compiler_params=params(16),
        name="pack",
    )(pair_rows, pair_count, basis_rows)
    codes_below, codes_above = neighbours(codes)
    own_pieces = exchanged(pieces)
    below, above = neighbours(own_pieces)

    block = tables * size // tables
    rotations, axials = pl.pallas_call(
        functools.partial(tables_kernel, modes, tables),
        grid=(tables,),
        in_specs=[
            pl.BlockSpec((1, modes, 2, modes), lambda g: (g, 0, 0, 0)),
            pl.BlockSpec((block, modes), lambda g: (g, 0)),
        ],
        out_specs=[
            pl.BlockSpec((tables, size, size), lambda g: (0, 0, 0)),
            pl.BlockSpec((1, 2 * size, size), lambda g: (g, 0, 0)),
        ],
        out_shape=[
            jax.ShapeDtypeStruct((tables, size, size), BF16),
            jax.ShapeDtypeStruct((tables, 2 * size, size), BF16),
        ],
        scratch_shapes=[pltpu.VMEM((2 * size, size), BF16)],
        compiler_params=params(32),
        cost_estimate=pl.CostEstimate(flops=tables * 8 * 256 * 256 * size, bytes_accessed=6 * tables * size * size * 2, transcendentals=0),
        name="tables",
    )(axial_rows, rot_rows)

    weights = pl.pallas_call(
        functools.partial(weights_kernel, own, part),
        in_specs=[whole()] * 3,
        out_specs=whole(),
        out_shape=jax.ShapeDtypeStruct((tables, 2 * group, 3 * group), BF16),
        compiler_params=params(24),
        name="weights",
    )(codes, codes_below, codes_above)

    field = pl.pallas_call(
        field_kernel,
        grid=(tables,),
        in_specs=[
            pl.BlockSpec((1, 2 * group, 3 * group), lambda g: (g, 0, 0)),
            pl.BlockSpec((1, size, size), lambda g: (g, 0, 0)),
            pl.BlockSpec((1, 2 * size, size), lambda g: (g, 0, 0)),
            whole(),
            whole(),
            whole(),
        ],
        out_specs=whole(),
        out_shape=jax.ShapeDtypeStruct(pieces_shape, BF16),
        scratch_shapes=[pltpu.VMEM((2, 3 * group, size), BF16), pltpu.VMEM((2 * group, size), F32)],
        compiler_params=params(32),
        name="field",
    )(weights, rotations, axials, below, own_pieces, above)
    field_pieces = exchanged(field)

    pair_block = (1, 2 * rows, columns)
    image, sums = pl.pallas_call(
        functools.partial(image_kernel, quarter, modes),
        grid=(pairs_of_vectors,),
        in_specs=[
            pl.BlockSpec(pair_block, lambda i: (pairs_of_vectors - 1 - i, 0, 0)),
            whole(),
            whole(),
        ],
        out_specs=[whole(), whole()],
        out_shape=[jax.ShapeDtypeStruct((full, columns), F32), jax.ShapeDtypeStruct((8, 128), F32)],
        scratch_shapes=[pltpu.VMEM((full, columns), F32), pltpu.VMEM((4, full, columns), F32)],
        compiler_params=params(24),
        name="image",
    )(basis_rows, mie_rows, field_pieces)

    mean_scale = 1.0 / (own * blk_ways * modes * columns)
    dots = butterfly(butterfly(sums, "pair"), "blk") * mean_scale

    remainder, squares = pl.pallas_call(
        functools.partial(remainder_kernel, quarter, modes),
        grid=(pairs_of_vectors,),
        in_specs=[
            pl.BlockSpec(memory_space=pltpu.SMEM),
            pl.BlockSpec(pair_block, lambda i: (i, 0, 0)),
            whole(),
        ],
        out_specs=[whole(), whole()],
        out_shape=[jax.ShapeDtypeStruct((rows, columns), F32), jax.ShapeDtypeStruct((8, 128), F32)],
        scratch_shapes=[pltpu.VMEM((4, full, columns), F32)],
        compiler_params=params(24),
        name="remainder",
    )(dots, basis_rows, image)
    norm_square = lax.psum(lax.psum(squares[0, 0], "pair"), "blk") * mean_scale
    next_basis = (remainder * lax.rsqrt(norm_square)).reshape(modes, quarter, columns).transpose(1, 0, 2)
    return dots[:vectors, :2].T, next_basis


def solution(mesh):
    placed = (
        P(None, ("blk", "pair"), None, None),
        P(("blk", "pair"), None, None),
        P(),
        P(),
        P("blk", None, None),
        P("blk"),
    )
    return jax.shard_map(
        shards,
        mesh=mesh,
        in_specs=placed,
        out_specs=(P(), P(("blk", "pair"), None, None)),
        check_vma=False,
    )
```

time: 659 us -> 120 us (0.18); the launches traced: 651 us -> 120 us
  local copies, waits for them, and re-layouts: 230 us -> 14.4 us
  matrix products: 136 us -> 0 us
  waiting for transfers between devices: 92.9 us -> 14.8 us
  other arithmetic: 71.5 us -> 0.05 us
  blocking collectives: 91.9 us -> 37.8 us
  Pallas kernels: 0 us -> 26.4 us
  between operations: 15.8 us -> 2.13 us
  starting transfers between devices: 12.1 us -> 23.9 us
    gather x24 -> x0, local copies, waits for them, and re-layouts: 214 us -> none  [the longest x8 170 us: accumulate(): axial_pair = axial_table[table_rows]]
    dot_general x20 -> x0, matrix products: 136 us -> none  [the longest x8 77.4 us: translate(): jnp.einsum('pji,pjk->pik', rotation, moved, preferred_element_type=jnp.fl...]
    ppermute x4 -> x9, waiting for transfers between devices: 69.3 us -> 9.16 us  [the longest x5 9.15 us: butterfly(): lax.ppermute(value, axis, [(i, i ^ distance) for i in range(count)])]
    psum x2, blocking collectives: 80.5 us -> 27.5 us  [shards(): norm_square = lax.psum(lax.psum(squares[0, 0], 'pair'), 'blk') * mean_scale]
    scatter-add x8 -> x0, other arithmetic: 39.7 us -> none  [accumulate(): return scattered.at[target_rows].add(forward).at[source_rows].add(backward)]
    pallas_call x0 -> x6, Pallas kernels: none -> 26.4 us  [the longest x1 13.3 us: shards(): pl.pallas_call(field_kernel, grid=(tables,), in_specs=[pl.BlockSpec((1, 2...]
    reduce_scatter x1 -> x0, waiting for transfers between devices: 23.6 us -> none  [shards(): lax.psum_scatter(middle.astype(jnp.bfloat16), 'pair', scatter_dimension=0...]
    neg x10 -> x0, other arithmetic: 11.8 us -> none  [swap_parts(): -packed[..., half_width:]]
  transfers between devices with their start and end apart: 5 -> 10, of which waited for: 4 -> 6; matrix products, arithmetic and copies ran while one was open for 3% -> 0% of each run, Pallas kernels for 0% -> 7%
where the time goes in v1:
time: 120 us
  blocking collectives  37.8 us (31%)
  Pallas kernels  26.4 us (22%)
  starting transfers between devices  23.9 us (20%)
  waiting for transfers between devices  14.8 us (12%)
  local copies, waits for them, and re-layouts  14.4 us (12%)
  between operations  2.13 us (2%)
    psum x2, blocking collectives, shards(): norm_square = lax.psum(lax.psum(squares[0, 0], 'pair'), 'blk') * mean_scale  27.5 us
    pallas_call x1, Pallas kernels, shards(): pl.pallas_call(field_kernel, grid=(tables,), in_specs=[pl.BlockSpec((1, 2...  13.3 us
    unnamed x15, local copies, waits for them, and re-layouts  12.4 us
    ppermute x4, starting transfers between devices, neighbours(): return (lax.ppermute(value, 'blk', up), lax.ppermute(value, 'blk', down))  10.6 us
    all_to_all x1, blocking collectives, exchanged(): lax.all_to_all(value, 'pair', split_axis=0, concat_axis=0, tiled=True)  10.3 us
    ppermute x5, starting transfers between devices, butterfly(): lax.ppermute(value, axis, [(i, i ^ distance) for i in range(count)])  9.98 us
    ppermute x5, waiting for transfers between devices, butterfly(): lax.ppermute(value, axis, [(i, i ^ distance) for i in range(count)])  9.15 us
    pallas_call x1, Pallas kernels, shards(): pl.pallas_call(functools.partial(tables_kernel, modes, tables), grid=(tab...  7.12 us
  transfers between devices with their start and end apart: 10, of which 6 were waited for; matrix products, arithmetic and copies ran while one was open for 0% of the time, Pallas kernels for 7%

profile of v1, /device:TPU:0, one launch (start us, length us, event | category | flops | bytes accessed | tf_op | source)
XLA Modules:
  0.0 119.5 jit_solution(8853121240647952219)
XLA Ops:
  1.3 0.0 copy-start
  1.3 2.2 %copy-done = f32[8,2,510,128]{3,1,2,0:T(2,128)S(1)} copy-done((f32[8,2,510,128]{3,1,2,0:T(2,128)S(1)}, f32[8,2,510,128]{3,1,2,0:T(2,128)}, u32[]{:S(2)}) %copy-start) | copy-done | bytes 4177944
  3.5 0.0 copy-start.5
  3.5 0.7 copy-done.5
  4.1 0.0 copy-start.4
  4.1 0.1 pack.1
  4.3 10.3 %all_to_all.10.own_ref = bf16[4,2,2,16,512]{4,3,2,1,0:T(8,128)(2,1)S(1)} all-to-all(bf16[4,2,2,16,512]{4,3,2,1,0:T(8,128)(2,1)S(1)} %get-tuple-element.13), channel_id=1, replica_groups=mesh['blk'=8,'pair'=4] {'pair'}, dimensions={0} | all-to-all | bytes 524288 | tf_op jit(solution)/shard_map/all_to_all | solution.py:251
  14.6 3.4 %collective-permute-start.2 = (bf16[4,2,2,16,512]{4,3,2,1,0:T(8,128)(2,1)S(1)}, bf16[4,2,2,16,512]{4,3,2,1,0:T(8,128)(2,1)S(1)}, u32[]{:S(2)}, u32[]{:S(2)}) collective-permute-start(bf16[4,2,2,16,512]{4,3,2,1,0:T(8,128)(2,1)S(1)} %all_to_all.10.own_ref), channel_id=1, source_target_pairs={{0,4},{4,8},{8,12},{12,16},{16,20},{20,24},{24,28},{1,5},{5,9},{9,... | collective-permute-start | bytes 786440 | tf_op jit(solution)/shard_map/ppermute | solution.py:258
  18.0 1.3 %collective-permute-start.3 = (bf16[4,2,2,16,512]{4,3,2,1,0:T(8,128)(2,1)S(1)}, bf16[4,2,2,16,512]{4,3,2,1,0:T(8,128)(2,1)S(1)}, u32[]{:S(2)}, u32[]{:S(2)}) collective-permute-start(bf16[4,2,2,16,512]{4,3,2,1,0:T(8,128)(2,1)S(1)} %all_to_all.10.own_ref), channel_id=1, source_target_pairs={{4,0},{8,4},{12,8},{16,12},{20,16},{24,20},{28,24},{5,1},{9,5},{13... | collective-permute-start | bytes 786440 | tf_op jit(solution)/shard_map/ppermute | solution.py:258
  19.3 4.5 %collective-permute-start = (s32[8,128]{1,0:T(8,128)S(1)}, s32[8,128]{1,0:T(8,128)S(1)}, u32[]{:S(2)}, u32[]{:S(2)}) collective-permute-start(s32[8,128]{1,0:T(8,128)S(1)} %get-tuple-element.10.codes_ref), channel_id=1, source_target_pairs={{0,4},{4,8},{8,12},{12,16},{16,20},{20,24},{24,28},{1,5},{5,9},{9,... | collective-permute-start | bytes 12296 | tf_op jit(solution)/shard_map/ppermute | solution.py:258
  23.9 1.3 %collective-permute-start.1 = (s32[8,128]{1,0:T(8,128)S(1)}, s32[8,128]{1,0:T(8,128)S(1)}, u32[]{:S(2)}, u32[]{:S(2)}) collective-permute-start(s32[8,128]{1,0:T(8,128)S(1)} %get-tuple-element.10.codes_ref), channel_id=1, source_target_pairs={{4,0},{8,4},{12,8},{16,12},{20,16},{24,20},{28,24},{5,1},{9,5},{13... | collective-permute-start | bytes 12296 | tf_op jit(solution)/shard_map/ppermute | solution.py:258
  25.2 0.0 copy-done.4
  25.2 0.0 copy-start.3
  25.2 3.4 %copy-done.3 = bf16[8,2,510,510]{3,1,2,0:T(2,128)(2,1)S(1)} copy-done((bf16[8,2,510,510]{3,1,2,0:T(2,128)(2,1)S(1)}, bf16[8,2,510,510]{3,1,2,0:T(2,128)(2,1)}, u32[]{:S(2)}) %copy-start.3) | copy-done | bytes 8323224
  28.6 7.1 %tables.1 = (bf16[8,512,512]{2,1,0:T(8,128)(2,1)S(1)}, bf16[8,1024,512]{2,1,0:T(8,128)(2,1)}) custom-call(bf16[8,510,2,510]{3,2,1,0:T(2,128)(2,1)S(1)} %bitcast.16, bf16[4080,510]{1,0:T(8,128)(2,1)S(1)} %bitcast.17), custom_call_target="tpu_custom_call" | custom-call | flops 2147483648 | bytes 25165824 | tf_op jit(solution)/shard_map/tables/pallas_call | solution.py:301
  35.7 0.0 collective-permute-done.below_ref
  35.7 0.0 collective-permute-done.1.above_ref
  35.7 1.0 weights.1.weights_ref
  36.7 0.0 collective-permute-done.2.below_ref
  36.7 0.0 collective-permute-done.3.above_ref
  36.7 0.0 copy-start.2
  36.7 3.4 %copy-done.2 = bf16[8,1024,512]{2,1,0:T(8,128)(2,1)S(1)} copy-done((bf16[8,1024,512]{2,1,0:T(8,128)(2,1)S(1)}, bf16[8,1024,512]{2,1,0:T(8,128)(2,1)}, u32[]{:S(2)}) %copy-start.2) | copy-done | bytes 8388632
  40.1 0.0 copy-start.6
  40.1 13.3 %field.1 = bf16[4,2,2,16,512]{4,3,2,1,0:T(8,128)(2,1)} custom-call(bf16[8,256,384]{2,1,0:T(8,128)(2,1)S(1)} %weights.1.weights_ref, bf16[8,512,512]{2,1,0:T(8,128)(2,1)S(1)} %get-tuple-element.11.rot_ref, bf16[8,1024,512]{2,1,0:T(8,128)(2,1)S(1)} %copy-done.2, bf16[4,2,2,16,512]{4,3,2,1,0:T(8,128)(2,1)S(1)} %collective-permute-done.2.below_ref, ...), custom_call_target="tpu_custom_call" | custom-call | tf_op jit(solution)/shard_map/field/pallas_call | solution.py:331
  53.3 3.4 %all-to-all-start.1 = ((bf16[4,2,2,16,512]{4,3,2,1,0:T(8,128)(2,1)}), bf16[4,2,2,16,512]{4,3,2,1,0:T(8,128)(2,1)S(1)}, u32[]{:S(2)}, u32[]{:S(2)}) async-start(bf16[4,2,2,16,512]{4,3,2,1,0:T(8,128)(2,1)} %field.1), calls=%async_computation.1 | async-start | bytes 524288 | tf_op jit(solution)/shard_map/all_to_all | solution.py:251
  56.7 0.0 copy-done.6
  56.8 0.4 reshape.17.mie_ref
  57.1 5.6 %all-to-all-done.1.pieces_ref = bf16[4,2,2,16,512]{4,3,2,1,0:T(8,128)(2,1)S(1)} async-done(((bf16[4,2,2,16,512]{4,3,2,1,0:T(8,128)(2,1)}), bf16[4,2,2,16,512]{4,3,2,1,0:T(8,128)(2,1)S(1)}, u32[]{:S(2)}, u32[]{:S(2)}) %all-to-all-start.1) | async-done | bytes 262176 | tf_op jit(solution)/shard_map/all_to_all | solution.py:251
  62.7 0.0 copy-start.1
  62.7 2.2 %copy-done.1 = f32[8,2,510,128]{3,1,2,0:T(2,128)S(1)} copy-done((f32[8,2,510,128]{3,1,2,0:T(2,128)S(1)}, f32[8,2,510,128]{3,1,2,0:T(2,128)}, u32[]{:S(2)}) %copy-start.1) | copy-done | bytes 4177944
  64.9 2.5 %image.1 = (f32[1024,128]{1,0:T(8,128)S(1)}, f32[8,128]{1,0:T(8,128)S(1)}) custom-call(f32[4,2040,128]{2,1,0:T(8,128)S(1)} %bitcast.14, f32[1020,128]{1,0:T(8,128)S(1)} %reshape.17.mie_ref, bf16[4,2,2,16,512]{4,3,2,1,0:T(8,128)(2,1)S(1)} %all-to-all-done.1.pieces_ref), custom_call_target="tpu_custom_call" | custom-call | tf_op jit(solution)/shard_map/image/pallas_call | solution.py:351
  67.5 0.1 collective-permute-start.4
  67.5 1.2 collective-permute-done.4
  68.7 0.4 collective-permute-start.5
  69.1 3.2 %collective-permute-done.5 = f32[8,128]{1,0:T(8,128)S(1)} collective-permute-done((f32[8,128]{1,0:T(8,128)S(1)}, f32[8,128]{1,0:T(8,128)S(1)}, u32[]{:S(2)}, u32[]{:S(2)}) %collective-permute-start.5) | collective-permute-done | bytes 4128 | tf_op jit(solution)/shard_map/ppermute | solution.py:245
  72.3 3.0 %collective-permute-start.6 = (f32[8,128]{1,0:T(8,128)S(1)}, f32[8,128]{1,0:T(8,128)S(1)}, u32[]{:S(2)}, u32[]{:S(2)}) collective-permute-start(f32[8,128]{1,0:T(8,128)S(1)} %add.20), channel_id=1, source_target_pairs={{0,4},{4,0},{8,12},{12,8},{16,20},{20,16},{24,28},{28,24},{1,5},{5... | collective-permute-start | bytes 12296 | tf_op jit(solution)/shard_map/ppermute | solution.py:245
  75.4 1.6 %collective-permute-done.6 = f32[8,128]{1,0:T(8,128)S(1)} collective-permute-done((f32[8,128]{1,0:T(8,128)S(1)}, f32[8,128]{1,0:T(8,128)S(1)}, u32[]{:S(2)}, u32[]{:S(2)}) %collective-permute-start.6) | collective-permute-done | bytes 4128 | tf_op jit(solution)/shard_map/ppermute | solution.py:245
  77.0 3.5 %collective-permute-start.7 = (f32[8,128]{1,0:T(8,128)S(1)}, f32[8,128]{1,0:T(8,128)S(1)}, u32[]{:S(2)}, u32[]{:S(2)}) collective-permute-start(f32[8,128]{1,0:T(8,128)S(1)} %add.21), channel_id=1, source_target_pairs={{0,8},{4,12},{8,0},{12,4},{16,24},{20,28},{24,16},{28,20},{1,9},{5... | collective-permute-start | bytes 12296 | tf_op jit(solution)/shard_map/ppermute | solution.py:245
  80.4 1.6 %collective-permute-done.7 = f32[8,128]{1,0:T(8,128)S(1)} collective-permute-done((f32[8,128]{1,0:T(8,128)S(1)}, f32[8,128]{1,0:T(8,128)S(1)}, u32[]{:S(2)}, u32[]{:S(2)}) %collective-permute-start.7) | collective-permute-done | bytes 4128 | tf_op jit(solution)/shard_map/ppermute | solution.py:245
  82.0 3.0 %collective-permute-start.8 = (f32[8,128]{1,0:T(8,128)S(1)}, f32[8,128]{1,0:T(8,128)S(1)}, u32[]{:S(2)}, u32[]{:S(2)}) collective-permute-start(f32[8,128]{1,0:T(8,128)S(1)} %add.22), channel_id=1, source_target_pairs={{0,16},{4,20},{8,24},{12,28},{16,0},{20,4},{24,8},{28,12},{1,17},{... | collective-permute-start | bytes 12296 | tf_op jit(solution)/shard_map/ppermute | solution.py:245
  85.0 1.6 %collective-permute-done.8 = f32[8,128]{1,0:T(8,128)S(1)} collective-permute-done((f32[8,128]{1,0:T(8,128)S(1)}, f32[8,128]{1,0:T(8,128)S(1)}, u32[]{:S(2)}, u32[]{:S(2)}) %collective-permute-start.8) | collective-permute-done | bytes 4128 | tf_op jit(solution)/shard_map/ppermute | solution.py:245
  86.6 2.4 %remainder.1 = (f32[1020,128]{1,0:T(8,128)S(1)}, f32[8,128]{1,0:T(8,128)S(1)}) custom-call(f32[8,128]{1,0:T(8,128)S(1)} %add_multiply_fusion.dots_ref, f32[4,2040,128]{2,1,0:T(8,128)S(1)} %bitcast.15, f32[1024,128]{1,0:T(8,128)S(1)} %get-tuple-element.15.image_ref), custom_call_target="tpu_custom_call" | custom-call | tf_op jit(solution)/shard_map/remainder/pallas_call | solution.py:369
  89.0 0.5 slice.7
  89.6 6.4 %psum.14 = f32[]{:T(128)} all-reduce(f32[]{:T(128)} %bitcast.9), channel_id=1, replica_groups=mesh['blk'=8,'pair'=4] {'pair'}, use_global_device_ids=true, to_apply=%region_0.0 | all-reduce | flops 1 | bytes 8 | tf_op jit(solution)/shard_map/psum | solution.py:383
  95.9 21.1 %psum.15 = f32[]{:T(128)} all-reduce(f32[]{:T(128)} %psum.14), channel_id=1, replica_groups=mesh['blk'=8,'pair'=4] {'blk'}, use_global_device_ids=true, to_apply=%region_1.0 | all-reduce | flops 1 | bytes 8 | tf_op jit(solution)/shard_map/psum | solution.py:383
  117.8 1.1 reshape.19
  118.9 0.6 copy.8
  (7 shorter events, 0.1 us)
Async XLA Ops:
  1.3 2.2 %copy-start = (f32[8,2,510,128]{3,1,2,0:T(2,128)S(1)}, f32[8,2,510,128]{3,1,2,0:T(2,128)}, u32[]{:S(2)}) copy-start(f32[8,2,510,128]{3,1,2,0:T(2,128)} %param.6) | copy-start | bytes 12533764
  3.5 0.7 copy-start.5
  4.1 21.1 %copy-start.4 = (bf16[8,510,510]{2,0,1:T(8,128)(2,1)S(1)}, bf16[8,510,510]{2,0,1:T(8,128)(2,1)}, u32[]{:S(2)}) copy-start(bf16[8,510,510]{2,0,1:T(8,128)(2,1)} %param.8) | copy-start | bytes 12484804
  14.6 22.1 %collective-permute-start.2 = (bf16[4,2,2,16,512]{4,3,2,1,0:T(8,128)(2,1)S(1)}, bf16[4,2,2,16,512]{4,3,2,1,0:T(8,128)(2,1)S(1)}, u32[]{:S(2)}, u32[]{:S(2)}) collective-permute-start(bf16[4,2,2,16,512]{4,3,2,1,0:T(8,128)(2,1)S(1)} %all_to_all.10.own_ref), channel_id=1, source_target_pairs={{0,4},{4,8},{8,12},{12,16},{16,20},{20,24},{24,28},{1,5},{5,9},{9,... | collective-permute-start | bytes 786440 | tf_op jit(solution)/shard_map/ppermute | solution.py:258
  18.0 18.6 %collective-permute-start.3 = (bf16[4,2,2,16,512]{4,3,2,1,0:T(8,128)(2,1)S(1)}, bf16[4,2,2,16,512]{4,3,2,1,0:T(8,128)(2,1)S(1)}, u32[]{:S(2)}, u32[]{:S(2)}) collective-permute-start(bf16[4,2,2,16,512]{4,3,2,1,0:T(8,128)(2,1)S(1)} %all_to_all.10.own_ref), channel_id=1, source_target_pairs={{4,0},{8,4},{12,8},{16,12},{20,16},{24,20},{28,24},{5,1},{9,5},{13... | collective-permute-start | bytes 786440 | tf_op jit(solution)/shard_map/ppermute | solution.py:258
  19.3 16.4 %collective-permute-start = (s32[8,128]{1,0:T(8,128)S(1)}, s32[8,128]{1,0:T(8,128)S(1)}, u32[]{:S(2)}, u32[]{:S(2)}) collective-permute-start(s32[8,128]{1,0:T(8,128)S(1)} %get-tuple-element.10.codes_ref), channel_id=1, source_target_pairs={{0,4},{4,8},{8,12},{12,16},{16,20},{20,24},{24,28},{1,5},{5,9},{9,... | collective-permute-start | bytes 12296 | tf_op jit(solution)/shard_map/ppermute | solution.py:258
  23.9 11.8 %collective-permute-start.1 = (s32[8,128]{1,0:T(8,128)S(1)}, s32[8,128]{1,0:T(8,128)S(1)}, u32[]{:S(2)}, u32[]{:S(2)}) collective-permute-start(s32[8,128]{1,0:T(8,128)S(1)} %get-tuple-element.10.codes_ref), channel_id=1, source_target_pairs={{4,0},{8,4},{12,8},{16,12},{20,16},{24,20},{28,24},{5,1},{9,5},{13... | collective-permute-start | bytes 12296 | tf_op jit(solution)/shard_map/ppermute | solution.py:258
  25.2 3.4 %copy-start.3 = (bf16[8,2,510,510]{3,1,2,0:T(2,128)(2,1)S(1)}, bf16[8,2,510,510]{3,1,2,0:T(2,128)(2,1)}, u32[]{:S(2)}) copy-start(bf16[8,2,510,510]{3,1,2,0:T(2,128)(2,1)} %param.9) | copy-start | bytes 24969604
  36.7 3.4 %copy-start.2 = (bf16[8,1024,512]{2,1,0:T(8,128)(2,1)S(1)}, bf16[8,1024,512]{2,1,0:T(8,128)(2,1)}, u32[]{:S(2)}) copy-start(bf16[8,1024,512]{2,1,0:T(8,128)(2,1)} %get-tuple-element.12.axial_ref) | copy-start | bytes 25165828
  40.1 16.7 %copy-start.6 = (f32[2,510,128]{2,0,1:T(2,128)S(1)}, f32[2,510,128]{2,0,1:T(2,128)}, u32[]{:S(2)}) copy-start(f32[2,510,128]{2,0,1:T(2,128)} %param.7) | copy-start | bytes 1566724
  53.3 9.4 %all-to-all-start.1 = ((bf16[4,2,2,16,512]{4,3,2,1,0:T(8,128)(2,1)}), bf16[4,2,2,16,512]{4,3,2,1,0:T(8,128)(2,1)S(1)}, u32[]{:S(2)}, u32[]{:S(2)}) async-start(bf16[4,2,2,16,512]{4,3,2,1,0:T(8,128)(2,1)} %field.1), calls=%async_computation.1 | async-start | bytes 524288 | tf_op jit(solution)/shard_map/all_to_all | solution.py:251
  62.7 2.2 %copy-start.1 = (f32[8,2,510,128]{3,1,2,0:T(2,128)S(1)}, f32[8,2,510,128]{3,1,2,0:T(2,128)}, u32[]{:S(2)}) copy-start(f32[8,2,510,128]{3,1,2,0:T(2,128)} %param.6) | copy-start | bytes 12533764
  67.5 1.2 %collective-permute-start.4 = (f32[8,128]{1,0:T(8,128)S(1)}, f32[8,128]{1,0:T(8,128)S(1)}, u32[]{:S(2)}, u32[]{:S(2)}) collective-permute-start(f32[8,128]{1,0:T(8,128)S(1)} %get-tuple-element.14), channel_id=1, source_target_pairs={{0,1},{1,0},{2,3},{3,2},{4,5},{5,4},{6,7},{7,6},{8,9},{9,8},{10,11... | collective-permute-start | bytes 12296 | tf_op jit(solution)/shard_map/ppermute | solution.py:245
  68.7 3.6 %collective-permute-start.5 = (f32[8,128]{1,0:T(8,128)S(1)}, f32[8,128]{1,0:T(8,128)S(1)}, u32[]{:S(2)}, u32[]{:S(2)}) collective-permute-start(f32[8,128]{1,0:T(8,128)S(1)} %add.19), channel_id=1, source_target_pairs={{0,2},{1,3},{2,0},{3,1},{4,6},{5,7},{6,4},{7,5},{8,10},{9,11},{10,... | collective-permute-start | bytes 12296 | tf_op jit(solution)/shard_map/ppermute | solution.py:245
  72.3 4.6 %collective-permute-start.6 = (f32[8,128]{1,0:T(8,128)S(1)}, f32[8,128]{1,0:T(8,128)S(1)}, u32[]{:S(2)}, u32[]{:S(2)}) collective-permute-start(f32[8,128]{1,0:T(8,128)S(1)} %add.20), channel_id=1, source_target_pairs={{0,4},{4,0},{8,12},{12,8},{16,20},{20,16},{24,28},{28,24},{1,5},{5... | collective-permute-start | bytes 12296 | tf_op jit(solution)/shard_map/ppermute | solution.py:245
  77.0 5.0 %collective-permute-start.7 = (f32[8,128]{1,0:T(8,128)S(1)}, f32[8,128]{1,0:T(8,128)S(1)}, u32[]{:S(2)}, u32[]{:S(2)}) collective-permute-start(f32[8,128]{1,0:T(8,128)S(1)} %add.21), channel_id=1, source_target_pairs={{0,8},{4,12},{8,0},{12,4},{16,24},{20,28},{24,16},{28,20},{1,9},{5... | collective-permute-start | bytes 12296 | tf_op jit(solution)/shard_map/ppermute | solution.py:245
  82.0 4.6 %collective-permute-start.8 = (f32[8,128]{1,0:T(8,128)S(1)}, f32[8,128]{1,0:T(8,128)S(1)}, u32[]{:S(2)}, u32[]{:S(2)}) collective-permute-start(f32[8,128]{1,0:T(8,128)S(1)} %add.22), channel_id=1, source_target_pairs={{0,16},{4,20},{8,24},{12,28},{16,0},{20,4},{24,8},{28,12},{1,17},{... | collective-permute-start | bytes 12296 | tf_op jit(solution)/shard_map/ppermute | solution.py:245

commit v2 on v1

v2 whole, which is shorter than its diff:
```python
import functools

import jax
import jax.numpy as jnp
from jax import lax
from jax.experimental import pallas as pl
from jax.experimental.pallas import tpu as pltpu
from jax.sharding import PartitionSpec as P

MIB = 1024 * 1024
F32 = jnp.float32
BF16 = jnp.bfloat16


def params(mib):
    return pltpu.CompilerParams(vmem_limit_bytes=mib * MIB)


def whole():
    return pl.BlockSpec(memory_space=pltpu.VMEM)


def in_hbm(value):
    return pltpu.with_memory_space_constraint(value, pltpu.HBM)


def rounded_up(value, unit):
    return (value + unit - 1) // unit * unit


def iota(shape, dim):
    return lax.broadcasted_iota(jnp.int32, shape, dim)


def dot_nn(left, right):
    return lax.dot_general(left, right, (((1,), (0,)), ((), ())), preferred_element_type=F32)


def dot_nt(left, right):
    return lax.dot_general(left, right, (((1,), (1,)), ((), ())), preferred_element_type=F32)


def pack_kernel(quarter, modes, ways, own, pair_rows_ref, count_ref, basis_ref, out_ref, lines_ref, pad_ref, codes_ref, sem):
    full, columns = lines_ref.shape
    rows = quarter * modes
    part = columns // 2 // ways
    copy = pltpu.make_async_copy(basis_ref.at[basis_ref.shape[0] - 1, pl.ds(2 * rows - full, full)], lines_ref, sem)
    copy.start()
    slots = pair_rows_ref.shape[2]
    live = iota((1, slots), 1) < count_ref[0]
    marks = jnp.where(live, own * (pair_rows_ref[2] + 1) + pair_rows_ref[0], 0)
    line = iota((slots, slots), 0)
    stacked = jnp.where(line == 0, marks, jnp.where(line == 1, pair_rows_ref[1], 0))
    turned = jnp.transpose(stacked.astype(F32))
    codes_ref[0:slots, :] = turned
    codes_ref[slots : 2 * slots, :] = pltpu.roll(turned, slots - 1, axis=1)
    share = 2 * quarter * part
    mine = codes_ref[pl.ds(pl.multiple_of(lax.axis_index("pair") * share, share), share), :][:, 0:1]
    pad_ref[...] = jnp.zeros_like(pad_ref)
    copy.wait()
    for j in range(quarter):
        pad_ref[0:modes, :] = lines_ref[pl.ds(full - rows + j, modes, quarter), :]
        turned = jnp.transpose(pad_ref[...])
        for c in range(2):
            codes = mine[(c * quarter + j) * part : (c * quarter + j + 1) * part]
            for p in range(ways):
                row = c * (columns // 2) + p * part
                piece = turned[row : row + part]
                out_ref[p, c, j] = jnp.where(iota(piece.shape, 1) == modes, codes, piece).astype(BF16)


def tables_kernel(modes, tables, axial_ref, rot_ref, rot_out_ref, axial_out_ref, lines_ref):
    step = pl.program_id(0)
    size = rot_out_ref.shape[1]
    chunk = 256

    @pl.when(step == 0)
    def _():
        rot_out_ref[...] = jnp.zeros_like(rot_out_ref)
        lines_ref[...] = jnp.zeros_like(lines_ref)

    out_row, in_row = iota((chunk, chunk), 0), iota((chunk, chunk), 1)
    each = chunk // 2
    halves = (in_row == 2 * lax.rem(out_row, each) + lax.div(out_row, each)).astype(F32).astype(BF16)
    lines_ref[0 : 2 * modes, 0:modes] = axial_ref[0].reshape(2 * modes, modes)
    for q in range(2 * size // chunk):
        sorted_rows = dot_nn(halves, lines_ref[q * chunk : (q + 1) * chunk, :]).astype(BF16)
        for c in range(2):
            axial_out_ref[0, c * size + q * each : c * size + (q + 1) * each, :] = sorted_rows[c * each : (c + 1) * each]
    each = chunk // tables
    entries = (in_row == tables * lax.rem(out_row, each) + lax.div(out_row, each)).astype(F32).astype(BF16)
    block = rot_ref.shape[0]
    left = tables * modes - step * block
    rows = jnp.where(iota((block, modes), 0) < left, rot_ref[...], jnp.zeros((), BF16))
    for q in range(block // chunk):
        sorted_rows = dot_nn(entries, rows[q * chunk : (q + 1) * chunk]).astype(BF16)
        start = pl.multiple_of(step * (block // tables) + q * each, each)
        for g in range(tables):
            rot_out_ref[g, pl.ds(start, each), 0:modes] = sorted_rows[g * each : (g + 1) * each]


def weights_kernel(own, part, modes, below_ref, own_ref, above_ref, out_ref):
    tables = out_ref.shape[0]
    group = own * part
    size = own_ref.shape[4]
    lane = modes % 128
    wanted = lax.div(iota((tables * group, group), 0), part) + own

    def lists(ref):
        values = ref[:, :, :, :, size - 128 : size].reshape(2 * group, 128).astype(F32)
        marks, sources = values[:group], values[group:]
        lines = [jnp.transpose(side)[lane : lane + 1].astype(jnp.int32) for side in (marks, sources)]
        return lines, [side[:, lane : lane + 1].astype(jnp.int32) for side in (marks, sources)]

    def one_hot(hit):
        return jnp.where(hit, 1.0, 0.0).astype(BF16)

    def store(direction, first, counts):
        lanes = counts.shape[1]
        same = lax.rem(iota(counts.shape, 0), part) == lax.rem(iota(counts.shape, 1), part)
        kept = jnp.where(same, counts, 0.0).astype(BF16)
        for g in range(tables):
            out_ref[g, direction * group : (direction + 1) * group, first : first + lanes] = kept[g * group : (g + 1) * group]

    for window, ref in enumerate((below_ref, own_ref, above_ref)):
        (marks, sources), (marks_column, sources_column) = lists(ref)
        if window == 1:
            spread = one_hot(sources_column == lax.div(iota((group, 3 * group), 1), part))
            store(0, 0, dot_nn(one_hot(marks == wanted), spread))
        block = sources - (2 - window) * own
        inside = (block >= 0) & (block < own) & (marks >= own)
        hits = one_hot(jnp.where(inside, lax.div(marks, own) * own + block, -1) == wanted)
        spread = one_hot(lax.rem(marks_column, own) == lax.div(iota((group, group), 1), part))
        store(1, window * group, dot_nn(hits, spread))


def swapped(value):
    half = value.shape[0] // 2
    return jnp.concatenate([-value[half:], value[:half]], axis=0)


def field_kernel(weights_ref, rot_ref, axial_ref, below_ref, own_ref, above_ref, out_ref, window_ref, total_ref):
    step = pl.program_id(0)
    group = weights_ref.shape[1] // 2
    size = window_ref.shape[2]

    @pl.when(step == 0)
    def _():
        for w, ref in enumerate((below_ref, own_ref, above_ref)):
            for c in range(2):
                window_ref[c, w * group : (w + 1) * group, :] = ref[:, c].reshape(group, size)
        total_ref[...] = jnp.zeros_like(total_ref)

    weights = weights_ref[0]
    real = dot_nn(weights, window_ref[0]).astype(BF16)
    imag = dot_nn(weights, window_ref[1]).astype(BF16)
    sums = jnp.concatenate([real[:group], imag[:group], real[group:], imag[group:]], axis=0)
    rotation = rot_ref[0]
    turned = dot_nt(sums, rotation).astype(BF16)
    forward, backward = turned[: 2 * group], turned[2 * group :]
    moved = dot_nt(forward, axial_ref[0, :size]) + dot_nt(swapped(forward), axial_ref[0, size:])
    moved += dot_nn(jnp.concatenate([backward, swapped(backward)], axis=1), axial_ref[0])
    total_ref[...] += dot_nn(moved.astype(BF16), rotation)

    @pl.when(step == pl.num_programs(0) - 1)
    def _():
        for c in range(2):
            out_ref[:, c] = total_ref[c * group : (c + 1) * group].astype(BF16).reshape(out_ref[:, c].shape)


def lane_swap(value):
    half = value.shape[1] // 2
    rolled = pltpu.roll(value, half, axis=1)
    return jnp.where(iota(value.shape, 1) < half, -rolled, rolled)


def folded(value):
    return jnp.sum(value.reshape(value.shape[0] // 8, 8, value.shape[1]), axis=0)


def gram_kernel(quarter, modes, basis_ref, aligned_ref, gram_ref, blocks_ref, sums_ref, sems):
    vectors, full, columns = aligned_ref.shape
    rows = quarter * modes
    copies = [pltpu.make_async_copy(basis_ref.at[i], blocks_ref.at[i], sems.at[i]) for i in range(vectors // 2)]
    for copy in copies:
        copy.start()
    sums_ref[...] = jnp.zeros_like(sums_ref)
    for i, copy in enumerate(copies):
        copy.wait()
        for side in range(2):
            aligned_ref[2 * i + side, 0:rows, :] = blocks_ref[i, side * rows : (side + 1) * rows, :]
            aligned_ref[2 * i + side, rows:full, :] = jnp.zeros((full - rows, columns), F32)
    chunk = 32

    def body(i, carry):
        here = pl.ds(pl.multiple_of(i * chunk, chunk), chunk)
        values = [aligned_ref[k, here, :] for k in range(vectors)]
        for l in range(vectors):
            other = lane_swap(values[l])
            for k in range(l + 1):
                sums_ref[0, l, k] += folded(values[k] * values[l])
                if k < l:
                    sums_ref[1, l, k] -= folded(values[k] * other)
        return carry

    lax.fori_loop(0, full // chunk, body, 0)
    totals = jnp.sum(jnp.sum(sums_ref[...].reshape(2 * vectors * vectors, 8, columns), axis=1), axis=1, keepdims=True)
    lane = iota(gram_ref.shape, 1)
    tile = jnp.zeros(gram_ref.shape, F32)
    for l in range(2 * vectors):
        tile = jnp.where(lane == l, totals[l * vectors : (l + 1) * vectors], tile)
    gram_ref[...] = tile


def image_kernel(quarter, modes, aligned_ref, gram_ref, mie_ref, pieces_ref, image_ref, sums_ref, lines_ref):
    vectors, full, columns = aligned_ref.shape
    rows = quarter * modes
    ways, _, _, part, size = pieces_ref.shape
    lines_ref[rows:full, :] = jnp.zeros((full - rows, columns), F32)
    for j in range(quarter):
        turned = jnp.concatenate([pieces_ref[:, c, j].reshape(ways * part, size) for c in range(2)], axis=0)
        lines_ref[pl.ds(j, modes, quarter), :] = jnp.transpose(turned.astype(F32))[:modes]
    half = columns // 2
    chunk = 64
    totals = [jnp.zeros((8, columns), F32) for _ in range(2 * vectors + 1)]
    for first in range(0, full, chunk):
        count = min(chunk, rows - first)
        here = slice(first, first + chunk)
        field = lines_ref[here, :]
        mie = mie_ref[first : first + count, :]
        if count < chunk:
            mie = jnp.concatenate([mie, jnp.zeros((chunk - count, columns), F32)], axis=0)
        left = iota(mie.shape, 1) < half
        other = pltpu.roll(mie, half, axis=1)
        product = jnp.where(left, mie, other) * field + jnp.where(left, -other, mie) * pltpu.roll(field, half, axis=1)
        image = aligned_ref[vectors - 1, here, :] - product
        image_ref[here, :] = image
        turned = lane_swap(image)
        for k in range(vectors):
            values = aligned_ref[k, here, :]
            totals[k] += folded(values * image)
            totals[vectors + k] -= folded(values * turned)
        totals[2 * vectors] += folded(image * image)
    lane = iota(gram_ref.shape, 1)
    tile = gram_ref[...]
    for part_index in range(2):
        stacked = jnp.stack(totals[part_index * vectors : (part_index + 1) * vectors], axis=0)
        column = jnp.sum(jnp.sum(stacked, axis=1), axis=1, keepdims=True)
        tile = jnp.where(lane == 2 * vectors + part_index, column, tile)
    square = jnp.sum(totals[2 * vectors], axis=(0, 1), keepdims=True)
    tile = jnp.where((lane == 2 * vectors + 2) & (iota(tile.shape, 0) == 0), square, tile)
    sums_ref[...] = jnp.broadcast_to(tile[None], sums_ref.shape)


def remainder_kernel(quarter, modes, mean_scale, sums_ref, aligned_ref, image_ref, dots_ref, out_ref):
    vectors, full, columns = aligned_ref.shape
    rows = quarter * modes
    total = jnp.sum(sums_ref[...], axis=0)
    row, lane = iota(total.shape, 0), iota(total.shape, 1)

    def lane_at(index):
        return jnp.sum(jnp.where(lane == index, total, 0.0), axis=1, keepdims=True)

    def on_lanes(column, first):
        return jnp.sum(jnp.where(row + first == lane, column, 0.0), axis=0, keepdims=True)

    real, imag = lane_at(2 * vectors) * mean_scale, lane_at(2 * vectors + 1) * mean_scale
    real_line, imag_line = on_lanes(real, 0), on_lanes(imag, 0)
    dots_ref[0:1, :] = real_line[:, :vectors]
    dots_ref[1:2, :] = imag_line[:, :vectors]
    same = jnp.where(lane < vectors, real * real_line + imag * imag_line, 0.0)
    cross = imag * on_lanes(real, vectors) - real * on_lanes(imag, vectors)
    cross = jnp.where((lane >= vectors) & (lane < 2 * vectors), cross, 0.0)
    often = jnp.where(row == lane, 1.0, 2.0)
    spread = jnp.sum(total * often * (same + cross), axis=(0, 1), keepdims=True)
    square = lane_at(2 * vectors + 2)[0:1]
    inside = jnp.sum(real * real + imag * imag, axis=0, keepdims=True)
    norm_square = (square + spread) * mean_scale - 2.0 * inside
    scale = lax.rsqrt(norm_square)
    image_scale = jnp.broadcast_to(scale, (8, columns))
    reals = [jnp.broadcast_to(real[k : k + 1] * scale, (8, columns)) for k in range(vectors)]
    imags = [jnp.broadcast_to(imag[k : k + 1] * scale, (8, columns)) for k in range(vectors)]
    chunk = 64
    for first in range(0, full, chunk):
        here = slice(first, first + chunk)
        values = [aligned_ref[k, here, :].reshape(chunk // 8, 8, columns) for k in range(vectors)]
        along = image_ref[here, :].reshape(chunk // 8, 8, columns) * image_scale
        turned = jnp.zeros_like(along)
        for k in range(vectors):
            along -= reals[k] * values[k]
            turned += imags[k] * values[k]
        result = along.reshape(chunk, columns) - lane_swap(turned.reshape(chunk, columns))
        count = min(chunk, rows - first)
        height = out_ref.shape[1]
        out_ref[first // height : (first + count) // height] = result.reshape(chunk // height, height, columns)[: count // height]


def exchanged(value):
    return lax.all_to_all(value, "pair", split_axis=0, concat_axis=0, tiled=True)


def neighbours(value):
    count = lax.axis_size("blk")
    up = [(i, i + 1) for i in range(count - 1)]
    down = [(j, i) for i, j in up]
    return lax.ppermute(value, "blk", up), lax.ppermute(value, "blk", down)


def shards(basis, mie_coeffs, rot_table, axial_table, pair_table, pair_count):
    vectors, quarter, modes, columns = basis.shape
    ways = lax.axis_size("pair")
    blk_ways = lax.axis_size("blk")
    tables = rot_table.shape[0]
    slots = pair_table.shape[1]
    own = quarter * ways
    part = columns // 2 // ways
    group = own * part
    size = rounded_up(modes, 128)
    rows = quarter * modes
    full = rounded_up(rows, 8)
    pairs_of_vectors = vectors // 2

    basis_rows = in_hbm(basis.transpose(0, 2, 1, 3).reshape(pairs_of_vectors, 2 * rows, columns))
    mie_rows = mie_coeffs.transpose(1, 0, 2).reshape(rows, columns)
    rot_rows = in_hbm(rot_table.transpose(1, 0, 2).reshape(modes * tables, modes))
    axial_rows = in_hbm(axial_table.transpose(0, 2, 1, 3))
    pair_rows = pair_table.transpose(2, 0, 1)

    pieces_shape = (ways, 2, quarter, part, size)
    pieces = pl.pallas_call(
        functools.partial(pack_kernel, quarter, modes, ways, own),
        in_specs=[whole(), pl.BlockSpec(memory_space=pltpu.SMEM), pl.BlockSpec(memory_space=pltpu.HBM)],
        out_specs=whole(),
        out_shape=jax.ShapeDtypeStruct(pieces_shape, BF16),
        scratch_shapes=[
            pltpu.VMEM((full, columns), F32),
            pltpu.VMEM((size, columns), F32),
            pltpu.VMEM((2 * slots, slots), F32),
            pltpu.SemaphoreType.DMA,
        ],
        compiler_params=params(16),
        name="pack",
    )(pair_rows, pair_count, basis_rows)
    own_pieces = exchanged(pieces)

    rotations, axials = pl.pallas_call(
        functools.partial(tables_kernel, modes, tables),
        grid=(tables,),
        in_specs=[
            pl.BlockSpec((1, modes, 2, modes), lambda g: (g, 0, 0, 0)),
            pl.BlockSpec((size, modes), lambda g: (g, 0)),
        ],
        out_specs=[
            pl.BlockSpec((tables, size, size), lambda g: (0, 0, 0)),
            pl.BlockSpec((1, 2 * size, size), lambda g: (g, 0, 0)),
        ],
        out_shape=[
            jax.ShapeDtypeStruct((tables, size, size), BF16),
            jax.ShapeDtypeStruct((tables, 2 * size, size), BF16),
        ],
        scratch_shapes=[pltpu.VMEM((2 * size, size), BF16)],
        compiler_params=params(32),
        cost_estimate=pl.CostEstimate(flops=tables * 8 * 256 * 256 * size, bytes_accessed=6 * tables * size * size * 2, transcendentals=0),
        name="tables",
    )(axial_rows, rot_rows)
    own_pieces, rotations, axials = lax.optimization_barrier((own_pieces, rotations, axials))
    below, above = neighbours(own_pieces)

    aligned, gram = pl.pallas_call(
        functools.partial(gram_kernel, quarter, modes),
        in_specs=[pl.BlockSpec(memory_space=pltpu.HBM)],
        out_specs=[whole(), whole()],
        out_shape=[jax.ShapeDtypeStruct((vectors, full, columns), F32), jax.ShapeDtypeStruct((vectors, 128), F32)],
        scratch_shapes=[
            pltpu.VMEM((pairs_of_vectors, 2 * rows, columns), F32),
            pltpu.VMEM((2, vectors, vectors, 8, columns), F32),
            pltpu.SemaphoreType.DMA((pairs_of_vectors,)),
        ],
        compiler_params=params(16),
        name="gram",
    )(basis_rows)
    below, above, aligned, gram = lax.optimization_barrier((below, above, aligned, gram))

    weights = pl.pallas_call(
        functools.partial(weights_kernel, own, part, modes),
        in_specs=[whole()] * 3,
        out_specs=whole(),
        out_shape=jax.ShapeDtypeStruct((tables, 2 * group, 3 * group), BF16),
        compiler_params=params(24),
        name="weights",
    )(below, own_pieces, above)

    field = pl.pallas_call(
        field_kernel,
        grid=(tables,),
        in_specs=[
            pl.BlockSpec((1, 2 * group, 3 * group), lambda g: (g, 0, 0)),
            pl.BlockSpec((1, size, size), lambda g: (g, 0, 0)),
            pl.BlockSpec((1, 2 * size, size), lambda g: (g, 0, 0)),
            whole(),
            whole(),
            whole(),
        ],
        out_specs=whole(),
        out_shape=jax.ShapeDtypeStruct(pieces_shape, BF16),
        scratch_shapes=[pltpu.VMEM((2, 3 * group, size), BF16), pltpu.VMEM((2 * group, size), F32)],
        compiler_params=params(24),
        name="field",
    )(weights, rotations, axials, below, own_pieces, above)
    field_pieces = exchanged(field)

    devices = ways * blk_ways
    image, sums = pl.pallas_call(
        functools.partial(image_kernel, quarter, modes),
        in_specs=[whole()] * 4,
        out_specs=[whole(), whole()],
        out_shape=[jax.ShapeDtypeStruct((full, columns), F32), jax.ShapeDtypeStruct((devices, vectors, 128), F32)],
        scratch_shapes=[pltpu.VMEM((full, columns), F32)],
        compiler_params=params(16),
        name="image",
    )(aligned, gram, mie_rows, field_pieces)
    sums = lax.all_to_all(sums, ("blk", "pair"), split_axis=0, concat_axis=0, tiled=True)

    mean_scale = 1.0 / (own * blk_ways * modes * columns)
    height = 4
    dots, next_rows = pl.pallas_call(
        functools.partial(remainder_kernel, quarter, modes, mean_scale),
        in_specs=[whole()] * 3,
        out_specs=[whole(), whole()],
        out_shape=[jax.ShapeDtypeStruct((2, vectors), F32), jax.ShapeDtypeStruct((rows // height, height, columns), F32)],
        compiler_params=params(16),
        name="remainder",
    )(sums, aligned, image)
    return dots, next_rows.reshape(modes, quarter, columns).transpose(1, 0, 2)


def solution(mesh):
    placed = (
        P(None, ("blk", "pair"), None, None),
        P(("blk", "pair"), None, None),
        P(),
        P(),
        P("blk", None, None),
        P("blk"),
    )
    return jax.shard_map(
        shards,
        mesh=mesh,
        in_specs=placed,
        out_specs=(P(), P(("blk", "pair"), None, None)),
        check_vma=False,
    )
```

time: 120 us -> 85.5 us (0.71)
  blocking collectives: 37.8 us -> 13.9 us
  starting transfers between devices: 23.9 us -> 13.3 us
  Pallas kernels: 26.4 us -> 34.5 us
  waiting for transfers between devices: 14.8 us -> 8.09 us
    psum x2 -> x0, blocking collectives: 27.5 us -> none  [shards(): norm_square = lax.psum(lax.psum(squares[0, 0], 'pair'), 'blk') * mean_scale]
    ppermute x5 -> x0, starting transfers between devices: 9.98 us -> none  [butterfly(): lax.ppermute(value, axis, [(i, i ^ distance) for i in range(count)])]
    ppermute x5 -> x0, waiting for transfers between devices: 9.15 us -> none  [butterfly(): lax.ppermute(value, axis, [(i, i ^ distance) for i in range(count)])]
    pallas_call x4 -> x5, Pallas kernels: 6.03 us -> 11.8 us  [the longest x1 6.04 us: shards(): pl.pallas_call(functools.partial(gram_kernel, quarter, modes), in_specs=[...]
    ppermute x4 -> x2, starting transfers between devices: 10.6 us -> 5.65 us  [neighbours(): return (lax.ppermute(value, 'blk', up), lax.ppermute(value, 'blk', down))]
    all_to_all x1 -> x2, starting transfers between devices: 3.41 us -> 7.63 us  [exchanged(): lax.all_to_all(value, 'pair', split_axis=0, concat_axis=0, tiled=True)]
    all_to_all x1, blocking collectives: 10.3 us -> 13.9 us  [shards(): lax.all_to_all(sums, ('blk', 'pair'), split_axis=0, concat_axis=0, tiled=...]
    ppermute x4 -> x2, waiting for transfers between devices: 0.01 us -> 2.47 us  [neighbours(): return (lax.ppermute(value, 'blk', up), lax.ppermute(value, 'blk', down))]
  transfers between devices with their start and end apart: 10 -> 4, of which waited for: 6 -> 2; matrix products, arithmetic and copies ran while one was open for 0% -> 0% of each run, Pallas kernels for 7% -> 18%
where the time goes in v2:
time: 85.5 us; the launch traced here: 84.9 us
  Pallas kernels  34.5 us (40%)
  blocking collectives  13.9 us (16%)
  local copies, waits for them, and re-layouts  13.7 us (16%)
  starting transfers between devices  13.3 us (16%)
  waiting for transfers between devices  8.09 us (9%)
  between operations  1.4 us (2%)
    all_to_all x1, blocking collectives, shards(): lax.all_to_all(sums, ('blk', 'pair'), split_axis=0, concat_axis=0, tiled=...  13.9 us
    unnamed x16, local copies, waits for them, and re-layouts  13.4 us
    pallas_call x1, Pallas kernels, shards(): pl.pallas_call(field_kernel, grid=(tables,), in_specs=[pl.BlockSpec((1, 2...  13.3 us
    pallas_call x1, Pallas kernels, shards(): pl.pallas_call(functools.partial(tables_kernel, modes, tables), grid=(tab...  9.46 us
    all_to_all x2, starting transfers between devices, exchanged(): lax.all_to_all(value, 'pair', split_axis=0, concat_axis=0, tiled=True)  7.63 us
    pallas_call x1, Pallas kernels, shards(): pl.pallas_call(functools.partial(gram_kernel, quarter, modes), in_specs=[...  6.04 us
    ppermute x2, starting transfers between devices, neighbours(): return (lax.ppermute(value, 'blk', up), lax.ppermute(value, 'blk', down))  5.65 us
    all_to_all x2, waiting for transfers between devices, exchanged(): lax.all_to_all(value, 'pair', split_axis=0, concat_axis=0, tiled=True)  5.63 us
  transfers between devices with their start and end apart: 4, of which 2 were waited for; matrix products, arithmetic and copies ran while one was open for 0% of the time, Pallas kernels for 18%

profile of v2, /device:TPU:0, one launch (start us, length us, event | category | flops | bytes accessed | tf_op | source)
XLA Modules:
  0.0 84.9 jit_solution(13862358293827767370)
XLA Ops:
  1.3 0.0 copy-start.6
  1.3 0.7 copy-done.6
  2.0 1.9 %pack.1 = bf16[4,2,2,16,512]{4,3,2,1,0:T(8,128)(2,1)} custom-call(s32[3,1,128]{2,1,0:T(1,128)S(1)} %bitcast.12, s32[1]{0:T(128)S(6)} %copy.8.count_ref, f32[4,2040,128]{2,1,0:T(8,128)} %bitcast.13), custom_call_target="tpu_custom_call" | custom-call | tf_op jit(solution)/shard_map/pack/pallas_call | solution.py:330
  3.9 4.2 %all-to-all-start = ((bf16[4,2,2,16,512]{4,3,2,1,0:T(8,128)(2,1)}), bf16[4,2,2,16,512]{4,3,2,1,0:T(8,128)(2,1)S(1)}, u32[]{:S(2)}, u32[]{:S(2)}) async-start(bf16[4,2,2,16,512]{4,3,2,1,0:T(8,128)(2,1)} %pack.1), calls=%async_computation | async-start | bytes 524288 | tf_op jit(solution)/shard_map/all_to_all | solution.py:299
  8.1 9.5 %tables.1 = (bf16[8,512,512]{2,1,0:T(8,128)(2,1)S(1)}, bf16[8,1024,512]{2,1,0:T(8,128)(2,1)S(1)}) custom-call(bf16[8,510,2,510]{3,2,1,0:T(2,128)(2,1)} %bitcast.15, bf16[4080,510]{1,0:T(8,128)(2,1)} %bitcast.16), custom_call_target="tpu_custom_call" | custom-call | flops 2147483648 | bytes 25165824 | tf_op jit(solution)/shard_map/tables/pallas_call | solution.py:346
  17.6 0.0 copy-start.2
  17.6 3.2 %copy-done.2 = bf16[8,1024,512]{2,1,0:T(8,128)(2,1)} copy-done((bf16[8,1024,512]{2,1,0:T(8,128)(2,1)}, bf16[8,1024,512]{2,1,0:T(8,128)(2,1)S(1)}, u32[]{:S(2)}) %copy-start.2) | copy-done | bytes 8388632
  20.8 0.0 copy-start.4
  20.8 1.9 %copy-done.4 = bf16[8,512,512]{2,1,0:T(8,128)(2,1)} copy-done((bf16[8,512,512]{2,1,0:T(8,128)(2,1)}, bf16[8,512,512]{2,1,0:T(8,128)(2,1)S(1)}, u32[]{:S(2)}) %copy-start.4) | copy-done | bytes 4194328
  22.7 0.0 all-to-all-done.own_ref
  22.7 0.0 copy-start.5
  22.7 4.4 %collective-permute-start = (bf16[4,2,2,16,512]{4,3,2,1,0:T(8,128)(2,1)S(1)}, bf16[4,2,2,16,512]{4,3,2,1,0:T(8,128)(2,1)S(1)}, u32[]{:S(2)}, u32[]{:S(2)}) collective-permute-start(bf16[4,2,2,16,512]{4,3,2,1,0:T(8,128)(2,1)S(1)} %all-to-all-done.own_ref), channel_id=1, source_target_pairs={{0,4},{4,8},{8,12},{12,16},{16,20},{20,24},{24,28},{1,5},{5,9},{9,... | collective-permute-start | bytes 786440 | tf_op jit(solution)/shard_map/ppermute | solution.py:306
  27.1 1.3 %collective-permute-start.1 = (bf16[4,2,2,16,512]{4,3,2,1,0:T(8,128)(2,1)S(1)}, bf16[4,2,2,16,512]{4,3,2,1,0:T(8,128)(2,1)S(1)}, u32[]{:S(2)}, u32[]{:S(2)}) collective-permute-start(bf16[4,2,2,16,512]{4,3,2,1,0:T(8,128)(2,1)S(1)} %all-to-all-done.own_ref), channel_id=1, source_target_pairs={{4,0},{8,4},{12,8},{16,12},{20,16},{24,20},{28,24},{5,1},{9,5},{13... | collective-permute-start | bytes 786440 | tf_op jit(solution)/shard_map/ppermute | solution.py:306
  28.4 6.0 %gram.1 = (f32[8,1024,128]{2,1,0:T(8,128)S(1)}, f32[8,128]{1,0:T(8,128)S(1)}) custom-call(f32[4,2040,128]{2,1,0:T(8,128)} %bitcast.14), custom_call_target="tpu_custom_call" | custom-call | tf_op jit(solution)/shard_map/gram/pallas_call | solution.py:369
  34.4 0.0 copy-start
  34.5 2.0 %copy-done = f32[8,1024,128]{2,1,0:T(8,128)} copy-done((f32[8,1024,128]{2,1,0:T(8,128)}, f32[8,1024,128]{2,1,0:T(8,128)S(1)}, u32[]{:S(2)}) %copy-start) | copy-done | bytes 4194328
  36.4 2.5 %collective-permute-done.below_ref = bf16[4,2,2,16,512]{4,3,2,1,0:T(8,128)(2,1)S(1)} collective-permute-done((bf16[4,2,2,16,512]{4,3,2,1,0:T(8,128)(2,1)S(1)}, bf16[4,2,2,16,512]{4,3,2,1,0:T(8,128)(2,1)S(1)}, u32[]{:S(2)}, u32[]{:S(2)}) %collective-permute-start) | collective-permute-done | bytes 262176 | tf_op jit(solution)/shard_map/ppermute | solution.py:306
  38.9 0.0 collective-permute-done.1.above_ref
  38.9 0.8 weights.1.weights_ref
  39.6 0.0 copy-done.5
  39.7 0.0 copy-start.3
  39.7 3.4 %copy-done.3 = bf16[8,1024,512]{2,1,0:T(8,128)(2,1)S(1)} copy-done((bf16[8,1024,512]{2,1,0:T(8,128)(2,1)S(1)}, bf16[8,1024,512]{2,1,0:T(8,128)(2,1)}, u32[]{:S(2)}) %copy-start.3) | copy-done | bytes 8388632
  43.0 0.0 copy-start.7
  43.0 13.3 %field.1 = bf16[4,2,2,16,512]{4,3,2,1,0:T(8,128)(2,1)} custom-call(bf16[8,256,384]{2,1,0:T(8,128)(2,1)S(1)} %weights.1.weights_ref, bf16[8,512,512]{2,1,0:T(8,128)(2,1)S(1)} %copy-done.5, bf16[8,1024,512]{2,1,0:T(8,128)(2,1)S(1)} %copy-done.3, bf16[4,2,2,16,512]{4,3,2,1,0:T(8,128)(2,1)S(1)} %collective-permute-done.below_ref, ...), custom_call_target="tpu_custom_call" | custom-call | tf_op jit(solution)/shard_map/field/pallas_call | solution.py:393
  56.3 3.4 %all-to-all-start.1 = ((bf16[4,2,2,16,512]{4,3,2,1,0:T(8,128)(2,1)}), bf16[4,2,2,16,512]{4,3,2,1,0:T(8,128)(2,1)S(1)}, u32[]{:S(2)}, u32[]{:S(2)}) async-start(bf16[4,2,2,16,512]{4,3,2,1,0:T(8,128)(2,1)} %field.1), calls=%async_computation.1 | async-start | bytes 524288 | tf_op jit(solution)/shard_map/all_to_all | solution.py:299
  59.7 0.0 copy-done.7
  59.7 0.4 reshape.18.mie_ref
  60.1 5.6 %all-to-all-done.1.pieces_ref = bf16[4,2,2,16,512]{4,3,2,1,0:T(8,128)(2,1)S(1)} async-done(((bf16[4,2,2,16,512]{4,3,2,1,0:T(8,128)(2,1)}), bf16[4,2,2,16,512]{4,3,2,1,0:T(8,128)(2,1)S(1)}, u32[]{:S(2)}, u32[]{:S(2)}) %all-to-all-start.1) | async-done | bytes 262176 | tf_op jit(solution)/shard_map/all_to_all | solution.py:299
  65.7 0.0 copy-start.1
  65.7 2.2 %copy-done.1 = f32[8,1024,128]{2,1,0:T(8,128)S(1)} copy-done((f32[8,1024,128]{2,1,0:T(8,128)S(1)}, f32[8,1024,128]{2,1,0:T(8,128)}, u32[]{:S(2)}) %copy-start.1) | copy-done | bytes 4194328
  67.9 1.4 %image.1 = (f32[1024,128]{1,0:T(8,128)S(1)}, f32[32,8,128]{2,1,0:T(8,128)S(1)}) custom-call(f32[8,1024,128]{2,1,0:T(8,128)S(1)} %copy-done.1, f32[8,128]{1,0:T(8,128)S(1)} %get-tuple-element.23.gram_ref, f32[1020,128]{1,0:T(8,128)S(1)} %reshape.18.mie_ref, bf16[4,2,2,16,512]{4,3,2,1,0:T(8,128)(2,1)S(1)} %all-to-all-done.1.pieces_ref), custom_call_target="tpu_custom_call" | custom-call | tf_op jit(solution)/shard_map/image/pallas_call | solution.py:413
  69.3 13.9 %all_to_all.15.sums_ref = f32[32,8,128]{2,1,0:T(8,128)S(1)} all-to-all(f32[32,8,128]{2,1,0:T(8,128)S(1)} %get-tuple-element.28), channel_id=1, replica_groups=mesh['blk'=8,'pair'=4] {'blk','pair'}, dimensions={0} | all-to-all | bytes 262144 | tf_op jit(solution)/shard_map/all_to_all | solution.py:422
  83.2 1.7 %remainder.1 = (f32[2,8]{1,0:T(2,128)}, f32[255,4,128]{2,1,0:T(4,128)}) custom-call(f32[32,8,128]{2,1,0:T(8,128)S(1)} %all_to_all.15.sums_ref, f32[8,1024,128]{2,1,0:T(8,128)S(1)} %copy-done.1, f32[1024,128]{1,0:T(8,128)S(1)} %get-tuple-element.29.image_ref), custom_call_target="tpu_custom_call" | custom-call | tf_op jit(solution)/shard_map/remainder/pallas_call | solution.py:426
Async XLA Ops:
  1.3 0.7 copy-start.6
  3.9 18.9 %all-to-all-start = ((bf16[4,2,2,16,512]{4,3,2,1,0:T(8,128)(2,1)}), bf16[4,2,2,16,512]{4,3,2,1,0:T(8,128)(2,1)S(1)}, u32[]{:S(2)}, u32[]{:S(2)}) async-start(bf16[4,2,2,16,512]{4,3,2,1,0:T(8,128)(2,1)} %pack.1), calls=%async_computation | async-start | bytes 524288 | tf_op jit(solution)/shard_map/all_to_all | solution.py:299
  17.6 3.2 %copy-start.2 = (bf16[8,1024,512]{2,1,0:T(8,128)(2,1)}, bf16[8,1024,512]{2,1,0:T(8,128)(2,1)S(1)}, u32[]{:S(2)}) copy-start(bf16[8,1024,512]{2,1,0:T(8,128)(2,1)S(1)} %get-tuple-element.27.axial_ref) | copy-start | bytes 25165828
  20.8 1.9 %copy-start.4 = (bf16[8,512,512]{2,1,0:T(8,128)(2,1)}, bf16[8,512,512]{2,1,0:T(8,128)(2,1)S(1)}, u32[]{:S(2)}) copy-start(bf16[8,512,512]{2,1,0:T(8,128)(2,1)S(1)} %get-tuple-element.26.rot_ref) | copy-start | bytes 12582916
  22.7 16.9 %copy-start.5 = (bf16[8,512,512]{2,1,0:T(8,128)(2,1)S(1)}, bf16[8,512,512]{2,1,0:T(8,128)(2,1)}, u32[]{:S(2)}) copy-start(bf16[8,512,512]{2,1,0:T(8,128)(2,1)} %copy-done.4) | copy-start | bytes 12582916
  22.7 16.1 %collective-permute-start = (bf16[4,2,2,16,512]{4,3,2,1,0:T(8,128)(2,1)S(1)}, bf16[4,2,2,16,512]{4,3,2,1,0:T(8,128)(2,1)S(1)}, u32[]{:S(2)}, u32[]{:S(2)}) collective-permute-start(bf16[4,2,2,16,512]{4,3,2,1,0:T(8,128)(2,1)S(1)} %all-to-all-done.own_ref), channel_id=1, source_target_pairs={{0,4},{4,8},{8,12},{12,16},{16,20},{20,24},{24,28},{1,5},{5,9},{9,... | collective-permute-start | bytes 786440 | tf_op jit(solution)/shard_map/ppermute | solution.py:306
  27.1 11.8 %collective-permute-start.1 = (bf16[4,2,2,16,512]{4,3,2,1,0:T(8,128)(2,1)S(1)}, bf16[4,2,2,16,512]{4,3,2,1,0:T(8,128)(2,1)S(1)}, u32[]{:S(2)}, u32[]{:S(2)}) collective-permute-start(bf16[4,2,2,16,512]{4,3,2,1,0:T(8,128)(2,1)S(1)} %all-to-all-done.own_ref), channel_id=1, source_target_pairs={{4,0},{8,4},{12,8},{16,12},{20,16},{24,20},{28,24},{5,1},{9,5},{13... | collective-permute-start | bytes 786440 | tf_op jit(solution)/shard_map/ppermute | solution.py:306
  34.4 2.0 %copy-start = (f32[8,1024,128]{2,1,0:T(8,128)}, f32[8,1024,128]{2,1,0:T(8,128)S(1)}, u32[]{:S(2)}) copy-start(f32[8,1024,128]{2,1,0:T(8,128)S(1)} %get-tuple-element.22.aligned_ref) | copy-start | bytes 12582916
  39.7 3.4 %copy-start.3 = (bf16[8,1024,512]{2,1,0:T(8,128)(2,1)S(1)}, bf16[8,1024,512]{2,1,0:T(8,128)(2,1)}, u32[]{:S(2)}) copy-start(bf16[8,1024,512]{2,1,0:T(8,128)(2,1)} %copy-done.2) | copy-start | bytes 25165828
  43.0 16.7 %copy-start.7 = (f32[2,510,128]{2,0,1:T(2,128)S(1)}, f32[2,510,128]{2,0,1:T(2,128)}, u32[]{:S(2)}) copy-start(f32[2,510,128]{2,0,1:T(2,128)} %param.7) | copy-start | bytes 1566724
  56.3 9.4 %all-to-all-start.1 = ((bf16[4,2,2,16,512]{4,3,2,1,0:T(8,128)(2,1)}), bf16[4,2,2,16,512]{4,3,2,1,0:T(8,128)(2,1)S(1)}, u32[]{:S(2)}, u32[]{:S(2)}) async-start(bf16[4,2,2,16,512]{4,3,2,1,0:T(8,128)(2,1)} %field.1), calls=%async_computation.1 | async-start | bytes 524288 | tf_op jit(solution)/shard_map/all_to_all | solution.py:299
  65.7 2.2 %copy-start.1 = (f32[8,1024,128]{2,1,0:T(8,128)S(1)}, f32[8,1024,128]{2,1,0:T(8,128)}, u32[]{:S(2)}) copy-start(f32[8,1024,128]{2,1,0:T(8,128)} %copy-done) | copy-start | bytes 12582916

commit v3 on v2

v3 whole, which is shorter than its diff:
```python
import functools

import jax
import jax.numpy as jnp
from jax import lax
from jax.experimental import pallas as pl
from jax.experimental.pallas import tpu as pltpu
from jax.sharding import PartitionSpec as P

MIB = 1024 * 1024
F32 = jnp.float32
BF16 = jnp.bfloat16


def params(mib):
    return pltpu.CompilerParams(vmem_limit_bytes=mib * MIB)


def hbm():
    return pl.BlockSpec(memory_space=pltpu.HBM)


def whole():
    return pl.BlockSpec(memory_space=pltpu.VMEM)


def in_hbm(value):
    return pltpu.with_memory_space_constraint(value, pltpu.HBM)


def rounded_up(value, unit):
    return (value + unit - 1) // unit * unit


def iota(shape, dim):
    return lax.broadcasted_iota(jnp.int32, shape, dim)


def dot_nn(left, right):
    return lax.dot_general(left, right, (((1,), (0,)), ((), ())), preferred_element_type=F32)


def dot_nt(left, right):
    return lax.dot_general(left, right, (((1,), (1,)), ((), ())), preferred_element_type=F32)


def pack_kernel(quarter, modes, ways, own, list_ref, count_ref, basis_ref, out_ref, pair_rows_ref, lines_ref, pad_ref, codes_ref, sems):
    full, columns = lines_ref.shape
    rows = quarter * modes
    part = columns // 2 // ways
    copy = pltpu.make_async_copy(basis_ref.at[basis_ref.shape[0] - 1, pl.ds(2 * rows - full, full)], lines_ref, sems.at[0])
    copy.start()
    list_copy = pltpu.make_async_copy(list_ref, pair_rows_ref, sems.at[1])
    list_copy.start()
    pad_ref[...] = jnp.zeros_like(pad_ref)
    list_copy.wait()
    slots = pair_rows_ref.shape[2]
    live = iota((1, slots), 1) < count_ref[0]
    marks = jnp.where(live, own * (pair_rows_ref[2] + 1) + pair_rows_ref[0], 0)
    line = iota((slots, slots), 0)
    stacked = jnp.where(line == 0, marks, jnp.where(line == 1, pair_rows_ref[1], 0))
    turned = jnp.transpose(stacked.astype(F32))
    codes_ref[0:slots, :] = turned
    codes_ref[slots : 2 * slots, :] = pltpu.roll(turned, slots - 1, axis=1)
    share = 2 * quarter * part
    mine = codes_ref[pl.ds(pl.multiple_of(lax.axis_index("pair") * share, share), share), :][:, 0:1]
    copy.wait()
    for j in range(quarter):
        pad_ref[0:modes, :] = lines_ref[pl.ds(full - rows + j, modes, quarter), :]
        turned = jnp.transpose(pad_ref[...])
        for c in range(2):
            codes = mine[(c * quarter + j) * part : (c * quarter + j + 1) * part]
            for p in range(ways):
                row = c * (columns // 2) + p * part
                piece = turned[row : row + part]
                out_ref[p, c, j] = jnp.where(iota(piece.shape, 1) == modes, codes, piece).astype(BF16)


def tables_kernel(modes, tables, axial_ref, rot_ref, rot_out_ref, axial_out_ref, lines_ref):
    step = pl.program_id(0)
    size = rot_out_ref.shape[2]
    chunk = 256

    @pl.when(step == 0)
    def _():
        lines_ref[...] = jnp.zeros_like(lines_ref)

    out_row, in_row = iota((chunk, chunk), 0), iota((chunk, chunk), 1)
    each = chunk // 2
    halves = (in_row == 2 * lax.rem(out_row, each) + lax.div(out_row, each)).astype(F32).astype(BF16)
    lines_ref[0 : 2 * modes, 0:modes] = axial_ref[0].reshape(2 * modes, modes)
    for q in range(2 * size // chunk):
        sorted_rows = dot_nn(halves, lines_ref[q * chunk : (q + 1) * chunk, :]).astype(BF16)
        for c in range(2):
            axial_out_ref[0, c * size + q * each : c * size + (q + 1) * each, :] = sorted_rows[c * each : (c + 1) * each]
    each = chunk // tables
    entries = (in_row == tables * lax.rem(out_row, each) + lax.div(out_row, each)).astype(F32).astype(BF16)
    block = rot_ref.shape[0]
    left = tables * modes - step * block
    rows = jnp.where(iota((block, modes), 0) < left, rot_ref[...], jnp.zeros((), BF16))
    rot_out_ref[:, :, size - 128 : size] = jnp.zeros((tables, block // tables, 128), BF16)
    for q in range(block // chunk):
        sorted_rows = dot_nn(entries, rows[q * chunk : (q + 1) * chunk]).astype(BF16)
        for g in range(tables):
            rot_out_ref[g, q * each : (q + 1) * each, 0:modes] = sorted_rows[g * each : (g + 1) * each]


def weights_kernel(own, part, modes, below_ref, own_ref, above_ref, out_ref):
    tables = out_ref.shape[0]
    group = own * part
    size = own_ref.shape[4]
    lane = modes % 128
    wanted = lax.div(iota((tables * group, group), 0), part) + own

    def lists(ref):
        values = ref[:, :, :, :, size - 128 : size].reshape(2 * group, 128).astype(F32)
        marks, sources = values[:group], values[group:]
        lines = [jnp.transpose(side)[lane : lane + 1].astype(jnp.int32) for side in (marks, sources)]
        return lines, [side[:, lane : lane + 1].astype(jnp.int32) for side in (marks, sources)]

    def one_hot(hit):
        return jnp.where(hit, 1.0, 0.0).astype(BF16)

    def store(direction, first, counts):
        lanes = counts.shape[1]
        same = lax.rem(iota(counts.shape, 0), part) == lax.rem(iota(counts.shape, 1), part)
        kept = jnp.where(same, counts, 0.0).astype(BF16)
        for g in range(tables):
            out_ref[g, direction * group : (direction + 1) * group, first : first + lanes] = kept[g * group : (g + 1) * group]

    for window, ref in enumerate((below_ref, own_ref, above_ref)):
        (marks, sources), (marks_column, sources_column) = lists(ref)
        if window == 1:
            spread = one_hot(sources_column == lax.div(iota((group, 3 * group), 1), part))
            store(0, 0, dot_nn(one_hot(marks == wanted), spread))
        block = sources - (2 - window) * own
        inside = (block >= 0) & (block < own) & (marks >= own)
        hits = one_hot(jnp.where(inside, lax.div(marks, own) * own + block, -1) == wanted)
        spread = one_hot(lax.rem(marks_column, own) == lax.div(iota((group, group), 1), part))
        store(1, window * group, dot_nn(hits, spread))


def swapped(value):
    half = value.shape[0] // 2
    return jnp.concatenate([-value[half:], value[:half]], axis=0)


def field_kernel(weights_ref, rot_ref, axial_ref, below_ref, own_ref, above_ref, out_ref, window_ref, total_ref):
    step = pl.program_id(0)
    group = weights_ref.shape[1] // 2
    size = window_ref.shape[2]

    @pl.when(step == 0)
    def _():
        for w, ref in enumerate((below_ref, own_ref, above_ref)):
            for c in range(2):
                window_ref[c, w * group : (w + 1) * group, :] = ref[:, c].reshape(group, size)
        total_ref[...] = jnp.zeros_like(total_ref)

    entries = range(weights_ref.shape[0])
    real = [dot_nn(weights_ref[g], window_ref[0]).astype(BF16) for g in entries]
    imag = [dot_nn(weights_ref[g], window_ref[1]).astype(BF16) for g in entries]
    sums = [jnp.concatenate([r[:group], i[:group], r[group:], i[group:]], axis=0) for r, i in zip(real, imag)]
    turned = [dot_nt(sums[g], rot_ref[g]).astype(BF16) for g in entries]
    moved = []
    for g in entries:
        forward, backward = turned[g][: 2 * group], turned[g][2 * group :]
        result = dot_nt(forward, axial_ref[g, :size]) + dot_nt(swapped(forward), axial_ref[g, size:])
        result += dot_nn(jnp.concatenate([backward, swapped(backward)], axis=1), axial_ref[g])
        moved.append(result.astype(BF16))
    total_ref[...] += sum(dot_nn(moved[g], rot_ref[g]) for g in entries)

    @pl.when(step == pl.num_programs(0) - 1)
    def _():
        for c in range(2):
            out_ref[:, c] = total_ref[c * group : (c + 1) * group].astype(BF16).reshape(out_ref[:, c].shape)


def lane_swap(value):
    half = value.shape[1] // 2
    rolled = pltpu.roll(value, half, axis=1)
    return jnp.where(iota(value.shape, 1) < half, -rolled, rolled)


def folded(value):
    return jnp.sum(value.reshape(value.shape[0] // 8, 8, value.shape[1]), axis=0)


def gram_kernel(quarter, modes, basis_ref, gram_ref, aligned_ref, blocks_ref, sums_ref, sems):
    vectors, full, columns = aligned_ref.shape
    rows = quarter * modes
    copies = [pltpu.make_async_copy(basis_ref.at[i], blocks_ref.at[i], sems.at[i]) for i in range(vectors // 2)]
    for copy in copies:
        copy.start()
    sums_ref[...] = jnp.zeros_like(sums_ref)
    for i, copy in enumerate(copies):
        copy.wait()
        for side in range(2):
            aligned_ref[2 * i + side, 0:rows, :] = blocks_ref[i, side * rows : (side + 1) * rows, :]
            aligned_ref[2 * i + side, rows:full, :] = jnp.zeros((full - rows, columns), F32)
    chunk = 32

    def body(i, carry):
        here = pl.ds(pl.multiple_of(i * chunk, chunk), chunk)
        values = [aligned_ref[k, here, :] for k in range(vectors)]
        for l in range(vectors):
            other = lane_swap(values[l])
            for k in range(l + 1):
                sums_ref[k, l] += folded(values[k] * values[l])
                if k < l:
                    sums_ref[l, k] -= folded(values[k] * other)
        return carry

    lax.fori_loop(0, full // chunk, body, 0)
    totals = jnp.sum(jnp.sum(sums_ref[...].reshape(vectors * vectors, 8, columns), axis=1), axis=1, keepdims=True)
    row, lane = iota((vectors, 128), 0), iota((vectors, 128), 1)
    line = jnp.zeros((1, 128), F32)
    for k in range(vectors):
        column = totals[k * vectors : (k + 1) * vectors]
        line += jnp.sum(jnp.where(row + k * vectors == lane, column, 0.0), axis=0, keepdims=True)
    gram_ref[...] = line


def image_kernel(quarter, modes, basis_ref, mie_ref, gram_ref, pieces_ref, blocks_ref, image_ref, sums_ref, lines_ref, mies_ref, tile_ref, sems):
    blocks = blocks_ref.shape[0]
    vectors = 2 * blocks
    full, columns = image_ref.shape
    rows = quarter * modes
    height = mies_ref.shape[1]
    ways, _, _, part, size = pieces_ref.shape
    small = [pltpu.make_async_copy(mie_ref, mies_ref, sems.at[blocks]), pltpu.make_async_copy(gram_ref, tile_ref, sems.at[blocks + 1])]
    copies = [pltpu.make_async_copy(basis_ref.at[i], blocks_ref.at[i, pl.ds(0, 2 * rows)], sems.at[i]) for i in range(blocks)]
    for copy in [copies[-1]] + small + copies[:-1]:
        copy.start()
    for i in range(blocks):
        blocks_ref[i, 2 * rows :, :] = jnp.zeros((blocks_ref.shape[1] - 2 * rows, columns), F32)
    lines_ref[rows:full, :] = jnp.zeros((full - rows, columns), F32)
    for j in range(quarter):
        turned = jnp.concatenate([pieces_ref[:, c, j].reshape(ways * part, size) for c in range(2)], axis=0)
        lines_ref[pl.ds(j, modes, quarter), :] = jnp.transpose(turned.astype(F32))[:modes]
    half = columns // 2
    chunk = 64
    copies[-1].wait()
    for copy in small:
        copy.wait()
    square = jnp.zeros((8, columns), F32)
    for first in range(0, full, chunk):
        count = min(chunk, rows - first)
        here = slice(first, first + chunk)
        field = lines_ref[here, :]
        mie = mies_ref[first // height : (first + count) // height].reshape(count, columns)
        if count < chunk:
            mie = jnp.concatenate([mie, jnp.zeros((chunk - count, columns), F32)], axis=0)
        left = iota(mie.shape, 1) < half
        other = pltpu.roll(mie, half, axis=1)
        product = jnp.where(left, mie, other) * field + jnp.where(left, -other, mie) * pltpu.roll(field, half, axis=1)
        image = blocks_ref[blocks - 1, rows + first : rows + first + chunk, :] - product
        image_ref[here, :] = image
        square += folded(image * image)
    lane = iota(tile_ref.shape, 1)
    tile = tile_ref[...]
    for i in reversed(range(blocks)):
        if i < blocks - 1:
            copies[i].wait()
        totals = [jnp.zeros((8, columns), F32) for _ in range(4)]
        for first in range(0, full, chunk):
            image = image_ref[first : first + chunk, :]
            turned = lane_swap(image)
            for side in range(2):
                values = blocks_ref[i, side * rows + first : side * rows + first + chunk, :]
                totals[2 * side] += folded(values * image)
                totals[2 * side + 1] -= folded(values * turned)
        for index, total in enumerate(totals):
            total = jnp.sum(total, axis=(0, 1), keepdims=True)
            tile = jnp.where(lane == vectors * vectors + 4 * i + index, total, tile)
    square = jnp.sum(square, axis=(0, 1), keepdims=True)
    tile = jnp.where(lane == vectors * vectors + 2 * vectors, square, tile)
    sums_ref[...] = jnp.broadcast_to(tile[None], sums_ref.shape)


def remainder_kernel(quarter, modes, mean_scale, sums_ref, blocks_ref, image_ref, dots_ref, out_ref):
    vectors = 2 * blocks_ref.shape[0]
    full, columns = image_ref.shape
    rows = quarter * modes
    total = jnp.sum(sums_ref[...], axis=0)
    lane = iota(total.shape, 1)

    def lane_at(index):
        return jnp.sum(jnp.where(lane == index, total, 0.0), axis=1, keepdims=True)

    def on_lanes(parts, places):
        line = jnp.zeros(total.shape, F32)
        for k in range(vectors):
            line = jnp.where(places == k, parts[k], line)
        return line

    start = vectors * vectors
    real = [lane_at(start + 2 * k) * mean_scale for k in range(vectors)]
    imag = [lane_at(start + 2 * k + 1) * mean_scale for k in range(vectors)]
    real_line, imag_line = on_lanes(real, lane), on_lanes(imag, lane)
    dots_ref[0:1, :] = real_line[:, :vectors]
    dots_ref[1:2, :] = imag_line[:, :vectors]
    first_index, last_index = lax.div(lane, vectors), lax.rem(lane, vectors)
    real_first, real_last = on_lanes(real, first_index), on_lanes(real, last_index)
    imag_first, imag_last = on_lanes(imag, first_index), on_lanes(imag, last_index)
    same = real_first * real_last + imag_first * imag_last
    cross = imag_last * real_first - real_last * imag_first
    often = jnp.where(first_index == last_index, 1.0, 2.0)
    spread = jnp.where(lane < start, total * often * jnp.where(first_index <= last_index, same, cross), 0.0)
    spread = jnp.sum(spread, axis=1, keepdims=True)
    inside = jnp.sum(real_line * real_line + imag_line * imag_line, axis=1, keepdims=True)
    norm_square = (lane_at(start + 2 * vectors) + spread) * mean_scale - 2.0 * inside
    scale = lax.rsqrt(norm_square)
    image_scale = jnp.broadcast_to(scale, (8, columns))
    reals = [jnp.broadcast_to(real[k] * scale, (8, columns)) for k in range(vectors)]
    imags = [jnp.broadcast_to(imag[k] * scale, (8, columns)) for k in range(vectors)]
    chunk = 64
    for first in range(0, full, chunk):
        here = slice(first, first + chunk)
        values = []
        for k in range(vectors):
            start = k % 2 * rows + first
            values.append(blocks_ref[k // 2, start : start + chunk, :].reshape(chunk // 8, 8, columns))
        along = image_ref[here, :].reshape(chunk // 8, 8, columns) * image_scale
        turned = jnp.zeros_like(along)
        for k in range(vectors):
            along -= reals[k] * values[k]
            turned += imags[k] * values[k]
        result = along.reshape(chunk, columns) - lane_swap(turned.reshape(chunk, columns))
        count = min(chunk, rows - first)
        height = out_ref.shape[1]
        out_ref[first // height : (first + count) // height] = result.reshape(chunk // height, height, columns)[: count // height]


def exchanged(value):
    return lax.all_to_all(value, "pair", split_axis=0, concat_axis=0, tiled=True)


def neighbours(value):
    count = lax.axis_size("blk")
    up = [(i, i + 1) for i in range(count - 1)]
    down = [(j, i) for i, j in up]
    return lax.ppermute(value, "blk", up), lax.ppermute(value, "blk", down)


def shards(basis, mie_coeffs, rot_table, axial_table, pair_table, pair_count):
    vectors, quarter, modes, columns = basis.shape
    ways = lax.axis_size("pair")
    blk_ways = lax.axis_size("blk")
    tables = rot_table.shape[0]
    slots = pair_table.shape[1]
    own = quarter * ways
    part = columns // 2 // ways
    group = own * part
    size = rounded_up(modes, 128)
    rows = quarter * modes
    full = rounded_up(rows, 8)
    pairs_of_vectors = vectors // 2

    basis_rows = in_hbm(basis.transpose(0, 2, 1, 3).reshape(pairs_of_vectors, 2 * rows, columns))
    mie_rows = in_hbm(mie_coeffs.transpose(1, 0, 2).reshape(rows // 4, 4, columns))
    rot_rows = in_hbm(rot_table.transpose(1, 0, 2).reshape(modes * tables, modes))
    axial_rows = in_hbm(axial_table.transpose(0, 2, 1, 3))
    pair_rows = in_hbm(pair_table.transpose(2, 0, 1))

    pieces_shape = (ways, 2, quarter, part, size)
    pieces = pl.pallas_call(
        functools.partial(pack_kernel, quarter, modes, ways, own),
        in_specs=[hbm(), pl.BlockSpec(memory_space=pltpu.SMEM), hbm()],
        out_specs=whole(),
        out_shape=jax.ShapeDtypeStruct(pieces_shape, BF16),
        scratch_shapes=[
            pltpu.VMEM(pair_rows.shape, jnp.int32),
            pltpu.VMEM((full, columns), F32),
            pltpu.VMEM((size, columns), F32),
            pltpu.VMEM((2 * slots, slots), F32),
            pltpu.SemaphoreType.DMA((2,)),
        ],
        compiler_params=params(16),
        name="pack",
    )(pair_rows, pair_count, basis_rows)
    pieces, basis_later = lax.optimization_barrier((pieces, basis_rows))
    own_pieces = exchanged(pieces)

    gram = pl.pallas_call(
        functools.partial(gram_kernel, quarter, modes),
        grid=(1,),
        in_specs=[hbm()],
        out_specs=pl.BlockSpec((1, 128), lambda i: (0, 0)),
        out_shape=pltpu.HBM((1, 128), F32),
        scratch_shapes=[
            pltpu.VMEM((vectors, full, columns), F32),
            pltpu.VMEM((pairs_of_vectors, 2 * rows, columns), F32),
            pltpu.VMEM((vectors, vectors, 8, columns), F32),
            pltpu.SemaphoreType.DMA((pairs_of_vectors,)),
        ],
        compiler_params=params(16),
        name="gram",
    )(basis_later)
    own_pieces, gram = lax.optimization_barrier((own_pieces, gram))
    below, above = neighbours(own_pieces)

    rotations, axials = pl.pallas_call(
        functools.partial(tables_kernel, modes, tables),
        grid=(tables,),
        in_specs=[
            pl.BlockSpec((1, modes, 2, modes), lambda g: (g, 0, 0, 0)),
            pl.BlockSpec((size, modes), lambda g: (g, 0)),
        ],
        out_specs=[
            pl.BlockSpec((tables, size // tables, size), lambda g: (0, g, 0)),
            pl.BlockSpec((1, 2 * size, size), lambda g: (g, 0, 0)),
        ],
        out_shape=[pltpu.HBM((tables, size, size), BF16), pltpu.HBM((tables, 2 * size, size), BF16)],
        scratch_shapes=[pltpu.VMEM((2 * size, size), BF16)],
        compiler_params=params(32),
        cost_estimate=pl.CostEstimate(flops=tables * 8 * 256 * 256 * size, bytes_accessed=6 * tables * size * size * 2, transcendentals=0),
        name="tables",
    )(axial_rows, rot_rows)

    below, above, rotations, axials = lax.optimization_barrier((below, above, rotations, axials))
    weights = pl.pallas_call(
        functools.partial(weights_kernel, own, part, modes),
        in_specs=[whole()] * 3,
        out_specs=whole(),
        out_shape=jax.ShapeDtypeStruct((tables, 2 * group, 3 * group), BF16),
        compiler_params=params(24),
        name="weights",
    )(below, own_pieces, above)

    entries = 2 if tables % 2 == 0 else 1
    field = pl.pallas_call(
        field_kernel,
        grid=(tables // entries,),
        in_specs=[
            pl.BlockSpec((entries, 2 * group, 3 * group), lambda g: (g, 0, 0)),
            pl.BlockSpec((entries, size, size), lambda g: (g, 0, 0)),
            pl.BlockSpec((entries, 2 * size, size), lambda g: (g, 0, 0)),
            whole(),
            whole(),
            whole(),
        ],
        out_specs=whole(),
        out_shape=jax.ShapeDtypeStruct(pieces_shape, BF16),
        scratch_shapes=[pltpu.VMEM((2, 3 * group, size), BF16), pltpu.VMEM((2 * group, size), F32)],
        compiler_params=params(24),
        name="field",
    )(weights, in_hbm(rotations), in_hbm(axials), below, own_pieces, above)
    field_pieces = exchanged(field)

    height = 4
    tall = rounded_up(rows + full, 8)
    blocks, image, sums = pl.pallas_call(
        functools.partial(image_kernel, quarter, modes),
        in_specs=[hbm(), hbm(), hbm(), whole()],
        out_specs=[whole()] * 3,
        out_shape=[
            jax.ShapeDtypeStruct((pairs_of_vectors, tall, columns), F32),
            jax.ShapeDtypeStruct((full, columns), F32),
            jax.ShapeDtypeStruct((ways * blk_ways, 1, 128), F32),
        ],
        scratch_shapes=[
            pltpu.VMEM((full, columns), F32),
            pltpu.VMEM((rows // height, height, columns), F32),
            pltpu.VMEM((1, 128), F32),
            pltpu.SemaphoreType.DMA((pairs_of_vectors + 2,)),
        ],
        compiler_params=params(16),
        name="image",
    )(basis_rows, mie_rows, gram, field_pieces)
    sums = lax.all_to_all(sums, ("blk", "pair"), split_axis=0, concat_axis=0, tiled=True)

    mean_scale = 1.0 / (own * blk_ways * modes * columns)
    dots, next_rows = pl.pallas_call(
        functools.partial(remainder_kernel, quarter, modes, mean_scale),
        in_specs=[whole()] * 3,
        out_specs=[whole(), whole()],
        out_shape=[jax.ShapeDtypeStruct((2, vectors), F32), jax.ShapeDtypeStruct((rows // height, height, columns), F32)],
        compiler_params=params(16),
        name="remainder",
    )(sums, blocks, image)
    return dots, next_rows.reshape(modes, quarter, columns).transpose(1, 0, 2)


def solution(mesh):
    placed = (
        P(None, ("blk", "pair"), None, None),
        P(("blk", "pair"), None, None),
        P(),
        P(),
        P("blk", None, None),
        P("blk"),
    )
    return jax.shard_map(
        shards,
        mesh=mesh,
        in_specs=placed,
        out_specs=(P(), P(("blk", "pair"), None, None)),
        check_vma=False,
    )
```

time: 85.5 us -> 74.2 us (0.87)
  local copies, waits for them, and re-layouts: 13.7 us -> 0.01 us
  waiting for transfers between devices: 8.09 us -> 0.01 us
  blocking collectives: 13.9 us -> 21.3 us
  Pallas kernels: 34.5 us -> 40.7 us
  starting transfers between devices: 13.3 us -> 10.2 us
    unnamed x16 -> x2, local copies, waits for them, and re-layouts: 13.4 us -> 0.01 us
    all_to_all x0 -> x1, blocking collectives: none -> 9.09 us  [exchanged(): lax.all_to_all(value, 'pair', split_axis=0, concat_axis=0, tiled=True)]
    all_to_all x2 -> x1, waiting for transfers between devices: 5.63 us -> 0.01 us  [exchanged(): lax.all_to_all(value, 'pair', split_axis=0, concat_axis=0, tiled=True)]
    pallas_call x1, Pallas kernels: 9.46 us -> 13.6 us  [shards(): pl.pallas_call(functools.partial(tables_kernel, modes, tables), grid=(tab...]
    all_to_all x2 -> x1, starting transfers between devices: 7.63 us -> 4.22 us  [exchanged(): lax.all_to_all(value, 'pair', split_axis=0, concat_axis=0, tiled=True)]
    ppermute x2, waiting for transfers between devices: 2.47 us -> 0.01 us  [neighbours(): return (lax.ppermute(value, 'blk', up), lax.ppermute(value, 'blk', down))]
    pallas_call x1, Pallas kernels: 1.39 us -> 3.4 us  [shards(): pl.pallas_call(functools.partial(image_kernel, quarter, modes), in_specs=...]
    all_to_all x1, blocking collectives: 13.9 us -> 12.2 us  [shards(): lax.all_to_all(sums, ('blk', 'pair'), split_axis=0, concat_axis=0, tiled=...]
  transfers between devices with their start and end apart: 4 -> 3, of which waited for: 2 -> 0; matrix products, arithmetic and copies ran while one was open for 0% -> 0% of each run, Pallas kernels for 18% -> 27%
where the time goes in v3:
time: 74.2 us; the launch traced here: 73.7 us
  Pallas kernels  40.7 us (55%)
  blocking collectives  21.3 us (29%)
  starting transfers between devices  10.2 us (14%)
  between operations  1.35 us (2%)
    pallas_call x1, Pallas kernels, shards(): pl.pallas_call(functools.partial(tables_kernel, modes, tables), grid=(tab...  13.6 us
    pallas_call x1, Pallas kernels, shards(): pl.pallas_call(field_kernel, grid=(tables // entries,), in_specs=[pl.Bloc...  12.9 us
    all_to_all x1, blocking collectives, shards(): lax.all_to_all(sums, ('blk', 'pair'), split_axis=0, concat_axis=0, tiled=...  12.2 us
    all_to_all x1, blocking collectives, exchanged(): lax.all_to_all(value, 'pair', split_axis=0, concat_axis=0, tiled=True)  9.09 us
    pallas_call x1, Pallas kernels, shards(): pl.pallas_call(functools.partial(gram_kernel, quarter, modes), grid=(1,),...  6.49 us
    ppermute x2, starting transfers between devices, neighbours(): return (lax.ppermute(value, 'blk', up), lax.ppermute(value, 'blk', down))  6.02 us
    all_to_all x1, starting transfers between devices, exchanged(): lax.all_to_all(value, 'pair', split_axis=0, concat_axis=0, tiled=True)  4.22 us
    pallas_call x1, Pallas kernels, shards(): pl.pallas_call(functools.partial(image_kernel, quarter, modes), in_specs=...  3.4 us
  transfers between devices with their start and end apart: 3, of which 0 were waited for; matrix products, arithmetic and copies ran while one was open for 0% of the time, Pallas kernels for 27%

profile of v3, /device:TPU:0, one launch (start us, length us, event | category | flops | bytes accessed | tf_op | source)
XLA Modules:
  0.0 73.7 jit_solution(16501032688797442806)
XLA Ops:
  1.3 1.9 %pack.1 = bf16[4,2,2,16,512]{4,3,2,1,0:T(8,128)(2,1)} custom-call(s32[3,1,128]{2,1,0:T(1,128)} %bitcast.20, s32[1]{0:T(128)S(6)} %copy.8.count_ref, f32[4,2040,128]{2,1,0:T(8,128)} %bitcast.14), custom_call_target="tpu_custom_call" | custom-call | tf_op jit(solution)/shard_map/pack/pallas_call | solution.py:367
  3.2 4.2 %all-to-all-start = ((bf16[4,2,2,16,512]{4,3,2,1,0:T(8,128)(2,1)}), bf16[4,2,2,16,512]{4,3,2,1,0:T(8,128)(2,1)S(1)}, u32[]{:S(2)}, u32[]{:S(2)}) async-start(bf16[4,2,2,16,512]{4,3,2,1,0:T(8,128)(2,1)} %pack.1), calls=%async_computation | async-start | bytes 524288 | tf_op jit(solution)/shard_map/all_to_all | solution.py:336
  7.4 6.5 %gram.1.gram_ref = f32[1,128]{1,0:T(1,128)} custom-call(f32[4,2040,128]{2,1,0:T(8,128)} %bitcast.15), custom_call_target="tpu_custom_call" | custom-call | tf_op jit(solution)/shard_map/gram/pallas_call | solution.py:385
  13.9 0.0 all-to-all-done.own_ref
  13.9 1.3 %collective-permute-start.1 = (bf16[4,2,2,16,512]{4,3,2,1,0:T(8,128)(2,1)S(1)}, bf16[4,2,2,16,512]{4,3,2,1,0:T(8,128)(2,1)S(1)}, u32[]{:S(2)}, u32[]{:S(2)}) collective-permute-start(bf16[4,2,2,16,512]{4,3,2,1,0:T(8,128)(2,1)S(1)} %all-to-all-done.own_ref), channel_id=1, source_target_pairs={{4,0},{8,4},{12,8},{16,12},{20,16},{24,20},{28,24},{5,1},{9,5},{13... | collective-permute-start | bytes 786440 | tf_op jit(solution)/shard_map/ppermute | solution.py:343
  15.2 4.7 %collective-permute-start = (bf16[4,2,2,16,512]{4,3,2,1,0:T(8,128)(2,1)S(1)}, bf16[4,2,2,16,512]{4,3,2,1,0:T(8,128)(2,1)S(1)}, u32[]{:S(2)}, u32[]{:S(2)}) collective-permute-start(bf16[4,2,2,16,512]{4,3,2,1,0:T(8,128)(2,1)S(1)} %all-to-all-done.own_ref), channel_id=1, source_target_pairs={{0,4},{4,8},{8,12},{12,16},{16,20},{20,24},{24,28},{1,5},{5,9},{9,... | collective-permute-start | bytes 786440 | tf_op jit(solution)/shard_map/ppermute | solution.py:343
  20.0 13.6 %tables.1 = (bf16[8,512,512]{2,1,0:T(8,128)(2,1)}, bf16[8,1024,512]{2,1,0:T(8,128)(2,1)}) custom-call(bf16[8,510,2,510]{3,2,1,0:T(2,128)(2,1)} %bitcast.17, bf16[4080,510]{1,0:T(8,128)(2,1)} %bitcast.18), custom_call_target="tpu_custom_call" | custom-call | flops 2147483648 | bytes 25165824 | tf_op jit(solution)/shard_map/tables/pallas_call | solution.py:403
  33.6 0.0 collective-permute-done.1.above_ref
  33.6 0.0 collective-permute-done.below_ref
  33.6 0.8 %weights.1.weights_ref = bf16[8,256,384]{2,1,0:T(8,128)(2,1)S(1)} custom-call(bf16[4,2,2,16,512]{4,3,2,1,0:T(8,128)(2,1)S(1)} %collective-permute-done.below_ref, bf16[4,2,2,16,512]{4,3,2,1,0:T(8,128)(2,1)S(1)} %all-to-all-done.own_ref, bf16[4,2,2,16,512]{4,3,2,1,0:T(8,128)(2,1)S(1)} %collective-permute-done.1.above_ref), custom_call_target="tpu_custom_call" | custom-call | tf_op jit(solution)/shard_map/weights/pallas_call | solution.py:422
  34.3 0.0 copy-start
  34.3 12.9 %field.1 = bf16[4,2,2,16,512]{4,3,2,1,0:T(8,128)(2,1)S(1)} custom-call(bf16[8,256,384]{2,1,0:T(8,128)(2,1)S(1)} %weights.1.weights_ref, bf16[8,512,512]{2,1,0:T(8,128)(2,1)} %get-tuple-element.25.rot_ref, bf16[8,1024,512]{2,1,0:T(8,128)(2,1)} %get-tuple-element.26.axial_ref, bf16[4,2,2,16,512]{4,3,2,1,0:T(8,128)(2,1)S(1)} %collective-permute-done.below_ref, ...), custom_call_target="tpu_custom_call" | custom-call | tf_op jit(solution)/shard_map/field/pallas_call | solution.py:432
  47.2 9.1 %all_to_all.15.pieces_ref = bf16[4,2,2,16,512]{4,3,2,1,0:T(8,128)(2,1)S(1)} all-to-all(bf16[4,2,2,16,512]{4,3,2,1,0:T(8,128)(2,1)S(1)} %field.1), channel_id=1, replica_groups=mesh['blk'=8,'pair'=4] {'pair'}, dimensions={0} | all-to-all | bytes 524288 | tf_op jit(solution)/shard_map/all_to_all | solution.py:336
  56.3 0.0 copy-done
  56.3 3.4 %image.1 = (f32[4,2048,128]{2,1,0:T(8,128)S(1)}, f32[1024,128]{1,0:T(8,128)S(1)}, f32[32,1,128]{2,1,0:T(1,128)S(1)}) custom-call(f32[4,2040,128]{2,1,0:T(8,128)} %bitcast.16, f32[255,4,128]{2,1,0:T(4,128)} %bitcast.19, f32[1,128]{1,0:T(1,128)S(1)} %copy-done, bf16[4,2,2,16,512]{4,3,2,1,0:T(8,128)(2,1)S(1)} %all_to_all.15.pieces_ref), custom_call_target="tpu_custom_call" | custom-call | tf_op jit(solution)/shard_map/image/pallas_call | solution.py:453
  59.7 12.2 %all_to_all.16.sums_ref = f32[32,1,128]{2,1,0:T(1,128)S(1)} all-to-all(f32[32,1,128]{2,1,0:T(1,128)S(1)} %get-tuple-element.27), channel_id=1, replica_groups=mesh['blk'=8,'pair'=4] {'blk','pair'}, dimensions={0} | all-to-all | bytes 32768 | tf_op jit(solution)/shard_map/all_to_all | solution.py:471
  72.0 1.7 %remainder.1 = (f32[2,8]{1,0:T(2,128)}, f32[255,4,128]{2,1,0:T(4,128)}) custom-call(f32[32,1,128]{2,1,0:T(1,128)S(1)} %all_to_all.16.sums_ref, f32[4,2048,128]{2,1,0:T(8,128)S(1)} %get-tuple-element.28.blocks_ref, f32[1024,128]{1,0:T(8,128)S(1)} %get-tuple-element.29.image_ref), custom_call_target="tpu_custom_call" | custom-call | tf_op jit(solution)/shard_map/remainder/pallas_call | solution.py:474
Async XLA Ops:
  3.2 10.7 %all-to-all-start = ((bf16[4,2,2,16,512]{4,3,2,1,0:T(8,128)(2,1)}), bf16[4,2,2,16,512]{4,3,2,1,0:T(8,128)(2,1)S(1)}, u32[]{:S(2)}, u32[]{:S(2)}) async-start(bf16[4,2,2,16,512]{4,3,2,1,0:T(8,128)(2,1)} %pack.1), calls=%async_computation | async-start | bytes 524288 | tf_op jit(solution)/shard_map/all_to_all | solution.py:336
  13.9 19.6 %collective-permute-start.1 = (bf16[4,2,2,16,512]{4,3,2,1,0:T(8,128)(2,1)S(1)}, bf16[4,2,2,16,512]{4,3,2,1,0:T(8,128)(2,1)S(1)}, u32[]{:S(2)}, u32[]{:S(2)}) collective-permute-start(bf16[4,2,2,16,512]{4,3,2,1,0:T(8,128)(2,1)S(1)} %all-to-all-done.own_ref), channel_id=1, source_target_pairs={{4,0},{8,4},{12,8},{16,12},{20,16},{24,20},{28,24},{5,1},{9,5},{13... | collective-permute-start | bytes 786440 | tf_op jit(solution)/shard_map/ppermute | solution.py:343
  15.2 18.3 %collective-permute-start = (bf16[4,2,2,16,512]{4,3,2,1,0:T(8,128)(2,1)S(1)}, bf16[4,2,2,16,512]{4,3,2,1,0:T(8,128)(2,1)S(1)}, u32[]{:S(2)}, u32[]{:S(2)}) collective-permute-start(bf16[4,2,2,16,512]{4,3,2,1,0:T(8,128)(2,1)S(1)} %all-to-all-done.own_ref), channel_id=1, source_target_pairs={{0,4},{4,8},{8,12},{12,16},{16,20},{20,24},{24,28},{1,5},{5,9},{9,... | collective-permute-start | bytes 786440 | tf_op jit(solution)/shard_map/ppermute | solution.py:343
  34.3 22.0 %copy-start = (f32[1,128]{1,0:T(1,128)S(1)}, f32[1,128]{1,0:T(1,128)}, u32[]{:S(2)}) copy-start(f32[1,128]{1,0:T(1,128)} %gram.1.gram_ref) | copy-start | bytes 1540

commit v4 on v3

--- a/solution.py
+++ b/solution.py
@@ -105,75 +105,81 @@
             rot_out_ref[g, q * each : (q + 1) * each, 0:modes] = sorted_rows[g * each : (g + 1) * each]
 
 
-def weights_kernel(own, part, modes, below_ref, own_ref, above_ref, out_ref):
-    tables = out_ref.shape[0]
-    group = own * part
-    size = own_ref.shape[4]
-    lane = modes % 128
-    wanted = lax.div(iota((tables * group, group), 0), part) + own
-
-    def lists(ref):
-        values = ref[:, :, :, :, size - 128 : size].reshape(2 * group, 128).astype(F32)
-        marks, sources = values[:group], values[group:]
-        lines = [jnp.transpose(side)[lane : lane + 1].astype(jnp.int32) for side in (marks, sources)]
-        return lines, [side[:, lane : lane + 1].astype(jnp.int32) for side in (marks, sources)]
+def swapped(value):
+    half = value.shape[0] // 2
+    return jnp.concatenate([-value[half:], value[:half]], axis=0)
+
+
+def pair_counts(own, tables, lane, refs):
+    group, size = refs[0].shape[0] * refs[0].shape[2] * refs[0].shape[3], refs[0].shape[4]
+    wanted = iota((tables * own, group), 0) + own
 
     def one_hot(hit):
         return jnp.where(hit, 1.0, 0.0).astype(BF16)
 
-    def store(direction, first, counts):
-        lanes = counts.shape[1]
-        same = lax.rem(iota(counts.shape, 0), part) == lax.rem(iota(counts.shape, 1), part)
-        kept = jnp.where(same, counts, 0.0).astype(BF16)
-        for g in range(tables):
-            out_ref[g, direction * group : (direction + 1) * group, first : first + lanes] = kept[g * group : (g + 1) * group]
-
-    for window, ref in enumerate((below_ref, own_ref, above_ref)):
-        (marks, sources), (marks_column, sources_column) = lists(ref)
+    forward, backward = None, []
+    for window, ref in enumerate(refs):
+        values = ref[:, :, :, :, size - 128 : size].reshape(2 * group, 128).astype(F32)
+        marks_column, sources_column = (values[h * group : (h + 1) * group, lane : lane + 1].astype(jnp.int32) for h in range(2))
+        marks, sources = (jnp.transpose(values[h * group : (h + 1) * group])[lane : lane + 1].astype(jnp.int32) for h in range(2))
         if window == 1:
-            spread = one_hot(sources_column == lax.div(iota((group, 3 * group), 1), part))
-            store(0, 0, dot_nn(one_hot(marks == wanted), spread))
+            forward = dot_nn(one_hot(marks == wanted), one_hot(sources_column == iota((group, 3 * own), 1)))
         block = sources - (2 - window) * own
         inside = (block >= 0) & (block < own) & (marks >= own)
         hits = one_hot(jnp.where(inside, lax.div(marks, own) * own + block, -1) == wanted)
-        spread = one_hot(lax.rem(marks_column, own) == lax.div(iota((group, group), 1), part))
-        store(1, window * group, dot_nn(hits, spread))
-
-
-def swapped(value):
-    half = value.shape[0] // 2
-    return jnp.concatenate([-value[half:], value[:half]], axis=0)
-
-
-def field_kernel(weights_ref, rot_ref, axial_ref, below_ref, own_ref, above_ref, out_ref, window_ref, total_ref):
-    step = pl.program_id(0)
-    group = weights_ref.shape[1] // 2
-    size = window_ref.shape[2]
-
-    @pl.when(step == 0)
-    def _():
-        for w, ref in enumerate((below_ref, own_ref, above_ref)):
-            for c in range(2):
-                window_ref[c, w * group : (w + 1) * group, :] = ref[:, c].reshape(group, size)
-        total_ref[...] = jnp.zeros_like(total_ref)
-
-    entries = range(weights_ref.shape[0])
-    real = [dot_nn(weights_ref[g], window_ref[0]).astype(BF16) for g in entries]
-    imag = [dot_nn(weights_ref[g], window_ref[1]).astype(BF16) for g in entries]
-    sums = [jnp.concatenate([r[:group], i[:group], r[group:], i[group:]], axis=0) for r, i in zip(real, imag)]
-    turned = [dot_nt(sums[g], rot_ref[g]).astype(BF16) for g in entries]
-    moved = []
-    for g in entries:
-        forward, backward = turned[g][: 2 * group], turned[g][2 * group :]
-        result = dot_nt(forward, axial_ref[g, :size]) + dot_nt(swapped(forward), axial_ref[g, size:])
-        result += dot_nn(jnp.concatenate([backward, swapped(backward)], axis=1), axial_ref[g])
-        moved.append(result.astype(BF16))
-    total_ref[...] += sum(dot_nn(moved[g], rot_ref[g]) for g in entries)
-
-    @pl.when(step == pl.num_programs(0) - 1)
-    def _():
+        place = lax.rem(marks_column, own) + window * own
+        backward.append(dot_nn(hits, one_hot(place == iota((group, 3 * own), 1))))
+    return jnp.concatenate([forward, sum(backward)], axis=0).astype(BF16)
+
+
+def field_kernel(own, modes, together, rot_ref, axial_ref, below_ref, own_ref, above_ref, out_ref, window_ref, sums_ref, total_ref):
+    tables, _, size = rot_ref.shape
+    refs = (below_ref, own_ref, above_ref)
+    ways, _, quarter, part, _ = own_ref.shape
+    group = own * part
+    counts = pair_counts(own, tables, modes % 128, refs)
+    for w, ref in enumerate(refs):
         for c in range(2):
-            out_ref[:, c] = total_ref[c * group : (c + 1) * group].astype(BF16).reshape(out_ref[:, c].shape)
+            for t in range(size // 128):
+                window_ref[w, c, t] = ref[:, c, :, :, t * 128 : (t + 1) * 128].reshape(group, 128).astype(F32)
+    for c in range(2):
+        for s in range(0, part, 2):
+            results = []
+            for sphere in (s, s + 1):
+                blocks = []
+                for t in range(size // 128):
+                    lists = [window_ref[w, c, t, pl.ds(sphere, own, part), :] for w in range(3)]
+                    blocks.append(jnp.concatenate(lists, axis=0).astype(BF16))
+                results.append(dot_nn(counts, jnp.concatenate(blocks, axis=1)))
+            for direction in range(2):
+                for g in range(tables):
+                    first = (direction * tables + g) * own
+                    rows = jnp.concatenate([result[first : first + own] for result in results], axis=0)
+                    place = (direction * 2 + c) * group + s * own
+                    sums_ref[g, place : place + 2 * own, :] = rows.astype(BF16)
+    total_ref[...] = jnp.zeros_like(total_ref)
+
+    def body(step, carry):
+        entries = [step * together + i for i in range(together)]
+        turned = [dot_nt(sums_ref[g], rot_ref[g]).astype(BF16) for g in entries]
+        moved = []
+        for g, both in zip(entries, turned):
+            forward, backward = both[: 2 * group], both[2 * group :]
+            result = dot_nt(forward, axial_ref[g, :size]) + dot_nt(swapped(forward), axial_ref[g, size:])
+            result += dot_nn(jnp.concatenate([backward, swapped(backward)], axis=1), axial_ref[g])
+            moved.append(result.astype(BF16))
+        total_ref[...] += sum(dot_nn(value, rot_ref[g]) for g, value in zip(entries, moved))
+        return carry
+
+    lax.fori_loop(0, tables // together, body, 0)
+    for c in range(2):
+        for t in range(size // 128):
+            lanes = slice(t * 128, (t + 1) * 128)
+            window_ref[0, c, t] = total_ref[c * group : (c + 1) * group, lanes]
+            for p in range(ways):
+                for j in range(quarter):
+                    rows = window_ref[0, c, t, pl.ds(p * quarter + j, part, own), :]
+                    out_ref[p, c, j, :, lanes] = rows.astype(BF16)
 
 
 def lane_swap(value):
@@ -186,23 +192,28 @@
     return jnp.sum(value.reshape(value.shape[0] // 8, 8, value.shape[1]), axis=0)
 
 
-def gram_kernel(quarter, modes, basis_ref, gram_ref, aligned_ref, blocks_ref, sums_ref, sems):
-    vectors, full, columns = aligned_ref.shape
+def gram_kernel(quarter, modes, basis_ref, gram_ref, blocks_ref, odd_ref, sums_ref, sems):
+    blocks, full, columns = odd_ref.shape
+    vectors = 2 * blocks
     rows = quarter * modes
-    copies = [pltpu.make_async_copy(basis_ref.at[i], blocks_ref.at[i], sems.at[i]) for i in range(vectors // 2)]
-    for copy in copies:
+    gap = full - rows
+    middle = full // 2
+    cuts = ((0, middle), (rows - gap, rows + middle + gap)), ((middle, rows - gap), (rows + middle + gap, 2 * rows))
+    copies = []
+    for h, ranges in enumerate(cuts):
+        copies.append([])
+        for i in range(blocks):
+            for side, (first, last) in enumerate(ranges):
+                here = pl.ds(first, last - first)
+                copies[h].append(pltpu.make_async_copy(basis_ref.at[i, here], blocks_ref.at[i, here], sems.at[h, i, side]))
+    for copy in copies[0] + copies[1]:
         copy.start()
     sums_ref[...] = jnp.zeros_like(sums_ref)
-    for i, copy in enumerate(copies):
-        copy.wait()
-        for side in range(2):
-            aligned_ref[2 * i + side, 0:rows, :] = blocks_ref[i, side * rows : (side + 1) * rows, :]
-            aligned_ref[2 * i + side, rows:full, :] = jnp.zeros((full - rows, columns), F32)
     chunk = 32
 
     def body(i, carry):
         here = pl.ds(pl.multiple_of(i * chunk, chunk), chunk)
-        values = [aligned_ref[k, here, :] for k in range(vectors)]
+        values = [odd_ref[k // 2, here, :] if k % 2 else blocks_ref[k // 2, here, :] for k in range(vectors)]
         for l in range(vectors):
             other = lane_swap(values[l])
             for k in range(l + 1):
@@ -211,7 +222,15 @@
                     sums_ref[l, k] -= folded(values[k] * other)
         return carry
 
-    lax.fori_loop(0, full // chunk, body, 0)
+    for h, (first, last) in enumerate(((0, middle), (middle, rows))):
+        for copy in copies[h]:
+            copy.wait()
+        for i in range(blocks):
+            odd_ref[i, first:last, :] = blocks_ref[i, rows + first : rows + last, :]
+            if last == rows:
+                blocks_ref[i, rows:full, :] = jnp.zeros((gap, columns), F32)
+                odd_ref[i, rows:full, :] = jnp.zeros((gap, columns), F32)
+        lax.fori_loop(first // chunk, rounded_up(last, chunk) // chunk, body, 0)
     totals = jnp.sum(jnp.sum(sums_ref[...].reshape(vectors * vectors, 8, columns), axis=1), axis=1, keepdims=True)
     row, lane = iota((vectors, 128), 0), iota((vectors, 128), 1)
     line = jnp.zeros((1, 128), F32)
@@ -221,61 +240,56 @@
     gram_ref[...] = line
 
 
-def image_kernel(quarter, modes, basis_ref, mie_ref, gram_ref, pieces_ref, blocks_ref, image_ref, sums_ref, lines_ref, mies_ref, tile_ref, sems):
-    blocks = blocks_ref.shape[0]
-    vectors = 2 * blocks
+def stage_kernel(basis_ref, mie_ref, blocks_ref, mie_out_ref, mies_ref, sems):
+    blocks, _, columns = blocks_ref.shape
+    rows = basis_ref.shape[1]
+    mie_rows = mies_ref.shape[0] * mies_ref.shape[1]
+    copies = [pltpu.make_async_copy(basis_ref.at[i], blocks_ref.at[i, pl.ds(0, rows)], sems.at[i]) for i in range(blocks)]
+    mie_copy = pltpu.make_async_copy(mie_ref, mies_ref, sems.at[blocks])
+    mie_copy.start()
+    for i, copy in enumerate(copies):
+        copy.start()
+        blocks_ref[i, rows:, :] = jnp.zeros((blocks_ref.shape[1] - rows, columns), F32)
+    mie_out_ref[mie_rows:, :] = jnp.zeros((mie_out_ref.shape[0] - mie_rows, columns), F32)
+    mie_copy.wait()
+    mie_out_ref[0:mie_rows, :] = mies_ref[...].reshape(mie_rows, columns)
+    for copy in copies:
+        copy.wait()
+
+
+def image_kernel(quarter, modes, blocks_ref, mie_ref, gram_ref, pieces_ref, image_ref, sums_ref, lines_ref):
+    vectors = 2 * blocks_ref.shape[0]
     full, columns = image_ref.shape
     rows = quarter * modes
-    height = mies_ref.shape[1]
     ways, _, _, part, size = pieces_ref.shape
-    small = [pltpu.make_async_copy(mie_ref, mies_ref, sems.at[blocks]), pltpu.make_async_copy(gram_ref, tile_ref, sems.at[blocks + 1])]
-    copies = [pltpu.make_async_copy(basis_ref.at[i], blocks_ref.at[i, pl.ds(0, 2 * rows)], sems.at[i]) for i in range(blocks)]
-    for copy in [copies[-1]] + small + copies[:-1]:
-        copy.start()
-    for i in range(blocks):
-        blocks_ref[i, 2 * rows :, :] = jnp.zeros((blocks_ref.shape[1] - 2 * rows, columns), F32)
     lines_ref[rows:full, :] = jnp.zeros((full - rows, columns), F32)
     for j in range(quarter):
         turned = jnp.concatenate([pieces_ref[:, c, j].reshape(ways * part, size) for c in range(2)], axis=0)
         lines_ref[pl.ds(j, modes, quarter), :] = jnp.transpose(turned.astype(F32))[:modes]
     half = columns // 2
     chunk = 64
-    copies[-1].wait()
-    for copy in small:
-        copy.wait()
-    square = jnp.zeros((8, columns), F32)
+    totals = [jnp.zeros((8, columns), F32) for _ in range(2 * vectors + 1)]
     for first in range(0, full, chunk):
-        count = min(chunk, rows - first)
         here = slice(first, first + chunk)
-        field = lines_ref[here, :]
-        mie = mies_ref[first // height : (first + count) // height].reshape(count, columns)
-        if count < chunk:
-            mie = jnp.concatenate([mie, jnp.zeros((chunk - count, columns), F32)], axis=0)
+        field, mie = lines_ref[here, :], mie_ref[here, :]
         left = iota(mie.shape, 1) < half
         other = pltpu.roll(mie, half, axis=1)
         product = jnp.where(left, mie, other) * field + jnp.where(left, -other, mie) * pltpu.roll(field, half, axis=1)
-        image = blocks_ref[blocks - 1, rows + first : rows + first + chunk, :] - product
+        last = (vectors - 1) % 2 * rows + first
+        image = blocks_ref[(vectors - 1) // 2, last : last + chunk, :] - product
         image_ref[here, :] = image
-        square += folded(image * image)
-    lane = iota(tile_ref.shape, 1)
-    tile = tile_ref[...]
-    for i in reversed(range(blocks)):
-        if i < blocks - 1:
-            copies[i].wait()
-        totals = [jnp.zeros((8, columns), F32) for _ in range(4)]
-        for first in range(0, full, chunk):
-            image = image_ref[first : first + chunk, :]
-            turned = lane_swap(image)
-            for side in range(2):
-                values = blocks_ref[i, side * rows + first : side * rows + first + chunk, :]
-                totals[2 * side] += folded(values * image)
-                totals[2 * side + 1] -= folded(values * turned)
-        for index, total in enumerate(totals):
-            total = jnp.sum(total, axis=(0, 1), keepdims=True)
-            tile = jnp.where(lane == vectors * vectors + 4 * i + index, total, tile)
-    square = jnp.sum(square, axis=(0, 1), keepdims=True)
-    tile = jnp.where(lane == vectors * vectors + 2 * vectors, square, tile)
-    sums_ref[...] = jnp.broadcast_to(tile[None], sums_ref.shape)
+        turned = lane_swap(image)
+        for k in range(vectors):
+            start = k % 2 * rows + first
+            values = blocks_ref[k // 2, start : start + chunk, :]
+            totals[2 * k] += folded(values * image)
+            totals[2 * k + 1] -= folded(values * turned)
+        totals[2 * vectors] += folded(image * image)
+    lane = iota(gram_ref.shape, 1)
+    line = gram_ref[...]
+    for index, total in enumerate(totals):
+        line = jnp.where(lane == vectors * vectors + index, jnp.sum(total, axis=(0, 1), keepdims=True), line)
+    sums_ref[...] = jnp.broadcast_to(line[None], sums_ref.shape)
 
 
 def remainder_kernel(quarter, modes, mean_scale, sums_ref, blocks_ref, image_ref, dots_ref, out_ref):
@@ -389,15 +403,16 @@
         out_specs=pl.BlockSpec((1, 128), lambda i: (0, 0)),
         out_shape=pltpu.HBM((1, 128), F32),
         scratch_shapes=[
-            pltpu.VMEM((vectors, full, columns), F32),
             pltpu.VMEM((pairs_of_vectors, 2 * rows, columns), F32),
+            pltpu.VMEM((pairs_of_vectors, full, columns), F32),
             pltpu.VMEM((vectors, vectors, 8, columns), F32),
-            pltpu.SemaphoreType.DMA((pairs_of_vectors,)),
+            pltpu.SemaphoreType.DMA((2, pairs_of_vectors, 2)),
         ],
         compiler_params=params(16),
         name="gram",
     )(basis_later)
-    own_pieces, gram = lax.optimization_barrier((own_pieces, gram))
+    own_pieces, gram, *inputs = lax.optimization_barrier((own_pieces, gram, basis_rows, mie_rows, rot_rows, axial_rows))
+    basis_rows, mie_rows, rot_rows, axial_rows = inputs
     below, above = neighbours(own_pieces)
 
     rotations, axials = pl.pallas_call(
@@ -411,65 +426,60 @@
             pl.BlockSpec((tables, size // tables, size), lambda g: (0, g, 0)),
             pl.BlockSpec((1, 2 * size, size), lambda g: (g, 0, 0)),
         ],
-        out_shape=[pltpu.HBM((tables, size, size), BF16), pltpu.HBM((tables, 2 * size, size), BF16)],
+        out_shape=[
+            jax.ShapeDtypeStruct((tables, size, size), BF16),
+            jax.ShapeDtypeStruct((tables, 2 * size, size), BF16),
+        ],
         scratch_shapes=[pltpu.VMEM((2 * size, size), BF16)],
         compiler_params=params(32),
         cost_estimate=pl.CostEstimate(flops=tables * 8 * 256 * 256 * size, bytes_accessed=6 * tables * size * size * 2, transcendentals=0),
         name="tables",
     )(axial_rows, rot_rows)
 
-    below, above, rotations, axials = lax.optimization_barrier((below, above, rotations, axials))
-    weights = pl.pallas_call(
-        functools.partial(weights_kernel, own, part, modes),
-        in_specs=[whole()] * 3,
-        out_specs=whole(),
-        out_shape=jax.ShapeDtypeStruct((tables, 2 * group, 3 * group), BF16),
-        compiler_params=params(24),
-        name="weights",
-    )(below, own_pieces, above)
-
-    entries = 2 if tables % 2 == 0 else 1
-    field = pl.pallas_call(
-        field_kernel,
-        grid=(tables // entries,),
-        in_specs=[
-            pl.BlockSpec((entries, 2 * group, 3 * group), lambda g: (g, 0, 0)),
-            pl.BlockSpec((entries, size, size), lambda g: (g, 0, 0)),
-            pl.BlockSpec((entries, 2 * size, size), lambda g: (g, 0, 0)),
-            whole(),
-            whole(),
-            whole(),
-        ],
-        out_specs=whole(),
-        out_shape=jax.ShapeDtypeStruct(pieces_shape, BF16),
-        scratch_shapes=[pltpu.VMEM((2, 3 * group, size), BF16), pltpu.VMEM((2 * group, size), F32)],
-        compiler_params=params(24),
-        name="field",
-    )(weights, in_hbm(rotations), in_hbm(axials), below, own_pieces, above)
-    field_pieces = exchanged(field)
-
-    height = 4
     tall = rounded_up(rows + full, 8)
-    blocks, image, sums = pl.pallas_call(
-        functools.partial(image_kernel, quarter, modes),
-        in_specs=[hbm(), hbm(), hbm(), whole()],
-        out_specs=[whole()] * 3,
+    blocks, mies = pl.pallas_call(
+        stage_kernel,
+        in_specs=[hbm(), hbm()],
+        out_specs=[whole()] * 2,
         out_shape=[
             jax.ShapeDtypeStruct((pairs_of_vectors, tall, columns), F32),
             jax.ShapeDtypeStruct((full, columns), F32),
-            jax.ShapeDtypeStruct((ways * blk_ways, 1, 128), F32),
-        ],
+        ],
+        scratch_shapes=[pltpu.VMEM(mie_rows.shape, F32), pltpu.SemaphoreType.DMA((pairs_of_vectors + 1,))],
+        compiler_params=params(8),
+        name="stage",
+    )(basis_rows, mie_rows)
+    held = lax.optimization_barrier((below, above, rotations, axials, blocks, mies))
+    below, above, rotations, axials, blocks, mies = held
+
+    together = 2 if tables % 2 == 0 else 1
+    field = pl.pallas_call(
+        functools.partial(field_kernel, own, modes, together),
+        in_specs=[whole()] * 5,
+        out_specs=whole(),
+        out_shape=jax.ShapeDtypeStruct(pieces_shape, BF16),
         scratch_shapes=[
-            pltpu.VMEM((full, columns), F32),
-            pltpu.VMEM((rows // height, height, columns), F32),
-            pltpu.VMEM((1, 128), F32),
-            pltpu.SemaphoreType.DMA((pairs_of_vectors + 2,)),
-        ],
-        compiler_params=params(16),
+            pltpu.VMEM((3, 2, size // 128, group, 128), F32),
+            pltpu.VMEM((tables, 4 * group, size), BF16),
+            pltpu.VMEM((2 * group, size), F32),
+        ],
+        compiler_params=params(20),
+        name="field",
+    )(rotations, axials, below, own_pieces, above)
+    field_pieces = exchanged(field)
+
+    image, sums = pl.pallas_call(
+        functools.partial(image_kernel, quarter, modes),
+        in_specs=[whole()] * 4,
+        out_specs=[whole()] * 2,
+        out_shape=[jax.ShapeDtypeStruct((full, columns), F32), jax.ShapeDtypeStruct((ways * blk_ways, 1, 128), F32)],
+        scratch_shapes=[pltpu.VMEM((full, columns), F32)],
+        compiler_params=params(8),
         name="image",
-    )(basis_rows, mie_rows, gram, field_pieces)
+    )(blocks, mies, gram, field_pieces)
     sums = lax.all_to_all(sums, ("blk", "pair"), split_axis=0, concat_axis=0, tiled=True)
 
+    height = 4
     mean_scale = 1.0 / (own * blk_ways * modes * columns)
     dots, next_rows = pl.pallas_call(
         functools.partial(remainder_kernel, quarter, modes, mean_scale),

time: 74.2 us -> 66.8 us (0.900)
  Pallas kernels: 40.7 us -> 33.4 us
    pallas_call x1, Pallas kernels: 13.6 us -> 9.45 us  [shards(): pl.pallas_call(functools.partial(tables_kernel, modes, tables), grid=(tab...]
    pallas_call x1, Pallas kernels: 3.4 us -> 1.41 us  [shards(): pl.pallas_call(functools.partial(image_kernel, quarter, modes), in_specs=...]
    pallas_call x2, Pallas kernels: 13.6 us -> 12.8 us  [the longest x1 10.5 us: shards(): pl.pallas_call(functools.partial(field_kernel, own, modes, together), in_...]
where the time goes in v4:
time: 66.8 us; the launch traced here: 66.3 us
  Pallas kernels  33.4 us (50%)
  blocking collectives  21.3 us (32%)
  starting transfers between devices  10.2 us (15%)
  between operations  1.37 us (2%)
    all_to_all x1, blocking collectives, shards(): lax.all_to_all(sums, ('blk', 'pair'), split_axis=0, concat_axis=0, tiled=...  12.2 us
    pallas_call x1, Pallas kernels, shards(): pl.pallas_call(functools.partial(field_kernel, own, modes, together), in_...  10.5 us
    pallas_call x1, Pallas kernels, shards(): pl.pallas_call(functools.partial(tables_kernel, modes, tables), grid=(tab...  9.45 us
    all_to_all x1, blocking collectives, exchanged(): lax.all_to_all(value, 'pair', split_axis=0, concat_axis=0, tiled=True)  9.09 us
    pallas_call x1, Pallas kernels, shards(): pl.pallas_call(functools.partial(gram_kernel, quarter, modes), grid=(1,),...  6.07 us
    ppermute x2, starting transfers between devices, neighbours(): return (lax.ppermute(value, 'blk', up), lax.ppermute(value, 'blk', down))  6.02 us
    all_to_all x1, starting transfers between devices, exchanged(): lax.all_to_all(value, 'pair', split_axis=0, concat_axis=0, tiled=True)  4.22 us
    pallas_call x1, Pallas kernels, shards(): pl.pallas_call(stage_kernel, in_specs=[hbm(), hbm()], out_specs=[whole()]...  2.38 us
  transfers between devices with their start and end apart: 3, of which 0 were waited for; matrix products, arithmetic and copies ran while one was open for 0% of the time, Pallas kernels for 27%

profile of v4, /device:TPU:0, one launch (start us, length us, event | category | flops | bytes accessed | tf_op | source)
XLA Modules:
  0.0 66.3 jit_solution(4483516272018450847)
XLA Ops:
  1.3 2.0 %pack.1 = bf16[4,2,2,16,512]{4,3,2,1,0:T(8,128)(2,1)} custom-call(s32[3,1,128]{2,1,0:T(1,128)} %bitcast.20, s32[1]{0:T(128)S(6)} %copy.8.count_ref, f32[4,2040,128]{2,1,0:T(8,128)} %bitcast.14), custom_call_target="tpu_custom_call" | custom-call | tf_op jit(solution)/shard_map/pack/pallas_call | solution.py:381
  3.2 4.2 %all-to-all-start = ((bf16[4,2,2,16,512]{4,3,2,1,0:T(8,128)(2,1)}), bf16[4,2,2,16,512]{4,3,2,1,0:T(8,128)(2,1)S(1)}, u32[]{:S(2)}, u32[]{:S(2)}) async-start(bf16[4,2,2,16,512]{4,3,2,1,0:T(8,128)(2,1)} %pack.1), calls=%async_computation | async-start | bytes 524288 | tf_op jit(solution)/shard_map/all_to_all | solution.py:350
  7.5 6.1 %gram.1.gram_ref = f32[1,128]{1,0:T(1,128)} custom-call(f32[4,2040,128]{2,1,0:T(8,128)} %bitcast.15), custom_call_target="tpu_custom_call" | custom-call | tf_op jit(solution)/shard_map/gram/pallas_call | solution.py:399
  13.5 0.0 all-to-all-done.own_ref
  13.5 1.3 %collective-permute-start.1 = (bf16[4,2,2,16,512]{4,3,2,1,0:T(8,128)(2,1)S(1)}, bf16[4,2,2,16,512]{4,3,2,1,0:T(8,128)(2,1)S(1)}, u32[]{:S(2)}, u32[]{:S(2)}) collective-permute-start(bf16[4,2,2,16,512]{4,3,2,1,0:T(8,128)(2,1)S(1)} %all-to-all-done.own_ref), channel_id=1, source_target_pairs={{4,0},{8,4},{12,8},{16,12},{20,16},{24,20},{28,24},{5,1},{9,5},{13... | collective-permute-start | bytes 786440 | tf_op jit(solution)/shard_map/ppermute | solution.py:357
  14.8 4.7 %collective-permute-start = (bf16[4,2,2,16,512]{4,3,2,1,0:T(8,128)(2,1)S(1)}, bf16[4,2,2,16,512]{4,3,2,1,0:T(8,128)(2,1)S(1)}, u32[]{:S(2)}, u32[]{:S(2)}) collective-permute-start(bf16[4,2,2,16,512]{4,3,2,1,0:T(8,128)(2,1)S(1)} %all-to-all-done.own_ref), channel_id=1, source_target_pairs={{0,4},{4,8},{8,12},{12,16},{16,20},{20,24},{24,28},{1,5},{5,9},{9,... | collective-permute-start | bytes 786440 | tf_op jit(solution)/shard_map/ppermute | solution.py:357
  19.6 2.4 %stage.1 = (f32[4,2048,128]{2,1,0:T(8,128)S(1)}, f32[1024,128]{1,0:T(8,128)S(1)}) custom-call(f32[4,2040,128]{2,1,0:T(8,128)} %bitcast.16, f32[255,4,128]{2,1,0:T(4,128)} %bitcast.19), custom_call_target="tpu_custom_call" | custom-call | tf_op jit(solution)/shard_map/stage/pallas_call | solution.py:440
  22.0 9.5 %tables.1 = (bf16[8,512,512]{2,1,0:T(8,128)(2,1)S(1)}, bf16[8,1024,512]{2,1,0:T(8,128)(2,1)S(1)}) custom-call(bf16[8,510,2,510]{3,2,1,0:T(2,128)(2,1)} %bitcast.17, bf16[4080,510]{1,0:T(8,128)(2,1)} %bitcast.18), custom_call_target="tpu_custom_call" | custom-call | flops 2147483648 | bytes 25165824 | tf_op jit(solution)/shard_map/tables/pallas_call | solution.py:418
  31.4 0.0 collective-permute-done.1.above_ref
  31.4 0.0 collective-permute-done.below_ref
  31.4 0.0 copy-start
  31.5 10.5 %field.1 = bf16[4,2,2,16,512]{4,3,2,1,0:T(8,128)(2,1)S(1)} custom-call(bf16[8,512,512]{2,1,0:T(8,128)(2,1)S(1)} %get-tuple-element.38.rot_ref, bf16[8,1024,512]{2,1,0:T(8,128)(2,1)S(1)} %get-tuple-element.39.axial_ref, bf16[4,2,2,16,512]{4,3,2,1,0:T(8,128)(2,1)S(1)} %collective-permute-done.below_ref, bf16[4,2,2,16,512]{4,3,2,1,0:T(8,128)(2,1)S(1)} %all-to-all-done.own_ref, ...), custom_call_target="tpu_custom_call" | custom-call | tf_op jit(solution)/shard_map/field/pallas_call | solution.py:456
  41.9 9.1 %all_to_all.15.pieces_ref = bf16[4,2,2,16,512]{4,3,2,1,0:T(8,128)(2,1)S(1)} all-to-all(bf16[4,2,2,16,512]{4,3,2,1,0:T(8,128)(2,1)S(1)} %field.1), channel_id=1, replica_groups=mesh['blk'=8,'pair'=4] {'pair'}, dimensions={0} | all-to-all | bytes 524288 | tf_op jit(solution)/shard_map/all_to_all | solution.py:350
  51.0 0.0 copy-done
  51.0 1.4 %image.1 = (f32[1024,128]{1,0:T(8,128)S(1)}, f32[32,1,128]{2,1,0:T(1,128)S(1)}) custom-call(f32[4,2048,128]{2,1,0:T(8,128)S(1)} %get-tuple-element.35.blocks_ref, f32[1024,128]{1,0:T(8,128)S(1)} %get-tuple-element.36.mie_ref, f32[1,128]{1,0:T(1,128)S(1)} %copy-done, bf16[4,2,2,16,512]{4,3,2,1,0:T(8,128)(2,1)S(1)} %all_to_all.15.pieces_ref), custom_call_target="tpu_custom_call" | custom-call | tf_op jit(solution)/shard_map/image/pallas_call | solution.py:471
  52.4 12.2 %all_to_all.16.sums_ref = f32[32,1,128]{2,1,0:T(1,128)S(1)} all-to-all(f32[32,1,128]{2,1,0:T(1,128)S(1)} %get-tuple-element.42), channel_id=1, replica_groups=mesh['blk'=8,'pair'=4] {'blk','pair'}, dimensions={0} | all-to-all | bytes 32768 | tf_op jit(solution)/shard_map/all_to_all | solution.py:480
  64.7 1.6 %remainder.1 = (f32[2,8]{1,0:T(2,128)}, f32[255,4,128]{2,1,0:T(4,128)}) custom-call(f32[32,1,128]{2,1,0:T(1,128)S(1)} %all_to_all.16.sums_ref, f32[4,2048,128]{2,1,0:T(8,128)S(1)} %get-tuple-element.35.blocks_ref, f32[1024,128]{1,0:T(8,128)S(1)} %get-tuple-element.43.image_ref), custom_call_target="tpu_custom_call" | custom-call | tf_op jit(solution)/shard_map/remainder/pallas_call | solution.py:484
Async XLA Ops:
  3.2 10.3 %all-to-all-start = ((bf16[4,2,2,16,512]{4,3,2,1,0:T(8,128)(2,1)}), bf16[4,2,2,16,512]{4,3,2,1,0:T(8,128)(2,1)S(1)}, u32[]{:S(2)}, u32[]{:S(2)}) async-start(bf16[4,2,2,16,512]{4,3,2,1,0:T(8,128)(2,1)} %pack.1), calls=%async_computation | async-start | bytes 524288 | tf_op jit(solution)/shard_map/all_to_all | solution.py:350
  13.5 17.9 %collective-permute-start.1 = (bf16[4,2,2,16,512]{4,3,2,1,0:T(8,128)(2,1)S(1)}, bf16[4,2,2,16,512]{4,3,2,1,0:T(8,128)(2,1)S(1)}, u32[]{:S(2)}, u32[]{:S(2)}) collective-permute-start(bf16[4,2,2,16,512]{4,3,2,1,0:T(8,128)(2,1)S(1)} %all-to-all-done.own_ref), channel_id=1, source_target_pairs={{4,0},{8,4},{12,8},{16,12},{20,16},{24,20},{28,24},{5,1},{9,5},{13... | collective-permute-start | bytes 786440 | tf_op jit(solution)/shard_map/ppermute | solution.py:357
  14.8 16.6 %collective-permute-start = (bf16[4,2,2,16,512]{4,3,2,1,0:T(8,128)(2,1)S(1)}, bf16[4,2,2,16,512]{4,3,2,1,0:T(8,128)(2,1)S(1)}, u32[]{:S(2)}, u32[]{:S(2)}) collective-permute-start(bf16[4,2,2,16,512]{4,3,2,1,0:T(8,128)(2,1)S(1)} %all-to-all-done.own_ref), channel_id=1, source_target_pairs={{0,4},{4,8},{8,12},{12,16},{16,20},{20,24},{24,28},{1,5},{5,9},{9,... | collective-permute-start | bytes 786440 | tf_op jit(solution)/shard_map/ppermute | solution.py:357
  31.4 19.6 %copy-start = (f32[1,128]{1,0:T(1,128)S(1)}, f32[1,128]{1,0:T(1,128)}, u32[]{:S(2)}) copy-start(f32[1,128]{1,0:T(1,128)} %gram.1.gram_ref) | copy-start | bytes 1540

commit v5 on v4

--- a/solution.py
+++ b/solution.py
@@ -132,8 +132,19 @@
     return jnp.concatenate([forward, sum(backward)], axis=0).astype(BF16)
 
 
-def field_kernel(own, modes, together, rot_ref, axial_ref, below_ref, own_ref, above_ref, out_ref, window_ref, sums_ref, total_ref):
+def field_kernel(
+    own, modes, together, rot_ref, axial_ref, below_ref, own_ref, above_ref, basis_ref, mie_ref,
+    out_ref, blocks_ref, mies_ref, window_ref, sums_ref, total_ref, sems,
+):
     tables, _, size = rot_ref.shape
+    vector_blocks, rows, columns = basis_ref.shape
+    copies = [pltpu.make_async_copy(mie_ref, mies_ref, sems.at[vector_blocks])]
+    for i in range(vector_blocks):
+        copies.append(pltpu.make_async_copy(basis_ref.at[i], blocks_ref.at[i, pl.ds(0, rows)], sems.at[i]))
+    for copy in copies:
+        copy.start()
+    for i in range(vector_blocks):
+        blocks_ref[i, rows:, :] = jnp.zeros((blocks_ref.shape[1] - rows, columns), F32)
     refs = (below_ref, own_ref, above_ref)
     ways, _, quarter, part, _ = own_ref.shape
     group = own * part
@@ -180,6 +191,8 @@
                 for j in range(quarter):
                     rows = window_ref[0, c, t, pl.ds(p * quarter + j, part, own), :]
                     out_ref[p, c, j, :, lanes] = rows.astype(BF16)
+    for copy in copies:
+        copy.wait()
 
 
 def lane_swap(value):
@@ -240,23 +253,6 @@
     gram_ref[...] = line
 
 
-def stage_kernel(basis_ref, mie_ref, blocks_ref, mie_out_ref, mies_ref, sems):
-    blocks, _, columns = blocks_ref.shape
-    rows = basis_ref.shape[1]
-    mie_rows = mies_ref.shape[0] * mies_ref.shape[1]
-    copies = [pltpu.make_async_copy(basis_ref.at[i], blocks_ref.at[i, pl.ds(0, rows)], sems.at[i]) for i in range(blocks)]
-    mie_copy = pltpu.make_async_copy(mie_ref, mies_ref, sems.at[blocks])
-    mie_copy.start()
-    for i, copy in enumerate(copies):
-        copy.start()
-        blocks_ref[i, rows:, :] = jnp.zeros((blocks_ref.shape[1] - rows, columns), F32)
-    mie_out_ref[mie_rows:, :] = jnp.zeros((mie_out_ref.shape[0] - mie_rows, columns), F32)
-    mie_copy.wait()
-    mie_out_ref[0:mie_rows, :] = mies_ref[...].reshape(mie_rows, columns)
-    for copy in copies:
-        copy.wait()
-
-
 def image_kernel(quarter, modes, blocks_ref, mie_ref, gram_ref, pieces_ref, image_ref, sums_ref, lines_ref):
     vectors = 2 * blocks_ref.shape[0]
     full, columns = image_ref.shape
@@ -271,7 +267,12 @@
     totals = [jnp.zeros((8, columns), F32) for _ in range(2 * vectors + 1)]
     for first in range(0, full, chunk):
         here = slice(first, first + chunk)
-        field, mie = lines_ref[here, :], mie_ref[here, :]
+        field = lines_ref[here, :]
+        count = min(chunk, rows - first)
+        height = mie_ref.shape[1]
+        mie = mie_ref[first // height : (first + count) // height].reshape(count, columns)
+        if count < chunk:
+            mie = jnp.concatenate([mie, jnp.zeros((chunk - count, columns), F32)], axis=0)
         left = iota(mie.shape, 1) < half
         other = pltpu.roll(mie, half, axis=1)
         product = jnp.where(left, mie, other) * field + jnp.where(left, -other, mie) * pltpu.roll(field, half, axis=1)
@@ -437,35 +438,27 @@
     )(axial_rows, rot_rows)
 
     tall = rounded_up(rows + full, 8)
-    blocks, mies = pl.pallas_call(
-        stage_kernel,
-        in_specs=[hbm(), hbm()],
-        out_specs=[whole()] * 2,
+    below, above, rotations, axials = lax.optimization_barrier((below, above, rotations, axials))
+
+    together = 2 if tables % 2 == 0 else 1
+    field, blocks, mies = pl.pallas_call(
+        functools.partial(field_kernel, own, modes, together),
+        in_specs=[whole()] * 5 + [hbm()] * 2,
+        out_specs=[whole()] * 3,
         out_shape=[
+            jax.ShapeDtypeStruct(pieces_shape, BF16),
             jax.ShapeDtypeStruct((pairs_of_vectors, tall, columns), F32),
-            jax.ShapeDtypeStruct((full, columns), F32),
-        ],
-        scratch_shapes=[pltpu.VMEM(mie_rows.shape, F32), pltpu.SemaphoreType.DMA((pairs_of_vectors + 1,))],
-        compiler_params=params(8),
-        name="stage",
-    )(basis_rows, mie_rows)
-    held = lax.optimization_barrier((below, above, rotations, axials, blocks, mies))
-    below, above, rotations, axials, blocks, mies = held
-
-    together = 2 if tables % 2 == 0 else 1
-    field = pl.pallas_call(
-        functools.partial(field_kernel, own, modes, together),
-        in_specs=[whole()] * 5,
-        out_specs=whole(),
-        out_shape=jax.ShapeDtypeStruct(pieces_shape, BF16),
+            jax.ShapeDtypeStruct(mie_rows.shape, F32),
+        ],
         scratch_shapes=[
             pltpu.VMEM((3, 2, size // 128, group, 128), F32),
             pltpu.VMEM((tables, 4 * group, size), BF16),
             pltpu.VMEM((2 * group, size), F32),
+            pltpu.SemaphoreType.DMA((pairs_of_vectors + 1,)),
         ],
         compiler_params=params(20),
         name="field",
-    )(rotations, axials, below, own_pieces, above)
+    )(rotations, axials, below, own_pieces, above, basis_rows, mie_rows)
     field_pieces = exchanged(field)
 
     image, sums = pl.pallas_call(

time: 66.8 us -> 65 us (0.973)
  Pallas kernels: 33.4 us -> 31 us
  waiting for transfers between devices: 0.01 us -> 1.3 us
  blocking collectives: 21.3 us -> 20.6 us
    pallas_call x1 -> x0, Pallas kernels: 2.38 us -> none  [shards(): pl.pallas_call(stage_kernel, in_specs=[hbm(), hbm()], out_specs=[whole()]...]
    ppermute x2, waiting for transfers between devices: 0.01 us -> 1.3 us  [neighbours(): return (lax.ppermute(value, 'blk', up), lax.ppermute(value, 'blk', down))]
  transfers between devices with their start and end apart: 3 -> 3, of which waited for: 0 -> 1; matrix products, arithmetic and copies ran while one was open for 0% -> 0% of each run, Pallas kernels for 27% -> 24%
where the time goes in v5:
time: 65 us; the launch traced here: 64.5 us
  Pallas kernels  31 us (48%)
  blocking collectives  20.6 us (32%)
  starting transfers between devices  10.2 us (16%)
  between operations  1.35 us (2%)
  waiting for transfers between devices  1.3 us (2%)
    all_to_all x1, blocking collectives, shards(): lax.all_to_all(sums, ('blk', 'pair'), split_axis=0, concat_axis=0, tiled=...  11.8 us
    pallas_call x1, Pallas kernels, shards(): pl.pallas_call(functools.partial(field_kernel, own, modes, together), in_...  10.5 us
    pallas_call x1, Pallas kernels, shards(): pl.pallas_call(functools.partial(tables_kernel, modes, tables), grid=(tab...  9.45 us
    all_to_all x1, blocking collectives, exchanged(): lax.all_to_all(value, 'pair', split_axis=0, concat_axis=0, tiled=True)  8.78 us
    pallas_call x1, Pallas kernels, shards(): pl.pallas_call(functools.partial(gram_kernel, quarter, modes), grid=(1,),...  6.07 us
    ppermute x2, starting transfers between devices, neighbours(): return (lax.ppermute(value, 'blk', up), lax.ppermute(value, 'blk', down))  6.02 us
    all_to_all x1, starting transfers between devices, exchanged(): lax.all_to_all(value, 'pair', split_axis=0, concat_axis=0, tiled=True)  4.22 us
    pallas_call x1, Pallas kernels, shards(): pl.pallas_call(functools.partial(pack_kernel, quarter, modes, ways, own),...  1.95 us
  transfers between devices with their start and end apart: 3, of which 1 were waited for; matrix products, arithmetic and copies ran while one was open for 0% of the time, Pallas kernels for 24%

profile of v5, /device:TPU:0, one launch (start us, length us, event | category | flops | bytes accessed | tf_op | source)
XLA Modules:
  0.0 64.5 jit_solution(11139927812568953940)
XLA Ops:
  1.3 2.0 %pack.1 = bf16[4,2,2,16,512]{4,3,2,1,0:T(8,128)(2,1)} custom-call(s32[3,1,128]{2,1,0:T(1,128)} %bitcast.20, s32[1]{0:T(128)S(6)} %copy.8.count_ref, f32[4,2040,128]{2,1,0:T(8,128)} %bitcast.14), custom_call_target="tpu_custom_call" | custom-call | tf_op jit(solution)/shard_map/pack/pallas_call | solution.py:382
  3.2 4.2 %all-to-all-start = ((bf16[4,2,2,16,512]{4,3,2,1,0:T(8,128)(2,1)}), bf16[4,2,2,16,512]{4,3,2,1,0:T(8,128)(2,1)S(1)}, u32[]{:S(2)}, u32[]{:S(2)}) async-start(bf16[4,2,2,16,512]{4,3,2,1,0:T(8,128)(2,1)} %pack.1), calls=%async_computation | async-start | bytes 524288 | tf_op jit(solution)/shard_map/all_to_all | solution.py:351
  7.5 6.1 %gram.1.gram_ref = f32[1,128]{1,0:T(1,128)} custom-call(f32[4,2040,128]{2,1,0:T(8,128)} %bitcast.15), custom_call_target="tpu_custom_call" | custom-call | tf_op jit(solution)/shard_map/gram/pallas_call | solution.py:400
  13.5 0.0 all-to-all-done.own_ref
  13.5 1.3 %collective-permute-start.1 = (bf16[4,2,2,16,512]{4,3,2,1,0:T(8,128)(2,1)S(1)}, bf16[4,2,2,16,512]{4,3,2,1,0:T(8,128)(2,1)S(1)}, u32[]{:S(2)}, u32[]{:S(2)}) collective-permute-start(bf16[4,2,2,16,512]{4,3,2,1,0:T(8,128)(2,1)S(1)} %all-to-all-done.own_ref), channel_id=1, source_target_pairs={{4,0},{8,4},{12,8},{16,12},{20,16},{24,20},{28,24},{5,1},{9,5},{13... | collective-permute-start | bytes 786440 | tf_op jit(solution)/shard_map/ppermute | solution.py:358
  14.8 4.7 %collective-permute-start = (bf16[4,2,2,16,512]{4,3,2,1,0:T(8,128)(2,1)S(1)}, bf16[4,2,2,16,512]{4,3,2,1,0:T(8,128)(2,1)S(1)}, u32[]{:S(2)}, u32[]{:S(2)}) collective-permute-start(bf16[4,2,2,16,512]{4,3,2,1,0:T(8,128)(2,1)S(1)} %all-to-all-done.own_ref), channel_id=1, source_target_pairs={{0,4},{4,8},{8,12},{12,16},{16,20},{20,24},{24,28},{1,5},{5,9},{9,... | collective-permute-start | bytes 786440 | tf_op jit(solution)/shard_map/ppermute | solution.py:358
  19.6 9.5 %tables.1 = (bf16[8,512,512]{2,1,0:T(8,128)(2,1)S(1)}, bf16[8,1024,512]{2,1,0:T(8,128)(2,1)S(1)}) custom-call(bf16[8,510,2,510]{3,2,1,0:T(2,128)(2,1)} %bitcast.17, bf16[4080,510]{1,0:T(8,128)(2,1)} %bitcast.18), custom_call_target="tpu_custom_call" | custom-call | flops 2147483648 | bytes 25165824 | tf_op jit(solution)/shard_map/tables/pallas_call | solution.py:419
  29.0 0.0 collective-permute-done.1.above_ref
  29.1 1.3 %collective-permute-done.below_ref = bf16[4,2,2,16,512]{4,3,2,1,0:T(8,128)(2,1)S(1)} collective-permute-done((bf16[4,2,2,16,512]{4,3,2,1,0:T(8,128)(2,1)S(1)}, bf16[4,2,2,16,512]{4,3,2,1,0:T(8,128)(2,1)S(1)}, u32[]{:S(2)}, u32[]{:S(2)}) %collective-permute-start) | collective-permute-done | bytes 262176 | tf_op jit(solution)/shard_map/ppermute | solution.py:358
  30.3 0.0 copy-start
  30.3 10.5 %field.1 = (bf16[4,2,2,16,512]{4,3,2,1,0:T(8,128)(2,1)S(1)}, f32[4,2048,128]{2,1,0:T(8,128)S(1)}, f32[255,4,128]{2,1,0:T(4,128)S(1)}) custom-call(bf16[8,512,512]{2,1,0:T(8,128)(2,1)S(1)} %get-tuple-element.30.rot_ref, bf16[8,1024,512]{2,1,0:T(8,128)(2,1)S(1)} %get-tuple-element.31.axial_ref, bf16[4,2,2,16,512]{4,3,2,1,0:T(8,128)(2,1)S(1)} %collective-permute-done.below_ref, ...), custom_call_target="tpu_custom_call" | custom-call | tf_op jit(solution)/shard_map/field/pallas_call | solution.py:444
  40.9 8.8 %all_to_all.15.pieces_ref = bf16[4,2,2,16,512]{4,3,2,1,0:T(8,128)(2,1)S(1)} all-to-all(bf16[4,2,2,16,512]{4,3,2,1,0:T(8,128)(2,1)S(1)} %get-tuple-element.39), channel_id=1, replica_groups=mesh['blk'=8,'pair'=4] {'pair'}, dimensions={0} | all-to-all | bytes 524288 | tf_op jit(solution)/shard_map/all_to_all | solution.py:351
  49.6 0.0 copy-done
  49.7 1.4 %image.1 = (f32[1024,128]{1,0:T(8,128)S(1)}, f32[32,1,128]{2,1,0:T(1,128)S(1)}) custom-call(f32[4,2048,128]{2,1,0:T(8,128)S(1)} %get-tuple-element.36.blocks_ref, f32[255,4,128]{2,1,0:T(4,128)S(1)} %get-tuple-element.37.mie_ref, f32[1,128]{1,0:T(1,128)S(1)} %copy-done, bf16[4,2,2,16,512]{4,3,2,1,0:T(8,128)(2,1)S(1)} %all_to_all.15.pieces_ref), custom_call_target="tpu_custom_call" | custom-call | tf_op jit(solution)/shard_map/image/pallas_call | solution.py:464
  51.1 11.8 %all_to_all.16.sums_ref = f32[32,1,128]{2,1,0:T(1,128)S(1)} all-to-all(f32[32,1,128]{2,1,0:T(1,128)S(1)} %get-tuple-element.40), channel_id=1, replica_groups=mesh['blk'=8,'pair'=4] {'blk','pair'}, dimensions={0} | all-to-all | bytes 32768 | tf_op jit(solution)/shard_map/all_to_all | solution.py:473
  62.9 1.6 %remainder.1 = (f32[2,8]{1,0:T(2,128)}, f32[255,4,128]{2,1,0:T(4,128)}) custom-call(f32[32,1,128]{2,1,0:T(1,128)S(1)} %all_to_all.16.sums_ref, f32[4,2048,128]{2,1,0:T(8,128)S(1)} %get-tuple-element.36.blocks_ref, f32[1024,128]{1,0:T(8,128)S(1)} %get-tuple-element.41.image_ref), custom_call_target="tpu_custom_call" | custom-call | tf_op jit(solution)/shard_map/remainder/pallas_call | solution.py:477
Async XLA Ops:
  3.2 10.3 %all-to-all-start = ((bf16[4,2,2,16,512]{4,3,2,1,0:T(8,128)(2,1)}), bf16[4,2,2,16,512]{4,3,2,1,0:T(8,128)(2,1)S(1)}, u32[]{:S(2)}, u32[]{:S(2)}) async-start(bf16[4,2,2,16,512]{4,3,2,1,0:T(8,128)(2,1)} %pack.1), calls=%async_computation | async-start | bytes 524288 | tf_op jit(solution)/shard_map/all_to_all | solution.py:351
  13.5 15.5 %collective-permute-start.1 = (bf16[4,2,2,16,512]{4,3,2,1,0:T(8,128)(2,1)S(1)}, bf16[4,2,2,16,512]{4,3,2,1,0:T(8,128)(2,1)S(1)}, u32[]{:S(2)}, u32[]{:S(2)}) collective-permute-start(bf16[4,2,2,16,512]{4,3,2,1,0:T(8,128)(2,1)S(1)} %all-to-all-done.own_ref), channel_id=1, source_target_pairs={{4,0},{8,4},{12,8},{16,12},{20,16},{24,20},{28,24},{5,1},{9,5},{13... | collective-permute-start | bytes 786440 | tf_op jit(solution)/shard_map/ppermute | solution.py:358
  14.8 15.5 %collective-permute-start = (bf16[4,2,2,16,512]{4,3,2,1,0:T(8,128)(2,1)S(1)}, bf16[4,2,2,16,512]{4,3,2,1,0:T(8,128)(2,1)S(1)}, u32[]{:S(2)}, u32[]{:S(2)}) collective-permute-start(bf16[4,2,2,16,512]{4,3,2,1,0:T(8,128)(2,1)S(1)} %all-to-all-done.own_ref), channel_id=1, source_target_pairs={{0,4},{4,8},{8,12},{12,16},{16,20},{20,24},{24,28},{1,5},{5,9},{9,... | collective-permute-start | bytes 786440 | tf_op jit(solution)/shard_map/ppermute | solution.py:358
  30.3 19.3 %copy-start = (f32[1,128]{1,0:T(1,128)S(1)}, f32[1,128]{1,0:T(1,128)}, u32[]{:S(2)}) copy-start(f32[1,128]{1,0:T(1,128)} %gram.1.gram_ref) | copy-start | bytes 1540

commit v6 on v5

--- a/solution.py
+++ b/solution.py
@@ -132,9 +132,45 @@
     return jnp.concatenate([forward, sum(backward)], axis=0).astype(BF16)
 
 
+def folded(value):
+    return jnp.sum(value.reshape(value.shape[0] // 8, 8, value.shape[1]), axis=0)
+
+
+def add_products(blocks_ref, products_ref, rows, first, count):
+    vectors = products_ref.shape[0]
+    values = []
+    for k in range(vectors):
+        start = k % 2 * rows + first
+        value = blocks_ref[k // 2, start : start + count, :]
+        if k % 2 == 0 and first + count > rows:
+            value = jnp.where(iota(value.shape, 0) < rows - first, value, 0.0)
+        values.append(value)
+    for l in range(vectors):
+        other = pltpu.roll(values[l], values[l].shape[1] // 2, axis=1)
+        for k in range(l + 1):
+            products_ref[k, l] += folded(values[k] * values[l])
+            if k < l:
+                products_ref[l, k] += folded(values[k] * other)
+
+
+def products_line(products_ref):
+    vectors, _, _, columns = products_ref.shape
+    pairs = vectors * vectors
+    totals = jnp.sum(products_ref[...].reshape(pairs, 8, columns), axis=1)
+    pair = iota(totals.shape, 0)
+    signed = (lax.div(pair, vectors) > lax.rem(pair, vectors)) & (iota(totals.shape, 1) >= columns // 2)
+    totals = jnp.sum(jnp.where(signed, -totals, totals), axis=1, keepdims=True)
+    row, lane = iota((vectors, 128), 0), iota((vectors, 128), 1)
+    line = jnp.zeros((1, 128), F32)
+    for k in range(vectors):
+        column = totals[k * vectors : (k + 1) * vectors]
+        line += jnp.sum(jnp.where(row + k * vectors == lane, column, 0.0), axis=0, keepdims=True)
+    return line
+
+
 def field_kernel(
-    own, modes, together, rot_ref, axial_ref, below_ref, own_ref, above_ref, basis_ref, mie_ref,
-    out_ref, blocks_ref, mies_ref, window_ref, sums_ref, total_ref, sems,
+    own, quarter, modes, rot_ref, axial_ref, below_ref, own_ref, above_ref, basis_ref, mie_ref,
+    out_ref, blocks_ref, mies_ref, line_ref, window_ref, sums_ref, total_ref, products_ref, sems,
 ):
     tables, _, size = rot_ref.shape
     vector_blocks, rows, columns = basis_ref.shape
@@ -146,7 +182,7 @@
     for i in range(vector_blocks):
         blocks_ref[i, rows:, :] = jnp.zeros((blocks_ref.shape[1] - rows, columns), F32)
     refs = (below_ref, own_ref, above_ref)
-    ways, _, quarter, part, _ = own_ref.shape
+    ways, part = own_ref.shape[0], own_ref.shape[3]
     group = own * part
     counts = pair_counts(own, tables, modes % 128, refs)
     for w, ref in enumerate(refs):
@@ -168,21 +204,22 @@
                     rows = jnp.concatenate([result[first : first + own] for result in results], axis=0)
                     place = (direction * 2 + c) * group + s * own
                     sums_ref[g, place : place + 2 * own, :] = rows.astype(BF16)
-    total_ref[...] = jnp.zeros_like(total_ref)
-
-    def body(step, carry):
-        entries = [step * together + i for i in range(together)]
-        turned = [dot_nt(sums_ref[g], rot_ref[g]).astype(BF16) for g in entries]
-        moved = []
-        for g, both in zip(entries, turned):
-            forward, backward = both[: 2 * group], both[2 * group :]
-            result = dot_nt(forward, axial_ref[g, :size]) + dot_nt(swapped(forward), axial_ref[g, size:])
-            result += dot_nn(jnp.concatenate([backward, swapped(backward)], axis=1), axial_ref[g])
-            moved.append(result.astype(BF16))
-        total_ref[...] += sum(dot_nn(value, rot_ref[g]) for g, value in zip(entries, moved))
-        return carry
-
-    lax.fori_loop(0, tables // together, body, 0)
+    products_ref[...] = jnp.zeros_like(products_ref)
+    for copy in copies:
+        copy.wait()
+    chunk = 32
+    chunks = [first * chunk for first in range(rounded_up(quarter * modes, chunk) // chunk)]
+    each = (len(chunks) + tables - 1) // tables
+    for g in range(tables):
+        turned = dot_nt(sums_ref[g], rot_ref[g]).astype(BF16)
+        forward, backward = turned[: 2 * group], turned[2 * group :]
+        moved = dot_nt(forward, axial_ref[g, :size]) + dot_nt(swapped(forward), axial_ref[g, size:])
+        moved += dot_nn(jnp.concatenate([backward, swapped(backward)], axis=1), axial_ref[g])
+        back = dot_nn(moved.astype(BF16), rot_ref[g])
+        total_ref[...] = back if g == 0 else total_ref[...] + back
+        for first in chunks[g * each : (g + 1) * each]:
+            add_products(blocks_ref, products_ref, quarter * modes, first, chunk)
+    line_ref[...] = products_line(products_ref)
     for c in range(2):
         for t in range(size // 128):
             lanes = slice(t * 128, (t + 1) * 128)
@@ -191,66 +228,12 @@
                 for j in range(quarter):
                     rows = window_ref[0, c, t, pl.ds(p * quarter + j, part, own), :]
                     out_ref[p, c, j, :, lanes] = rows.astype(BF16)
-    for copy in copies:
-        copy.wait()
 
 
 def lane_swap(value):
     half = value.shape[1] // 2
     rolled = pltpu.roll(value, half, axis=1)
     return jnp.where(iota(value.shape, 1) < half, -rolled, rolled)
-
-
-def folded(value):
-    return jnp.sum(value.reshape(value.shape[0] // 8, 8, value.shape[1]), axis=0)
-
-
-def gram_kernel(quarter, modes, basis_ref, gram_ref, blocks_ref, odd_ref, sums_ref, sems):
-    blocks, full, columns = odd_ref.shape
-    vectors = 2 * blocks
-    rows = quarter * modes
-    gap = full - rows
-    middle = full // 2
-    cuts = ((0, middle), (rows - gap, rows + middle + gap)), ((middle, rows - gap), (rows + middle + gap, 2 * rows))
-    copies = []
-    for h, ranges in enumerate(cuts):
-        copies.append([])
-        for i in range(blocks):
-            for side, (first, last) in enumerate(ranges):
-                here = pl.ds(first, last - first)
-                copies[h].append(pltpu.make_async_copy(basis_ref.at[i, here], blocks_ref.at[i, here], sems.at[h, i, side]))
-    for copy in copies[0] + copies[1]:
-        copy.start()
-    sums_ref[...] = jnp.zeros_like(sums_ref)
-    chunk = 32
-
-    def body(i, carry):
-        here = pl.ds(pl.multiple_of(i * chunk, chunk), chunk)
-        values = [odd_ref[k // 2, here, :] if k % 2 else blocks_ref[k // 2, here, :] for k in range(vectors)]
-        for l in range(vectors):
-            other = lane_swap(values[l])
-            for k in range(l + 1):
-                sums_ref[k, l] += folded(values[k] * values[l])
-                if k < l:
-                    sums_ref[l, k] -= folded(values[k] * other)
-        return carry
-
-    for h, (first, last) in enumerate(((0, middle), (middle, rows))):
-        for copy in copies[h]:
-            copy.wait()
-        for i in range(blocks):
-            odd_ref[i, first:last, :] = blocks_ref[i, rows + first : rows + last, :]
-            if last == rows:
-                blocks_ref[i, rows:full, :] = jnp.zeros((gap, columns), F32)
-                odd_ref[i, rows:full, :] = jnp.zeros((gap, columns), F32)
-        lax.fori_loop(first // chunk, rounded_up(last, chunk) // chunk, body, 0)
-    totals = jnp.sum(jnp.sum(sums_ref[...].reshape(vectors * vectors, 8, columns), axis=1), axis=1, keepdims=True)
-    row, lane = iota((vectors, 128), 0), iota((vectors, 128), 1)
-    line = jnp.zeros((1, 128), F32)
-    for k in range(vectors):
-        column = totals[k * vectors : (k + 1) * vectors]
-        line += jnp.sum(jnp.where(row + k * vectors == lane, column, 0.0), axis=0, keepdims=True)
-    gram_ref[...] = line
 
 
 def image_kernel(quarter, modes, blocks_ref, mie_ref, gram_ref, pieces_ref, image_ref, sums_ref, lines_ref):
@@ -279,16 +262,19 @@
         last = (vectors - 1) % 2 * rows + first
         image = blocks_ref[(vectors - 1) // 2, last : last + chunk, :] - product
         image_ref[here, :] = image
-        turned = lane_swap(image)
+        turned = pltpu.roll(image, half, axis=1)
         for k in range(vectors):
             start = k % 2 * rows + first
             values = blocks_ref[k // 2, start : start + chunk, :]
             totals[2 * k] += folded(values * image)
-            totals[2 * k + 1] -= folded(values * turned)
+            totals[2 * k + 1] += folded(values * turned)
         totals[2 * vectors] += folded(image * image)
     lane = iota(gram_ref.shape, 1)
     line = gram_ref[...]
+    left = iota((8, columns), 1) < half
     for index, total in enumerate(totals):
+        if index % 2 and index < 2 * vectors:
+            total = jnp.where(left, total, -total)
         line = jnp.where(lane == vectors * vectors + index, jnp.sum(total, axis=(0, 1), keepdims=True), line)
     sums_ref[...] = jnp.broadcast_to(line[None], sums_ref.shape)
 
@@ -394,26 +380,10 @@
         compiler_params=params(16),
         name="pack",
     )(pair_rows, pair_count, basis_rows)
-    pieces, basis_later = lax.optimization_barrier((pieces, basis_rows))
     own_pieces = exchanged(pieces)
-
-    gram = pl.pallas_call(
-        functools.partial(gram_kernel, quarter, modes),
-        grid=(1,),
-        in_specs=[hbm()],
-        out_specs=pl.BlockSpec((1, 128), lambda i: (0, 0)),
-        out_shape=pltpu.HBM((1, 128), F32),
-        scratch_shapes=[
-            pltpu.VMEM((pairs_of_vectors, 2 * rows, columns), F32),
-            pltpu.VMEM((pairs_of_vectors, full, columns), F32),
-            pltpu.VMEM((vectors, vectors, 8, columns), F32),
-            pltpu.SemaphoreType.DMA((2, pairs_of_vectors, 2)),
-        ],
-        compiler_params=params(16),
-        name="gram",
-    )(basis_later)
-    own_pieces, gram, *inputs = lax.optimization_barrier((own_pieces, gram, basis_rows, mie_rows, rot_rows, axial_rows))
-    basis_rows, mie_rows, rot_rows, axial_rows = inputs
+    own_pieces, basis_rows, mie_rows, rot_rows, axial_rows = lax.optimization_barrier(
+        (own_pieces, basis_rows, mie_rows, rot_rows, axial_rows)
+    )
     below, above = neighbours(own_pieces)
 
     rotations, axials = pl.pallas_call(
@@ -440,20 +410,21 @@
     tall = rounded_up(rows + full, 8)
     below, above, rotations, axials = lax.optimization_barrier((below, above, rotations, axials))
 
-    together = 2 if tables % 2 == 0 else 1
-    field, blocks, mies = pl.pallas_call(
-        functools.partial(field_kernel, own, modes, together),
+    field, blocks, mies, line = pl.pallas_call(
+        functools.partial(field_kernel, own, quarter, modes),
         in_specs=[whole()] * 5 + [hbm()] * 2,
-        out_specs=[whole()] * 3,
+        out_specs=[whole()] * 4,
         out_shape=[
             jax.ShapeDtypeStruct(pieces_shape, BF16),
             jax.ShapeDtypeStruct((pairs_of_vectors, tall, columns), F32),
             jax.ShapeDtypeStruct(mie_rows.shape, F32),
+            jax.ShapeDtypeStruct((1, 128), F32),
         ],
         scratch_shapes=[
             pltpu.VMEM((3, 2, size // 128, group, 128), F32),
             pltpu.VMEM((tables, 4 * group, size), BF16),
             pltpu.VMEM((2 * group, size), F32),
+            pltpu.VMEM((vectors, vectors, 8, columns), F32),
             pltpu.SemaphoreType.DMA((pairs_of_vectors + 1,)),
         ],
         compiler_params=params(20),
@@ -469,7 +440,7 @@
         scratch_shapes=[pltpu.VMEM((full, columns), F32)],
         compiler_params=params(8),
         name="image",
-    )(blocks, mies, gram, field_pieces)
+    )(blocks, mies, line, field_pieces)
     sums = lax.all_to_all(sums, ("blk", "pair"), split_axis=0, concat_axis=0, tiled=True)
 
     height = 4

time: 65 us -> 65.4 us (level)
  blocking collectives: 20.6 us -> 30.2 us
  starting transfers between devices: 10.2 us -> 5.84 us
  Pallas kernels: 31 us -> 27.6 us
  waiting for transfers between devices: 1.3 us -> 0.01 us
    all_to_all x1 -> x2, blocking collectives: 8.78 us -> 18.5 us  [exchanged(): lax.all_to_all(value, 'pair', split_axis=0, concat_axis=0, tiled=True)]
    all_to_all x1 -> x0, starting transfers between devices: 4.22 us -> none  [exchanged(): lax.all_to_all(value, 'pair', split_axis=0, concat_axis=0, tiled=True)]
    pallas_call x2 -> x1, Pallas kernels: 16.6 us -> 13.8 us  [shards(): pl.pallas_call(functools.partial(field_kernel, own, quarter, modes), in_s...]
    ppermute x2, waiting for transfers between devices: 1.3 us -> 0.01 us  [neighbours(): return (lax.ppermute(value, 'blk', up), lax.ppermute(value, 'blk', down))]
    pallas_call x1, Pallas kernels: 1.95 us -> 1.25 us  [shards(): pl.pallas_call(functools.partial(pack_kernel, quarter, modes, ways, own),...]
  transfers between devices with their start and end apart: 3 -> 2, of which waited for: 1 -> 0; matrix products, arithmetic and copies ran while one was open for 0% -> 0% of each run, Pallas kernels for 24% -> 15%
where the time goes in v6:
time: 65.4 us; the launch traced here: 65 us
  blocking collectives  30.2 us (46%)
  Pallas kernels  27.6 us (42%)
  starting transfers between devices  5.84 us (9%)
  between operations  1.34 us (2%)
    all_to_all x2, blocking collectives, exchanged(): lax.all_to_all(value, 'pair', split_axis=0, concat_axis=0, tiled=True)  18.5 us
    pallas_call x1, Pallas kernels, shards(): pl.pallas_call(functools.partial(field_kernel, own, quarter, modes), in_s...  13.8 us
    all_to_all x1, blocking collectives, shards(): lax.all_to_all(sums, ('blk', 'pair'), split_axis=0, concat_axis=0, tiled=...  11.8 us
    pallas_call x1, Pallas kernels, shards(): pl.pallas_call(functools.partial(tables_kernel, modes, tables), grid=(tab...  9.45 us
    ppermute x2, starting transfers between devices, neighbours(): return (lax.ppermute(value, 'blk', up), lax.ppermute(value, 'blk', down))  5.84 us
    pallas_call x1, Pallas kernels, shards(): pl.pallas_call(functools.partial(remainder_kernel, quarter, modes, mean_s...  1.64 us
    pallas_call x1, Pallas kernels, shards(): pl.pallas_call(functools.partial(image_kernel, quarter, modes), in_specs=...  1.43 us
  transfers between devices with their start and end apart: 2, of which 0 were waited for; matrix products, arithmetic and copies ran while one was open for 0% of the time, Pallas kernels for 15%

profile of v6, /device:TPU:0, one launch (start us, length us, event | category | flops | bytes accessed | tf_op | source)
XLA Modules:
  0.0 65.0 jit_solution(6982960935822116409)
XLA Ops:
  1.3 1.2 %pack.1 = bf16[4,2,2,16,512]{4,3,2,1,0:T(8,128)(2,1)S(1)} custom-call(s32[3,1,128]{2,1,0:T(1,128)} %bitcast.19, s32[1]{0:T(128)S(6)} %copy.8.count_ref, f32[4,2040,128]{2,1,0:T(8,128)} %bitcast.14), custom_call_target="tpu_custom_call" | custom-call | tf_op jit(solution)/shard_map/pack/pallas_call | solution.py:368
  2.5 10.0 %all_to_all.15.own_ref = bf16[4,2,2,16,512]{4,3,2,1,0:T(8,128)(2,1)S(1)} all-to-all(bf16[4,2,2,16,512]{4,3,2,1,0:T(8,128)(2,1)S(1)} %pack.1), channel_id=1, replica_groups=mesh['blk'=8,'pair'=4] {'pair'}, dimensions={0} | all-to-all | bytes 524288 | tf_op jit(solution)/shard_map/all_to_all | solution.py:337
  12.6 1.3 %collective-permute-start.1 = (bf16[4,2,2,16,512]{4,3,2,1,0:T(8,128)(2,1)S(1)}, bf16[4,2,2,16,512]{4,3,2,1,0:T(8,128)(2,1)S(1)}, u32[]{:S(2)}, u32[]{:S(2)}) collective-permute-start(bf16[4,2,2,16,512]{4,3,2,1,0:T(8,128)(2,1)S(1)} %all_to_all.15.own_ref), channel_id=1, source_target_pairs={{4,0},{8,4},{12,8},{16,12},{20,16},{24,20},{28,24},{5,1},{9,5},{13... | collective-permute-start | bytes 786440 | tf_op jit(solution)/shard_map/ppermute | solution.py:344
  13.9 4.6 %collective-permute-start = (bf16[4,2,2,16,512]{4,3,2,1,0:T(8,128)(2,1)S(1)}, bf16[4,2,2,16,512]{4,3,2,1,0:T(8,128)(2,1)S(1)}, u32[]{:S(2)}, u32[]{:S(2)}) collective-permute-start(bf16[4,2,2,16,512]{4,3,2,1,0:T(8,128)(2,1)S(1)} %all_to_all.15.own_ref), channel_id=1, source_target_pairs={{0,4},{4,8},{8,12},{12,16},{16,20},{20,24},{24,28},{1,5},{5,9},{9,... | collective-permute-start | bytes 786440 | tf_op jit(solution)/shard_map/ppermute | solution.py:344
  18.4 9.4 %tables.1 = (bf16[8,512,512]{2,1,0:T(8,128)(2,1)S(1)}, bf16[8,1024,512]{2,1,0:T(8,128)(2,1)S(1)}) custom-call(bf16[8,510,2,510]{3,2,1,0:T(2,128)(2,1)} %bitcast.16, bf16[4080,510]{1,0:T(8,128)(2,1)} %bitcast.17), custom_call_target="tpu_custom_call" | custom-call | flops 2147483648 | bytes 25165824 | tf_op jit(solution)/shard_map/tables/pallas_call | solution.py:389
  27.9 0.0 collective-permute-done.1.above_ref
  27.9 0.0 collective-permute-done.below_ref
  27.9 13.8 %field.1 = (bf16[4,2,2,16,512]{4,3,2,1,0:T(8,128)(2,1)S(1)}, f32[4,2048,128]{2,1,0:T(8,128)S(1)}, f32[255,4,128]{2,1,0:T(4,128)S(1)}, f32[1,128]{1,0:T(1,128)S(1)}) custom-call(bf16[8,512,512]{2,1,0:T(8,128)(2,1)S(1)} %get-tuple-element.26.rot_ref, bf16[8,1024,512]{2,1,0:T(8,128)(2,1)S(1)} %get-tuple-element.27.axial_ref, ...), custom_call_target="tpu_custom_call" | custom-call | tf_op jit(solution)/shard_map/field/pallas_call | solution.py:413
  41.7 8.4 %all_to_all.16.pieces_ref = bf16[4,2,2,16,512]{4,3,2,1,0:T(8,128)(2,1)S(1)} all-to-all(bf16[4,2,2,16,512]{4,3,2,1,0:T(8,128)(2,1)S(1)} %get-tuple-element.35), channel_id=1, replica_groups=mesh['blk'=8,'pair'=4] {'pair'}, dimensions={0} | all-to-all | bytes 524288 | tf_op jit(solution)/shard_map/all_to_all | solution.py:337
  50.1 1.4 %image.1 = (f32[1024,128]{1,0:T(8,128)S(1)}, f32[32,1,128]{2,1,0:T(1,128)S(1)}) custom-call(f32[4,2048,128]{2,1,0:T(8,128)S(1)} %get-tuple-element.32.blocks_ref, f32[255,4,128]{2,1,0:T(4,128)S(1)} %get-tuple-element.33.mie_ref, f32[1,128]{1,0:T(1,128)S(1)} %get-tuple-element.34.gram_ref, bf16[4,2,2,16,512]{4,3,2,1,0:T(8,128)(2,1)S(1)} %all_to_all.16.pieces_ref), custom_call_target="tpu_custom_call" | custom-call | tf_op jit(solution)/shard_map/image/pallas_call | solution.py:435
  51.6 11.8 %all_to_all.17.sums_ref = f32[32,1,128]{2,1,0:T(1,128)S(1)} all-to-all(f32[32,1,128]{2,1,0:T(1,128)S(1)} %get-tuple-element.36), channel_id=1, replica_groups=mesh['blk'=8,'pair'=4] {'blk','pair'}, dimensions={0} | all-to-all | bytes 32768 | tf_op jit(solution)/shard_map/all_to_all | solution.py:444
  63.3 1.6 %remainder.1 = (f32[2,8]{1,0:T(2,128)}, f32[255,4,128]{2,1,0:T(4,128)}) custom-call(f32[32,1,128]{2,1,0:T(1,128)S(1)} %all_to_all.17.sums_ref, f32[4,2048,128]{2,1,0:T(8,128)S(1)} %get-tuple-element.32.blocks_ref, f32[1024,128]{1,0:T(8,128)S(1)} %get-tuple-element.37.image_ref), custom_call_target="tpu_custom_call" | custom-call | tf_op jit(solution)/shard_map/remainder/pallas_call | solution.py:448
Async XLA Ops:
  12.6 15.3 %collective-permute-start.1 = (bf16[4,2,2,16,512]{4,3,2,1,0:T(8,128)(2,1)S(1)}, bf16[4,2,2,16,512]{4,3,2,1,0:T(8,128)(2,1)S(1)}, u32[]{:S(2)}, u32[]{:S(2)}) collective-permute-start(bf16[4,2,2,16,512]{4,3,2,1,0:T(8,128)(2,1)S(1)} %all_to_all.15.own_ref), channel_id=1, source_target_pairs={{4,0},{8,4},{12,8},{16,12},{20,16},{24,20},{28,24},{5,1},{9,5},{13... | collective-permute-start | bytes 786440 | tf_op jit(solution)/shard_map/ppermute | solution.py:344
  13.9 14.0 %collective-permute-start = (bf16[4,2,2,16,512]{4,3,2,1,0:T(8,128)(2,1)S(1)}, bf16[4,2,2,16,512]{4,3,2,1,0:T(8,128)(2,1)S(1)}, u32[]{:S(2)}, u32[]{:S(2)}) collective-permute-start(bf16[4,2,2,16,512]{4,3,2,1,0:T(8,128)(2,1)S(1)} %all_to_all.15.own_ref), channel_id=1, source_target_pairs={{0,4},{4,8},{8,12},{12,16},{16,20},{20,24},{24,28},{1,5},{5,9},{9,... | collective-permute-start | bytes 786440 | tf_op jit(solution)/shard_map/ppermute | solution.py:344

commit v7 on v5

--- a/solution.py
+++ b/solution.py
@@ -132,8 +132,12 @@
     return jnp.concatenate([forward, sum(backward)], axis=0).astype(BF16)
 
 
+def folded(value):
+    return jnp.sum(value.reshape(value.shape[0] // 8, 8, value.shape[1]), axis=0)
+
+
 def field_kernel(
-    own, modes, together, rot_ref, axial_ref, below_ref, own_ref, above_ref, basis_ref, mie_ref,
+    own, modes, rot_ref, axial_ref, below_ref, own_ref, above_ref, basis_ref, mie_ref,
     out_ref, blocks_ref, mies_ref, window_ref, sums_ref, total_ref, sems,
 ):
     tables, _, size = rot_ref.shape
@@ -168,21 +172,13 @@
                     rows = jnp.concatenate([result[first : first + own] for result in results], axis=0)
                     place = (direction * 2 + c) * group + s * own
                     sums_ref[g, place : place + 2 * own, :] = rows.astype(BF16)
-    total_ref[...] = jnp.zeros_like(total_ref)
-
-    def body(step, carry):
-        entries = [step * together + i for i in range(together)]
-        turned = [dot_nt(sums_ref[g], rot_ref[g]).astype(BF16) for g in entries]
-        moved = []
-        for g, both in zip(entries, turned):
-            forward, backward = both[: 2 * group], both[2 * group :]
-            result = dot_nt(forward, axial_ref[g, :size]) + dot_nt(swapped(forward), axial_ref[g, size:])
-            result += dot_nn(jnp.concatenate([backward, swapped(backward)], axis=1), axial_ref[g])
-            moved.append(result.astype(BF16))
-        total_ref[...] += sum(dot_nn(value, rot_ref[g]) for g, value in zip(entries, moved))
-        return carry
-
-    lax.fori_loop(0, tables // together, body, 0)
+    for g in range(tables):
+        turned = dot_nt(sums_ref[g], rot_ref[g]).astype(BF16)
+        forward, backward = turned[: 2 * group], turned[2 * group :]
+        moved = dot_nt(forward, axial_ref[g, :size]) + dot_nt(swapped(forward), axial_ref[g, size:])
+        moved += dot_nn(jnp.concatenate([backward, swapped(backward)], axis=1), axial_ref[g])
+        back = dot_nn(moved.astype(BF16), rot_ref[g])
+        total_ref[...] = back if g == 0 else total_ref[...] + back
     for c in range(2):
         for t in range(size // 128):
             lanes = slice(t * 128, (t + 1) * 128)
@@ -201,56 +197,63 @@
     return jnp.where(iota(value.shape, 1) < half, -rolled, rolled)
 
 
-def folded(value):
-    return jnp.sum(value.reshape(value.shape[0] // 8, 8, value.shape[1]), axis=0)
-
-
-def gram_kernel(quarter, modes, basis_ref, gram_ref, blocks_ref, odd_ref, sums_ref, sems):
-    blocks, full, columns = odd_ref.shape
-    vectors = 2 * blocks
-    rows = quarter * modes
-    gap = full - rows
-    middle = full // 2
-    cuts = ((0, middle), (rows - gap, rows + middle + gap)), ((middle, rows - gap), (rows + middle + gap, 2 * rows))
-    copies = []
-    for h, ranges in enumerate(cuts):
-        copies.append([])
-        for i in range(blocks):
-            for side, (first, last) in enumerate(ranges):
-                here = pl.ds(first, last - first)
-                copies[h].append(pltpu.make_async_copy(basis_ref.at[i, here], blocks_ref.at[i, here], sems.at[h, i, side]))
-    for copy in copies[0] + copies[1]:
-        copy.start()
-    sums_ref[...] = jnp.zeros_like(sums_ref)
-    chunk = 32
-
-    def body(i, carry):
-        here = pl.ds(pl.multiple_of(i * chunk, chunk), chunk)
-        values = [odd_ref[k // 2, here, :] if k % 2 else blocks_ref[k // 2, here, :] for k in range(vectors)]
-        for l in range(vectors):
-            other = lane_swap(values[l])
-            for k in range(l + 1):
-                sums_ref[k, l] += folded(values[k] * values[l])
-                if k < l:
-                    sums_ref[l, k] -= folded(values[k] * other)
-        return carry
-
-    for h, (first, last) in enumerate(((0, middle), (middle, rows))):
-        for copy in copies[h]:
-            copy.wait()
-        for i in range(blocks):
-            odd_ref[i, first:last, :] = blocks_ref[i, rows + first : rows + last, :]
-            if last == rows:
-                blocks_ref[i, rows:full, :] = jnp.zeros((gap, columns), F32)
-                odd_ref[i, rows:full, :] = jnp.zeros((gap, columns), F32)
-        lax.fori_loop(first // chunk, rounded_up(last, chunk) // chunk, body, 0)
-    totals = jnp.sum(jnp.sum(sums_ref[...].reshape(vectors * vectors, 8, columns), axis=1), axis=1, keepdims=True)
+def add_products(blocks_ref, products_ref, rows, first, count):
+    vectors = products_ref.shape[0]
+    values = []
+    for k in range(vectors):
+        start = k % 2 * rows + first
+        value = blocks_ref[k // 2, start : start + count, :]
+        if k % 2 == 0 and first + count > rows:
+            value = jnp.where(iota(value.shape, 0) < rows - first, value, 0.0)
+        values.append(value)
+    for l in range(vectors):
+        other = pltpu.roll(values[l], values[l].shape[1] // 2, axis=1)
+        for k in range(l + 1):
+            products_ref[k, l] += folded(values[k] * values[l])
+            if k < l:
+                products_ref[l, k] += folded(values[k] * other)
+
+
+def products_line(products_ref):
+    vectors, _, _, columns = products_ref.shape
+    pairs = vectors * vectors
+    totals = jnp.sum(products_ref[...].reshape(pairs, 8, columns), axis=1)
+    pair = iota(totals.shape, 0)
+    signed = (lax.div(pair, vectors) > lax.rem(pair, vectors)) & (iota(totals.shape, 1) >= columns // 2)
+    totals = jnp.sum(jnp.where(signed, -totals, totals), axis=1, keepdims=True)
     row, lane = iota((vectors, 128), 0), iota((vectors, 128), 1)
     line = jnp.zeros((1, 128), F32)
     for k in range(vectors):
         column = totals[k * vectors : (k + 1) * vectors]
         line += jnp.sum(jnp.where(row + k * vectors == lane, column, 0.0), axis=0, keepdims=True)
-    gram_ref[...] = line
+    return line
+
+
+def gram_kernel(quarter, modes, basis_ref, line_ref, blocks_ref, products_ref, sems):
+    blocks, _, columns = basis_ref.shape
+    rows = quarter * modes
+    parts, chunk = 4, 32
+    tile_end = rows // 8 * 8
+    step = rounded_up(rows, 8 * parts) // parts
+    even = [0] + [step * q for q in range(1, parts)] + [tile_end]
+    odd = [tile_end] + [rounded_up(rows, 8) + step * q for q in range(1, parts)] + [2 * rows]
+    copies = []
+    for q in range(parts):
+        for i in range(blocks):
+            for side, cuts in enumerate((even, odd)):
+                here = pl.ds(cuts[q], cuts[q + 1] - cuts[q])
+                copies.append(pltpu.make_async_copy(basis_ref.at[i, here], blocks_ref.at[i, here], sems.at[q, i, side]))
+    for copy in copies:
+        copy.start()
+    products_ref[...] = jnp.zeros_like(products_ref)
+    for i in range(blocks):
+        blocks_ref[i, 2 * rows :, :] = jnp.zeros((blocks_ref.shape[1] - 2 * rows, columns), F32)
+    for q in range(parts):
+        for copy in copies[2 * blocks * q : 2 * blocks * (q + 1)]:
+            copy.wait()
+        for first in range(step * q, min(step * (q + 1), rows), chunk):
+            add_products(blocks_ref, products_ref, rows, first, chunk)
+    line_ref[...] = products_line(products_ref)
 
 
 def image_kernel(quarter, modes, blocks_ref, mie_ref, gram_ref, pieces_ref, image_ref, sums_ref, lines_ref):
@@ -279,16 +282,19 @@
         last = (vectors - 1) % 2 * rows + first
         image = blocks_ref[(vectors - 1) // 2, last : last + chunk, :] - product
         image_ref[here, :] = image
-        turned = lane_swap(image)
+        turned = pltpu.roll(image, half, axis=1)
         for k in range(vectors):
             start = k % 2 * rows + first
             values = blocks_ref[k // 2, start : start + chunk, :]
             totals[2 * k] += folded(values * image)
-            totals[2 * k + 1] -= folded(values * turned)
+            totals[2 * k + 1] += folded(values * turned)
         totals[2 * vectors] += folded(image * image)
     lane = iota(gram_ref.shape, 1)
     line = gram_ref[...]
+    left = iota((8, columns), 1) < half
     for index, total in enumerate(totals):
+        if index % 2 and index < 2 * vectors:
+            total = jnp.where(left, total, -total)
         line = jnp.where(lane == vectors * vectors + index, jnp.sum(total, axis=(0, 1), keepdims=True), line)
     sums_ref[...] = jnp.broadcast_to(line[None], sums_ref.shape)
 
@@ -394,25 +400,24 @@
         compiler_params=params(16),
         name="pack",
     )(pair_rows, pair_count, basis_rows)
+    tall = rounded_up(rows + full, 8)
     pieces, basis_later = lax.optimization_barrier((pieces, basis_rows))
     own_pieces = exchanged(pieces)
-
-    gram = pl.pallas_call(
+    line = pl.pallas_call(
         functools.partial(gram_kernel, quarter, modes),
         grid=(1,),
         in_specs=[hbm()],
         out_specs=pl.BlockSpec((1, 128), lambda i: (0, 0)),
         out_shape=pltpu.HBM((1, 128), F32),
         scratch_shapes=[
-            pltpu.VMEM((pairs_of_vectors, 2 * rows, columns), F32),
-            pltpu.VMEM((pairs_of_vectors, full, columns), F32),
+            pltpu.VMEM((pairs_of_vectors, tall, columns), F32),
             pltpu.VMEM((vectors, vectors, 8, columns), F32),
-            pltpu.SemaphoreType.DMA((2, pairs_of_vectors, 2)),
+            pltpu.SemaphoreType.DMA((4, pairs_of_vectors, 2)),
         ],
         compiler_params=params(16),
         name="gram",
     )(basis_later)
-    own_pieces, gram, *inputs = lax.optimization_barrier((own_pieces, gram, basis_rows, mie_rows, rot_rows, axial_rows))
+    own_pieces, line, *inputs = lax.optimization_barrier((own_pieces, line, basis_rows, mie_rows, rot_rows, axial_rows))
     basis_rows, mie_rows, rot_rows, axial_rows = inputs
     below, above = neighbours(own_pieces)
 
@@ -437,12 +442,10 @@
         name="tables",
     )(axial_rows, rot_rows)
 
-    tall = rounded_up(rows + full, 8)
     below, above, rotations, axials = lax.optimization_barrier((below, above, rotations, axials))
 
-    together = 2 if tables % 2 == 0 else 1
     field, blocks, mies = pl.pallas_call(
-        functools.partial(field_kernel, own, modes, together),
+        functools.partial(field_kernel, own, modes),
         in_specs=[whole()] * 5 + [hbm()] * 2,
         out_specs=[whole()] * 3,
         out_shape=[
@@ -469,7 +472,7 @@
         scratch_shapes=[pltpu.VMEM((full, columns), F32)],
         compiler_params=params(8),
         name="image",
-    )(blocks, mies, gram, field_pieces)
+    )(blocks, mies, line, field_pieces)
     sums = lax.all_to_all(sums, ("blk", "pair"), split_axis=0, concat_axis=0, tiled=True)
 
     height = 4

time: 65 us -> 65.1 us (level)
    pallas_call x1, Pallas kernels: 10.5 us -> 11.8 us  [shards(): pl.pallas_call(functools.partial(field_kernel, own, modes), in_specs=[who...]
    pallas_call x1, Pallas kernels: 6.07 us -> 4.85 us  [shards(): pl.pallas_call(functools.partial(gram_kernel, quarter, modes), grid=(1,),...]
    all_to_all x1, waiting for transfers between devices: 0.01 us -> 1.18 us  [exchanged(): lax.all_to_all(value, 'pair', split_axis=0, concat_axis=0, tiled=True)]
    ppermute x2, waiting for transfers between devices: 1.3 us -> 0.45 us  [neighbours(): return (lax.ppermute(value, 'blk', up), lax.ppermute(value, 'blk', down))]
  transfers between devices with their start and end apart: 3 -> 3, of which waited for: 1 -> 2; matrix products, arithmetic and copies ran while one was open for 0% -> 0% of each run, Pallas kernels for 24% -> 22%
where the time goes in v7:
time: 65.1 us; the launch traced here: 64.6 us
  Pallas kernels  31.1 us (48%)
  blocking collectives  20.3 us (31%)
  starting transfers between devices  10.2 us (16%)
  waiting for transfers between devices  1.63 us (3%)
  between operations  1.34 us (2%)
    all_to_all x1, blocking collectives, shards(): lax.all_to_all(sums, ('blk', 'pair'), split_axis=0, concat_axis=0, tiled=...  11.8 us
    pallas_call x1, Pallas kernels, shards(): pl.pallas_call(functools.partial(field_kernel, own, modes), in_specs=[who...  11.8 us
    pallas_call x1, Pallas kernels, shards(): pl.pallas_call(functools.partial(tables_kernel, modes, tables), grid=(tab...  9.46 us
    all_to_all x1, blocking collectives, exchanged(): lax.all_to_all(value, 'pair', split_axis=0, concat_axis=0, tiled=True)  8.5 us
    ppermute x2, starting transfers between devices, neighbours(): return (lax.ppermute(value, 'blk', up), lax.ppermute(value, 'blk', down))  5.97 us
    pallas_call x1, Pallas kernels, shards(): pl.pallas_call(functools.partial(gram_kernel, quarter, modes), grid=(1,),...  4.85 us
    all_to_all x1, starting transfers between devices, exchanged(): lax.all_to_all(value, 'pair', split_axis=0, concat_axis=0, tiled=True)  4.22 us
    pallas_call x1, Pallas kernels, shards(): pl.pallas_call(functools.partial(pack_kernel, quarter, modes, ways, own),...  1.95 us
  transfers between devices with their start and end apart: 3, of which 2 were waited for; matrix products, arithmetic and copies ran while one was open for 0% of the time, Pallas kernels for 22%

profile of v7, /device:TPU:0, one launch (start us, length us, event | category | flops | bytes accessed | tf_op | source)
XLA Modules:
  0.0 64.6 jit_solution(5720399451067185804)
XLA Ops:
  1.3 2.0 %pack.1 = bf16[4,2,2,16,512]{4,3,2,1,0:T(8,128)(2,1)} custom-call(s32[3,1,128]{2,1,0:T(1,128)} %bitcast.20, s32[1]{0:T(128)S(6)} %copy.8.count_ref, f32[4,2040,128]{2,1,0:T(8,128)} %bitcast.14), custom_call_target="tpu_custom_call" | custom-call | tf_op jit(solution)/shard_map/pack/pallas_call | solution.py:388
  3.2 4.2 %all-to-all-start = ((bf16[4,2,2,16,512]{4,3,2,1,0:T(8,128)(2,1)}), bf16[4,2,2,16,512]{4,3,2,1,0:T(8,128)(2,1)S(1)}, u32[]{:S(2)}, u32[]{:S(2)}) async-start(bf16[4,2,2,16,512]{4,3,2,1,0:T(8,128)(2,1)} %pack.1), calls=%async_computation | async-start | bytes 524288 | tf_op jit(solution)/shard_map/all_to_all | solution.py:357
  7.5 4.8 %gram.1.gram_ref = f32[1,128]{1,0:T(1,128)} custom-call(f32[4,2040,128]{2,1,0:T(8,128)} %bitcast.15), custom_call_target="tpu_custom_call" | custom-call | tf_op jit(solution)/shard_map/gram/pallas_call | solution.py:406
  12.3 1.2 %all-to-all-done.own_ref = bf16[4,2,2,16,512]{4,3,2,1,0:T(8,128)(2,1)S(1)} async-done(((bf16[4,2,2,16,512]{4,3,2,1,0:T(8,128)(2,1)}), bf16[4,2,2,16,512]{4,3,2,1,0:T(8,128)(2,1)S(1)}, u32[]{:S(2)}, u32[]{:S(2)}) %all-to-all-start) | async-done | bytes 262176 | tf_op jit(solution)/shard_map/all_to_all | solution.py:357
  13.5 1.3 %collective-permute-start.1 = (bf16[4,2,2,16,512]{4,3,2,1,0:T(8,128)(2,1)S(1)}, bf16[4,2,2,16,512]{4,3,2,1,0:T(8,128)(2,1)S(1)}, u32[]{:S(2)}, u32[]{:S(2)}) collective-permute-start(bf16[4,2,2,16,512]{4,3,2,1,0:T(8,128)(2,1)S(1)} %all-to-all-done.own_ref), channel_id=1, source_target_pairs={{4,0},{8,4},{12,8},{16,12},{20,16},{24,20},{28,24},{5,1},{9,5},{13... | collective-permute-start | bytes 786440 | tf_op jit(solution)/shard_map/ppermute | solution.py:364
  14.8 4.7 %collective-permute-start = (bf16[4,2,2,16,512]{4,3,2,1,0:T(8,128)(2,1)S(1)}, bf16[4,2,2,16,512]{4,3,2,1,0:T(8,128)(2,1)S(1)}, u32[]{:S(2)}, u32[]{:S(2)}) collective-permute-start(bf16[4,2,2,16,512]{4,3,2,1,0:T(8,128)(2,1)S(1)} %all-to-all-done.own_ref), channel_id=1, source_target_pairs={{0,4},{4,8},{8,12},{12,16},{16,20},{20,24},{24,28},{1,5},{5,9},{9,... | collective-permute-start | bytes 786440 | tf_op jit(solution)/shard_map/ppermute | solution.py:364
  19.5 9.5 %tables.1 = (bf16[8,512,512]{2,1,0:T(8,128)(2,1)S(1)}, bf16[8,1024,512]{2,1,0:T(8,128)(2,1)S(1)}) custom-call(bf16[8,510,2,510]{3,2,1,0:T(2,128)(2,1)} %bitcast.17, bf16[4080,510]{1,0:T(8,128)(2,1)} %bitcast.18), custom_call_target="tpu_custom_call" | custom-call | flops 2147483648 | bytes 25165824 | tf_op jit(solution)/shard_map/tables/pallas_call | solution.py:424
  28.9 0.0 collective-permute-done.1.above_ref
  28.9 0.4 collective-permute-done.below_ref
  29.4 0.0 copy-start
  29.4 11.8 %field.1 = (bf16[4,2,2,16,512]{4,3,2,1,0:T(8,128)(2,1)S(1)}, f32[4,2048,128]{2,1,0:T(8,128)S(1)}, f32[255,4,128]{2,1,0:T(4,128)S(1)}) custom-call(bf16[8,512,512]{2,1,0:T(8,128)(2,1)S(1)} %get-tuple-element.30.rot_ref, bf16[8,1024,512]{2,1,0:T(8,128)(2,1)S(1)} %get-tuple-element.31.axial_ref, bf16[4,2,2,16,512]{4,3,2,1,0:T(8,128)(2,1)S(1)} %collective-permute-done.below_ref, ...), custom_call_target="tpu_custom_call" | custom-call | tf_op jit(solution)/shard_map/field/pallas_call | solution.py:447
  41.2 8.5 %all_to_all.15.pieces_ref = bf16[4,2,2,16,512]{4,3,2,1,0:T(8,128)(2,1)S(1)} all-to-all(bf16[4,2,2,16,512]{4,3,2,1,0:T(8,128)(2,1)S(1)} %get-tuple-element.39), channel_id=1, replica_groups=mesh['blk'=8,'pair'=4] {'pair'}, dimensions={0} | all-to-all | bytes 524288 | tf_op jit(solution)/shard_map/all_to_all | solution.py:357
  49.7 0.0 copy-done
  49.7 1.4 %image.1 = (f32[1024,128]{1,0:T(8,128)S(1)}, f32[32,1,128]{2,1,0:T(1,128)S(1)}) custom-call(f32[4,2048,128]{2,1,0:T(8,128)S(1)} %get-tuple-element.36.blocks_ref, f32[255,4,128]{2,1,0:T(4,128)S(1)} %get-tuple-element.37.mie_ref, f32[1,128]{1,0:T(1,128)S(1)} %copy-done, bf16[4,2,2,16,512]{4,3,2,1,0:T(8,128)(2,1)S(1)} %all_to_all.15.pieces_ref), custom_call_target="tpu_custom_call" | custom-call | tf_op jit(solution)/shard_map/image/pallas_call | solution.py:467
  51.1 11.8 %all_to_all.16.sums_ref = f32[32,1,128]{2,1,0:T(1,128)S(1)} all-to-all(f32[32,1,128]{2,1,0:T(1,128)S(1)} %get-tuple-element.40), channel_id=1, replica_groups=mesh['blk'=8,'pair'=4] {'blk','pair'}, dimensions={0} | all-to-all | bytes 32768 | tf_op jit(solution)/shard_map/all_to_all | solution.py:476
  62.9 1.6 %remainder.1 = (f32[2,8]{1,0:T(2,128)}, f32[255,4,128]{2,1,0:T(4,128)}) custom-call(f32[32,1,128]{2,1,0:T(1,128)S(1)} %all_to_all.16.sums_ref, f32[4,2048,128]{2,1,0:T(8,128)S(1)} %get-tuple-element.36.blocks_ref, f32[1024,128]{1,0:T(8,128)S(1)} %get-tuple-element.41.image_ref), custom_call_target="tpu_custom_call" | custom-call | tf_op jit(solution)/shard_map/remainder/pallas_call | solution.py:480
Async XLA Ops:
  3.2 10.3 %all-to-all-start = ((bf16[4,2,2,16,512]{4,3,2,1,0:T(8,128)(2,1)}), bf16[4,2,2,16,512]{4,3,2,1,0:T(8,128)(2,1)S(1)}, u32[]{:S(2)}, u32[]{:S(2)}) async-start(bf16[4,2,2,16,512]{4,3,2,1,0:T(8,128)(2,1)} %pack.1), calls=%async_computation | async-start | bytes 524288 | tf_op jit(solution)/shard_map/all_to_all | solution.py:357
  13.5 15.4 %collective-permute-start.1 = (bf16[4,2,2,16,512]{4,3,2,1,0:T(8,128)(2,1)S(1)}, bf16[4,2,2,16,512]{4,3,2,1,0:T(8,128)(2,1)S(1)}, u32[]{:S(2)}, u32[]{:S(2)}) collective-permute-start(bf16[4,2,2,16,512]{4,3,2,1,0:T(8,128)(2,1)S(1)} %all-to-all-done.own_ref), channel_id=1, source_target_pairs={{4,0},{8,4},{12,8},{16,12},{20,16},{24,20},{28,24},{5,1},{9,5},{13... | collective-permute-start | bytes 786440 | tf_op jit(solution)/shard_map/ppermute | solution.py:364
  14.8 14.6 %collective-permute-start = (bf16[4,2,2,16,512]{4,3,2,1,0:T(8,128)(2,1)S(1)}, bf16[4,2,2,16,512]{4,3,2,1,0:T(8,128)(2,1)S(1)}, u32[]{:S(2)}, u32[]{:S(2)}) collective-permute-start(bf16[4,2,2,16,512]{4,3,2,1,0:T(8,128)(2,1)S(1)} %all-to-all-done.own_ref), channel_id=1, source_target_pairs={{0,4},{4,8},{8,12},{12,16},{16,20},{20,24},{24,28},{1,5},{5,9},{9,... | collective-permute-start | bytes 786440 | tf_op jit(solution)/shard_map/ppermute | solution.py:364
  29.4 20.3 %copy-start = (f32[1,128]{1,0:T(1,128)S(1)}, f32[1,128]{1,0:T(1,128)}, u32[]{:S(2)}) copy-start(f32[1,128]{1,0:T(1,128)} %gram.1.gram_ref) | copy-start | bytes 1540

commit v8 on v7

--- a/solution.py
+++ b/solution.py
@@ -137,12 +137,13 @@
 
 
 def field_kernel(
-    own, modes, rot_ref, axial_ref, below_ref, own_ref, above_ref, basis_ref, mie_ref,
+    own, modes, together, rot_ref, axial_ref, below_ref, own_ref, above_ref, basis_ref, mie_ref,
     out_ref, blocks_ref, mies_ref, window_ref, sums_ref, total_ref, sems,
 ):
     tables, _, size = rot_ref.shape
     vector_blocks, rows, columns = basis_ref.shape
-    copies = [pltpu.make_async_copy(mie_ref, mies_ref, sems.at[vector_blocks])]
+    copies = [pltpu.make_async_copy(mie_ref, mies_ref.at[pl.ds(0, mie_ref.shape[0])], sems.at[vector_blocks])]
+    mies_ref[mie_ref.shape[0] :] = jnp.zeros((mies_ref.shape[0] - mie_ref.shape[0],) + mies_ref.shape[1:], F32)
     for i in range(vector_blocks):
         copies.append(pltpu.make_async_copy(basis_ref.at[i], blocks_ref.at[i, pl.ds(0, rows)], sems.at[i]))
     for copy in copies:
@@ -157,28 +158,40 @@
         for c in range(2):
             for t in range(size // 128):
                 window_ref[w, c, t] = ref[:, c, :, :, t * 128 : (t + 1) * 128].reshape(group, 128).astype(F32)
-    for c in range(2):
-        for s in range(0, part, 2):
+
+    def sums(pair, carry):
+        for c in range(2):
             results = []
-            for sphere in (s, s + 1):
+            for i in range(2):
                 blocks = []
                 for t in range(size // 128):
-                    lists = [window_ref[w, c, t, pl.ds(sphere, own, part), :] for w in range(3)]
+                    lists = [window_ref[w, c, t, pl.ds(2 * pair + i, own, part), :] for w in range(3)]
                     blocks.append(jnp.concatenate(lists, axis=0).astype(BF16))
                 results.append(dot_nn(counts, jnp.concatenate(blocks, axis=1)))
             for direction in range(2):
                 for g in range(tables):
                     first = (direction * tables + g) * own
                     rows = jnp.concatenate([result[first : first + own] for result in results], axis=0)
-                    place = (direction * 2 + c) * group + s * own
-                    sums_ref[g, place : place + 2 * own, :] = rows.astype(BF16)
-    for g in range(tables):
-        turned = dot_nt(sums_ref[g], rot_ref[g]).astype(BF16)
-        forward, backward = turned[: 2 * group], turned[2 * group :]
-        moved = dot_nt(forward, axial_ref[g, :size]) + dot_nt(swapped(forward), axial_ref[g, size:])
-        moved += dot_nn(jnp.concatenate([backward, swapped(backward)], axis=1), axial_ref[g])
-        back = dot_nn(moved.astype(BF16), rot_ref[g])
-        total_ref[...] = back if g == 0 else total_ref[...] + back
+                    place = pl.multiple_of((direction * 2 + c) * group + pair * 2 * own, 2 * own)
+                    sums_ref[g, pl.ds(place, 2 * own), :] = rows.astype(BF16)
+        return carry
+
+    lax.fori_loop(0, part // 2, sums, 0)
+    total_ref[...] = jnp.zeros_like(total_ref)
+
+    def body(step, carry):
+        entries = [step * together + i for i in range(together)]
+        turned = [dot_nt(sums_ref[g], rot_ref[g]).astype(BF16) for g in entries]
+        moved = []
+        for g, both in zip(entries, turned):
+            forward, backward = both[: 2 * group], both[2 * group :]
+            result = dot_nt(forward, axial_ref[g, :size]) + dot_nt(swapped(forward), axial_ref[g, size:])
+            result += dot_nn(jnp.concatenate([backward, swapped(backward)], axis=1), axial_ref[g])
+            moved.append(result.astype(BF16))
+        total_ref[...] += sum(dot_nn(value, rot_ref[g]) for g, value in zip(entries, moved))
+        return carry
+
+    lax.fori_loop(0, tables // together, body, 0)
     for c in range(2):
         for t in range(size // 128):
             lanes = slice(t * 128, (t + 1) * 128)
@@ -197,13 +210,13 @@
     return jnp.where(iota(value.shape, 1) < half, -rolled, rolled)
 
 
-def add_products(blocks_ref, products_ref, rows, first, count):
+def add_products(blocks_ref, products_ref, rows, first, count, ends):
     vectors = products_ref.shape[0]
     values = []
     for k in range(vectors):
         start = k % 2 * rows + first
-        value = blocks_ref[k // 2, start : start + count, :]
-        if k % 2 == 0 and first + count > rows:
+        value = blocks_ref[k // 2, pl.ds(start, count), :]
+        if k % 2 == 0 and ends:
             value = jnp.where(iota(value.shape, 0) < rows - first, value, 0.0)
         values.append(value)
     for l in range(vectors):
@@ -251,8 +264,15 @@
     for q in range(parts):
         for copy in copies[2 * blocks * q : 2 * blocks * (q + 1)]:
             copy.wait()
-        for first in range(step * q, min(step * (q + 1), rows), chunk):
-            add_products(blocks_ref, products_ref, rows, first, chunk)
+        last = min(step * (q + 1), rows) // chunk
+
+        def body(i, carry):
+            add_products(blocks_ref, products_ref, rows, pl.multiple_of(i * chunk, chunk), chunk, False)
+            return carry
+
+        lax.fori_loop(step * q // chunk, last, body, 0)
+        if rows < (last + 1) * chunk and rows < step * (q + 1):
+            add_products(blocks_ref, products_ref, rows, last * chunk, chunk, True)
     line_ref[...] = products_line(products_ref)
 
 
@@ -267,28 +287,27 @@
         lines_ref[pl.ds(j, modes, quarter), :] = jnp.transpose(turned.astype(F32))[:modes]
     half = columns // 2
     chunk = 64
-    totals = [jnp.zeros((8, columns), F32) for _ in range(2 * vectors + 1)]
-    for first in range(0, full, chunk):
-        here = slice(first, first + chunk)
+    height = mie_ref.shape[1]
+
+    def body(i, totals):
+        first = pl.multiple_of(i * chunk, chunk)
+        here = pl.ds(first, chunk)
         field = lines_ref[here, :]
-        count = min(chunk, rows - first)
-        height = mie_ref.shape[1]
-        mie = mie_ref[first // height : (first + count) // height].reshape(count, columns)
-        if count < chunk:
-            mie = jnp.concatenate([mie, jnp.zeros((chunk - count, columns), F32)], axis=0)
+        mie = mie_ref[pl.ds(i * (chunk // height), chunk // height)].reshape(chunk, columns)
         left = iota(mie.shape, 1) < half
         other = pltpu.roll(mie, half, axis=1)
         product = jnp.where(left, mie, other) * field + jnp.where(left, -other, mie) * pltpu.roll(field, half, axis=1)
-        last = (vectors - 1) % 2 * rows + first
-        image = blocks_ref[(vectors - 1) // 2, last : last + chunk, :] - product
+        image = blocks_ref[(vectors - 1) // 2, pl.ds((vectors - 1) % 2 * rows + first, chunk), :] - product
         image_ref[here, :] = image
         turned = pltpu.roll(image, half, axis=1)
+        added = []
         for k in range(vectors):
-            start = k % 2 * rows + first
-            values = blocks_ref[k // 2, start : start + chunk, :]
-            totals[2 * k] += folded(values * image)
-            totals[2 * k + 1] += folded(values * turned)
-        totals[2 * vectors] += folded(image * image)
+            values = blocks_ref[k // 2, pl.ds(k % 2 * rows + first, chunk), :]
+            added += [folded(values * image), folded(values * turned)]
+        added.append(folded(image * image))
+        return [total + part_sum for total, part_sum in zip(totals, added)]
+
+    totals = lax.fori_loop(0, full // chunk, body, [jnp.zeros((8, columns), F32)] * (2 * vectors + 1))
     lane = iota(gram_ref.shape, 1)
     line = gram_ref[...]
     left = iota((8, columns), 1) < half
@@ -336,21 +355,28 @@
     reals = [jnp.broadcast_to(real[k] * scale, (8, columns)) for k in range(vectors)]
     imags = [jnp.broadcast_to(imag[k] * scale, (8, columns)) for k in range(vectors)]
     chunk = 64
-    for first in range(0, full, chunk):
-        here = slice(first, first + chunk)
+    height = out_ref.shape[1]
+
+    def write(first, place, count):
         values = []
         for k in range(vectors):
-            start = k % 2 * rows + first
-            values.append(blocks_ref[k // 2, start : start + chunk, :].reshape(chunk // 8, 8, columns))
-        along = image_ref[here, :].reshape(chunk // 8, 8, columns) * image_scale
+            value = blocks_ref[k // 2, pl.ds(k % 2 * rows + first, chunk), :]
+            values.append(value.reshape(chunk // 8, 8, columns))
+        along = image_ref[pl.ds(first, chunk), :].reshape(chunk // 8, 8, columns) * image_scale
         turned = jnp.zeros_like(along)
         for k in range(vectors):
             along -= reals[k] * values[k]
             turned += imags[k] * values[k]
         result = along.reshape(chunk, columns) - lane_swap(turned.reshape(chunk, columns))
-        count = min(chunk, rows - first)
-        height = out_ref.shape[1]
-        out_ref[first // height : (first + count) // height] = result.reshape(chunk // height, height, columns)[: count // height]
+        out_ref[pl.ds(place, count // height)] = result.reshape(chunk // height, height, columns)[: count // height]
+
+    def body(i, carry):
+        write(pl.multiple_of(i * chunk, chunk), i * (chunk // height), chunk)
+        return carry
+
+    lax.fori_loop(0, rows // chunk, body, 0)
+    if rows % chunk:
+        write(rows // chunk * chunk, rows // chunk * (chunk // height), rows % chunk)
 
 
 def exchanged(value):
@@ -377,9 +403,10 @@
     rows = quarter * modes
     full = rounded_up(rows, 8)
     pairs_of_vectors = vectors // 2
+    height = 4
 
     basis_rows = in_hbm(basis.transpose(0, 2, 1, 3).reshape(pairs_of_vectors, 2 * rows, columns))
-    mie_rows = in_hbm(mie_coeffs.transpose(1, 0, 2).reshape(rows // 4, 4, columns))
+    mie_rows = in_hbm(mie_coeffs.transpose(1, 0, 2).reshape(rows // height, height, columns))
     rot_rows = in_hbm(rot_table.transpose(1, 0, 2).reshape(modes * tables, modes))
     axial_rows = in_hbm(axial_table.transpose(0, 2, 1, 3))
     pair_rows = in_hbm(pair_table.transpose(2, 0, 1))
@@ -444,14 +471,15 @@
 
     below, above, rotations, axials = lax.optimization_barrier((below, above, rotations, axials))
 
+    together = 2 if tables % 2 == 0 else 1
     field, blocks, mies = pl.pallas_call(
-        functools.partial(field_kernel, own, modes),
+        functools.partial(field_kernel, own, modes, together),
         in_specs=[whole()] * 5 + [hbm()] * 2,
         out_specs=[whole()] * 3,
         out_shape=[
             jax.ShapeDtypeStruct(pieces_shape, BF16),
             jax.ShapeDtypeStruct((pairs_of_vectors, tall, columns), F32),
-            jax.ShapeDtypeStruct(mie_rows.shape, F32),
+            jax.ShapeDtypeStruct((full // height, height, columns), F32),
         ],
         scratch_shapes=[
             pltpu.VMEM((3, 2, size // 128, group, 128), F32),
@@ -475,7 +503,6 @@
     )(blocks, mies, line, field_pieces)
     sums = lax.all_to_all(sums, ("blk", "pair"), split_axis=0, concat_axis=0, tiled=True)
 
-    height = 4
     mean_scale = 1.0 / (own * blk_ways * modes * columns)
     dots, next_rows = pl.pallas_call(
         functools.partial(remainder_kernel, quarter, modes, mean_scale),

time: 65.1 us -> 68.2 us (1.048)
  Pallas kernels: 31.1 us -> 34.3 us
    pallas_call x1, Pallas kernels: 1.43 us -> 2.9 us  [shards(): pl.pallas_call(functools.partial(image_kernel, quarter, modes), in_specs=...]
    pallas_call x1, Pallas kernels: 1.64 us -> 2.6 us  [shards(): pl.pallas_call(functools.partial(remainder_kernel, quarter, modes, mean_s...]
    all_to_all x1, waiting for transfers between devices: 1.18 us -> 0.39 us  [exchanged(): lax.all_to_all(value, 'pair', split_axis=0, concat_axis=0, tiled=True)]
    pallas_call x1, Pallas kernels: 4.85 us -> 5.64 us  [shards(): pl.pallas_call(functools.partial(gram_kernel, quarter, modes), grid=(1,),...]
where the time goes in v8:
time: 68.2 us; the launch traced here: 67.8 us
  Pallas kernels  34.3 us (50%)
  blocking collectives  20.6 us (30%)
  starting transfers between devices  10.2 us (15%)
  waiting for transfers between devices  1.34 us (2%)
  between operations  1.34 us (2%)
    all_to_all x1, blocking collectives, shards(): lax.all_to_all(sums, ('blk', 'pair'), split_axis=0, concat_axis=0, tiled=...  11.8 us
    pallas_call x1, Pallas kernels, shards(): pl.pallas_call(functools.partial(field_kernel, own, modes, together), in_...  11.7 us
    pallas_call x1, Pallas kernels, shards(): pl.pallas_call(functools.partial(tables_kernel, modes, tables), grid=(tab...  9.46 us
    all_to_all x1, blocking collectives, exchanged(): lax.all_to_all(value, 'pair', split_axis=0, concat_axis=0, tiled=True)  8.79 us
    ppermute x2, starting transfers between devices, neighbours(): return (lax.ppermute(value, 'blk', up), lax.ppermute(value, 'blk', down))  5.97 us
    pallas_call x1, Pallas kernels, shards(): pl.pallas_call(functools.partial(gram_kernel, quarter, modes), grid=(1,),...  5.64 us
    all_to_all x1, starting transfers between devices, exchanged(): lax.all_to_all(value, 'pair', split_axis=0, concat_axis=0, tiled=True)  4.22 us
    pallas_call x1, Pallas kernels, shards(): pl.pallas_call(functools.partial(image_kernel, quarter, modes), in_specs=...  2.9 us
  transfers between devices with their start and end apart: 3, of which 2 were waited for; matrix products, arithmetic and copies ran while one was open for 0% of the time, Pallas kernels for 22%

profile of v8, /device:TPU:0, one launch (start us, length us, event | category | flops | bytes accessed | tf_op | source)
XLA Modules:
  0.0 67.8 jit_solution(5520736283747264705)
XLA Ops:
  1.3 2.0 %pack.1 = bf16[4,2,2,16,512]{4,3,2,1,0:T(8,128)(2,1)} custom-call(s32[3,1,128]{2,1,0:T(1,128)} %bitcast.20, s32[1]{0:T(128)S(6)} %copy.8.count_ref, f32[4,2040,128]{2,1,0:T(8,128)} %bitcast.14), custom_call_target="tpu_custom_call" | custom-call | tf_op jit(solution)/shard_map/pack/pallas_call | solution.py:415
  3.2 4.2 %all-to-all-start = ((bf16[4,2,2,16,512]{4,3,2,1,0:T(8,128)(2,1)}), bf16[4,2,2,16,512]{4,3,2,1,0:T(8,128)(2,1)S(1)}, u32[]{:S(2)}, u32[]{:S(2)}) async-start(bf16[4,2,2,16,512]{4,3,2,1,0:T(8,128)(2,1)} %pack.1), calls=%async_computation | async-start | bytes 524288 | tf_op jit(solution)/shard_map/all_to_all | solution.py:383
  7.5 5.6 %gram.1.gram_ref = f32[1,128]{1,0:T(1,128)} custom-call(f32[4,2040,128]{2,1,0:T(8,128)} %bitcast.15), custom_call_target="tpu_custom_call" | custom-call | tf_op jit(solution)/shard_map/gram/pallas_call | solution.py:433
  13.1 0.4 all-to-all-done.own_ref
  13.5 1.3 %collective-permute-start.1 = (bf16[4,2,2,16,512]{4,3,2,1,0:T(8,128)(2,1)S(1)}, bf16[4,2,2,16,512]{4,3,2,1,0:T(8,128)(2,1)S(1)}, u32[]{:S(2)}, u32[]{:S(2)}) collective-permute-start(bf16[4,2,2,16,512]{4,3,2,1,0:T(8,128)(2,1)S(1)} %all-to-all-done.own_ref), channel_id=1, source_target_pairs={{4,0},{8,4},{12,8},{16,12},{20,16},{24,20},{28,24},{5,1},{9,5},{13... | collective-permute-start | bytes 786440 | tf_op jit(solution)/shard_map/ppermute | solution.py:390
  14.8 4.7 %collective-permute-start = (bf16[4,2,2,16,512]{4,3,2,1,0:T(8,128)(2,1)S(1)}, bf16[4,2,2,16,512]{4,3,2,1,0:T(8,128)(2,1)S(1)}, u32[]{:S(2)}, u32[]{:S(2)}) collective-permute-start(bf16[4,2,2,16,512]{4,3,2,1,0:T(8,128)(2,1)S(1)} %all-to-all-done.own_ref), channel_id=1, source_target_pairs={{0,4},{4,8},{8,12},{12,16},{16,20},{20,24},{24,28},{1,5},{5,9},{9,... | collective-permute-start | bytes 786440 | tf_op jit(solution)/shard_map/ppermute | solution.py:390
  19.5 9.5 %tables.1 = (bf16[8,512,512]{2,1,0:T(8,128)(2,1)S(1)}, bf16[8,1024,512]{2,1,0:T(8,128)(2,1)S(1)}) custom-call(bf16[8,510,2,510]{3,2,1,0:T(2,128)(2,1)} %bitcast.17, bf16[4080,510]{1,0:T(8,128)(2,1)} %bitcast.18), custom_call_target="tpu_custom_call" | custom-call | flops 2147483648 | bytes 25165824 | tf_op jit(solution)/shard_map/tables/pallas_call | solution.py:451
  28.9 0.0 collective-permute-done.1.above_ref
  28.9 0.9 %collective-permute-done.below_ref = bf16[4,2,2,16,512]{4,3,2,1,0:T(8,128)(2,1)S(1)} collective-permute-done((bf16[4,2,2,16,512]{4,3,2,1,0:T(8,128)(2,1)S(1)}, bf16[4,2,2,16,512]{4,3,2,1,0:T(8,128)(2,1)S(1)}, u32[]{:S(2)}, u32[]{:S(2)}) %collective-permute-start) | collective-permute-done | bytes 262176 | tf_op jit(solution)/shard_map/ppermute | solution.py:390
  29.9 0.0 copy-start
  29.9 11.7 %field.1 = (bf16[4,2,2,16,512]{4,3,2,1,0:T(8,128)(2,1)S(1)}, f32[4,2048,128]{2,1,0:T(8,128)S(1)}, f32[256,4,128]{2,1,0:T(4,128)S(1)}) custom-call(bf16[8,512,512]{2,1,0:T(8,128)(2,1)S(1)} %get-tuple-element.30.rot_ref, bf16[8,1024,512]{2,1,0:T(8,128)(2,1)S(1)} %get-tuple-element.31.axial_ref, bf16[4,2,2,16,512]{4,3,2,1,0:T(8,128)(2,1)S(1)} %collective-permute-done.below_ref, ...), custom_call_target="tpu_custom_call" | custom-call | tf_op jit(solution)/shard_map/field/pallas_call | solution.py:475
  41.6 8.8 %all_to_all.15.pieces_ref = bf16[4,2,2,16,512]{4,3,2,1,0:T(8,128)(2,1)S(1)} all-to-all(bf16[4,2,2,16,512]{4,3,2,1,0:T(8,128)(2,1)S(1)} %get-tuple-element.39), channel_id=1, replica_groups=mesh['blk'=8,'pair'=4] {'pair'}, dimensions={0} | all-to-all | bytes 524288 | tf_op jit(solution)/shard_map/all_to_all | solution.py:383
  50.4 0.0 copy-done
  50.4 2.9 %image.1 = (f32[1024,128]{1,0:T(8,128)S(1)}, f32[32,1,128]{2,1,0:T(1,128)S(1)}) custom-call(f32[4,2048,128]{2,1,0:T(8,128)S(1)} %get-tuple-element.36.blocks_ref, f32[256,4,128]{2,1,0:T(4,128)S(1)} %get-tuple-element.37.mie_ref, f32[1,128]{1,0:T(1,128)S(1)} %copy-done, bf16[4,2,2,16,512]{4,3,2,1,0:T(8,128)(2,1)S(1)} %all_to_all.15.pieces_ref), custom_call_target="tpu_custom_call" | custom-call | tf_op jit(solution)/shard_map/image/pallas_call | solution.py:495
  53.3 11.8 %all_to_all.16.sums_ref = f32[32,1,128]{2,1,0:T(1,128)S(1)} all-to-all(f32[32,1,128]{2,1,0:T(1,128)S(1)} %get-tuple-element.40), channel_id=1, replica_groups=mesh['blk'=8,'pair'=4] {'blk','pair'}, dimensions={0} | all-to-all | bytes 32768 | tf_op jit(solution)/shard_map/all_to_all | solution.py:504
  65.2 2.6 %remainder.1 = (f32[2,8]{1,0:T(2,128)}, f32[255,4,128]{2,1,0:T(4,128)}) custom-call(f32[32,1,128]{2,1,0:T(1,128)S(1)} %all_to_all.16.sums_ref, f32[4,2048,128]{2,1,0:T(8,128)S(1)} %get-tuple-element.36.blocks_ref, f32[1024,128]{1,0:T(8,128)S(1)} %get-tuple-element.41.image_ref), custom_call_target="tpu_custom_call" | custom-call | tf_op jit(solution)/shard_map/remainder/pallas_call | solution.py:507
Async XLA Ops:
  3.2 10.3 %all-to-all-start = ((bf16[4,2,2,16,512]{4,3,2,1,0:T(8,128)(2,1)}), bf16[4,2,2,16,512]{4,3,2,1,0:T(8,128)(2,1)S(1)}, u32[]{:S(2)}, u32[]{:S(2)}) async-start(bf16[4,2,2,16,512]{4,3,2,1,0:T(8,128)(2,1)} %pack.1), calls=%async_computation | async-start | bytes 524288 | tf_op jit(solution)/shard_map/all_to_all | solution.py:383
  13.5 15.4 %collective-permute-start.1 = (bf16[4,2,2,16,512]{4,3,2,1,0:T(8,128)(2,1)S(1)}, bf16[4,2,2,16,512]{4,3,2,1,0:T(8,128)(2,1)S(1)}, u32[]{:S(2)}, u32[]{:S(2)}) collective-permute-start(bf16[4,2,2,16,512]{4,3,2,1,0:T(8,128)(2,1)S(1)} %all-to-all-done.own_ref), channel_id=1, source_target_pairs={{4,0},{8,4},{12,8},{16,12},{20,16},{24,20},{28,24},{5,1},{9,5},{13... | collective-permute-start | bytes 786440 | tf_op jit(solution)/shard_map/ppermute | solution.py:390
  14.8 15.1 %collective-permute-start = (bf16[4,2,2,16,512]{4,3,2,1,0:T(8,128)(2,1)S(1)}, bf16[4,2,2,16,512]{4,3,2,1,0:T(8,128)(2,1)S(1)}, u32[]{:S(2)}, u32[]{:S(2)}) collective-permute-start(bf16[4,2,2,16,512]{4,3,2,1,0:T(8,128)(2,1)S(1)} %all-to-all-done.own_ref), channel_id=1, source_target_pairs={{0,4},{4,8},{8,12},{12,16},{16,20},{20,24},{24,28},{1,5},{5,9},{9,... | collective-permute-start | bytes 786440 | tf_op jit(solution)/shard_map/ppermute | solution.py:390
  29.9 20.5 %copy-start = (f32[1,128]{1,0:T(1,128)S(1)}, f32[1,128]{1,0:T(1,128)}, u32[]{:S(2)}) copy-start(f32[1,128]{1,0:T(1,128)} %gram.1.gram_ref) | copy-start | bytes 1540

commit v9 on v7

--- a/solution.py
+++ b/solution.py
@@ -65,15 +65,19 @@
     share = 2 * quarter * part
     mine = codes_ref[pl.ds(pl.multiple_of(lax.axis_index("pair") * share, share), share), :][:, 0:1]
     copy.wait()
+    turned = []
     for j in range(quarter):
         pad_ref[0:modes, :] = lines_ref[pl.ds(full - rows + j, modes, quarter), :]
-        turned = jnp.transpose(pad_ref[...])
-        for c in range(2):
-            codes = mine[(c * quarter + j) * part : (c * quarter + j + 1) * part]
+        turned.append(jnp.transpose(pad_ref[...]))
+    height = part * quarter // out_ref.shape[2]
+    for c in range(2):
+        for o in range(out_ref.shape[2]):
+            place = (c * out_ref.shape[2] + o) * height
+            codes = mine[place : place + height]
             for p in range(ways):
-                row = c * (columns // 2) + p * part
-                piece = turned[row : row + part]
-                out_ref[p, c, j] = jnp.where(iota(piece.shape, 1) == modes, codes, piece).astype(BF16)
+                row = c * (columns // 2) + p * part + o * (height // quarter)
+                piece = jnp.concatenate([value[row : row + height // quarter] for value in turned], axis=0)
+                out_ref[p, c, o] = jnp.where(iota(piece.shape, 1) == modes, codes, piece).astype(BF16)
 
 
 def tables_kernel(modes, tables, axial_ref, rot_ref, rot_out_ref, axial_out_ref, lines_ref):
@@ -111,7 +115,8 @@
 
 
 def pair_counts(own, tables, lane, refs):
-    group, size = refs[0].shape[0] * refs[0].shape[2] * refs[0].shape[3], refs[0].shape[4]
+    ways, parts, octets, height, size = refs[0].shape
+    group = ways * octets * height
     wanted = iota((tables * own, group), 0) + own
 
     def one_hot(hit):
@@ -137,56 +142,60 @@
 
 
 def field_kernel(
-    own, modes, rot_ref, axial_ref, below_ref, own_ref, above_ref, basis_ref, mie_ref,
-    out_ref, blocks_ref, mies_ref, window_ref, sums_ref, total_ref, sems,
+    own, modes, together, rot_ref, axial_ref, below_ref, own_ref, above_ref, basis_ref, mie_ref,
+    out_ref, blocks_ref, mies_ref, sums_ref, total_ref, sems,
 ):
     tables, _, size = rot_ref.shape
-    vector_blocks, rows, columns = basis_ref.shape
+    vector_blocks, vector_rows, columns = basis_ref.shape
     copies = [pltpu.make_async_copy(mie_ref, mies_ref, sems.at[vector_blocks])]
     for i in range(vector_blocks):
-        copies.append(pltpu.make_async_copy(basis_ref.at[i], blocks_ref.at[i, pl.ds(0, rows)], sems.at[i]))
+        copies.append(pltpu.make_async_copy(basis_ref.at[i], blocks_ref.at[i, pl.ds(0, vector_rows)], sems.at[i]))
     for copy in copies:
         copy.start()
     for i in range(vector_blocks):
-        blocks_ref[i, rows:, :] = jnp.zeros((blocks_ref.shape[1] - rows, columns), F32)
+        blocks_ref[i, vector_rows:, :] = jnp.zeros((blocks_ref.shape[1] - vector_rows, columns), F32)
     refs = (below_ref, own_ref, above_ref)
-    ways, _, quarter, part, _ = own_ref.shape
+    ways, _, octets, height, _ = own_ref.shape
+    quarter = own // ways
+    each = height // quarter
+    part = octets * each
     group = own * part
     counts = pair_counts(own, tables, modes % 128, refs)
-    for w, ref in enumerate(refs):
-        for c in range(2):
-            for t in range(size // 128):
-                window_ref[w, c, t] = ref[:, c, :, :, t * 128 : (t + 1) * 128].reshape(group, 128).astype(F32)
+    spread = jnp.where(iota((3 * own, 3 * own * each), 0) == lax.div(iota((3 * own, 3 * own * each), 1), each), 1.0, 0.0)
+    counts = dot_nn(counts, spread.astype(BF16))
+    sphere = lax.rem(iota(counts.shape, 1), each)
+    chosen = jnp.concatenate([jnp.where(sphere == i, counts, 0.0).astype(BF16) for i in range(each)], axis=0)
+    kinds = 2 * tables * own
     for c in range(2):
-        for s in range(0, part, 2):
-            results = []
-            for sphere in (s, s + 1):
-                blocks = []
-                for t in range(size // 128):
-                    lists = [window_ref[w, c, t, pl.ds(sphere, own, part), :] for w in range(3)]
-                    blocks.append(jnp.concatenate(lists, axis=0).astype(BF16))
-                results.append(dot_nn(counts, jnp.concatenate(blocks, axis=1)))
-            for direction in range(2):
-                for g in range(tables):
-                    first = (direction * tables + g) * own
-                    rows = jnp.concatenate([result[first : first + own] for result in results], axis=0)
-                    place = (direction * 2 + c) * group + s * own
-                    sums_ref[g, place : place + 2 * own, :] = rows.astype(BF16)
-    for g in range(tables):
-        turned = dot_nt(sums_ref[g], rot_ref[g]).astype(BF16)
-        forward, backward = turned[: 2 * group], turned[2 * group :]
-        moved = dot_nt(forward, axial_ref[g, :size]) + dot_nt(swapped(forward), axial_ref[g, size:])
-        moved += dot_nn(jnp.concatenate([backward, swapped(backward)], axis=1), axial_ref[g])
-        back = dot_nn(moved.astype(BF16), rot_ref[g])
-        total_ref[...] = back if g == 0 else total_ref[...] + back
-    for c in range(2):
-        for t in range(size // 128):
-            lanes = slice(t * 128, (t + 1) * 128)
-            window_ref[0, c, t] = total_ref[c * group : (c + 1) * group, lanes]
-            for p in range(ways):
-                for j in range(quarter):
-                    rows = window_ref[0, c, t, pl.ds(p * quarter + j, part, own), :]
-                    out_ref[p, c, j, :, lanes] = rows.astype(BF16)
+        for o in range(octets):
+            blocks = jnp.concatenate([ref[:, c, o].reshape(ways * height, size) for ref in refs], axis=0)
+            for i in range(0, each, 2):
+                results = dot_nn(chosen[i * kinds : (i + 2) * kinds], blocks)
+                for kind in range(2 * tables):
+                    direction, g = kind // tables, kind % tables
+                    rows = [results[start + kind * own : start + (kind + 1) * own] for start in (0, kinds)]
+                    place = (direction * 2 + c) * group + (o * each + i) * own
+                    sums_ref[g, place : place + 2 * own, :] = jnp.concatenate(rows, axis=0).astype(BF16)
+    total_ref[...] = jnp.zeros_like(total_ref)
+
+    def body(step, carry):
+        entries = [step * together + i for i in range(together)]
+        turned = [dot_nt(sums_ref[g], rot_ref[g]).astype(BF16) for g in entries]
+        moved = []
+        for g, both in zip(entries, turned):
+            forward, backward = both[: 2 * group], both[2 * group :]
+            result = dot_nt(forward, axial_ref[g, :size]) + dot_nt(swapped(forward), axial_ref[g, size:])
+            result += dot_nn(jnp.concatenate([backward, swapped(backward)], axis=1), axial_ref[g])
+            moved.append(result.astype(BF16))
+        total_ref[...] += sum(dot_nn(value, rot_ref[g]) for g, value in zip(entries, moved))
+        return carry
+
+    lax.fori_loop(0, tables // together, body, 0)
+    row, source = iota((2 * group, 2 * group), 0), iota((2 * group, 2 * group), 1)
+    sphere, c = lax.rem(row, part), lax.rem(lax.div(row, quarter * part), 2)
+    block = lax.div(row, 2 * quarter * part) * quarter + lax.rem(lax.div(row, part), quarter)
+    order = jnp.where(source == c * group + sphere * own + block, 1.0, 0.0).astype(BF16)
+    out_ref[...] = dot_nn(order, total_ref[...].astype(BF16)).astype(BF16).reshape(out_ref.shape)
     for copy in copies:
         copy.wait()
 
@@ -385,11 +394,12 @@
     pair_rows = in_hbm(pair_table.transpose(2, 0, 1))
 
     pieces_shape = (ways, 2, quarter, part, size)
+    octets = part * quarter // 16
     pieces = pl.pallas_call(
         functools.partial(pack_kernel, quarter, modes, ways, own),
         in_specs=[hbm(), pl.BlockSpec(memory_space=pltpu.SMEM), hbm()],
         out_specs=whole(),
-        out_shape=jax.ShapeDtypeStruct(pieces_shape, BF16),
+        out_shape=jax.ShapeDtypeStruct((ways, 2, octets, 16, size), BF16),
         scratch_shapes=[
             pltpu.VMEM(pair_rows.shape, jnp.int32),
             pltpu.VMEM((full, columns), F32),
@@ -444,8 +454,9 @@
 
     below, above, rotations, axials = lax.optimization_barrier((below, above, rotations, axials))
 
+    together = 2 if tables % 2 == 0 else 1
     field, blocks, mies = pl.pallas_call(
-        functools.partial(field_kernel, own, modes),
+        functools.partial(field_kernel, own, modes, together),
         in_specs=[whole()] * 5 + [hbm()] * 2,
         out_specs=[whole()] * 3,
         out_shape=[
@@ -454,7 +465,6 @@
             jax.ShapeDtypeStruct(mie_rows.shape, F32),
         ],
         scratch_shapes=[
-            pltpu.VMEM((3, 2, size // 128, group, 128), F32),
             pltpu.VMEM((tables, 4 * group, size), BF16),
             pltpu.VMEM((2 * group, size), F32),
             pltpu.SemaphoreType.DMA((pairs_of_vectors + 1,)),

time: 65.1 us -> 64 us (0.983)
  Pallas kernels: 31.1 us -> 30 us
    pallas_call x1, Pallas kernels: 11.8 us -> 10.7 us  [shards(): pl.pallas_call(functools.partial(field_kernel, own, modes, together), in_...]
  transfers between devices with their start and end apart: 3 -> 3, of which waited for: 2 -> 2; matrix products, arithmetic and copies ran while one was open for 0% -> 0% of each run, Pallas kernels for 22% -> 23%
where the time goes in v9:
time: 64 us; the launch traced here: 63.5 us
  Pallas kernels  30 us (47%)
  blocking collectives  20.3 us (32%)
  starting transfers between devices  10.2 us (16%)
  waiting for transfers between devices  1.63 us (3%)
  between operations  1.34 us (2%)
    all_to_all x1, blocking collectives, shards(): lax.all_to_all(sums, ('blk', 'pair'), split_axis=0, concat_axis=0, tiled=...  11.8 us
    pallas_call x1, Pallas kernels, shards(): pl.pallas_call(functools.partial(field_kernel, own, modes, together), in_...  10.7 us
    pallas_call x1, Pallas kernels, shards(): pl.pallas_call(functools.partial(tables_kernel, modes, tables), grid=(tab...  9.46 us
    all_to_all x1, blocking collectives, exchanged(): lax.all_to_all(value, 'pair', split_axis=0, concat_axis=0, tiled=True)  8.5 us
    ppermute x2, starting transfers between devices, neighbours(): return (lax.ppermute(value, 'blk', up), lax.ppermute(value, 'blk', down))  5.97 us
    pallas_call x1, Pallas kernels, shards(): pl.pallas_call(functools.partial(gram_kernel, quarter, modes), grid=(1,),...  4.85 us
    all_to_all x1, starting transfers between devices, exchanged(): lax.all_to_all(value, 'pair', split_axis=0, concat_axis=0, tiled=True)  4.22 us
    pallas_call x1, Pallas kernels, shards(): pl.pallas_call(functools.partial(pack_kernel, quarter, modes, ways, own),...  1.95 us
  transfers between devices with their start and end apart: 3, of which 2 were waited for; matrix products, arithmetic and copies ran while one was open for 0% of the time, Pallas kernels for 23%

profile of v9, /device:TPU:0, one launch (start us, length us, event | category | flops | bytes accessed | tf_op | source)
XLA Modules:
  0.0 63.5 jit_solution(6452705532573300832)
XLA Ops:
  1.3 2.0 %pack.1 = bf16[4,2,2,16,512]{4,3,2,1,0:T(8,128)(2,1)} custom-call(s32[3,1,128]{2,1,0:T(1,128)} %bitcast.20, s32[1]{0:T(128)S(6)} %copy.8.count_ref, f32[4,2040,128]{2,1,0:T(8,128)} %bitcast.14), custom_call_target="tpu_custom_call" | custom-call | tf_op jit(solution)/shard_map/pack/pallas_call | solution.py:398
  3.2 4.2 %all-to-all-start = ((bf16[4,2,2,16,512]{4,3,2,1,0:T(8,128)(2,1)}), bf16[4,2,2,16,512]{4,3,2,1,0:T(8,128)(2,1)S(1)}, u32[]{:S(2)}, u32[]{:S(2)}) async-start(bf16[4,2,2,16,512]{4,3,2,1,0:T(8,128)(2,1)} %pack.1), calls=%async_computation | async-start | bytes 524288 | tf_op jit(solution)/shard_map/all_to_all | solution.py:366
  7.5 4.8 %gram.1.gram_ref = f32[1,128]{1,0:T(1,128)} custom-call(f32[4,2040,128]{2,1,0:T(8,128)} %bitcast.15), custom_call_target="tpu_custom_call" | custom-call | tf_op jit(solution)/shard_map/gram/pallas_call | solution.py:416
  12.3 1.2 %all-to-all-done.own_ref = bf16[4,2,2,16,512]{4,3,2,1,0:T(8,128)(2,1)S(1)} async-done(((bf16[4,2,2,16,512]{4,3,2,1,0:T(8,128)(2,1)}), bf16[4,2,2,16,512]{4,3,2,1,0:T(8,128)(2,1)S(1)}, u32[]{:S(2)}, u32[]{:S(2)}) %all-to-all-start) | async-done | bytes 262176 | tf_op jit(solution)/shard_map/all_to_all | solution.py:366
  13.5 1.3 %collective-permute-start.1 = (bf16[4,2,2,16,512]{4,3,2,1,0:T(8,128)(2,1)S(1)}, bf16[4,2,2,16,512]{4,3,2,1,0:T(8,128)(2,1)S(1)}, u32[]{:S(2)}, u32[]{:S(2)}) collective-permute-start(bf16[4,2,2,16,512]{4,3,2,1,0:T(8,128)(2,1)S(1)} %all-to-all-done.own_ref), channel_id=1, source_target_pairs={{4,0},{8,4},{12,8},{16,12},{20,16},{24,20},{28,24},{5,1},{9,5},{13... | collective-permute-start | bytes 786440 | tf_op jit(solution)/shard_map/ppermute | solution.py:373
  14.8 4.7 %collective-permute-start = (bf16[4,2,2,16,512]{4,3,2,1,0:T(8,128)(2,1)S(1)}, bf16[4,2,2,16,512]{4,3,2,1,0:T(8,128)(2,1)S(1)}, u32[]{:S(2)}, u32[]{:S(2)}) collective-permute-start(bf16[4,2,2,16,512]{4,3,2,1,0:T(8,128)(2,1)S(1)} %all-to-all-done.own_ref), channel_id=1, source_target_pairs={{0,4},{4,8},{8,12},{12,16},{16,20},{20,24},{24,28},{1,5},{5,9},{9,... | collective-permute-start | bytes 786440 | tf_op jit(solution)/shard_map/ppermute | solution.py:373
  19.5 9.5 %tables.1 = (bf16[8,512,512]{2,1,0:T(8,128)(2,1)S(1)}, bf16[8,1024,512]{2,1,0:T(8,128)(2,1)S(1)}) custom-call(bf16[8,510,2,510]{3,2,1,0:T(2,128)(2,1)} %bitcast.17, bf16[4080,510]{1,0:T(8,128)(2,1)} %bitcast.18), custom_call_target="tpu_custom_call" | custom-call | flops 2147483648 | bytes 25165824 | tf_op jit(solution)/shard_map/tables/pallas_call | solution.py:434
  28.9 0.0 collective-permute-done.1.above_ref
  28.9 0.4 collective-permute-done.below_ref
  29.4 0.0 copy-start
  29.4 10.7 %field.1 = (bf16[4,2,2,16,512]{4,3,2,1,0:T(8,128)(2,1)S(1)}, f32[4,2048,128]{2,1,0:T(8,128)S(1)}, f32[255,4,128]{2,1,0:T(4,128)S(1)}) custom-call(bf16[8,512,512]{2,1,0:T(8,128)(2,1)S(1)} %get-tuple-element.30.rot_ref, bf16[8,1024,512]{2,1,0:T(8,128)(2,1)S(1)} %get-tuple-element.31.axial_ref, bf16[4,2,2,16,512]{4,3,2,1,0:T(8,128)(2,1)S(1)} %collective-permute-done.below_ref, ...), custom_call_target="tpu_custom_call" | custom-call | tf_op jit(solution)/shard_map/field/pallas_call | solution.py:458
  40.1 8.5 %all_to_all.15.pieces_ref = bf16[4,2,2,16,512]{4,3,2,1,0:T(8,128)(2,1)S(1)} all-to-all(bf16[4,2,2,16,512]{4,3,2,1,0:T(8,128)(2,1)S(1)} %get-tuple-element.39), channel_id=1, replica_groups=mesh['blk'=8,'pair'=4] {'pair'}, dimensions={0} | all-to-all | bytes 524288 | tf_op jit(solution)/shard_map/all_to_all | solution.py:366
  48.6 0.0 copy-done
  48.6 1.4 %image.1 = (f32[1024,128]{1,0:T(8,128)S(1)}, f32[32,1,128]{2,1,0:T(1,128)S(1)}) custom-call(f32[4,2048,128]{2,1,0:T(8,128)S(1)} %get-tuple-element.36.blocks_ref, f32[255,4,128]{2,1,0:T(4,128)S(1)} %get-tuple-element.37.mie_ref, f32[1,128]{1,0:T(1,128)S(1)} %copy-done, bf16[4,2,2,16,512]{4,3,2,1,0:T(8,128)(2,1)S(1)} %all_to_all.15.pieces_ref), custom_call_target="tpu_custom_call" | custom-call | tf_op jit(solution)/shard_map/image/pallas_call | solution.py:477
  50.0 11.8 %all_to_all.16.sums_ref = f32[32,1,128]{2,1,0:T(1,128)S(1)} all-to-all(f32[32,1,128]{2,1,0:T(1,128)S(1)} %get-tuple-element.40), channel_id=1, replica_groups=mesh['blk'=8,'pair'=4] {'blk','pair'}, dimensions={0} | all-to-all | bytes 32768 | tf_op jit(solution)/shard_map/all_to_all | solution.py:486
  61.8 1.6 %remainder.1 = (f32[2,8]{1,0:T(2,128)}, f32[255,4,128]{2,1,0:T(4,128)}) custom-call(f32[32,1,128]{2,1,0:T(1,128)S(1)} %all_to_all.16.sums_ref, f32[4,2048,128]{2,1,0:T(8,128)S(1)} %get-tuple-element.36.blocks_ref, f32[1024,128]{1,0:T(8,128)S(1)} %get-tuple-element.41.image_ref), custom_call_target="tpu_custom_call" | custom-call | tf_op jit(solution)/shard_map/remainder/pallas_call | solution.py:490
Async XLA Ops:
  3.2 10.3 %all-to-all-start = ((bf16[4,2,2,16,512]{4,3,2,1,0:T(8,128)(2,1)}), bf16[4,2,2,16,512]{4,3,2,1,0:T(8,128)(2,1)S(1)}, u32[]{:S(2)}, u32[]{:S(2)}) async-start(bf16[4,2,2,16,512]{4,3,2,1,0:T(8,128)(2,1)} %pack.1), calls=%async_computation | async-start | bytes 524288 | tf_op jit(solution)/shard_map/all_to_all | solution.py:366
  13.5 15.4 %collective-permute-start.1 = (bf16[4,2,2,16,512]{4,3,2,1,0:T(8,128)(2,1)S(1)}, bf16[4,2,2,16,512]{4,3,2,1,0:T(8,128)(2,1)S(1)}, u32[]{:S(2)}, u32[]{:S(2)}) collective-permute-start(bf16[4,2,2,16,512]{4,3,2,1,0:T(8,128)(2,1)S(1)} %all-to-all-done.own_ref), channel_id=1, source_target_pairs={{4,0},{8,4},{12,8},{16,12},{20,16},{24,20},{28,24},{5,1},{9,5},{13... | collective-permute-start | bytes 786440 | tf_op jit(solution)/shard_map/ppermute | solution.py:373
  14.8 14.6 %collective-permute-start = (bf16[4,2,2,16,512]{4,3,2,1,0:T(8,128)(2,1)S(1)}, bf16[4,2,2,16,512]{4,3,2,1,0:T(8,128)(2,1)S(1)}, u32[]{:S(2)}, u32[]{:S(2)}) collective-permute-start(bf16[4,2,2,16,512]{4,3,2,1,0:T(8,128)(2,1)S(1)} %all-to-all-done.own_ref), channel_id=1, source_target_pairs={{0,4},{4,8},{8,12},{12,16},{16,20},{20,24},{24,28},{1,5},{5,9},{9,... | collective-permute-start | bytes 786440 | tf_op jit(solution)/shard_map/ppermute | solution.py:373
  29.4 19.2 %copy-start = (f32[1,128]{1,0:T(1,128)S(1)}, f32[1,128]{1,0:T(1,128)}, u32[]{:S(2)}) copy-start(f32[1,128]{1,0:T(1,128)} %gram.1.gram_ref) | copy-start | bytes 1540

commit v10 on v9

--- a/solution.py
+++ b/solution.py
@@ -143,8 +143,9 @@
 
 def field_kernel(
     own, modes, together, rot_ref, axial_ref, below_ref, own_ref, above_ref, basis_ref, mie_ref,
-    out_ref, blocks_ref, mies_ref, sums_ref, total_ref, sems,
+    *rest,
 ):
+    outs, (blocks_ref, mies_ref, sums_ref, total_ref, sems) = rest[:-5], rest[-5:]
     tables, _, size = rot_ref.shape
     vector_blocks, vector_rows, columns = basis_ref.shape
     copies = [pltpu.make_async_copy(mie_ref, mies_ref, sems.at[vector_blocks])]
@@ -193,9 +194,13 @@
     lax.fori_loop(0, tables // together, body, 0)
     row, source = iota((2 * group, 2 * group), 0), iota((2 * group, 2 * group), 1)
     sphere, c = lax.rem(row, part), lax.rem(lax.div(row, quarter * part), 2)
-    block = lax.div(row, 2 * quarter * part) * quarter + lax.rem(lax.div(row, part), quarter)
+    owner = lax.div(row, 2 * quarter * part) ^ lax.axis_index("pair")
+    block = owner * quarter + lax.rem(lax.div(row, part), quarter)
     order = jnp.where(source == c * group + sphere * own + block, 1.0, 0.0).astype(BF16)
-    out_ref[...] = dot_nn(order, total_ref[...].astype(BF16)).astype(BF16).reshape(out_ref.shape)
+    result = dot_nn(order, total_ref[...].astype(BF16)).astype(BF16)
+    share = 2 * quarter * part
+    for i, out_ref in enumerate(outs):
+        out_ref[...] = result[i * share : (i + 1) * share].reshape(out_ref.shape)
     for copy in copies:
         copy.wait()
 
@@ -265,15 +270,20 @@
     line_ref[...] = products_line(products_ref)
 
 
-def image_kernel(quarter, modes, blocks_ref, mie_ref, gram_ref, pieces_ref, image_ref, sums_ref, lines_ref):
+def image_kernel(quarter, modes, blocks_ref, mie_ref, gram_ref, *rest):
+    pieces, (image_ref, sums_ref, lines_ref, whole_ref) = rest[:-4], rest[-4:]
     vectors = 2 * blocks_ref.shape[0]
     full, columns = image_ref.shape
     rows = quarter * modes
-    ways, _, _, part, size = pieces_ref.shape
+    part = pieces[0].shape[2]
+    for i, piece_ref in enumerate(pieces):
+        place = pl.multiple_of((lax.axis_index("pair") ^ i) * part, part)
+        for j in range(quarter):
+            for c in range(2):
+                whole_ref[j, pl.ds(c * (columns // 2) + place, part), :] = piece_ref[c, j]
     lines_ref[rows:full, :] = jnp.zeros((full - rows, columns), F32)
     for j in range(quarter):
-        turned = jnp.concatenate([pieces_ref[:, c, j].reshape(ways * part, size) for c in range(2)], axis=0)
-        lines_ref[pl.ds(j, modes, quarter), :] = jnp.transpose(turned.astype(F32))[:modes]
+        lines_ref[pl.ds(j, modes, quarter), :] = jnp.transpose(whole_ref[j].astype(F32))[:modes]
     half = columns // 2
     chunk = 64
     totals = [jnp.zeros((8, columns), F32) for _ in range(2 * vectors + 1)]
@@ -393,7 +403,6 @@
     axial_rows = in_hbm(axial_table.transpose(0, 2, 1, 3))
     pair_rows = in_hbm(pair_table.transpose(2, 0, 1))
 
-    pieces_shape = (ways, 2, quarter, part, size)
     octets = part * quarter // 16
     pieces = pl.pallas_call(
         functools.partial(pack_kernel, quarter, modes, ways, own),
@@ -455,12 +464,12 @@
     below, above, rotations, axials = lax.optimization_barrier((below, above, rotations, axials))
 
     together = 2 if tables % 2 == 0 else 1
-    field, blocks, mies = pl.pallas_call(
+    *field, blocks, mies = pl.pallas_call(
         functools.partial(field_kernel, own, modes, together),
         in_specs=[whole()] * 5 + [hbm()] * 2,
-        out_specs=[whole()] * 3,
-        out_shape=[
-            jax.ShapeDtypeStruct(pieces_shape, BF16),
+        out_specs=[whole()] * (ways + 2),
+        out_shape=[jax.ShapeDtypeStruct((2, quarter, part, size), BF16)] * ways
+        + [
             jax.ShapeDtypeStruct((pairs_of_vectors, tall, columns), F32),
             jax.ShapeDtypeStruct(mie_rows.shape, F32),
         ],
@@ -472,17 +481,19 @@
         compiler_params=params(20),
         name="field",
     )(rotations, axials, below, own_pieces, above, basis_rows, mie_rows)
-    field_pieces = exchanged(field)
+    field_pieces = [field[0]]
+    for i in range(1, ways):
+        field_pieces.append(lax.ppermute(field[i], "pair", [(p, p ^ i) for p in range(ways)]))
 
     image, sums = pl.pallas_call(
         functools.partial(image_kernel, quarter, modes),
-        in_specs=[whole()] * 4,
+        in_specs=[whole()] * (ways + 3),
         out_specs=[whole()] * 2,
         out_shape=[jax.ShapeDtypeStruct((full, columns), F32), jax.ShapeDtypeStruct((ways * blk_ways, 1, 128), F32)],
-        scratch_shapes=[pltpu.VMEM((full, columns), F32)],
+        scratch_shapes=[pltpu.VMEM((full, columns), F32), pltpu.VMEM((quarter, columns, size), BF16)],
         compiler_params=params(8),
         name="image",
-    )(blocks, mies, line, field_pieces)
+    )(blocks, mies, line, *field_pieces)
     sums = lax.all_to_all(sums, ("blk", "pair"), split_axis=0, concat_axis=0, tiled=True)
 
     height = 4

time: 64 us -> 61.8 us (0.966)
  blocking collectives: 20.3 us -> 12.5 us
  waiting for transfers between devices: 1.63 us -> 5.4 us
  starting transfers between devices: 10.2 us -> 12.1 us
    all_to_all x1 -> x0, blocking collectives: 8.5 us -> none  [exchanged(): lax.all_to_all(value, 'pair', split_axis=0, concat_axis=0, tiled=True)]
    ppermute x0 -> x3, waiting for transfers between devices: none -> 3.77 us  [shards(): lax.ppermute(field[i], 'pair', [(p, p ^ i) for p in range(ways)])]
    ppermute x0 -> x3, starting transfers between devices: none -> 1.94 us  [shards(): lax.ppermute(field[i], 'pair', [(p, p ^ i) for p in range(ways)])]
    all_to_all x1, blocking collectives: 11.8 us -> 12.5 us  [shards(): lax.all_to_all(sums, ('blk', 'pair'), split_axis=0, concat_axis=0, tiled=...]
  transfers between devices with their start and end apart: 3 -> 6, of which waited for: 2 -> 4; matrix products, arithmetic and copies ran while one was open for 0% -> 0% of each run, Pallas kernels for 23% -> 23%
where the time goes in v10:
time: 61.8 us; the launch traced here: 61.3 us
  Pallas kernels  30 us (49%)
  blocking collectives  12.5 us (20%)
  starting transfers between devices  12.1 us (20%)
  waiting for transfers between devices  5.4 us (9%)
  between operations  1.35 us (2%)
    all_to_all x1, blocking collectives, shards(): lax.all_to_all(sums, ('blk', 'pair'), split_axis=0, concat_axis=0, tiled=...  12.5 us
    pallas_call x1, Pallas kernels, shards(): pl.pallas_call(functools.partial(field_kernel, own, modes, together), in_...  10.7 us
    pallas_call x1, Pallas kernels, shards(): pl.pallas_call(functools.partial(tables_kernel, modes, tables), grid=(tab...  9.46 us
    ppermute x2, starting transfers between devices, neighbours(): return (lax.ppermute(value, 'blk', up), lax.ppermute(value, 'blk', down))  5.97 us
    pallas_call x1, Pallas kernels, shards(): pl.pallas_call(functools.partial(gram_kernel, quarter, modes), grid=(1,),...  4.85 us
    all_to_all x1, starting transfers between devices, exchanged(): lax.all_to_all(value, 'pair', split_axis=0, concat_axis=0, tiled=True)  4.22 us
    ppermute x3, waiting for transfers between devices, shards(): lax.ppermute(field[i], 'pair', [(p, p ^ i) for p in range(ways)])  3.77 us
    pallas_call x1, Pallas kernels, shards(): pl.pallas_call(functools.partial(pack_kernel, quarter, modes, ways, own),...  1.95 us
  transfers between devices with their start and end apart: 6, of which 4 were waited for; matrix products, arithmetic and copies ran while one was open for 0% of the time, Pallas kernels for 23%

profile of v10, /device:TPU:0, one launch (start us, length us, event | category | flops | bytes accessed | tf_op | source)
XLA Modules:
  0.0 61.3 jit_solution(4840419541581619901)
XLA Ops:
  1.3 2.0 %pack.1 = bf16[4,2,2,16,512]{4,3,2,1,0:T(8,128)(2,1)} custom-call(s32[3,1,128]{2,1,0:T(1,128)} %bitcast.20, s32[1]{0:T(128)S(6)} %copy.8.count_ref, f32[4,2040,128]{2,1,0:T(8,128)} %bitcast.14), custom_call_target="tpu_custom_call" | custom-call | tf_op jit(solution)/shard_map/pack/pallas_call | solution.py:407
  3.2 4.2 %all-to-all-start = ((bf16[4,2,2,16,512]{4,3,2,1,0:T(8,128)(2,1)}), bf16[4,2,2,16,512]{4,3,2,1,0:T(8,128)(2,1)S(1)}, u32[]{:S(2)}, u32[]{:S(2)}) async-start(bf16[4,2,2,16,512]{4,3,2,1,0:T(8,128)(2,1)} %pack.1), calls=%async_computation | async-start | bytes 524288 | tf_op jit(solution)/shard_map/all_to_all | solution.py:376
  7.5 4.8 %gram.1.gram_ref = f32[1,128]{1,0:T(1,128)} custom-call(f32[4,2040,128]{2,1,0:T(8,128)} %bitcast.15), custom_call_target="tpu_custom_call" | custom-call | tf_op jit(solution)/shard_map/gram/pallas_call | solution.py:425
  12.3 1.2 %all-to-all-done.own_ref = bf16[4,2,2,16,512]{4,3,2,1,0:T(8,128)(2,1)S(1)} async-done(((bf16[4,2,2,16,512]{4,3,2,1,0:T(8,128)(2,1)}), bf16[4,2,2,16,512]{4,3,2,1,0:T(8,128)(2,1)S(1)}, u32[]{:S(2)}, u32[]{:S(2)}) %all-to-all-start) | async-done | bytes 262176 | tf_op jit(solution)/shard_map/all_to_all | solution.py:376
  13.5 1.3 %collective-permute-start.1 = (bf16[4,2,2,16,512]{4,3,2,1,0:T(8,128)(2,1)S(1)}, bf16[4,2,2,16,512]{4,3,2,1,0:T(8,128)(2,1)S(1)}, u32[]{:S(2)}, u32[]{:S(2)}) collective-permute-start(bf16[4,2,2,16,512]{4,3,2,1,0:T(8,128)(2,1)S(1)} %all-to-all-done.own_ref), channel_id=1, source_target_pairs={{4,0},{8,4},{12,8},{16,12},{20,16},{24,20},{28,24},{5,1},{9,5},{13... | collective-permute-start | bytes 786440 | tf_op jit(solution)/shard_map/ppermute | solution.py:383
  14.8 4.7 %collective-permute-start = (bf16[4,2,2,16,512]{4,3,2,1,0:T(8,128)(2,1)S(1)}, bf16[4,2,2,16,512]{4,3,2,1,0:T(8,128)(2,1)S(1)}, u32[]{:S(2)}, u32[]{:S(2)}) collective-permute-start(bf16[4,2,2,16,512]{4,3,2,1,0:T(8,128)(2,1)S(1)} %all-to-all-done.own_ref), channel_id=1, source_target_pairs={{0,4},{4,8},{8,12},{12,16},{16,20},{20,24},{24,28},{1,5},{5,9},{9,... | collective-permute-start | bytes 786440 | tf_op jit(solution)/shard_map/ppermute | solution.py:383
  19.5 9.5 %tables.1 = (bf16[8,512,512]{2,1,0:T(8,128)(2,1)S(1)}, bf16[8,1024,512]{2,1,0:T(8,128)(2,1)S(1)}) custom-call(bf16[8,510,2,510]{3,2,1,0:T(2,128)(2,1)} %bitcast.17, bf16[4080,510]{1,0:T(8,128)(2,1)} %bitcast.18), custom_call_target="tpu_custom_call" | custom-call | flops 2147483648 | bytes 25165824 | tf_op jit(solution)/shard_map/tables/pallas_call | solution.py:443
  28.9 0.0 collective-permute-done.1.above_ref
  28.9 0.4 collective-permute-done.below_ref
  29.4 0.0 copy-start
  29.4 10.7 %field.1 = (bf16[2,2,16,512]{3,2,1,0:T(8,128)(2,1)S(1)}, bf16[2,2,16,512]{3,2,1,0:T(8,128)(2,1)S(1)}, bf16[2,2,16,512]{3,2,1,0:T(8,128)(2,1)S(1)}, bf16[2,2,16,5...) custom-call(bf16[8,512,512]{2,1,0:T(8,128)(2,1)S(1)} %get-tuple-element.33.rot_ref, ...), custom_call_target="tpu_custom_call" | custom-call | tf_op jit(solution)/shard_map/field/pallas_call | solution.py:467
  40.1 0.1 collective-permute-start.2
  40.2 1.5 %collective-permute-start.3 = (bf16[2,2,16,512]{3,2,1,0:T(8,128)(2,1)S(1)}, bf16[2,2,16,512]{3,2,1,0:T(8,128)(2,1)S(1)}, u32[]{:S(2)}, u32[]{:S(2)}) collective-permute-start(bf16[2,2,16,512]{3,2,1,0:T(8,128)(2,1)S(1)} %get-tuple-element.44), channel_id=1, source_target_pairs={{0,2},{1,3},{2,0},{3,1},{4,6},{5,7},{6,4},{7,5},{8,10},{9,11},{10,... | collective-permute-start | bytes 196616 | tf_op jit(solution)/shard_map/ppermute | solution.py:486
  41.6 0.4 collective-permute-start.4
  42.0 0.0 collective-permute-done.2.rest_1_
  42.0 2.7 %collective-permute-done.3.rest_2_ = bf16[2,2,16,512]{3,2,1,0:T(8,128)(2,1)S(1)} collective-permute-done((bf16[2,2,16,512]{3,2,1,0:T(8,128)(2,1)S(1)}, bf16[2,2,16,512]{3,2,1,0:T(8,128)(2,1)S(1)}, u32[]{:S(2)}, u32[]{:S(2)}) %collective-permute-start.3) | collective-permute-done | bytes 65568 | tf_op jit(solution)/shard_map/ppermute | solution.py:486
  44.8 1.0 %collective-permute-done.4.rest_3_ = bf16[2,2,16,512]{3,2,1,0:T(8,128)(2,1)S(1)} collective-permute-done((bf16[2,2,16,512]{3,2,1,0:T(8,128)(2,1)S(1)}, bf16[2,2,16,512]{3,2,1,0:T(8,128)(2,1)S(1)}, u32[]{:S(2)}, u32[]{:S(2)}) %collective-permute-start.4) | collective-permute-done | bytes 65568 | tf_op jit(solution)/shard_map/ppermute | solution.py:486
  45.8 0.0 copy-done
  45.8 1.4 %image.1 = (f32[1024,128]{1,0:T(8,128)S(1)}, f32[32,1,128]{2,1,0:T(1,128)S(1)}) custom-call(f32[4,2048,128]{2,1,0:T(8,128)S(1)} %get-tuple-element.39.blocks_ref, f32[255,4,128]{2,1,0:T(4,128)S(1)} %get-tuple-element.40.mie_ref, f32[1,128]{1,0:T(1,128)S(1)} %copy-done, bf16[2,2,16,512]{3,2,1,0:T(8,128)(2,1)S(1)} %get-tuple-element.42.rest_0_, ...), custom_call_target="tpu_custom_call" | custom-call | tf_op jit(solution)/shard_map/image/pallas_call | solution.py:488
  47.2 12.5 %all_to_all.10.sums_ref = f32[32,1,128]{2,1,0:T(1,128)S(1)} all-to-all(f32[32,1,128]{2,1,0:T(1,128)S(1)} %get-tuple-element.46), channel_id=1, replica_groups=mesh['blk'=8,'pair'=4] {'blk','pair'}, dimensions={0} | all-to-all | bytes 32768 | tf_op jit(solution)/shard_map/all_to_all | solution.py:497
  59.7 1.6 %remainder.1 = (f32[2,8]{1,0:T(2,128)}, f32[255,4,128]{2,1,0:T(4,128)}) custom-call(f32[32,1,128]{2,1,0:T(1,128)S(1)} %all_to_all.10.sums_ref, f32[4,2048,128]{2,1,0:T(8,128)S(1)} %get-tuple-element.39.blocks_ref, f32[1024,128]{1,0:T(8,128)S(1)} %get-tuple-element.47.image_ref), custom_call_target="tpu_custom_call" | custom-call | tf_op jit(solution)/shard_map/remainder/pallas_call | solution.py:501
Async XLA Ops:
  3.2 10.3 %all-to-all-start = ((bf16[4,2,2,16,512]{4,3,2,1,0:T(8,128)(2,1)}), bf16[4,2,2,16,512]{4,3,2,1,0:T(8,128)(2,1)S(1)}, u32[]{:S(2)}, u32[]{:S(2)}) async-start(bf16[4,2,2,16,512]{4,3,2,1,0:T(8,128)(2,1)} %pack.1), calls=%async_computation | async-start | bytes 524288 | tf_op jit(solution)/shard_map/all_to_all | solution.py:376
  13.5 15.4 %collective-permute-start.1 = (bf16[4,2,2,16,512]{4,3,2,1,0:T(8,128)(2,1)S(1)}, bf16[4,2,2,16,512]{4,3,2,1,0:T(8,128)(2,1)S(1)}, u32[]{:S(2)}, u32[]{:S(2)}) collective-permute-start(bf16[4,2,2,16,512]{4,3,2,1,0:T(8,128)(2,1)S(1)} %all-to-all-done.own_ref), channel_id=1, source_target_pairs={{4,0},{8,4},{12,8},{16,12},{20,16},{24,20},{28,24},{5,1},{9,5},{13... | collective-permute-start | bytes 786440 | tf_op jit(solution)/shard_map/ppermute | solution.py:383
  14.8 14.6 %collective-permute-start = (bf16[4,2,2,16,512]{4,3,2,1,0:T(8,128)(2,1)S(1)}, bf16[4,2,2,16,512]{4,3,2,1,0:T(8,128)(2,1)S(1)}, u32[]{:S(2)}, u32[]{:S(2)}) collective-permute-start(bf16[4,2,2,16,512]{4,3,2,1,0:T(8,128)(2,1)S(1)} %all-to-all-done.own_ref), channel_id=1, source_target_pairs={{0,4},{4,8},{8,12},{12,16},{16,20},{20,24},{24,28},{1,5},{5,9},{9,... | collective-permute-start | bytes 786440 | tf_op jit(solution)/shard_map/ppermute | solution.py:383
  29.4 16.4 %copy-start = (f32[1,128]{1,0:T(1,128)S(1)}, f32[1,128]{1,0:T(1,128)}, u32[]{:S(2)}) copy-start(f32[1,128]{1,0:T(1,128)} %gram.1.gram_ref) | copy-start | bytes 1540
  40.1 1.9 %collective-permute-start.2 = (bf16[2,2,16,512]{3,2,1,0:T(8,128)(2,1)S(1)}, bf16[2,2,16,512]{3,2,1,0:T(8,128)(2,1)S(1)}, u32[]{:S(2)}, u32[]{:S(2)}) collective-permute-start(bf16[2,2,16,512]{3,2,1,0:T(8,128)(2,1)S(1)} %get-tuple-element.43), channel_id=1, source_target_pairs={{0,1},{1,0},{2,3},{3,2},{4,5},{5,4},{6,7},{7,6},{8,9},{9,8},{10,11... | collective-permute-start | bytes 196616 | tf_op jit(solution)/shard_map/ppermute | solution.py:486
  40.2 4.6 %collective-permute-start.3 = (bf16[2,2,16,512]{3,2,1,0:T(8,128)(2,1)S(1)}, bf16[2,2,16,512]{3,2,1,0:T(8,128)(2,1)S(1)}, u32[]{:S(2)}, u32[]{:S(2)}) collective-permute-start(bf16[2,2,16,512]{3,2,1,0:T(8,128)(2,1)S(1)} %get-tuple-element.44), channel_id=1, source_target_pairs={{0,2},{1,3},{2,0},{3,1},{4,6},{5,7},{6,4},{7,5},{8,10},{9,11},{10,... | collective-permute-start | bytes 196616 | tf_op jit(solution)/shard_map/ppermute | solution.py:486
  41.6 4.2 %collective-permute-start.4 = (bf16[2,2,16,512]{3,2,1,0:T(8,128)(2,1)S(1)}, bf16[2,2,16,512]{3,2,1,0:T(8,128)(2,1)S(1)}, u32[]{:S(2)}, u32[]{:S(2)}) collective-permute-start(bf16[2,2,16,512]{3,2,1,0:T(8,128)(2,1)S(1)} %get-tuple-element.45), channel_id=1, source_target_pairs={{0,3},{1,2},{2,1},{3,0},{4,7},{5,6},{6,5},{7,4},{8,11},{9,10},{10,... | collective-permute-start | bytes 196616 | tf_op jit(solution)/shard_map/ppermute | solution.py:486

commit v11 on v10

--- a/solution.py
+++ b/solution.py
@@ -44,7 +44,8 @@
     return lax.dot_general(left, right, (((1,), (1,)), ((), ())), preferred_element_type=F32)
 
 
-def pack_kernel(quarter, modes, ways, own, list_ref, count_ref, basis_ref, out_ref, pair_rows_ref, lines_ref, pad_ref, codes_ref, sems):
+def pack_kernel(quarter, modes, ways, own, list_ref, count_ref, basis_ref, *rest):
+    outs, (pair_rows_ref, lines_ref, pad_ref, codes_ref, turned_ref, sems) = rest[:ways], rest[ways:]
     full, columns = lines_ref.shape
     rows = quarter * modes
     part = columns // 2 // ways
@@ -65,19 +66,33 @@
     share = 2 * quarter * part
     mine = codes_ref[pl.ds(pl.multiple_of(lax.axis_index("pair") * share, share), share), :][:, 0:1]
     copy.wait()
-    turned = []
     for j in range(quarter):
         pad_ref[0:modes, :] = lines_ref[pl.ds(full - rows + j, modes, quarter), :]
-        turned.append(jnp.transpose(pad_ref[...]))
-    height = part * quarter // out_ref.shape[2]
-    for c in range(2):
-        for o in range(out_ref.shape[2]):
-            place = (c * out_ref.shape[2] + o) * height
-            codes = mine[place : place + height]
-            for p in range(ways):
-                row = c * (columns // 2) + p * part + o * (height // quarter)
-                piece = jnp.concatenate([value[row : row + height // quarter] for value in turned], axis=0)
-                out_ref[p, c, o] = jnp.where(iota(piece.shape, 1) == modes, codes, piece).astype(BF16)
+        turned_ref[j] = jnp.transpose(pad_ref[...])
+    _, octets, height, size = outs[0].shape
+    each = height // quarter
+    for i, out_ref in enumerate(outs):
+        place = (lax.axis_index("pair") ^ i) * part
+        for c in range(2):
+            for o in range(octets):
+                first = (c * octets + o) * height
+                here = pl.ds(pl.multiple_of(c * (columns // 2) + place + o * each, each), each)
+                piece = jnp.concatenate([turned_ref[j, here, :] for j in range(quarter)], axis=0)
+                piece = jnp.where(iota(piece.shape, 1) == modes, mine[first : first + height], piece)
+                out_ref[c, o] = piece.astype(BF16)
+
+
+def join_kernel(*refs):
+    out_ref = refs[-1]
+    for i, ref in enumerate(refs[:-1]):
+        out_ref[lax.axis_index("pair") ^ i] = ref[...]
+
+
+def added_kernel(*refs):
+    values = [ref[...] for ref in refs[:-1]]
+    while len(values) > 1:
+        values = [values[i] + values[i + 1] for i in range(0, len(values), 2)]
+    refs[-1][...] = values[0]
 
 
 def tables_kernel(modes, tables, axial_ref, rot_ref, rot_out_ref, axial_out_ref, lines_ref):
@@ -122,17 +137,21 @@
     def one_hot(hit):
         return jnp.where(hit, 1.0, 0.0).astype(BF16)
 
+    even = lax.rem(lax.axis_index("blk"), 2) == 0
+    near, far = jnp.where(even, 2, 0), jnp.where(even, 0, 2)
     forward, backward = None, []
-    for window, ref in enumerate(refs):
+    for order, (window, ref) in enumerate(zip((near, 1, far), refs)):
         values = ref[:, :, :, :, size - 128 : size].reshape(2 * group, 128).astype(F32)
         marks_column, sources_column = (values[h * group : (h + 1) * group, lane : lane + 1].astype(jnp.int32) for h in range(2))
         marks, sources = (jnp.transpose(values[h * group : (h + 1) * group])[lane : lane + 1].astype(jnp.int32) for h in range(2))
-        if window == 1:
+        if order == 1:
+            turned = (2 - lax.div(sources_column, own)) * own + lax.rem(sources_column, own)
+            sources_column = jnp.where(even, turned, sources_column)
             forward = dot_nn(one_hot(marks == wanted), one_hot(sources_column == iota((group, 3 * own), 1)))
         block = sources - (2 - window) * own
         inside = (block >= 0) & (block < own) & (marks >= own)
         hits = one_hot(jnp.where(inside, lax.div(marks, own) * own + block, -1) == wanted)
-        place = lax.rem(marks_column, own) + window * own
+        place = lax.rem(marks_column, own) + order * own
         backward.append(dot_nn(hits, one_hot(place == iota((group, 3 * own), 1))))
     return jnp.concatenate([forward, sum(backward)], axis=0).astype(BF16)
 
@@ -142,20 +161,11 @@
 
 
 def field_kernel(
-    own, modes, together, rot_ref, axial_ref, below_ref, own_ref, above_ref, basis_ref, mie_ref,
-    *rest,
+    own, modes, together, rot_ref, axial_ref, near_ref, own_ref, far_ref, *rest
 ):
-    outs, (blocks_ref, mies_ref, sums_ref, total_ref, sems) = rest[:-5], rest[-5:]
+    outs, (sums_ref, total_ref) = rest[:-2], rest[-2:]
     tables, _, size = rot_ref.shape
-    vector_blocks, vector_rows, columns = basis_ref.shape
-    copies = [pltpu.make_async_copy(mie_ref, mies_ref, sems.at[vector_blocks])]
-    for i in range(vector_blocks):
-        copies.append(pltpu.make_async_copy(basis_ref.at[i], blocks_ref.at[i, pl.ds(0, vector_rows)], sems.at[i]))
-    for copy in copies:
-        copy.start()
-    for i in range(vector_blocks):
-        blocks_ref[i, vector_rows:, :] = jnp.zeros((blocks_ref.shape[1] - vector_rows, columns), F32)
-    refs = (below_ref, own_ref, above_ref)
+    refs = (near_ref, own_ref, far_ref)
     ways, _, octets, height, _ = own_ref.shape
     quarter = own // ways
     each = height // quarter
@@ -201,8 +211,6 @@
     share = 2 * quarter * part
     for i, out_ref in enumerate(outs):
         out_ref[...] = result[i * share : (i + 1) * share].reshape(out_ref.shape)
-    for copy in copies:
-        copy.wait()
 
 
 def lane_swap(value):
@@ -243,7 +251,7 @@
     return line
 
 
-def gram_kernel(quarter, modes, basis_ref, line_ref, blocks_ref, products_ref, sems):
+def gram_kernel(quarter, modes, basis_ref, mie_ref, line_ref, blocks_ref, mies_ref, products_ref, mie_sem, sems):
     blocks, _, columns = basis_ref.shape
     rows = quarter * modes
     parts, chunk = 4, 32
@@ -259,6 +267,10 @@
                 copies.append(pltpu.make_async_copy(basis_ref.at[i, here], blocks_ref.at[i, here], sems.at[q, i, side]))
     for copy in copies:
         copy.start()
+    mie_rows = mie_ref.shape[0]
+    mie_copy = pltpu.make_async_copy(mie_ref, mies_ref.at[pl.ds(0, mie_rows)], mie_sem)
+    mie_copy.start()
+    mies_ref[mie_rows:] = jnp.zeros((mies_ref.shape[0] - mie_rows,) + mies_ref.shape[1:], F32)
     products_ref[...] = jnp.zeros_like(products_ref)
     for i in range(blocks):
         blocks_ref[i, 2 * rows :, :] = jnp.zeros((blocks_ref.shape[1] - 2 * rows, columns), F32)
@@ -268,6 +280,7 @@
         for first in range(step * q, min(step * (q + 1), rows), chunk):
             add_products(blocks_ref, products_ref, rows, first, chunk)
     line_ref[...] = products_line(products_ref)
+    mie_copy.wait()
 
 
 def image_kernel(quarter, modes, blocks_ref, mie_ref, gram_ref, *rest):
@@ -315,14 +328,14 @@
         if index % 2 and index < 2 * vectors:
             total = jnp.where(left, total, -total)
         line = jnp.where(lane == vectors * vectors + index, jnp.sum(total, axis=(0, 1), keepdims=True), line)
-    sums_ref[...] = jnp.broadcast_to(line[None], sums_ref.shape)
+    sums_ref[...] = line
 
 
 def remainder_kernel(quarter, modes, mean_scale, sums_ref, blocks_ref, image_ref, dots_ref, out_ref):
     vectors = 2 * blocks_ref.shape[0]
     full, columns = image_ref.shape
     rows = quarter * modes
-    total = jnp.sum(sums_ref[...], axis=0)
+    total = sums_ref[...]
     lane = iota(total.shape, 1)
 
     def lane_at(index):
@@ -372,15 +385,40 @@
         out_ref[first // height : (first + count) // height] = result.reshape(chunk // height, height, columns)[: count // height]
 
 
-def exchanged(value):
-    return lax.all_to_all(value, "pair", split_axis=0, concat_axis=0, tiled=True)
+def exchanged(pieces, axis):
+    count = lax.axis_size(axis)
+    received = [pieces[0]]
+    for i in range(1, len(pieces)):
+        received.append(lax.ppermute(pieces[i], axis, [(p, p ^ i) for p in range(count)]))
+    return received
+
+
+def summed(value, axis):
+    count, done = lax.axis_size(axis), 1
+    while done < count:
+        ways = min(4, count // done)
+        values = [value]
+        for i in range(1, ways):
+            values.append(lax.ppermute(value, axis, [(p, p ^ (i * done)) for p in range(count)]))
+        value = pl.pallas_call(
+            added_kernel,
+            in_specs=[whole()] * ways,
+            out_specs=whole(),
+            out_shape=jax.ShapeDtypeStruct(value.shape, F32),
+            compiler_params=params(2),
+            name="added",
+        )(*values)
+        done *= ways
+    return value
 
 
 def neighbours(value):
     count = lax.axis_size("blk")
-    up = [(i, i + 1) for i in range(count - 1)]
-    down = [(j, i) for i, j in up]
-    return lax.ppermute(value, "blk", up), lax.ppermute(value, "blk", down)
+    results = []
+    for first in range(2):
+        pairs = [(i, i + 1) for i in range(first, count - 1, 2)]
+        results.append(lax.ppermute(value, "blk", pairs + [(j, i) for i, j in pairs]))
+    return results
 
 
 def shards(basis, mie_coeffs, rot_table, axial_table, pair_table, pair_count):
@@ -396,6 +434,7 @@
     rows = quarter * modes
     full = rounded_up(rows, 8)
     pairs_of_vectors = vectors // 2
+    height = 4
 
     basis_rows = in_hbm(basis.transpose(0, 2, 1, 3).reshape(pairs_of_vectors, 2 * rows, columns))
     mie_rows = in_hbm(mie_coeffs.transpose(1, 0, 2).reshape(rows // 4, 4, columns))
@@ -404,41 +443,53 @@
     pair_rows = in_hbm(pair_table.transpose(2, 0, 1))
 
     octets = part * quarter // 16
+    piece = jax.ShapeDtypeStruct((2, octets, 16, size), BF16)
     pieces = pl.pallas_call(
         functools.partial(pack_kernel, quarter, modes, ways, own),
         in_specs=[hbm(), pl.BlockSpec(memory_space=pltpu.SMEM), hbm()],
-        out_specs=whole(),
-        out_shape=jax.ShapeDtypeStruct((ways, 2, octets, 16, size), BF16),
+        out_specs=[whole()] * ways,
+        out_shape=[piece] * ways,
         scratch_shapes=[
             pltpu.VMEM(pair_rows.shape, jnp.int32),
             pltpu.VMEM((full, columns), F32),
             pltpu.VMEM((size, columns), F32),
             pltpu.VMEM((2 * slots, slots), F32),
+            pltpu.VMEM((quarter, columns, size), F32),
             pltpu.SemaphoreType.DMA((2,)),
         ],
         compiler_params=params(16),
         name="pack",
     )(pair_rows, pair_count, basis_rows)
     tall = rounded_up(rows + full, 8)
-    pieces, basis_later = lax.optimization_barrier((pieces, basis_rows))
-    own_pieces = exchanged(pieces)
-    line = pl.pallas_call(
+    *pieces, basis_rows, mie_rows = lax.optimization_barrier((*pieces, basis_rows, mie_rows))
+    received = exchanged(pieces, "pair")
+    line, blocks, mies = pl.pallas_call(
         functools.partial(gram_kernel, quarter, modes),
-        grid=(1,),
-        in_specs=[hbm()],
-        out_specs=pl.BlockSpec((1, 128), lambda i: (0, 0)),
-        out_shape=pltpu.HBM((1, 128), F32),
+        in_specs=[hbm()] * 2,
+        out_specs=[whole()] * 3,
+        out_shape=[
+            jax.ShapeDtypeStruct((1, 128), F32),
+            jax.ShapeDtypeStruct((pairs_of_vectors, tall, columns), F32),
+            jax.ShapeDtypeStruct((full // height, height, columns), F32),
+        ],
         scratch_shapes=[
-            pltpu.VMEM((pairs_of_vectors, tall, columns), F32),
             pltpu.VMEM((vectors, vectors, 8, columns), F32),
+            pltpu.SemaphoreType.DMA,
             pltpu.SemaphoreType.DMA((4, pairs_of_vectors, 2)),
         ],
-        compiler_params=params(16),
+        compiler_params=params(8),
         name="gram",
-    )(basis_later)
-    own_pieces, line, *inputs = lax.optimization_barrier((own_pieces, line, basis_rows, mie_rows, rot_rows, axial_rows))
-    basis_rows, mie_rows, rot_rows, axial_rows = inputs
-    below, above = neighbours(own_pieces)
+    )(basis_rows, mie_rows)
+    *received, line, rot_rows, axial_rows = lax.optimization_barrier((*received, line, rot_rows, axial_rows))
+    own_pieces = pl.pallas_call(
+        join_kernel,
+        in_specs=[whole()] * ways,
+        out_specs=whole(),
+        out_shape=jax.ShapeDtypeStruct((ways, *piece.shape), BF16),
+        compiler_params=params(4),
+        name="join",
+    )(*received)
+    near, far = neighbours(own_pieces)
 
     rotations, axials = pl.pallas_call(
         functools.partial(tables_kernel, modes, tables),
@@ -461,42 +512,31 @@
         name="tables",
     )(axial_rows, rot_rows)
 
-    below, above, rotations, axials = lax.optimization_barrier((below, above, rotations, axials))
+    near, far, rotations, axials = lax.optimization_barrier((near, far, rotations, axials))
 
     together = 2 if tables % 2 == 0 else 1
-    *field, blocks, mies = pl.pallas_call(
+    field = pl.pallas_call(
         functools.partial(field_kernel, own, modes, together),
-        in_specs=[whole()] * 5 + [hbm()] * 2,
-        out_specs=[whole()] * (ways + 2),
-        out_shape=[jax.ShapeDtypeStruct((2, quarter, part, size), BF16)] * ways
-        + [
-            jax.ShapeDtypeStruct((pairs_of_vectors, tall, columns), F32),
-            jax.ShapeDtypeStruct(mie_rows.shape, F32),
-        ],
-        scratch_shapes=[
-            pltpu.VMEM((tables, 4 * group, size), BF16),
-            pltpu.VMEM((2 * group, size), F32),
-            pltpu.SemaphoreType.DMA((pairs_of_vectors + 1,)),
-        ],
+        in_specs=[whole()] * 5,
+        out_specs=[whole()] * ways,
+        out_shape=[jax.ShapeDtypeStruct((2, quarter, part, size), BF16)] * ways,
+        scratch_shapes=[pltpu.VMEM((tables, 4 * group, size), BF16), pltpu.VMEM((2 * group, size), F32)],
         compiler_params=params(20),
         name="field",
-    )(rotations, axials, below, own_pieces, above, basis_rows, mie_rows)
-    field_pieces = [field[0]]
-    for i in range(1, ways):
-        field_pieces.append(lax.ppermute(field[i], "pair", [(p, p ^ i) for p in range(ways)]))
+    )(rotations, axials, near, own_pieces, far)
+    field_pieces = exchanged(field, "pair")
 
     image, sums = pl.pallas_call(
         functools.partial(image_kernel, quarter, modes),
         in_specs=[whole()] * (ways + 3),
         out_specs=[whole()] * 2,
-        out_shape=[jax.ShapeDtypeStruct((full, columns), F32), jax.ShapeDtypeStruct((ways * blk_ways, 1, 128), F32)],
+        out_shape=[jax.ShapeDtypeStruct((full, columns), F32), jax.ShapeDtypeStruct((1, 128), F32)],
         scratch_shapes=[pltpu.VMEM((full, columns), F32), pltpu.VMEM((quarter, columns, size), BF16)],
         compiler_params=params(8),
         name="image",
     )(blocks, mies, line, *field_pieces)
-    sums = lax.all_to_all(sums, ("blk", "pair"), split_axis=0, concat_axis=0, tiled=True)
-
-    height = 4
+    sums = summed(summed(sums, "pair"), "blk")
+
     mean_scale = 1.0 / (own * blk_ways * modes * columns)
     dots, next_rows = pl.pallas_call(
         functools.partial(remainder_kernel, quarter, modes, mean_scale),

time: 61.8 us -> 62.7 us (1.015)
  blocking collectives: 12.5 us -> 0 us
  waiting for transfers between devices: 5.4 us -> 13.4 us
  starting transfers between devices: 12.1 us -> 19.1 us
  Pallas kernels: 30 us -> 28.6 us
    all_to_all x1 -> x0, blocking collectives: 12.5 us -> none  [shards(): lax.all_to_all(sums, ('blk', 'pair'), split_axis=0, concat_axis=0, tiled=...]
    ppermute x5 -> x15, starting transfers between devices: 7.91 us -> 19.1 us  [the longest x7 8.72 us: summed(): lax.ppermute(value, axis, [(p, p ^ i * done) for p in range(count)])]
    ppermute x5 -> x15, waiting for transfers between devices: 4.22 us -> 13.4 us  [the longest x7 8.11 us: summed(): lax.ppermute(value, axis, [(p, p ^ i * done) for p in range(count)])]
    all_to_all x1 -> x0, starting transfers between devices: 4.22 us -> none  [exchanged(): lax.all_to_all(value, 'pair', split_axis=0, concat_axis=0, tiled=True)]
    all_to_all x1 -> x0, waiting for transfers between devices: 1.18 us -> none  [exchanged(): lax.all_to_all(value, 'pair', split_axis=0, concat_axis=0, tiled=True)]
    pallas_call x1 -> x5, Pallas kernels: 4.85 us -> 4.19 us  [the longest x1 4.15 us: shards(): pl.pallas_call(functools.partial(gram_kernel, quarter, modes), in_specs=[...]
    pallas_call x1, Pallas kernels: 1.95 us -> 1.31 us  [shards(): pl.pallas_call(functools.partial(pack_kernel, quarter, modes, ways, own),...]
  transfers between devices with their start and end apart: 6 -> 15, of which waited for: 4 -> 9; matrix products, arithmetic and copies ran while one was open for 0% -> 0% of each run, Pallas kernels for 23% -> 22%
where the time goes in v11:
time: 62.7 us; the launch traced here: 62.4 us
  Pallas kernels  28.6 us (46%)
  starting transfers between devices  19.1 us (30%)
  waiting for transfers between devices  13.4 us (21%)
  between operations  1.38 us (2%)
    pallas_call x1, Pallas kernels, shards(): pl.pallas_call(functools.partial(field_kernel, own, modes, together), in_...  10.6 us
    pallas_call x1, Pallas kernels, shards(): pl.pallas_call(functools.partial(tables_kernel, modes, tables), grid=(tab...  9.44 us
    ppermute x7, starting transfers between devices, summed(): lax.ppermute(value, axis, [(p, p ^ i * done) for p in range(count)])  8.72 us
    ppermute x7, waiting for transfers between devices, summed(): lax.ppermute(value, axis, [(p, p ^ i * done) for p in range(count)])  8.11 us
    ppermute x2, starting transfers between devices, neighbours(): lax.ppermute(value, 'blk', pairs + [(j, i) for i, j in pairs])  5.25 us
    ppermute x6, starting transfers between devices, exchanged(): lax.ppermute(pieces[i], axis, [(p, p ^ i) for p in range(count)])  5.09 us
    pallas_call x1, Pallas kernels, shards(): pl.pallas_call(functools.partial(gram_kernel, quarter, modes), in_specs=[...  4.15 us
    ppermute x6, waiting for transfers between devices, exchanged(): lax.ppermute(pieces[i], axis, [(p, p ^ i) for p in range(count)])  3.75 us
  transfers between devices with their start and end apart: 15, of which 9 were waited for; matrix products, arithmetic and copies ran while one was open for 0% of the time, Pallas kernels for 22%

profile of v11, /device:TPU:0, one launch (start us, length us, event | category | flops | bytes accessed | tf_op | source)
XLA Modules:
  0.0 62.4 jit_solution(15738302689597638003)
XLA Ops:
  1.3 1.3 %pack.1 = (bf16[2,2,16,512]{3,2,1,0:T(8,128)(2,1)S(1)}, bf16[2,2,16,512]{3,2,1,0:T(8,128)(2,1)S(1)}, bf16[2,2,16,512]{3,2,1,0:T(8,128)(2,1)S(1)}, bf16[2,2,16,512]{3,2,1,0:T(8,128)(2,1)S(1)}) custom-call(s32[3,1,128]{2,1,0:T(1,128)} %bitcast.19, s32[1]{0:T(128)S(6)} %copy.8.count_ref, f32[4,2040,128]{2,1,0:T(8,128)} %bitcast.14), custom_call_target="tpu_custom_call" | custom-call | tf_op jit(solution)/shard_map/pack/pallas_call | solution.py:447
  2.6 0.5 collective-permute-start
  3.1 2.6 %collective-permute-start.1 = (bf16[2,2,16,512]{3,2,1,0:T(8,128)(2,1)S(1)}, bf16[2,2,16,512]{3,2,1,0:T(8,128)(2,1)S(1)}, u32[]{:S(2)}, u32[]{:S(2)}) collective-permute-start(bf16[2,2,16,512]{3,2,1,0:T(8,128)(2,1)S(1)} %get-tuple-element.46), channel_id=1, source_target_pairs={{0,2},{1,3},{2,0},{3,1},{4,6},{5,7},{6,4},{7,5},{8,10},{9,11},{10,... | collective-permute-start | bytes 196616 | tf_op jit(solution)/shard_map/ppermute | solution.py:392
  5.7 0.1 collective-permute-start.2
  5.7 4.2 %gram.1 = (f32[1,128]{1,0:T(1,128)S(1)}, f32[4,2048,128]{2,1,0:T(8,128)S(1)}, f32[256,4,128]{2,1,0:T(4,128)S(1)}) custom-call(f32[4,2040,128]{2,1,0:T(8,128)} %bitcast.15, f32[255,4,128]{2,1,0:T(4,128)} %bitcast.18), custom_call_target="tpu_custom_call" | custom-call | tf_op jit(solution)/shard_map/gram/pallas_call | solution.py:466
  9.9 0.0 collective-permute-done.refs_1_
  9.9 0.0 collective-permute-done.1.refs_2_
  9.9 0.0 collective-permute-done.2.refs_3_
  10.0 0.7 %collective-permute-start.4 = (bf16[4,2,2,16,512]{4,3,2,1,0:T(8,128)(2,1)S(1)}, bf16[4,2,2,16,512]{4,3,2,1,0:T(8,128)(2,1)S(1)}, u32[]{:S(2)}, u32[]{:S(2)}) collective-permute-start(bf16[4,2,2,16,512]{4,3,2,1,0:T(8,128)(2,1)S(1)} %join.1.own_ref), channel_id=1, source_target_pairs={{4,8},{12,16},{20,24},{8,4},{16,12},{24,20},{5,9},{13,17},{21,25},... | collective-permute-start | bytes 786440 | tf_op jit(solution)/shard_map/ppermute | solution.py:420
  10.7 4.6 %collective-permute-start.3 = (bf16[4,2,2,16,512]{4,3,2,1,0:T(8,128)(2,1)S(1)}, bf16[4,2,2,16,512]{4,3,2,1,0:T(8,128)(2,1)S(1)}, u32[]{:S(2)}, u32[]{:S(2)}) collective-permute-start(bf16[4,2,2,16,512]{4,3,2,1,0:T(8,128)(2,1)S(1)} %join.1.own_ref), channel_id=1, source_target_pairs={{0,4},{8,12},{16,20},{24,28},{4,0},{12,8},{20,16},{28,24},{1,5},{9... | collective-permute-start | bytes 786440 | tf_op jit(solution)/shard_map/ppermute | solution.py:420
  15.2 9.4 %tables.1 = (bf16[8,512,512]{2,1,0:T(8,128)(2,1)S(1)}, bf16[8,1024,512]{2,1,0:T(8,128)(2,1)S(1)}) custom-call(bf16[8,510,2,510]{3,2,1,0:T(2,128)(2,1)} %bitcast.16, bf16[4080,510]{1,0:T(8,128)(2,1)} %bitcast.17), custom_call_target="tpu_custom_call" | custom-call | flops 2147483648 | bytes 25165824 | tf_op jit(solution)/shard_map/tables/pallas_call | solution.py:494
  24.7 0.0 collective-permute-done.4.far_ref
  24.7 1.5 %collective-permute-done.3.near_ref = bf16[4,2,2,16,512]{4,3,2,1,0:T(8,128)(2,1)S(1)} collective-permute-done((bf16[4,2,2,16,512]{4,3,2,1,0:T(8,128)(2,1)S(1)}, bf16[4,2,2,16,512]{4,3,2,1,0:T(8,128)(2,1)S(1)}, u32[]{:S(2)}, u32[]{:S(2)}) %collective-permute-start.3) | collective-permute-done | bytes 262176 | tf_op jit(solution)/shard_map/ppermute | solution.py:420
  26.2 10.6 %field.1 = (bf16[2,2,16,512]{3,2,1,0:T(8,128)(2,1)S(1)}, bf16[2,2,16,512]{3,2,1,0:T(8,128)(2,1)S(1)}, bf16[2,2,16,512]{3,2,1,0:T(8,128)(2,1)S(1)}, bf16[2,2,16,512]{3,2,1,0:T(8,128)(2,1)S(1)}) custom-call(bf16[8,512,512]{2,1,0:T(8,128)(2,1)S(1)} %get-tuple-element.58.rot_ref, bf16[8,1024,512]{2,1,0:T(8,128)(2,1)S(1)} %get-tuple-element.59.axial_ref, ...), custom_call_target="tpu_custom_call" | custom-call | tf_op jit(solution)/shard_map/field/pallas_call | solution.py:518
  36.9 0.1 collective-permute-start.5
  36.9 1.5 %collective-permute-start.6 = (bf16[2,2,16,512]{3,2,1,0:T(8,128)(2,1)S(1)}, bf16[2,2,16,512]{3,2,1,0:T(8,128)(2,1)S(1)}, u32[]{:S(2)}, u32[]{:S(2)}) collective-permute-start(bf16[2,2,16,512]{3,2,1,0:T(8,128)(2,1)S(1)} %get-tuple-element.64), channel_id=1, source_target_pairs={{0,2},{1,3},{2,0},{3,1},{4,6},{5,7},{6,4},{7,5},{8,10},{9,11},{10,... | collective-permute-start | bytes 196616 | tf_op jit(solution)/shard_map/ppermute | solution.py:392
  38.5 0.3 collective-permute-start.7
  38.8 0.0 collective-permute-done.5.rest_1_
  38.8 2.6 %collective-permute-done.6.rest_2_ = bf16[2,2,16,512]{3,2,1,0:T(8,128)(2,1)S(1)} collective-permute-done((bf16[2,2,16,512]{3,2,1,0:T(8,128)(2,1)S(1)}, bf16[2,2,16,512]{3,2,1,0:T(8,128)(2,1)S(1)}, u32[]{:S(2)}, u32[]{:S(2)}) %collective-permute-start.6) | collective-permute-done | bytes 65568 | tf_op jit(solution)/shard_map/ppermute | solution.py:392
  41.4 1.1 %collective-permute-done.7.rest_3_ = bf16[2,2,16,512]{3,2,1,0:T(8,128)(2,1)S(1)} collective-permute-done((bf16[2,2,16,512]{3,2,1,0:T(8,128)(2,1)S(1)}, bf16[2,2,16,512]{3,2,1,0:T(8,128)(2,1)S(1)}, u32[]{:S(2)}, u32[]{:S(2)}) %collective-permute-start.7) | collective-permute-done | bytes 65568 | tf_op jit(solution)/shard_map/ppermute | solution.py:392
  42.5 1.4 %image.1 = (f32[1024,128]{1,0:T(8,128)S(1)}, f32[1,128]{1,0:T(1,128)S(1)}) custom-call(f32[4,2048,128]{2,1,0:T(8,128)S(1)} %get-tuple-element.42.blocks_ref, f32[256,4,128]{2,1,0:T(4,128)S(1)} %get-tuple-element.43.mie_ref, f32[1,128]{1,0:T(1,128)S(1)} %get-tuple-element.49.gram_ref, bf16[2,2,16,512]{3,2,1,0:T(8,128)(2,1)S(1)} %get-tuple-element.62.rest_0_, ...), custom_call_target="tpu_custom_call" | custom-call | tf_op jit(solution)/shard_map/image/pallas_call | solution.py:529
  44.0 1.3 %collective-permute-start.10 = (f32[1,128]{1,0:T(1,128)S(1)}, f32[1,128]{1,0:T(1,128)S(1)}, u32[]{:S(2)}, u32[]{:S(2)}) collective-permute-start(f32[1,128]{1,0:T(1,128)S(1)} %get-tuple-element.66.refs_0_), channel_id=1, source_target_pairs={{0,3},{1,2},{2,1},{3,0},{4,7},{5,6},{6,5},{7,4},{8,11},{9,10},{10,... | collective-permute-start | bytes 1544 | tf_op jit(solution)/shard_map/ppermute | solution.py:402
  45.3 0.6 collective-permute-start.9
  45.8 0.1 collective-permute-start.8
  45.9 1.1 %collective-permute-done.10.refs_3_ = f32[1,128]{1,0:T(1,128)S(1)} collective-permute-done((f32[1,128]{1,0:T(1,128)S(1)}, f32[1,128]{1,0:T(1,128)S(1)}, u32[]{:S(2)}, u32[]{:S(2)}) %collective-permute-start.10) | collective-permute-done | bytes 544 | tf_op jit(solution)/shard_map/ppermute | solution.py:402
  47.0 1.8 %collective-permute-done.9.refs_2_ = f32[1,128]{1,0:T(1,128)S(1)} collective-permute-done((f32[1,128]{1,0:T(1,128)S(1)}, f32[1,128]{1,0:T(1,128)S(1)}, u32[]{:S(2)}, u32[]{:S(2)}) %collective-permute-start.9) | collective-permute-done | bytes 544 | tf_op jit(solution)/shard_map/ppermute | solution.py:402
  48.8 0.0 collective-permute-done.8.refs_1_
  48.8 3.6 %collective-permute-start.13 = (f32[1,128]{1,0:T(1,128)S(1)}, f32[1,128]{1,0:T(1,128)S(1)}, u32[]{:S(2)}, u32[]{:S(2)}) collective-permute-start(f32[1,128]{1,0:T(1,128)S(1)} %added.3.refs_0_), channel_id=1, source_target_pairs={{0,12},{4,8},{8,4},{12,0},{16,28},{20,24},{24,20},{28,16},{1,13},{... | collective-permute-start | bytes 1544 | tf_op jit(solution)/shard_map/ppermute | solution.py:402
  52.4 0.4 collective-permute-start.12
  52.8 0.2 collective-permute-start.11
  53.0 0.9 %collective-permute-done.13.refs_3_ = f32[1,128]{1,0:T(1,128)S(1)} collective-permute-done((f32[1,128]{1,0:T(1,128)S(1)}, f32[1,128]{1,0:T(1,128)S(1)}, u32[]{:S(2)}, u32[]{:S(2)}) %collective-permute-start.13) | collective-permute-done | bytes 544 | tf_op jit(solution)/shard_map/ppermute | solution.py:402
  53.9 2.0 %collective-permute-done.12.refs_2_ = f32[1,128]{1,0:T(1,128)S(1)} collective-permute-done((f32[1,128]{1,0:T(1,128)S(1)}, f32[1,128]{1,0:T(1,128)S(1)}, u32[]{:S(2)}, u32[]{:S(2)}) %collective-permute-start.12) | collective-permute-done | bytes 544 | tf_op jit(solution)/shard_map/ppermute | solution.py:402
  55.9 0.4 collective-permute-done.11.refs_1_
  56.4 2.6 %collective-permute-start.14 = (f32[1,128]{1,0:T(1,128)S(1)}, f32[1,128]{1,0:T(1,128)S(1)}, u32[]{:S(2)}, u32[]{:S(2)}) collective-permute-start(f32[1,128]{1,0:T(1,128)S(1)} %added.4.refs_0_), channel_id=1, source_target_pairs={{0,16},{4,20},{8,24},{12,28},{16,0},{20,4},{24,8},{28,12},{1,17},{... | collective-permute-start | bytes 1544 | tf_op jit(solution)/shard_map/ppermute | solution.py:402
  59.0 1.9 %collective-permute-done.14.refs_1_ = f32[1,128]{1,0:T(1,128)S(1)} collective-permute-done((f32[1,128]{1,0:T(1,128)S(1)}, f32[1,128]{1,0:T(1,128)S(1)}, u32[]{:S(2)}, u32[]{:S(2)}) %collective-permute-start.14) | collective-permute-done | bytes 544 | tf_op jit(solution)/shard_map/ppermute | solution.py:402
  60.8 1.6 %remainder.1 = (f32[2,8]{1,0:T(2,128)}, f32[255,4,128]{2,1,0:T(4,128)}) custom-call(f32[1,128]{1,0:T(1,128)S(1)} %added.5.sums_ref, f32[4,2048,128]{2,1,0:T(8,128)S(1)} %get-tuple-element.42.blocks_ref, f32[1024,128]{1,0:T(8,128)S(1)} %get-tuple-element.67.image_ref), custom_call_target="tpu_custom_call" | custom-call | tf_op jit(solution)/shard_map/remainder/pallas_call | solution.py:541
  (4 shorter events, 0.0 us)
Async XLA Ops:
  2.6 7.3 %collective-permute-start = (bf16[2,2,16,512]{3,2,1,0:T(8,128)(2,1)S(1)}, bf16[2,2,16,512]{3,2,1,0:T(8,128)(2,1)S(1)}, u32[]{:S(2)}, u32[]{:S(2)}) collective-permute-start(bf16[2,2,16,512]{3,2,1,0:T(8,128)(2,1)S(1)} %get-tuple-element.45), channel_id=1, source_target_pairs={{0,1},{1,0},{2,3},{3,2},{4,5},{5,4},{6,7},{7,6},{8,9},{9,8},{10,11... | collective-permute-start | bytes 196616 | tf_op jit(solution)/shard_map/ppermute | solution.py:392
  3.1 6.8 %collective-permute-start.1 = (bf16[2,2,16,512]{3,2,1,0:T(8,128)(2,1)S(1)}, bf16[2,2,16,512]{3,2,1,0:T(8,128)(2,1)S(1)}, u32[]{:S(2)}, u32[]{:S(2)}) collective-permute-start(bf16[2,2,16,512]{3,2,1,0:T(8,128)(2,1)S(1)} %get-tuple-element.46), channel_id=1, source_target_pairs={{0,2},{1,3},{2,0},{3,1},{4,6},{5,7},{6,4},{7,5},{8,10},{9,11},{10,... | collective-permute-start | bytes 196616 | tf_op jit(solution)/shard_map/ppermute | solution.py:392
  5.7 4.3 %collective-permute-start.2 = (bf16[2,2,16,512]{3,2,1,0:T(8,128)(2,1)S(1)}, bf16[2,2,16,512]{3,2,1,0:T(8,128)(2,1)S(1)}, u32[]{:S(2)}, u32[]{:S(2)}) collective-permute-start(bf16[2,2,16,512]{3,2,1,0:T(8,128)(2,1)S(1)} %get-tuple-element.47), channel_id=1, source_target_pairs={{0,3},{1,2},{2,1},{3,0},{4,7},{5,6},{6,5},{7,4},{8,11},{9,10},{10,... | collective-permute-start | bytes 196616 | tf_op jit(solution)/shard_map/ppermute | solution.py:392
  10.0 14.7 %collective-permute-start.4 = (bf16[4,2,2,16,512]{4,3,2,1,0:T(8,128)(2,1)S(1)}, bf16[4,2,2,16,512]{4,3,2,1,0:T(8,128)(2,1)S(1)}, u32[]{:S(2)}, u32[]{:S(2)}) collective-permute-start(bf16[4,2,2,16,512]{4,3,2,1,0:T(8,128)(2,1)S(1)} %join.1.own_ref), channel_id=1, source_target_pairs={{4,8},{12,16},{20,24},{8,4},{16,12},{24,20},{5,9},{13,17},{21,25},... | collective-permute-start | bytes 786440 | tf_op jit(solution)/shard_map/ppermute | solution.py:420
  10.7 15.6 %collective-permute-start.3 = (bf16[4,2,2,16,512]{4,3,2,1,0:T(8,128)(2,1)S(1)}, bf16[4,2,2,16,512]{4,3,2,1,0:T(8,128)(2,1)S(1)}, u32[]{:S(2)}, u32[]{:S(2)}) collective-permute-start(bf16[4,2,2,16,512]{4,3,2,1,0:T(8,128)(2,1)S(1)} %join.1.own_ref), channel_id=1, source_target_pairs={{0,4},{8,12},{16,20},{24,28},{4,0},{12,8},{20,16},{28,24},{1,5},{9... | collective-permute-start | bytes 786440 | tf_op jit(solution)/shard_map/ppermute | solution.py:420
  36.9 1.9 %collective-permute-start.5 = (bf16[2,2,16,512]{3,2,1,0:T(8,128)(2,1)S(1)}, bf16[2,2,16,512]{3,2,1,0:T(8,128)(2,1)S(1)}, u32[]{:S(2)}, u32[]{:S(2)}) collective-permute-start(bf16[2,2,16,512]{3,2,1,0:T(8,128)(2,1)S(1)} %get-tuple-element.63), channel_id=1, source_target_pairs={{0,1},{1,0},{2,3},{3,2},{4,5},{5,4},{6,7},{7,6},{8,9},{9,8},{10,11... | collective-permute-start | bytes 196616 | tf_op jit(solution)/shard_map/ppermute | solution.py:392
  36.9 4.5 %collective-permute-start.6 = (bf16[2,2,16,512]{3,2,1,0:T(8,128)(2,1)S(1)}, bf16[2,2,16,512]{3,2,1,0:T(8,128)(2,1)S(1)}, u32[]{:S(2)}, u32[]{:S(2)}) collective-permute-start(bf16[2,2,16,512]{3,2,1,0:T(8,128)(2,1)S(1)} %get-tuple-element.64), channel_id=1, source_target_pairs={{0,2},{1,3},{2,0},{3,1},{4,6},{5,7},{6,4},{7,5},{8,10},{9,11},{10,... | collective-permute-start | bytes 196616 | tf_op jit(solution)/shard_map/ppermute | solution.py:392
  38.5 4.0 %collective-permute-start.7 = (bf16[2,2,16,512]{3,2,1,0:T(8,128)(2,1)S(1)}, bf16[2,2,16,512]{3,2,1,0:T(8,128)(2,1)S(1)}, u32[]{:S(2)}, u32[]{:S(2)}) collective-permute-start(bf16[2,2,16,512]{3,2,1,0:T(8,128)(2,1)S(1)} %get-tuple-element.65), channel_id=1, source_target_pairs={{0,3},{1,2},{2,1},{3,0},{4,7},{5,6},{6,5},{7,4},{8,11},{9,10},{10,... | collective-permute-start | bytes 196616 | tf_op jit(solution)/shard_map/ppermute | solution.py:392
  44.0 3.0 %collective-permute-start.10 = (f32[1,128]{1,0:T(1,128)S(1)}, f32[1,128]{1,0:T(1,128)S(1)}, u32[]{:S(2)}, u32[]{:S(2)}) collective-permute-start(f32[1,128]{1,0:T(1,128)S(1)} %get-tuple-element.66.refs_0_), channel_id=1, source_target_pairs={{0,3},{1,2},{2,1},{3,0},{4,7},{5,6},{6,5},{7,4},{8,11},{9,10},{10,... | collective-permute-start | bytes 1544 | tf_op jit(solution)/shard_map/ppermute | solution.py:402
  45.3 3.5 %collective-permute-start.9 = (f32[1,128]{1,0:T(1,128)S(1)}, f32[1,128]{1,0:T(1,128)S(1)}, u32[]{:S(2)}, u32[]{:S(2)}) collective-permute-start(f32[1,128]{1,0:T(1,128)S(1)} %get-tuple-element.66.refs_0_), channel_id=1, source_target_pairs={{0,2},{1,3},{2,0},{3,1},{4,6},{5,7},{6,4},{7,5},{8,10},{9,11},{10,... | collective-permute-start | bytes 1544 | tf_op jit(solution)/shard_map/ppermute | solution.py:402
  45.8 3.0 %collective-permute-start.8 = (f32[1,128]{1,0:T(1,128)S(1)}, f32[1,128]{1,0:T(1,128)S(1)}, u32[]{:S(2)}, u32[]{:S(2)}) collective-permute-start(f32[1,128]{1,0:T(1,128)S(1)} %get-tuple-element.66.refs_0_), channel_id=1, source_target_pairs={{0,1},{1,0},{2,3},{3,2},{4,5},{5,4},{6,7},{7,6},{8,9},{9,8},{10,11... | collective-permute-start | bytes 1544 | tf_op jit(solution)/shard_map/ppermute | solution.py:402
  48.8 5.1 %collective-permute-start.13 = (f32[1,128]{1,0:T(1,128)S(1)}, f32[1,128]{1,0:T(1,128)S(1)}, u32[]{:S(2)}, u32[]{:S(2)}) collective-permute-start(f32[1,128]{1,0:T(1,128)S(1)} %added.3.refs_0_), channel_id=1, source_target_pairs={{0,12},{4,8},{8,4},{12,0},{16,28},{20,24},{24,20},{28,16},{1,13},{... | collective-permute-start | bytes 1544 | tf_op jit(solution)/shard_map/ppermute | solution.py:402
  52.4 3.5 %collective-permute-start.12 = (f32[1,128]{1,0:T(1,128)S(1)}, f32[1,128]{1,0:T(1,128)S(1)}, u32[]{:S(2)}, u32[]{:S(2)}) collective-permute-start(f32[1,128]{1,0:T(1,128)S(1)} %added.3.refs_0_), channel_id=1, source_target_pairs={{0,8},{4,12},{8,0},{12,4},{16,24},{20,28},{24,16},{28,20},{1,9},{5... | collective-permute-start | bytes 1544 | tf_op jit(solution)/shard_map/ppermute | solution.py:402
  52.8 3.5 %collective-permute-start.11 = (f32[1,128]{1,0:T(1,128)S(1)}, f32[1,128]{1,0:T(1,128)S(1)}, u32[]{:S(2)}, u32[]{:S(2)}) collective-permute-start(f32[1,128]{1,0:T(1,128)S(1)} %added.3.refs_0_), channel_id=1, source_target_pairs={{0,4},{4,0},{8,12},{12,8},{16,20},{20,16},{24,28},{28,24},{1,5},{5... | collective-permute-start | bytes 1544 | tf_op jit(solution)/shard_map/ppermute | solution.py:402
  56.4 4.4 %collective-permute-start.14 = (f32[1,128]{1,0:T(1,128)S(1)}, f32[1,128]{1,0:T(1,128)S(1)}, u32[]{:S(2)}, u32[]{:S(2)}) collective-permute-start(f32[1,128]{1,0:T(1,128)S(1)} %added.4.refs_0_), channel_id=1, source_target_pairs={{0,16},{4,20},{8,24},{12,28},{16,0},{20,4},{24,8},{28,12},{1,17},{... | collective-permute-start | bytes 1544 | tf_op jit(solution)/shard_map/ppermute | solution.py:402

commit v12 on v11

--- a/solution.py
+++ b/solution.py
@@ -88,40 +88,50 @@
         out_ref[lax.axis_index("pair") ^ i] = ref[...]
 
 
-def added_kernel(*refs):
-    values = [ref[...] for ref in refs[:-1]]
-    while len(values) > 1:
-        values = [values[i] + values[i + 1] for i in range(0, len(values), 2)]
-    refs[-1][...] = values[0]
-
-
-def tables_kernel(modes, tables, axial_ref, rot_ref, rot_out_ref, axial_out_ref, lines_ref):
-    step = pl.program_id(0)
-    size = rot_out_ref.shape[2]
+def tables_kernel(axial_ref, rot_ref, rot_out_ref, axial_out_ref, axials_ref, rots_ref, sems):
+    tables, size, _ = rot_out_ref.shape
+    modes = axial_ref.shape[1]
+    listed = rot_ref.shape[0]
+
+    def fetch(g):
+        return pltpu.make_async_copy(axial_ref.at[g], axials_ref.at[g], sems.at[g])
+
+    for g in range(tables):
+        fetch(g).start()
+    rot_copy = pltpu.make_async_copy(rot_ref, rots_ref.at[pl.ds(0, listed)], sems.at[tables])
+    rot_copy.start()
     chunk = 256
-
-    @pl.when(step == 0)
-    def _():
-        lines_ref[...] = jnp.zeros_like(lines_ref)
-
     out_row, in_row = iota((chunk, chunk), 0), iota((chunk, chunk), 1)
     each = chunk // 2
     halves = (in_row == 2 * lax.rem(out_row, each) + lax.div(out_row, each)).astype(F32).astype(BF16)
-    lines_ref[0 : 2 * modes, 0:modes] = axial_ref[0].reshape(2 * modes, modes)
-    for q in range(2 * size // chunk):
-        sorted_rows = dot_nn(halves, lines_ref[q * chunk : (q + 1) * chunk, :]).astype(BF16)
-        for c in range(2):
-            axial_out_ref[0, c * size + q * each : c * size + (q + 1) * each, :] = sorted_rows[c * each : (c + 1) * each]
-    each = chunk // tables
-    entries = (in_row == tables * lax.rem(out_row, each) + lax.div(out_row, each)).astype(F32).astype(BF16)
-    block = rot_ref.shape[0]
-    left = tables * modes - step * block
-    rows = jnp.where(iota((block, modes), 0) < left, rot_ref[...], jnp.zeros((), BF16))
-    rot_out_ref[:, :, size - 128 : size] = jnp.zeros((tables, block // tables, 128), BF16)
-    for q in range(block // chunk):
-        sorted_rows = dot_nn(entries, rows[q * chunk : (q + 1) * chunk]).astype(BF16)
+    share = chunk // tables
+    entries = (in_row == tables * lax.rem(out_row, share) + lax.div(out_row, share)).astype(F32).astype(BF16)
+    for ref in (rot_out_ref, axial_out_ref):
+        ref[:, :, size - 128 : size] = jnp.zeros((tables, ref.shape[1], 128), BF16)
+    rots_ref[listed:, :] = jnp.zeros((rots_ref.shape[0] - listed, modes), BF16)
+
+    def split(g, carry):
+        fetch(g).wait()
+        for first in range(0, modes, each):
+            count = min(each, modes - first)
+            rows = axials_ref[g, first : first + count].reshape(2 * count, modes)
+            sorted_rows = dot_nn(halves[:, : 2 * count], rows).astype(BF16)
+            for c in range(2):
+                axial_out_ref[g, c * size + first : c * size + first + each, 0:modes] = sorted_rows[c * each : (c + 1) * each]
+        return carry
+
+    lax.fori_loop(0, tables, split, 0)
+    rot_copy.wait()
+
+    def pick(i, carry):
+        rows = rots_ref[pl.ds(pl.multiple_of(i * chunk, chunk), chunk), :]
+        sorted_rows = dot_nn(entries, rows).astype(BF16)
         for g in range(tables):
-            rot_out_ref[g, q * each : (q + 1) * each, 0:modes] = sorted_rows[g * each : (g + 1) * each]
+            here = pl.ds(pl.multiple_of(i * share, share), share)
+            rot_out_ref[g, here, 0:modes] = sorted_rows[g * share : (g + 1) * share]
+        return carry
+
+    lax.fori_loop(0, rots_ref.shape[0] // chunk, pick, 0)
 
 
 def swapped(value):
@@ -137,21 +147,17 @@
     def one_hot(hit):
         return jnp.where(hit, 1.0, 0.0).astype(BF16)
 
-    even = lax.rem(lax.axis_index("blk"), 2) == 0
-    near, far = jnp.where(even, 2, 0), jnp.where(even, 0, 2)
     forward, backward = None, []
-    for order, (window, ref) in enumerate(zip((near, 1, far), refs)):
+    for window, ref in enumerate(refs):
         values = ref[:, :, :, :, size - 128 : size].reshape(2 * group, 128).astype(F32)
         marks_column, sources_column = (values[h * group : (h + 1) * group, lane : lane + 1].astype(jnp.int32) for h in range(2))
         marks, sources = (jnp.transpose(values[h * group : (h + 1) * group])[lane : lane + 1].astype(jnp.int32) for h in range(2))
-        if order == 1:
-            turned = (2 - lax.div(sources_column, own)) * own + lax.rem(sources_column, own)
-            sources_column = jnp.where(even, turned, sources_column)
+        if window == 1:
             forward = dot_nn(one_hot(marks == wanted), one_hot(sources_column == iota((group, 3 * own), 1)))
         block = sources - (2 - window) * own
         inside = (block >= 0) & (block < own) & (marks >= own)
         hits = one_hot(jnp.where(inside, lax.div(marks, own) * own + block, -1) == wanted)
-        place = lax.rem(marks_column, own) + order * own
+        place = lax.rem(marks_column, own) + window * own
         backward.append(dot_nn(hits, one_hot(place == iota((group, 3 * own), 1))))
     return jnp.concatenate([forward, sum(backward)], axis=0).astype(BF16)
 
@@ -161,11 +167,11 @@
 
 
 def field_kernel(
-    own, modes, together, rot_ref, axial_ref, near_ref, own_ref, far_ref, *rest
+    own, modes, together, rot_ref, axial_ref, below_ref, own_ref, above_ref, *rest
 ):
     outs, (sums_ref, total_ref) = rest[:-2], rest[-2:]
     tables, _, size = rot_ref.shape
-    refs = (near_ref, own_ref, far_ref)
+    refs = (below_ref, own_ref, above_ref)
     ways, _, octets, height, _ = own_ref.shape
     quarter = own // ways
     each = height // quarter
@@ -328,14 +334,14 @@
         if index % 2 and index < 2 * vectors:
             total = jnp.where(left, total, -total)
         line = jnp.where(lane == vectors * vectors + index, jnp.sum(total, axis=(0, 1), keepdims=True), line)
-    sums_ref[...] = line
+    sums_ref[...] = jnp.broadcast_to(line[None], sums_ref.shape)
 
 
 def remainder_kernel(quarter, modes, mean_scale, sums_ref, blocks_ref, image_ref, dots_ref, out_ref):
     vectors = 2 * blocks_ref.shape[0]
     full, columns = image_ref.shape
     rows = quarter * modes
-    total = sums_ref[...]
+    total = jnp.sum(sums_ref[...], axis=0)
     lane = iota(total.shape, 1)
 
     def lane_at(index):
@@ -393,32 +399,11 @@
     return received
 
 
-def summed(value, axis):
-    count, done = lax.axis_size(axis), 1
-    while done < count:
-        ways = min(4, count // done)
-        values = [value]
-        for i in range(1, ways):
-            values.append(lax.ppermute(value, axis, [(p, p ^ (i * done)) for p in range(count)]))
-        value = pl.pallas_call(
-            added_kernel,
-            in_specs=[whole()] * ways,
-            out_specs=whole(),
-            out_shape=jax.ShapeDtypeStruct(value.shape, F32),
-            compiler_params=params(2),
-            name="added",
-        )(*values)
-        done *= ways
-    return value
-
-
 def neighbours(value):
     count = lax.axis_size("blk")
-    results = []
-    for first in range(2):
-        pairs = [(i, i + 1) for i in range(first, count - 1, 2)]
-        results.append(lax.ppermute(value, "blk", pairs + [(j, i) for i, j in pairs]))
-    return results
+    up = [(i, i + 1) for i in range(count - 1)]
+    down = [(j, i) for i, j in up]
+    return lax.ppermute(value, "blk", up), lax.ppermute(value, "blk", down)
 
 
 def shards(basis, mie_coeffs, rot_table, axial_table, pair_table, pair_count):
@@ -489,30 +474,26 @@
         compiler_params=params(4),
         name="join",
     )(*received)
-    near, far = neighbours(own_pieces)
+    below, above = neighbours(own_pieces)
 
     rotations, axials = pl.pallas_call(
-        functools.partial(tables_kernel, modes, tables),
-        grid=(tables,),
-        in_specs=[
-            pl.BlockSpec((1, modes, 2, modes), lambda g: (g, 0, 0, 0)),
-            pl.BlockSpec((size, modes), lambda g: (g, 0)),
-        ],
-        out_specs=[
-            pl.BlockSpec((tables, size // tables, size), lambda g: (0, g, 0)),
-            pl.BlockSpec((1, 2 * size, size), lambda g: (g, 0, 0)),
-        ],
+        tables_kernel,
+        in_specs=[hbm()] * 2,
+        out_specs=[whole()] * 2,
         out_shape=[
             jax.ShapeDtypeStruct((tables, size, size), BF16),
             jax.ShapeDtypeStruct((tables, 2 * size, size), BF16),
         ],
-        scratch_shapes=[pltpu.VMEM((2 * size, size), BF16)],
-        compiler_params=params(32),
+        scratch_shapes=[
+            pltpu.VMEM(axial_rows.shape, BF16),
+            pltpu.VMEM((tables * size, modes), BF16),
+            pltpu.SemaphoreType.DMA((tables + 1,)),
+        ],
+        compiler_params=params(20),
         cost_estimate=pl.CostEstimate(flops=tables * 8 * 256 * 256 * size, bytes_accessed=6 * tables * size * size * 2, transcendentals=0),
         name="tables",
     )(axial_rows, rot_rows)
-
-    near, far, rotations, axials = lax.optimization_barrier((near, far, rotations, axials))
+    below, above, rotations, axials = lax.optimization_barrier((below, above, rotations, axials))
 
     together = 2 if tables % 2 == 0 else 1
     field = pl.pallas_call(
@@ -523,19 +504,19 @@
         scratch_shapes=[pltpu.VMEM((tables, 4 * group, size), BF16), pltpu.VMEM((2 * group, size), F32)],
         compiler_params=params(20),
         name="field",
-    )(rotations, axials, near, own_pieces, far)
+    )(rotations, axials, below, own_pieces, above)
     field_pieces = exchanged(field, "pair")
 
     image, sums = pl.pallas_call(
         functools.partial(image_kernel, quarter, modes),
         in_specs=[whole()] * (ways + 3),
         out_specs=[whole()] * 2,
-        out_shape=[jax.ShapeDtypeStruct((full, columns), F32), jax.ShapeDtypeStruct((1, 128), F32)],
+        out_shape=[jax.ShapeDtypeStruct((full, columns), F32), jax.ShapeDtypeStruct((ways * blk_ways, 1, 128), F32)],
         scratch_shapes=[pltpu.VMEM((full, columns), F32), pltpu.VMEM((quarter, columns, size), BF16)],
         compiler_params=params(8),
         name="image",
     )(blocks, mies, line, *field_pieces)
-    sums = summed(summed(sums, "pair"), "blk")
+    sums = lax.all_to_all(sums, ("blk", "pair"), split_axis=0, concat_axis=0, tiled=True)
 
     mean_scale = 1.0 / (own * blk_ways * modes * columns)
     dots, next_rows = pl.pallas_call(

time: 62.7 us -> 58.5 us (0.933)
  blocking collectives: 0 us -> 12.6 us
  starting transfers between devices: 19.1 us -> 10.9 us
  waiting for transfers between devices: 13.4 us -> 5.33 us
  Pallas kernels: 28.6 us -> 27.9 us
    all_to_all x0 -> x1, blocking collectives: none -> 12.6 us  [shards(): lax.all_to_all(sums, ('blk', 'pair'), split_axis=0, concat_axis=0, tiled=...]
    ppermute x9 -> x2, starting transfers between devices: 14 us -> 5.85 us  [neighbours(): return (lax.ppermute(value, 'blk', up), lax.ppermute(value, 'blk', down))]
    ppermute x9 -> x2, waiting for transfers between devices: 9.64 us -> 1.59 us  [neighbours(): return (lax.ppermute(value, 'blk', up), lax.ppermute(value, 'blk', down))]
    pallas_call x4 -> x1, Pallas kernels: 9.45 us -> 8.77 us  [shards(): pl.pallas_call(tables_kernel, in_specs=[hbm()] * 2, out_specs=[whole()] *...]
  transfers between devices with their start and end apart: 15 -> 8, of which waited for: 9 -> 3; matrix products, arithmetic and copies ran while one was open for 0% -> 0% of each run, Pallas kernels for 22% -> 22%
where the time goes in v12:
time: 58.5 us; the launch traced here: 58.2 us
  Pallas kernels  27.9 us (48%)
  blocking collectives  12.6 us (22%)
  starting transfers between devices  10.9 us (19%)
  waiting for transfers between devices  5.33 us (9%)
  between operations  1.38 us (2%)
    all_to_all x1, blocking collectives, shards(): lax.all_to_all(sums, ('blk', 'pair'), split_axis=0, concat_axis=0, tiled=...  12.6 us
    pallas_call x1, Pallas kernels, shards(): pl.pallas_call(functools.partial(field_kernel, own, modes, together), in_...  10.6 us
    pallas_call x1, Pallas kernels, shards(): pl.pallas_call(tables_kernel, in_specs=[hbm()] * 2, out_specs=[whole()] *...  8.77 us
    ppermute x2, starting transfers between devices, neighbours(): return (lax.ppermute(value, 'blk', up), lax.ppermute(value, 'blk', down))  5.85 us
    ppermute x6, starting transfers between devices, exchanged(): lax.ppermute(pieces[i], axis, [(p, p ^ i) for p in range(count)])  5.09 us
    pallas_call x1, Pallas kernels, shards(): pl.pallas_call(functools.partial(gram_kernel, quarter, modes), in_specs=[...  4.15 us
    ppermute x6, waiting for transfers between devices, exchanged(): lax.ppermute(pieces[i], axis, [(p, p ^ i) for p in range(count)])  3.74 us
    pallas_call x1, Pallas kernels, shards(): pl.pallas_call(functools.partial(remainder_kernel, quarter, modes, mean_s...  1.64 us
  transfers between devices with their start and end apart: 8, of which 3 were waited for; matrix products, arithmetic and copies ran while one was open for 0% of the time, Pallas kernels for 22%

profile of v12, /device:TPU:0, one launch (start us, length us, event | category | flops | bytes accessed | tf_op | source)
XLA Modules:
  0.0 58.2 jit_solution(1839894026148181974)
XLA Ops:
  1.3 1.3 %pack.1 = (bf16[2,2,16,512]{3,2,1,0:T(8,128)(2,1)S(1)}, bf16[2,2,16,512]{3,2,1,0:T(8,128)(2,1)S(1)}, bf16[2,2,16,512]{3,2,1,0:T(8,128)(2,1)S(1)}, bf16[2,2,16,512]{3,2,1,0:T(8,128)(2,1)S(1)}) custom-call(s32[3,1,128]{2,1,0:T(1,128)} %bitcast.19, s32[1]{0:T(128)S(6)} %copy.8.count_ref, f32[4,2040,128]{2,1,0:T(8,128)} %bitcast.14), custom_call_target="tpu_custom_call" | custom-call | tf_op jit(solution)/shard_map/pack/pallas_call | solution.py:432
  2.6 0.5 collective-permute-start
  3.1 2.6 %collective-permute-start.1 = (bf16[2,2,16,512]{3,2,1,0:T(8,128)(2,1)S(1)}, bf16[2,2,16,512]{3,2,1,0:T(8,128)(2,1)S(1)}, u32[]{:S(2)}, u32[]{:S(2)}) collective-permute-start(bf16[2,2,16,512]{3,2,1,0:T(8,128)(2,1)S(1)} %get-tuple-element.46), channel_id=1, source_target_pairs={{0,2},{1,3},{2,0},{3,1},{4,6},{5,7},{6,4},{7,5},{8,10},{9,11},{10,... | collective-permute-start | bytes 196616 | tf_op jit(solution)/shard_map/ppermute | solution.py:398
  5.7 0.1 collective-permute-start.2
  5.8 4.2 %gram.1 = (f32[1,128]{1,0:T(1,128)S(1)}, f32[4,2048,128]{2,1,0:T(8,128)S(1)}, f32[256,4,128]{2,1,0:T(4,128)S(1)}) custom-call(f32[4,2040,128]{2,1,0:T(8,128)} %bitcast.15, f32[255,4,128]{2,1,0:T(4,128)} %bitcast.18), custom_call_target="tpu_custom_call" | custom-call | tf_op jit(solution)/shard_map/gram/pallas_call | solution.py:451
  9.9 0.0 collective-permute-done.refs_1_
  9.9 0.0 collective-permute-done.1.refs_2_
  9.9 0.0 collective-permute-done.2.refs_3_
  10.0 1.3 %collective-permute-start.4 = (bf16[4,2,2,16,512]{4,3,2,1,0:T(8,128)(2,1)S(1)}, bf16[4,2,2,16,512]{4,3,2,1,0:T(8,128)(2,1)S(1)}, u32[]{:S(2)}, u32[]{:S(2)}) collective-permute-start(bf16[4,2,2,16,512]{4,3,2,1,0:T(8,128)(2,1)S(1)} %join.1.own_ref), channel_id=1, source_target_pairs={{4,0},{8,4},{12,8},{16,12},{20,16},{24,20},{28,24},{5,1},{9,5},{13... | collective-permute-start | bytes 786440 | tf_op jit(solution)/shard_map/ppermute | solution.py:406
  11.3 4.6 %collective-permute-start.3 = (bf16[4,2,2,16,512]{4,3,2,1,0:T(8,128)(2,1)S(1)}, bf16[4,2,2,16,512]{4,3,2,1,0:T(8,128)(2,1)S(1)}, u32[]{:S(2)}, u32[]{:S(2)}) collective-permute-start(bf16[4,2,2,16,512]{4,3,2,1,0:T(8,128)(2,1)S(1)} %join.1.own_ref), channel_id=1, source_target_pairs={{0,4},{4,8},{8,12},{12,16},{16,20},{20,24},{24,28},{1,5},{5,9},{9,... | collective-permute-start | bytes 786440 | tf_op jit(solution)/shard_map/ppermute | solution.py:406
  15.8 8.8 %tables.1 = (bf16[8,512,512]{2,1,0:T(8,128)(2,1)S(1)}, bf16[8,1024,512]{2,1,0:T(8,128)(2,1)S(1)}) custom-call(bf16[8,510,2,510]{3,2,1,0:T(2,128)(2,1)} %bitcast.16, bf16[4080,510]{1,0:T(8,128)(2,1)} %bitcast.17), custom_call_target="tpu_custom_call" | custom-call | flops 2147483648 | bytes 25165824 | tf_op jit(solution)/shard_map/tables/pallas_call | solution.py:479
  24.6 0.0 collective-permute-done.4.above_ref
  24.6 1.6 %collective-permute-done.3.below_ref = bf16[4,2,2,16,512]{4,3,2,1,0:T(8,128)(2,1)S(1)} collective-permute-done((bf16[4,2,2,16,512]{4,3,2,1,0:T(8,128)(2,1)S(1)}, bf16[4,2,2,16,512]{4,3,2,1,0:T(8,128)(2,1)S(1)}, u32[]{:S(2)}, u32[]{:S(2)}) %collective-permute-start.3) | collective-permute-done | bytes 262176 | tf_op jit(solution)/shard_map/ppermute | solution.py:406
  26.2 10.6 %field.1 = (bf16[2,2,16,512]{3,2,1,0:T(8,128)(2,1)S(1)}, bf16[2,2,16,512]{3,2,1,0:T(8,128)(2,1)S(1)}, bf16[2,2,16,512]{3,2,1,0:T(8,128)(2,1)S(1)}, bf16[2,2,16,512]{3,2,1,0:T(8,128)(2,1)S(1)}) custom-call(bf16[8,512,512]{2,1,0:T(8,128)(2,1)S(1)} %get-tuple-element.58.rot_ref, bf16[8,1024,512]{2,1,0:T(8,128)(2,1)S(1)} %get-tuple-element.59.axial_ref, ...), custom_call_target="tpu_custom_call" | custom-call | tf_op jit(solution)/shard_map/field/pallas_call | solution.py:499
  36.8 0.1 collective-permute-start.5
  36.9 1.5 %collective-permute-start.6 = (bf16[2,2,16,512]{3,2,1,0:T(8,128)(2,1)S(1)}, bf16[2,2,16,512]{3,2,1,0:T(8,128)(2,1)S(1)}, u32[]{:S(2)}, u32[]{:S(2)}) collective-permute-start(bf16[2,2,16,512]{3,2,1,0:T(8,128)(2,1)S(1)} %get-tuple-element.64), channel_id=1, source_target_pairs={{0,2},{1,3},{2,0},{3,1},{4,6},{5,7},{6,4},{7,5},{8,10},{9,11},{10,... | collective-permute-start | bytes 196616 | tf_op jit(solution)/shard_map/ppermute | solution.py:398
  38.5 0.3 collective-permute-start.7
  38.8 0.0 collective-permute-done.5.rest_1_
  38.8 2.6 %collective-permute-done.6.rest_2_ = bf16[2,2,16,512]{3,2,1,0:T(8,128)(2,1)S(1)} collective-permute-done((bf16[2,2,16,512]{3,2,1,0:T(8,128)(2,1)S(1)}, bf16[2,2,16,512]{3,2,1,0:T(8,128)(2,1)S(1)}, u32[]{:S(2)}, u32[]{:S(2)}) %collective-permute-start.6) | collective-permute-done | bytes 65568 | tf_op jit(solution)/shard_map/ppermute | solution.py:398
  41.4 1.1 %collective-permute-done.7.rest_3_ = bf16[2,2,16,512]{3,2,1,0:T(8,128)(2,1)S(1)} collective-permute-done((bf16[2,2,16,512]{3,2,1,0:T(8,128)(2,1)S(1)}, bf16[2,2,16,512]{3,2,1,0:T(8,128)(2,1)S(1)}, u32[]{:S(2)}, u32[]{:S(2)}) %collective-permute-start.7) | collective-permute-done | bytes 65568 | tf_op jit(solution)/shard_map/ppermute | solution.py:398
  42.5 1.4 %image.1 = (f32[1024,128]{1,0:T(8,128)S(1)}, f32[32,1,128]{2,1,0:T(1,128)S(1)}) custom-call(f32[4,2048,128]{2,1,0:T(8,128)S(1)} %get-tuple-element.42.blocks_ref, f32[256,4,128]{2,1,0:T(4,128)S(1)} %get-tuple-element.43.mie_ref, f32[1,128]{1,0:T(1,128)S(1)} %get-tuple-element.49.gram_ref, bf16[2,2,16,512]{3,2,1,0:T(8,128)(2,1)S(1)} %get-tuple-element.62.rest_0_, ...), custom_call_target="tpu_custom_call" | custom-call | tf_op jit(solution)/shard_map/image/pallas_call | solution.py:510
  44.0 12.6 %all_to_all.5.sums_ref = f32[32,1,128]{2,1,0:T(1,128)S(1)} all-to-all(f32[32,1,128]{2,1,0:T(1,128)S(1)} %get-tuple-element.66), channel_id=1, replica_groups=mesh['blk'=8,'pair'=4] {'blk','pair'}, dimensions={0} | all-to-all | bytes 32768 | tf_op jit(solution)/shard_map/all_to_all | solution.py:519
  56.6 1.6 %remainder.1 = (f32[2,8]{1,0:T(2,128)}, f32[255,4,128]{2,1,0:T(4,128)}) custom-call(f32[32,1,128]{2,1,0:T(1,128)S(1)} %all_to_all.5.sums_ref, f32[4,2048,128]{2,1,0:T(8,128)S(1)} %get-tuple-element.42.blocks_ref, f32[1024,128]{1,0:T(8,128)S(1)} %get-tuple-element.67.image_ref), custom_call_target="tpu_custom_call" | custom-call | tf_op jit(solution)/shard_map/remainder/pallas_call | solution.py:522
  (1 shorter events, 0.0 us)
Async XLA Ops:
  2.6 7.3 %collective-permute-start = (bf16[2,2,16,512]{3,2,1,0:T(8,128)(2,1)S(1)}, bf16[2,2,16,512]{3,2,1,0:T(8,128)(2,1)S(1)}, u32[]{:S(2)}, u32[]{:S(2)}) collective-permute-start(bf16[2,2,16,512]{3,2,1,0:T(8,128)(2,1)S(1)} %get-tuple-element.45), channel_id=1, source_target_pairs={{0,1},{1,0},{2,3},{3,2},{4,5},{5,4},{6,7},{7,6},{8,9},{9,8},{10,11... | collective-permute-start | bytes 196616 | tf_op jit(solution)/shard_map/ppermute | solution.py:398
  3.1 6.8 %collective-permute-start.1 = (bf16[2,2,16,512]{3,2,1,0:T(8,128)(2,1)S(1)}, bf16[2,2,16,512]{3,2,1,0:T(8,128)(2,1)S(1)}, u32[]{:S(2)}, u32[]{:S(2)}) collective-permute-start(bf16[2,2,16,512]{3,2,1,0:T(8,128)(2,1)S(1)} %get-tuple-element.46), channel_id=1, source_target_pairs={{0,2},{1,3},{2,0},{3,1},{4,6},{5,7},{6,4},{7,5},{8,10},{9,11},{10,... | collective-permute-start | bytes 196616 | tf_op jit(solution)/shard_map/ppermute | solution.py:398
  5.7 4.3 %collective-permute-start.2 = (bf16[2,2,16,512]{3,2,1,0:T(8,128)(2,1)S(1)}, bf16[2,2,16,512]{3,2,1,0:T(8,128)(2,1)S(1)}, u32[]{:S(2)}, u32[]{:S(2)}) collective-permute-start(bf16[2,2,16,512]{3,2,1,0:T(8,128)(2,1)S(1)} %get-tuple-element.47), channel_id=1, source_target_pairs={{0,3},{1,2},{2,1},{3,0},{4,7},{5,6},{6,5},{7,4},{8,11},{9,10},{10,... | collective-permute-start | bytes 196616 | tf_op jit(solution)/shard_map/ppermute | solution.py:398
  10.0 14.6 %collective-permute-start.4 = (bf16[4,2,2,16,512]{4,3,2,1,0:T(8,128)(2,1)S(1)}, bf16[4,2,2,16,512]{4,3,2,1,0:T(8,128)(2,1)S(1)}, u32[]{:S(2)}, u32[]{:S(2)}) collective-permute-start(bf16[4,2,2,16,512]{4,3,2,1,0:T(8,128)(2,1)S(1)} %join.1.own_ref), channel_id=1, source_target_pairs={{4,0},{8,4},{12,8},{16,12},{20,16},{24,20},{28,24},{5,1},{9,5},{13... | collective-permute-start | bytes 786440 | tf_op jit(solution)/shard_map/ppermute | solution.py:406
  11.3 14.9 %collective-permute-start.3 = (bf16[4,2,2,16,512]{4,3,2,1,0:T(8,128)(2,1)S(1)}, bf16[4,2,2,16,512]{4,3,2,1,0:T(8,128)(2,1)S(1)}, u32[]{:S(2)}, u32[]{:S(2)}) collective-permute-start(bf16[4,2,2,16,512]{4,3,2,1,0:T(8,128)(2,1)S(1)} %join.1.own_ref), channel_id=1, source_target_pairs={{0,4},{4,8},{8,12},{12,16},{16,20},{20,24},{24,28},{1,5},{5,9},{9,... | collective-permute-start | bytes 786440 | tf_op jit(solution)/shard_map/ppermute | solution.py:406
  36.8 1.9 %collective-permute-start.5 = (bf16[2,2,16,512]{3,2,1,0:T(8,128)(2,1)S(1)}, bf16[2,2,16,512]{3,2,1,0:T(8,128)(2,1)S(1)}, u32[]{:S(2)}, u32[]{:S(2)}) collective-permute-start(bf16[2,2,16,512]{3,2,1,0:T(8,128)(2,1)S(1)} %get-tuple-element.63), channel_id=1, source_target_pairs={{0,1},{1,0},{2,3},{3,2},{4,5},{5,4},{6,7},{7,6},{8,9},{9,8},{10,11... | collective-permute-start | bytes 196616 | tf_op jit(solution)/shard_map/ppermute | solution.py:398
  36.9 4.5 %collective-permute-start.6 = (bf16[2,2,16,512]{3,2,1,0:T(8,128)(2,1)S(1)}, bf16[2,2,16,512]{3,2,1,0:T(8,128)(2,1)S(1)}, u32[]{:S(2)}, u32[]{:S(2)}) collective-permute-start(bf16[2,2,16,512]{3,2,1,0:T(8,128)(2,1)S(1)} %get-tuple-element.64), channel_id=1, source_target_pairs={{0,2},{1,3},{2,0},{3,1},{4,6},{5,7},{6,4},{7,5},{8,10},{9,11},{10,... | collective-permute-start | bytes 196616 | tf_op jit(solution)/shard_map/ppermute | solution.py:398
  38.5 4.0 %collective-permute-start.7 = (bf16[2,2,16,512]{3,2,1,0:T(8,128)(2,1)S(1)}, bf16[2,2,16,512]{3,2,1,0:T(8,128)(2,1)S(1)}, u32[]{:S(2)}, u32[]{:S(2)}) collective-permute-start(bf16[2,2,16,512]{3,2,1,0:T(8,128)(2,1)S(1)} %get-tuple-element.65), channel_id=1, source_target_pairs={{0,3},{1,2},{2,1},{3,0},{4,7},{5,6},{6,5},{7,4},{8,11},{9,10},{10,... | collective-permute-start | bytes 196616 | tf_op jit(solution)/shard_map/ppermute | solution.py:398

commit v13 on v12

--- a/solution.py
+++ b/solution.py
@@ -30,6 +30,10 @@
 
 def rounded_up(value, unit):
     return (value + unit - 1) // unit * unit
+
+
+def mask(i):
+    return (lax.axis_size("pair") - i) % lax.axis_size("pair")
 
 
 def iota(shape, dim):
@@ -72,7 +76,7 @@
     _, octets, height, size = outs[0].shape
     each = height // quarter
     for i, out_ref in enumerate(outs):
-        place = (lax.axis_index("pair") ^ i) * part
+        place = (lax.axis_index("pair") ^ mask(i)) * part
         for c in range(2):
             for o in range(octets):
                 first = (c * octets + o) * height
@@ -85,7 +89,7 @@
 def join_kernel(*refs):
     out_ref = refs[-1]
     for i, ref in enumerate(refs[:-1]):
-        out_ref[lax.axis_index("pair") ^ i] = ref[...]
+        out_ref[lax.axis_index("pair") ^ mask(i)] = ref[...]
 
 
 def tables_kernel(axial_ref, rot_ref, rot_out_ref, axial_out_ref, axials_ref, rots_ref, sems):
@@ -210,7 +214,7 @@
     lax.fori_loop(0, tables // together, body, 0)
     row, source = iota((2 * group, 2 * group), 0), iota((2 * group, 2 * group), 1)
     sphere, c = lax.rem(row, part), lax.rem(lax.div(row, quarter * part), 2)
-    owner = lax.div(row, 2 * quarter * part) ^ lax.axis_index("pair")
+    owner = lax.rem(ways - lax.div(row, 2 * quarter * part), ways) ^ lax.axis_index("pair")
     block = owner * quarter + lax.rem(lax.div(row, part), quarter)
     order = jnp.where(source == c * group + sphere * own + block, 1.0, 0.0).astype(BF16)
     result = dot_nn(order, total_ref[...].astype(BF16)).astype(BF16)
@@ -296,7 +300,7 @@
     rows = quarter * modes
     part = pieces[0].shape[2]
     for i, piece_ref in enumerate(pieces):
-        place = pl.multiple_of((lax.axis_index("pair") ^ i) * part, part)
+        place = pl.multiple_of((lax.axis_index("pair") ^ mask(i)) * part, part)
         for j in range(quarter):
             for c in range(2):
                 whole_ref[j, pl.ds(c * (columns // 2) + place, part), :] = piece_ref[c, j]
@@ -395,7 +399,7 @@
     count = lax.axis_size(axis)
     received = [pieces[0]]
     for i in range(1, len(pieces)):
-        received.append(lax.ppermute(pieces[i], axis, [(p, p ^ i) for p in range(count)]))
+        received.append(lax.ppermute(pieces[i], axis, [(p, p ^ mask(i)) for p in range(count)]))
     return received
 
 

time: 58.5 us -> 58.5 us (level)
  no operation moved by 1% of the time
where the time goes in v13:
time: 58.5 us; the launch traced here: 58.3 us
  Pallas kernels  27.9 us (48%)
  blocking collectives  12.6 us (22%)
  starting transfers between devices  10.9 us (19%)
  waiting for transfers between devices  5.44 us (9%)
  between operations  1.38 us (2%)
    all_to_all x1, blocking collectives, shards(): lax.all_to_all(sums, ('blk', 'pair'), split_axis=0, concat_axis=0, tiled=...  12.6 us
    pallas_call x1, Pallas kernels, shards(): pl.pallas_call(functools.partial(field_kernel, own, modes, together), in_...  10.6 us
    pallas_call x1, Pallas kernels, shards(): pl.pallas_call(tables_kernel, in_specs=[hbm()] * 2, out_specs=[whole()] *...  8.76 us
    ppermute x2, starting transfers between devices, neighbours(): return (lax.ppermute(value, 'blk', up), lax.ppermute(value, 'blk', down))  5.85 us
    ppermute x6, starting transfers between devices, exchanged(): lax.ppermute(pieces[i], axis, [(p, p ^ mask(i)) for p in range(count)])  5.05 us
    pallas_call x1, Pallas kernels, shards(): pl.pallas_call(functools.partial(gram_kernel, quarter, modes), in_specs=[...  4.15 us
    ppermute x6, waiting for transfers between devices, exchanged(): lax.ppermute(pieces[i], axis, [(p, p ^ mask(i)) for p in range(count)])  3.94 us
    pallas_call x1, Pallas kernels, shards(): pl.pallas_call(functools.partial(remainder_kernel, quarter, modes, mean_s...  1.64 us
  transfers between devices with their start and end apart: 8, of which 3 were waited for; matrix products, arithmetic and copies ran while one was open for 0% of the time, Pallas kernels for 22%

profile of v13, /device:TPU:0, one launch (start us, length us, event | category | flops | bytes accessed | tf_op | source)
XLA Modules:
  0.0 58.3 jit_solution(5478543112063193517)
XLA Ops:
  1.3 1.3 %pack.1 = (bf16[2,2,16,512]{3,2,1,0:T(8,128)(2,1)S(1)}, bf16[2,2,16,512]{3,2,1,0:T(8,128)(2,1)S(1)}, bf16[2,2,16,512]{3,2,1,0:T(8,128)(2,1)S(1)}, bf16[2,2,16,512]{3,2,1,0:T(8,128)(2,1)S(1)}) custom-call(s32[3,1,128]{2,1,0:T(1,128)} %bitcast.19, s32[1]{0:T(128)S(6)} %copy.8.count_ref, f32[4,2040,128]{2,1,0:T(8,128)} %bitcast.14), custom_call_target="tpu_custom_call" | custom-call | tf_op jit(solution)/shard_map/pack/pallas_call | solution.py:436
  2.6 2.5 %collective-permute-start = (bf16[2,2,16,512]{3,2,1,0:T(8,128)(2,1)S(1)}, bf16[2,2,16,512]{3,2,1,0:T(8,128)(2,1)S(1)}, u32[]{:S(2)}, u32[]{:S(2)}) collective-permute-start(bf16[2,2,16,512]{3,2,1,0:T(8,128)(2,1)S(1)} %get-tuple-element.45), channel_id=1, source_target_pairs={{0,3},{1,2},{2,1},{3,0},{4,7},{5,6},{6,5},{7,4},{8,11},{9,10},{10,... | collective-permute-start | bytes 196616 | tf_op jit(solution)/shard_map/ppermute | solution.py:402
  5.0 0.6 %collective-permute-start.1 = (bf16[2,2,16,512]{3,2,1,0:T(8,128)(2,1)S(1)}, bf16[2,2,16,512]{3,2,1,0:T(8,128)(2,1)S(1)}, u32[]{:S(2)}, u32[]{:S(2)}) collective-permute-start(bf16[2,2,16,512]{3,2,1,0:T(8,128)(2,1)S(1)} %get-tuple-element.46), channel_id=1, source_target_pairs={{0,2},{1,3},{2,0},{3,1},{4,6},{5,7},{6,4},{7,5},{8,10},{9,11},{10,... | collective-permute-start | bytes 196616 | tf_op jit(solution)/shard_map/ppermute | solution.py:402
  5.7 0.0 collective-permute-start.2
  5.7 4.2 %gram.1 = (f32[1,128]{1,0:T(1,128)S(1)}, f32[4,2048,128]{2,1,0:T(8,128)S(1)}, f32[256,4,128]{2,1,0:T(4,128)S(1)}) custom-call(f32[4,2040,128]{2,1,0:T(8,128)} %bitcast.15, f32[255,4,128]{2,1,0:T(4,128)} %bitcast.18), custom_call_target="tpu_custom_call" | custom-call | tf_op jit(solution)/shard_map/gram/pallas_call | solution.py:455
  9.9 0.0 collective-permute-done.refs_1_
  9.9 0.0 collective-permute-done.1.refs_2_
  9.9 0.0 collective-permute-done.2.refs_3_
  9.9 1.3 %collective-permute-start.4 = (bf16[4,2,2,16,512]{4,3,2,1,0:T(8,128)(2,1)S(1)}, bf16[4,2,2,16,512]{4,3,2,1,0:T(8,128)(2,1)S(1)}, u32[]{:S(2)}, u32[]{:S(2)}) collective-permute-start(bf16[4,2,2,16,512]{4,3,2,1,0:T(8,128)(2,1)S(1)} %join.1.own_ref), channel_id=1, source_target_pairs={{4,0},{8,4},{12,8},{16,12},{20,16},{24,20},{28,24},{5,1},{9,5},{13... | collective-permute-start | bytes 786440 | tf_op jit(solution)/shard_map/ppermute | solution.py:410
  11.2 4.6 %collective-permute-start.3 = (bf16[4,2,2,16,512]{4,3,2,1,0:T(8,128)(2,1)S(1)}, bf16[4,2,2,16,512]{4,3,2,1,0:T(8,128)(2,1)S(1)}, u32[]{:S(2)}, u32[]{:S(2)}) collective-permute-start(bf16[4,2,2,16,512]{4,3,2,1,0:T(8,128)(2,1)S(1)} %join.1.own_ref), channel_id=1, source_target_pairs={{0,4},{4,8},{8,12},{12,16},{16,20},{20,24},{24,28},{1,5},{5,9},{9,... | collective-permute-start | bytes 786440 | tf_op jit(solution)/shard_map/ppermute | solution.py:410
  15.8 8.8 %tables.1 = (bf16[8,512,512]{2,1,0:T(8,128)(2,1)S(1)}, bf16[8,1024,512]{2,1,0:T(8,128)(2,1)S(1)}) custom-call(bf16[8,510,2,510]{3,2,1,0:T(2,128)(2,1)} %bitcast.16, bf16[4080,510]{1,0:T(8,128)(2,1)} %bitcast.17), custom_call_target="tpu_custom_call" | custom-call | flops 2147483648 | bytes 25165824 | tf_op jit(solution)/shard_map/tables/pallas_call | solution.py:483
  24.6 0.0 collective-permute-done.4.above_ref
  24.6 1.5 %collective-permute-done.3.below_ref = bf16[4,2,2,16,512]{4,3,2,1,0:T(8,128)(2,1)S(1)} collective-permute-done((bf16[4,2,2,16,512]{4,3,2,1,0:T(8,128)(2,1)S(1)}, bf16[4,2,2,16,512]{4,3,2,1,0:T(8,128)(2,1)S(1)}, u32[]{:S(2)}, u32[]{:S(2)}) %collective-permute-start.3) | collective-permute-done | bytes 262176 | tf_op jit(solution)/shard_map/ppermute | solution.py:410
  26.1 10.6 %field.1 = (bf16[2,2,16,512]{3,2,1,0:T(8,128)(2,1)S(1)}, bf16[2,2,16,512]{3,2,1,0:T(8,128)(2,1)S(1)}, bf16[2,2,16,512]{3,2,1,0:T(8,128)(2,1)S(1)}, bf16[2,2,16,512]{3,2,1,0:T(8,128)(2,1)S(1)}) custom-call(bf16[8,512,512]{2,1,0:T(8,128)(2,1)S(1)} %get-tuple-element.58.rot_ref, bf16[8,1024,512]{2,1,0:T(8,128)(2,1)S(1)} %get-tuple-element.59.axial_ref, ...), custom_call_target="tpu_custom_call" | custom-call | tf_op jit(solution)/shard_map/field/pallas_call | solution.py:503
  36.7 1.1 %collective-permute-start.5 = (bf16[2,2,16,512]{3,2,1,0:T(8,128)(2,1)S(1)}, bf16[2,2,16,512]{3,2,1,0:T(8,128)(2,1)S(1)}, u32[]{:S(2)}, u32[]{:S(2)}) collective-permute-start(bf16[2,2,16,512]{3,2,1,0:T(8,128)(2,1)S(1)} %get-tuple-element.63), channel_id=1, source_target_pairs={{0,3},{1,2},{2,1},{3,0},{4,7},{5,6},{6,5},{7,4},{8,11},{9,10},{10,... | collective-permute-start | bytes 196616 | tf_op jit(solution)/shard_map/ppermute | solution.py:402
  37.8 0.7 %collective-permute-start.6 = (bf16[2,2,16,512]{3,2,1,0:T(8,128)(2,1)S(1)}, bf16[2,2,16,512]{3,2,1,0:T(8,128)(2,1)S(1)}, u32[]{:S(2)}, u32[]{:S(2)}) collective-permute-start(bf16[2,2,16,512]{3,2,1,0:T(8,128)(2,1)S(1)} %get-tuple-element.64), channel_id=1, source_target_pairs={{0,2},{1,3},{2,0},{3,1},{4,6},{5,7},{6,4},{7,5},{8,10},{9,11},{10,... | collective-permute-start | bytes 196616 | tf_op jit(solution)/shard_map/ppermute | solution.py:402
  38.4 0.2 collective-permute-start.7
  38.6 2.3 %collective-permute-done.5.rest_1_ = bf16[2,2,16,512]{3,2,1,0:T(8,128)(2,1)S(1)} collective-permute-done((bf16[2,2,16,512]{3,2,1,0:T(8,128)(2,1)S(1)}, bf16[2,2,16,512]{3,2,1,0:T(8,128)(2,1)S(1)}, u32[]{:S(2)}, u32[]{:S(2)}) %collective-permute-start.5) | collective-permute-done | bytes 65568 | tf_op jit(solution)/shard_map/ppermute | solution.py:402
  41.0 1.6 %collective-permute-done.6.rest_2_ = bf16[2,2,16,512]{3,2,1,0:T(8,128)(2,1)S(1)} collective-permute-done((bf16[2,2,16,512]{3,2,1,0:T(8,128)(2,1)S(1)}, bf16[2,2,16,512]{3,2,1,0:T(8,128)(2,1)S(1)}, u32[]{:S(2)}, u32[]{:S(2)}) %collective-permute-start.6) | collective-permute-done | bytes 65568 | tf_op jit(solution)/shard_map/ppermute | solution.py:402
  42.6 0.0 collective-permute-done.7.rest_3_
  42.6 1.4 %image.1 = (f32[1024,128]{1,0:T(8,128)S(1)}, f32[32,1,128]{2,1,0:T(1,128)S(1)}) custom-call(f32[4,2048,128]{2,1,0:T(8,128)S(1)} %get-tuple-element.42.blocks_ref, f32[256,4,128]{2,1,0:T(4,128)S(1)} %get-tuple-element.43.mie_ref, f32[1,128]{1,0:T(1,128)S(1)} %get-tuple-element.49.gram_ref, bf16[2,2,16,512]{3,2,1,0:T(8,128)(2,1)S(1)} %get-tuple-element.62.rest_0_, ...), custom_call_target="tpu_custom_call" | custom-call | tf_op jit(solution)/shard_map/image/pallas_call | solution.py:514
  44.0 12.6 %all_to_all.5.sums_ref = f32[32,1,128]{2,1,0:T(1,128)S(1)} all-to-all(f32[32,1,128]{2,1,0:T(1,128)S(1)} %get-tuple-element.66), channel_id=1, replica_groups=mesh['blk'=8,'pair'=4] {'blk','pair'}, dimensions={0} | all-to-all | bytes 32768 | tf_op jit(solution)/shard_map/all_to_all | solution.py:523
  56.7 1.6 %remainder.1 = (f32[2,8]{1,0:T(2,128)}, f32[255,4,128]{2,1,0:T(4,128)}) custom-call(f32[32,1,128]{2,1,0:T(1,128)S(1)} %all_to_all.5.sums_ref, f32[4,2048,128]{2,1,0:T(8,128)S(1)} %get-tuple-element.42.blocks_ref, f32[1024,128]{1,0:T(8,128)S(1)} %get-tuple-element.67.image_ref), custom_call_target="tpu_custom_call" | custom-call | tf_op jit(solution)/shard_map/remainder/pallas_call | solution.py:526
  (1 shorter events, 0.0 us)
Async XLA Ops:
  2.6 7.3 %collective-permute-start = (bf16[2,2,16,512]{3,2,1,0:T(8,128)(2,1)S(1)}, bf16[2,2,16,512]{3,2,1,0:T(8,128)(2,1)S(1)}, u32[]{:S(2)}, u32[]{:S(2)}) collective-permute-start(bf16[2,2,16,512]{3,2,1,0:T(8,128)(2,1)S(1)} %get-tuple-element.45), channel_id=1, source_target_pairs={{0,3},{1,2},{2,1},{3,0},{4,7},{5,6},{6,5},{7,4},{8,11},{9,10},{10,... | collective-permute-start | bytes 196616 | tf_op jit(solution)/shard_map/ppermute | solution.py:402
  5.0 4.8 %collective-permute-start.1 = (bf16[2,2,16,512]{3,2,1,0:T(8,128)(2,1)S(1)}, bf16[2,2,16,512]{3,2,1,0:T(8,128)(2,1)S(1)}, u32[]{:S(2)}, u32[]{:S(2)}) collective-permute-start(bf16[2,2,16,512]{3,2,1,0:T(8,128)(2,1)S(1)} %get-tuple-element.46), channel_id=1, source_target_pairs={{0,2},{1,3},{2,0},{3,1},{4,6},{5,7},{6,4},{7,5},{8,10},{9,11},{10,... | collective-permute-start | bytes 196616 | tf_op jit(solution)/shard_map/ppermute | solution.py:402
  5.7 4.2 %collective-permute-start.2 = (bf16[2,2,16,512]{3,2,1,0:T(8,128)(2,1)S(1)}, bf16[2,2,16,512]{3,2,1,0:T(8,128)(2,1)S(1)}, u32[]{:S(2)}, u32[]{:S(2)}) collective-permute-start(bf16[2,2,16,512]{3,2,1,0:T(8,128)(2,1)S(1)} %get-tuple-element.47), channel_id=1, source_target_pairs={{0,1},{1,0},{2,3},{3,2},{4,5},{5,4},{6,7},{7,6},{8,9},{9,8},{10,11... | collective-permute-start | bytes 196616 | tf_op jit(solution)/shard_map/ppermute | solution.py:402
  9.9 14.6 %collective-permute-start.4 = (bf16[4,2,2,16,512]{4,3,2,1,0:T(8,128)(2,1)S(1)}, bf16[4,2,2,16,512]{4,3,2,1,0:T(8,128)(2,1)S(1)}, u32[]{:S(2)}, u32[]{:S(2)}) collective-permute-start(bf16[4,2,2,16,512]{4,3,2,1,0:T(8,128)(2,1)S(1)} %join.1.own_ref), channel_id=1, source_target_pairs={{4,0},{8,4},{12,8},{16,12},{20,16},{24,20},{28,24},{5,1},{9,5},{13... | collective-permute-start | bytes 786440 | tf_op jit(solution)/shard_map/ppermute | solution.py:410
  11.2 14.8 %collective-permute-start.3 = (bf16[4,2,2,16,512]{4,3,2,1,0:T(8,128)(2,1)S(1)}, bf16[4,2,2,16,512]{4,3,2,1,0:T(8,128)(2,1)S(1)}, u32[]{:S(2)}, u32[]{:S(2)}) collective-permute-start(bf16[4,2,2,16,512]{4,3,2,1,0:T(8,128)(2,1)S(1)} %join.1.own_ref), channel_id=1, source_target_pairs={{0,4},{4,8},{8,12},{12,16},{16,20},{20,24},{24,28},{1,5},{5,9},{9,... | collective-permute-start | bytes 786440 | tf_op jit(solution)/shard_map/ppermute | solution.py:410
  36.7 4.3 %collective-permute-start.5 = (bf16[2,2,16,512]{3,2,1,0:T(8,128)(2,1)S(1)}, bf16[2,2,16,512]{3,2,1,0:T(8,128)(2,1)S(1)}, u32[]{:S(2)}, u32[]{:S(2)}) collective-permute-start(bf16[2,2,16,512]{3,2,1,0:T(8,128)(2,1)S(1)} %get-tuple-element.63), channel_id=1, source_target_pairs={{0,3},{1,2},{2,1},{3,0},{4,7},{5,6},{6,5},{7,4},{8,11},{9,10},{10,... | collective-permute-start | bytes 196616 | tf_op jit(solution)/shard_map/ppermute | solution.py:402
  37.8 4.8 %collective-permute-start.6 = (bf16[2,2,16,512]{3,2,1,0:T(8,128)(2,1)S(1)}, bf16[2,2,16,512]{3,2,1,0:T(8,128)(2,1)S(1)}, u32[]{:S(2)}, u32[]{:S(2)}) collective-permute-start(bf16[2,2,16,512]{3,2,1,0:T(8,128)(2,1)S(1)} %get-tuple-element.64), channel_id=1, source_target_pairs={{0,2},{1,3},{2,0},{3,1},{4,6},{5,7},{6,4},{7,5},{8,10},{9,11},{10,... | collective-permute-start | bytes 196616 | tf_op jit(solution)/shard_map/ppermute | solution.py:402
  38.4 4.1 %collective-permute-start.7 = (bf16[2,2,16,512]{3,2,1,0:T(8,128)(2,1)S(1)}, bf16[2,2,16,512]{3,2,1,0:T(8,128)(2,1)S(1)}, u32[]{:S(2)}, u32[]{:S(2)}) collective-permute-start(bf16[2,2,16,512]{3,2,1,0:T(8,128)(2,1)S(1)} %get-tuple-element.65), channel_id=1, source_target_pairs={{0,1},{1,0},{2,3},{3,2},{4,5},{5,4},{6,7},{7,6},{8,9},{9,8},{10,11... | collective-permute-start | bytes 196616 | tf_op jit(solution)/shard_map/ppermute | solution.py:402

commit v14 on v12

--- a/solution.py
+++ b/solution.py
@@ -257,7 +257,7 @@
     return line
 
 
-def gram_kernel(quarter, modes, basis_ref, mie_ref, line_ref, blocks_ref, mies_ref, products_ref, mie_sem, sems):
+def gram_kernel(quarter, modes, basis_ref, mie_ref, products_ref, blocks_ref, mies_ref, mie_sem, sems):
     blocks, _, columns = basis_ref.shape
     rows = quarter * modes
     parts, chunk = 4, 32
@@ -283,10 +283,19 @@
     for q in range(parts):
         for copy in copies[2 * blocks * q : 2 * blocks * (q + 1)]:
             copy.wait()
-        for first in range(step * q, min(step * (q + 1), rows), chunk):
-            add_products(blocks_ref, products_ref, rows, first, chunk)
-    line_ref[...] = products_line(products_ref)
+        if q < parts - 1:
+            for first in range(step * q, step * (q + 1), chunk):
+                add_products(blocks_ref, products_ref, rows, first, chunk)
     mie_copy.wait()
+
+
+def gram_end_kernel(quarter, modes, products_ref, blocks_ref, line_ref, totals_ref):
+    rows = quarter * modes
+    parts, chunk = 4, 32
+    totals_ref[...] = products_ref[...]
+    for first in range(rounded_up(rows, 8 * parts) // parts * (parts - 1), rows, chunk):
+        add_products(blocks_ref, totals_ref, rows, first, chunk)
+    line_ref[...] = products_line(totals_ref)
 
 
 def image_kernel(quarter, modes, blocks_ref, mie_ref, gram_ref, *rest):
@@ -337,7 +346,7 @@
     sums_ref[...] = jnp.broadcast_to(line[None], sums_ref.shape)
 
 
-def remainder_kernel(quarter, modes, mean_scale, sums_ref, blocks_ref, image_ref, dots_ref, out_ref):
+def remainder_kernel(quarter, modes, mean_scale, sums_ref, blocks_ref, image_ref, dots_ref, out_ref, rows_ref, sems):
     vectors = 2 * blocks_ref.shape[0]
     full, columns = image_ref.shape
     rows = quarter * modes
@@ -374,6 +383,8 @@
     reals = [jnp.broadcast_to(real[k] * scale, (8, columns)) for k in range(vectors)]
     imags = [jnp.broadcast_to(imag[k] * scale, (8, columns)) for k in range(vectors)]
     chunk = 64
+    height = out_ref.shape[1]
+    copies = []
     for first in range(0, full, chunk):
         here = slice(first, first + chunk)
         values = []
@@ -387,8 +398,14 @@
             turned += imags[k] * values[k]
         result = along.reshape(chunk, columns) - lane_swap(turned.reshape(chunk, columns))
         count = min(chunk, rows - first)
-        height = out_ref.shape[1]
-        out_ref[first // height : (first + count) // height] = result.reshape(chunk // height, height, columns)[: count // height]
+        rows_ref[first // height : (first + count) // height] = result.reshape(chunk // height, height, columns)[: count // height]
+        index = first // chunk
+        if index % 4 == 3 or first + chunk >= rows:
+            here = pl.ds(index // 4 * 4 * chunk // height, (first + count - index // 4 * 4 * chunk) // height)
+            copies.append(pltpu.make_async_copy(rows_ref.at[here], out_ref.at[here], sems.at[index // 4]))
+            copies[-1].start()
+    for copy in copies:
+        copy.wait()
 
 
 def exchanged(pieces, axis):
@@ -448,24 +465,23 @@
     tall = rounded_up(rows + full, 8)
     *pieces, basis_rows, mie_rows = lax.optimization_barrier((*pieces, basis_rows, mie_rows))
     received = exchanged(pieces, "pair")
-    line, blocks, mies = pl.pallas_call(
+    products, blocks, mies = pl.pallas_call(
         functools.partial(gram_kernel, quarter, modes),
         in_specs=[hbm()] * 2,
         out_specs=[whole()] * 3,
         out_shape=[
-            jax.ShapeDtypeStruct((1, 128), F32),
+            jax.ShapeDtypeStruct((vectors, vectors, 8, columns), F32),
             jax.ShapeDtypeStruct((pairs_of_vectors, tall, columns), F32),
             jax.ShapeDtypeStruct((full // height, height, columns), F32),
         ],
         scratch_shapes=[
-            pltpu.VMEM((vectors, vectors, 8, columns), F32),
             pltpu.SemaphoreType.DMA,
             pltpu.SemaphoreType.DMA((4, pairs_of_vectors, 2)),
         ],
         compiler_params=params(8),
         name="gram",
     )(basis_rows, mie_rows)
-    *received, line, rot_rows, axial_rows = lax.optimization_barrier((*received, line, rot_rows, axial_rows))
+    *received, products, rot_rows, axial_rows = lax.optimization_barrier((*received, products, rot_rows, axial_rows))
     own_pieces = pl.pallas_call(
         join_kernel,
         in_specs=[whole()] * ways,
@@ -493,9 +509,19 @@
         cost_estimate=pl.CostEstimate(flops=tables * 8 * 256 * 256 * size, bytes_accessed=6 * tables * size * size * 2, transcendentals=0),
         name="tables",
     )(axial_rows, rot_rows)
-    below, above, rotations, axials = lax.optimization_barrier((below, above, rotations, axials))
-
-    together = 2 if tables % 2 == 0 else 1
+    own_pieces, products = lax.optimization_barrier((own_pieces, products))
+    line = pl.pallas_call(
+        functools.partial(gram_end_kernel, quarter, modes),
+        in_specs=[whole()] * 2,
+        out_specs=whole(),
+        out_shape=jax.ShapeDtypeStruct((1, 128), F32),
+        scratch_shapes=[pltpu.VMEM((vectors, vectors, 8, columns), F32)],
+        compiler_params=params(4),
+        name="gram_end",
+    )(products, blocks)
+    below, above, rotations, axials, line = lax.optimization_barrier((below, above, rotations, axials, line))
+
+    together = 1
     field = pl.pallas_call(
         functools.partial(field_kernel, own, modes, together),
         in_specs=[whole()] * 5,
@@ -522,8 +548,9 @@
     dots, next_rows = pl.pallas_call(
         functools.partial(remainder_kernel, quarter, modes, mean_scale),
         in_specs=[whole()] * 3,
-        out_specs=[whole(), whole()],
+        out_specs=[whole(), hbm()],
         out_shape=[jax.ShapeDtypeStruct((2, vectors), F32), jax.ShapeDtypeStruct((rows // height, height, columns), F32)],
+        scratch_shapes=[pltpu.VMEM((rows // height, height, columns), F32), pltpu.SemaphoreType.DMA((rounded_up(full, 256) // 256,))],
         compiler_params=params(16),
         name="remainder",
     )(sums, blocks, image)

time: 58.5 us -> 59.7 us (1.021)
  Pallas kernels: 27.9 us -> 29.8 us
  waiting for transfers between devices: 5.33 us -> 4.71 us
    pallas_call x1, Pallas kernels: 10.6 us -> 12.1 us  [shards(): pl.pallas_call(functools.partial(field_kernel, own, modes, together), in_...]
    ppermute x2, waiting for transfers between devices: 1.59 us -> 0.4 us  [neighbours(): return (lax.ppermute(value, 'blk', up), lax.ppermute(value, 'blk', down))]
    pallas_call x1, Pallas kernels: 4.15 us -> 3.35 us  [shards(): pl.pallas_call(functools.partial(gram_kernel, quarter, modes), in_specs=[...]
    pallas_call x0 -> x1, Pallas kernels: none -> 0.8 us  [shards(): pl.pallas_call(functools.partial(gram_end_kernel, quarter, modes), in_spe...]
  transfers between devices with their start and end apart: 8 -> 8, of which waited for: 3 -> 4; matrix products, arithmetic and copies ran while one was open for 0% -> 0% of each run, Pallas kernels for 22% -> 22%
where the time goes in v14:
time: 59.7 us; the launch traced here: 59.5 us
  Pallas kernels  29.8 us (50%)
  blocking collectives  12.6 us (21%)
  starting transfers between devices  10.9 us (18%)
  waiting for transfers between devices  4.71 us (8%)
  between operations  1.37 us (2%)
    all_to_all x1, blocking collectives, shards(): lax.all_to_all(sums, ('blk', 'pair'), split_axis=0, concat_axis=0, tiled=...  12.6 us
    pallas_call x1, Pallas kernels, shards(): pl.pallas_call(functools.partial(field_kernel, own, modes, together), in_...  12.1 us
    pallas_call x1, Pallas kernels, shards(): pl.pallas_call(tables_kernel, in_specs=[hbm()] * 2, out_specs=[whole()] *...  8.74 us
    ppermute x2, starting transfers between devices, neighbours(): return (lax.ppermute(value, 'blk', up), lax.ppermute(value, 'blk', down))  5.85 us
    ppermute x6, starting transfers between devices, exchanged(): lax.ppermute(pieces[i], axis, [(p, p ^ i) for p in range(count)])  5.09 us
    ppermute x6, waiting for transfers between devices, exchanged(): lax.ppermute(pieces[i], axis, [(p, p ^ i) for p in range(count)])  4.31 us
    pallas_call x1, Pallas kernels, shards(): pl.pallas_call(functools.partial(gram_kernel, quarter, modes), in_specs=[...  3.35 us
    pallas_call x1, Pallas kernels, shards(): pl.pallas_call(functools.partial(remainder_kernel, quarter, modes, mean_s...  2.1 us
  transfers between devices with their start and end apart: 8, of which 4 were waited for; matrix products, arithmetic and copies ran while one was open for 0% of the time, Pallas kernels for 22%

profile of v14, /device:TPU:0, one launch (start us, length us, event | category | flops | bytes accessed | tf_op | source)
XLA Modules:
  0.0 59.5 jit_solution(3400790428224064134)
XLA Ops:
  1.3 1.3 %pack.1 = (bf16[2,2,16,512]{3,2,1,0:T(8,128)(2,1)S(1)}, bf16[2,2,16,512]{3,2,1,0:T(8,128)(2,1)S(1)}, bf16[2,2,16,512]{3,2,1,0:T(8,128)(2,1)S(1)}, bf16[2,2,16,512]{3,2,1,0:T(8,128)(2,1)S(1)}) custom-call(s32[3,1,128]{2,1,0:T(1,128)} %bitcast.19, s32[1]{0:T(128)S(6)} %copy.8.count_ref, f32[4,2040,128]{2,1,0:T(8,128)} %bitcast.14), custom_call_target="tpu_custom_call" | custom-call | tf_op jit(solution)/shard_map/pack/pallas_call | solution.py:449
  2.6 0.5 collective-permute-start
  3.1 2.6 %collective-permute-start.1 = (bf16[2,2,16,512]{3,2,1,0:T(8,128)(2,1)S(1)}, bf16[2,2,16,512]{3,2,1,0:T(8,128)(2,1)S(1)}, u32[]{:S(2)}, u32[]{:S(2)}) collective-permute-start(bf16[2,2,16,512]{3,2,1,0:T(8,128)(2,1)S(1)} %get-tuple-element.49), channel_id=1, source_target_pairs={{0,2},{1,3},{2,0},{3,1},{4,6},{5,7},{6,4},{7,5},{8,10},{9,11},{10,... | collective-permute-start | bytes 196616 | tf_op jit(solution)/shard_map/ppermute | solution.py:415
  5.7 0.1 collective-permute-start.2
  5.8 3.3 %gram.1 = (f32[8,8,8,128]{3,2,1,0:T(8,128)S(1)}, f32[4,2048,128]{2,1,0:T(8,128)S(1)}, f32[256,4,128]{2,1,0:T(4,128)S(1)}) custom-call(f32[4,2040,128]{2,1,0:T(8,128)} %bitcast.15, f32[255,4,128]{2,1,0:T(4,128)} %bitcast.18), custom_call_target="tpu_custom_call" | custom-call | tf_op jit(solution)/shard_map/gram/pallas_call | solution.py:468
  9.1 0.0 collective-permute-done.refs_1_
  9.1 0.0 collective-permute-done.1.refs_2_
  9.1 0.6 %collective-permute-done.2.refs_3_ = bf16[2,2,16,512]{3,2,1,0:T(8,128)(2,1)S(1)} collective-permute-done((bf16[2,2,16,512]{3,2,1,0:T(8,128)(2,1)S(1)}, bf16[2,2,16,512]{3,2,1,0:T(8,128)(2,1)S(1)}, u32[]{:S(2)}, u32[]{:S(2)}) %collective-permute-start.2) | collective-permute-done | bytes 65568 | tf_op jit(solution)/shard_map/ppermute | solution.py:415
  9.8 1.3 %collective-permute-start.4 = (bf16[4,2,2,16,512]{4,3,2,1,0:T(8,128)(2,1)S(1)}, bf16[4,2,2,16,512]{4,3,2,1,0:T(8,128)(2,1)S(1)}, u32[]{:S(2)}, u32[]{:S(2)}) collective-permute-start(bf16[4,2,2,16,512]{4,3,2,1,0:T(8,128)(2,1)S(1)} %join.1.own_ref), channel_id=1, source_target_pairs={{4,0},{8,4},{12,8},{16,12},{20,16},{24,20},{28,24},{5,1},{9,5},{13... | collective-permute-start | bytes 786440 | tf_op jit(solution)/shard_map/ppermute | solution.py:423
  11.1 4.6 %collective-permute-start.3 = (bf16[4,2,2,16,512]{4,3,2,1,0:T(8,128)(2,1)S(1)}, bf16[4,2,2,16,512]{4,3,2,1,0:T(8,128)(2,1)S(1)}, u32[]{:S(2)}, u32[]{:S(2)}) collective-permute-start(bf16[4,2,2,16,512]{4,3,2,1,0:T(8,128)(2,1)S(1)} %join.1.own_ref), channel_id=1, source_target_pairs={{0,4},{4,8},{8,12},{12,16},{16,20},{20,24},{24,28},{1,5},{5,9},{9,... | collective-permute-start | bytes 786440 | tf_op jit(solution)/shard_map/ppermute | solution.py:423
  15.6 0.8 %gram_end.1.gram_ref = f32[1,128]{1,0:T(1,128)S(1)} custom-call(f32[8,8,8,128]{3,2,1,0:T(8,128)S(1)} %get-tuple-element.61.products_ref, f32[4,2048,128]{2,1,0:T(8,128)S(1)} %get-tuple-element.45.blocks_ref), custom_call_target="tpu_custom_call" | custom-call | tf_op jit(solution)/shard_map/gram_end/pallas_call | solution.py:513
  16.4 8.7 %tables.1 = (bf16[8,512,512]{2,1,0:T(8,128)(2,1)S(1)}, bf16[8,1024,512]{2,1,0:T(8,128)(2,1)S(1)}) custom-call(bf16[8,510,2,510]{3,2,1,0:T(2,128)(2,1)} %bitcast.16, bf16[4080,510]{1,0:T(8,128)(2,1)} %bitcast.17), custom_call_target="tpu_custom_call" | custom-call | flops 2147483648 | bytes 25165824 | tf_op jit(solution)/shard_map/tables/pallas_call | solution.py:495
  25.2 0.0 collective-permute-done.4.above_ref
  25.2 0.4 collective-permute-done.3.below_ref
  25.6 12.1 %field.1 = (bf16[2,2,16,512]{3,2,1,0:T(8,128)(2,1)S(1)}, bf16[2,2,16,512]{3,2,1,0:T(8,128)(2,1)S(1)}, bf16[2,2,16,512]{3,2,1,0:T(8,128)(2,1)S(1)}, bf16[2,2,16,512]{3,2,1,0:T(8,128)(2,1)S(1)}) custom-call(bf16[8,512,512]{2,1,0:T(8,128)(2,1)S(1)} %get-tuple-element.63.rot_ref, bf16[8,1024,512]{2,1,0:T(8,128)(2,1)S(1)} %get-tuple-element.64.axial_ref, ...), custom_call_target="tpu_custom_call" | custom-call | tf_op jit(solution)/shard_map/field/pallas_call | solution.py:525
  37.7 0.1 collective-permute-start.5
  37.7 1.5 %collective-permute-start.6 = (bf16[2,2,16,512]{3,2,1,0:T(8,128)(2,1)S(1)}, bf16[2,2,16,512]{3,2,1,0:T(8,128)(2,1)S(1)}, u32[]{:S(2)}, u32[]{:S(2)}) collective-permute-start(bf16[2,2,16,512]{3,2,1,0:T(8,128)(2,1)S(1)} %get-tuple-element.70), channel_id=1, source_target_pairs={{0,2},{1,3},{2,0},{3,1},{4,6},{5,7},{6,4},{7,5},{8,10},{9,11},{10,... | collective-permute-start | bytes 196616 | tf_op jit(solution)/shard_map/ppermute | solution.py:415
  39.3 0.3 collective-permute-start.7
  39.6 0.0 collective-permute-done.5.rest_1_
  39.6 2.6 %collective-permute-done.6.rest_2_ = bf16[2,2,16,512]{3,2,1,0:T(8,128)(2,1)S(1)} collective-permute-done((bf16[2,2,16,512]{3,2,1,0:T(8,128)(2,1)S(1)}, bf16[2,2,16,512]{3,2,1,0:T(8,128)(2,1)S(1)}, u32[]{:S(2)}, u32[]{:S(2)}) %collective-permute-start.6) | collective-permute-done | bytes 65568 | tf_op jit(solution)/shard_map/ppermute | solution.py:415
  42.2 1.1 %collective-permute-done.7.rest_3_ = bf16[2,2,16,512]{3,2,1,0:T(8,128)(2,1)S(1)} collective-permute-done((bf16[2,2,16,512]{3,2,1,0:T(8,128)(2,1)S(1)}, bf16[2,2,16,512]{3,2,1,0:T(8,128)(2,1)S(1)}, u32[]{:S(2)}, u32[]{:S(2)}) %collective-permute-start.7) | collective-permute-done | bytes 65568 | tf_op jit(solution)/shard_map/ppermute | solution.py:415
  43.3 1.4 %image.1 = (f32[1024,128]{1,0:T(8,128)S(1)}, f32[32,1,128]{2,1,0:T(1,128)S(1)}) custom-call(f32[4,2048,128]{2,1,0:T(8,128)S(1)} %get-tuple-element.45.blocks_ref, f32[256,4,128]{2,1,0:T(4,128)S(1)} %get-tuple-element.46.mie_ref, f32[1,128]{1,0:T(1,128)S(1)} %gram_end.1.gram_ref, bf16[2,2,16,512]{3,2,1,0:T(8,128)(2,1)S(1)} %get-tuple-element.68.rest_0_, ...), custom_call_target="tpu_custom_call" | custom-call | tf_op jit(solution)/shard_map/image/pallas_call | solution.py:536
  44.7 12.6 %all_to_all.5.sums_ref = f32[32,1,128]{2,1,0:T(1,128)S(1)} all-to-all(f32[32,1,128]{2,1,0:T(1,128)S(1)} %get-tuple-element.72), channel_id=1, replica_groups=mesh['blk'=8,'pair'=4] {'blk','pair'}, dimensions={0} | all-to-all | bytes 32768 | tf_op jit(solution)/shard_map/all_to_all | solution.py:545
  57.4 2.1 %remainder.1 = (f32[2,8]{1,0:T(2,128)}, f32[255,4,128]{2,1,0:T(4,128)}) custom-call(f32[32,1,128]{2,1,0:T(1,128)S(1)} %all_to_all.5.sums_ref, f32[4,2048,128]{2,1,0:T(8,128)S(1)} %get-tuple-element.45.blocks_ref, f32[1024,128]{1,0:T(8,128)S(1)} %get-tuple-element.73.image_ref), custom_call_target="tpu_custom_call" | custom-call | tf_op jit(solution)/shard_map/remainder/pallas_call | solution.py:548
  (1 shorter events, 0.0 us)
Async XLA Ops:
  2.6 6.5 %collective-permute-start = (bf16[2,2,16,512]{3,2,1,0:T(8,128)(2,1)S(1)}, bf16[2,2,16,512]{3,2,1,0:T(8,128)(2,1)S(1)}, u32[]{:S(2)}, u32[]{:S(2)}) collective-permute-start(bf16[2,2,16,512]{3,2,1,0:T(8,128)(2,1)S(1)} %get-tuple-element.48), channel_id=1, source_target_pairs={{0,1},{1,0},{2,3},{3,2},{4,5},{5,4},{6,7},{7,6},{8,9},{9,8},{10,11... | collective-permute-start | bytes 196616 | tf_op jit(solution)/shard_map/ppermute | solution.py:415
  3.1 6.0 %collective-permute-start.1 = (bf16[2,2,16,512]{3,2,1,0:T(8,128)(2,1)S(1)}, bf16[2,2,16,512]{3,2,1,0:T(8,128)(2,1)S(1)}, u32[]{:S(2)}, u32[]{:S(2)}) collective-permute-start(bf16[2,2,16,512]{3,2,1,0:T(8,128)(2,1)S(1)} %get-tuple-element.49), channel_id=1, source_target_pairs={{0,2},{1,3},{2,0},{3,1},{4,6},{5,7},{6,4},{7,5},{8,10},{9,11},{10,... | collective-permute-start | bytes 196616 | tf_op jit(solution)/shard_map/ppermute | solution.py:415
  5.7 4.0 %collective-permute-start.2 = (bf16[2,2,16,512]{3,2,1,0:T(8,128)(2,1)S(1)}, bf16[2,2,16,512]{3,2,1,0:T(8,128)(2,1)S(1)}, u32[]{:S(2)}, u32[]{:S(2)}) collective-permute-start(bf16[2,2,16,512]{3,2,1,0:T(8,128)(2,1)S(1)} %get-tuple-element.50), channel_id=1, source_target_pairs={{0,3},{1,2},{2,1},{3,0},{4,7},{5,6},{6,5},{7,4},{8,11},{9,10},{10,... | collective-permute-start | bytes 196616 | tf_op jit(solution)/shard_map/ppermute | solution.py:415
  9.8 15.4 %collective-permute-start.4 = (bf16[4,2,2,16,512]{4,3,2,1,0:T(8,128)(2,1)S(1)}, bf16[4,2,2,16,512]{4,3,2,1,0:T(8,128)(2,1)S(1)}, u32[]{:S(2)}, u32[]{:S(2)}) collective-permute-start(bf16[4,2,2,16,512]{4,3,2,1,0:T(8,128)(2,1)S(1)} %join.1.own_ref), channel_id=1, source_target_pairs={{4,0},{8,4},{12,8},{16,12},{20,16},{24,20},{28,24},{5,1},{9,5},{13... | collective-permute-start | bytes 786440 | tf_op jit(solution)/shard_map/ppermute | solution.py:423
  11.1 14.5 %collective-permute-start.3 = (bf16[4,2,2,16,512]{4,3,2,1,0:T(8,128)(2,1)S(1)}, bf16[4,2,2,16,512]{4,3,2,1,0:T(8,128)(2,1)S(1)}, u32[]{:S(2)}, u32[]{:S(2)}) collective-permute-start(bf16[4,2,2,16,512]{4,3,2,1,0:T(8,128)(2,1)S(1)} %join.1.own_ref), channel_id=1, source_target_pairs={{0,4},{4,8},{8,12},{12,16},{16,20},{20,24},{24,28},{1,5},{5,9},{9,... | collective-permute-start | bytes 786440 | tf_op jit(solution)/shard_map/ppermute | solution.py:423
  37.7 1.9 %collective-permute-start.5 = (bf16[2,2,16,512]{3,2,1,0:T(8,128)(2,1)S(1)}, bf16[2,2,16,512]{3,2,1,0:T(8,128)(2,1)S(1)}, u32[]{:S(2)}, u32[]{:S(2)}) collective-permute-start(bf16[2,2,16,512]{3,2,1,0:T(8,128)(2,1)S(1)} %get-tuple-element.69), channel_id=1, source_target_pairs={{0,1},{1,0},{2,3},{3,2},{4,5},{5,4},{6,7},{7,6},{8,9},{9,8},{10,11... | collective-permute-start | bytes 196616 | tf_op jit(solution)/shard_map/ppermute | solution.py:415
  37.7 4.5 %collective-permute-start.6 = (bf16[2,2,16,512]{3,2,1,0:T(8,128)(2,1)S(1)}, bf16[2,2,16,512]{3,2,1,0:T(8,128)(2,1)S(1)}, u32[]{:S(2)}, u32[]{:S(2)}) collective-permute-start(bf16[2,2,16,512]{3,2,1,0:T(8,128)(2,1)S(1)} %get-tuple-element.70), channel_id=1, source_target_pairs={{0,2},{1,3},{2,0},{3,1},{4,6},{5,7},{6,4},{7,5},{8,10},{9,11},{10,... | collective-permute-start | bytes 196616 | tf_op jit(solution)/shard_map/ppermute | solution.py:415
  39.3 4.0 %collective-permute-start.7 = (bf16[2,2,16,512]{3,2,1,0:T(8,128)(2,1)S(1)}, bf16[2,2,16,512]{3,2,1,0:T(8,128)(2,1)S(1)}, u32[]{:S(2)}, u32[]{:S(2)}) collective-permute-start(bf16[2,2,16,512]{3,2,1,0:T(8,128)(2,1)S(1)} %get-tuple-element.71), channel_id=1, source_target_pairs={{0,3},{1,2},{2,1},{3,0},{4,7},{5,6},{6,5},{7,4},{8,11},{9,10},{10,... | collective-permute-start | bytes 196616 | tf_op jit(solution)/shard_map/ppermute | solution.py:415

commit v15 on v14

--- a/solution.py
+++ b/solution.py
@@ -346,7 +346,7 @@
     sums_ref[...] = jnp.broadcast_to(line[None], sums_ref.shape)
 
 
-def remainder_kernel(quarter, modes, mean_scale, sums_ref, blocks_ref, image_ref, dots_ref, out_ref, rows_ref, sems):
+def remainder_kernel(quarter, modes, mean_scale, sums_ref, blocks_ref, image_ref, dots_ref, out_ref):
     vectors = 2 * blocks_ref.shape[0]
     full, columns = image_ref.shape
     rows = quarter * modes
@@ -383,8 +383,6 @@
     reals = [jnp.broadcast_to(real[k] * scale, (8, columns)) for k in range(vectors)]
     imags = [jnp.broadcast_to(imag[k] * scale, (8, columns)) for k in range(vectors)]
     chunk = 64
-    height = out_ref.shape[1]
-    copies = []
     for first in range(0, full, chunk):
         here = slice(first, first + chunk)
         values = []
@@ -398,14 +396,8 @@
             turned += imags[k] * values[k]
         result = along.reshape(chunk, columns) - lane_swap(turned.reshape(chunk, columns))
         count = min(chunk, rows - first)
-        rows_ref[first // height : (first + count) // height] = result.reshape(chunk // height, height, columns)[: count // height]
-        index = first // chunk
-        if index % 4 == 3 or first + chunk >= rows:
-            here = pl.ds(index // 4 * 4 * chunk // height, (first + count - index // 4 * 4 * chunk) // height)
-            copies.append(pltpu.make_async_copy(rows_ref.at[here], out_ref.at[here], sems.at[index // 4]))
-            copies[-1].start()
-    for copy in copies:
-        copy.wait()
+        height = out_ref.shape[1]
+        out_ref[first // height : (first + count) // height] = result.reshape(chunk // height, height, columns)[: count // height]
 
 
 def exchanged(pieces, axis):
@@ -521,7 +513,7 @@
     )(products, blocks)
     below, above, rotations, axials, line = lax.optimization_barrier((below, above, rotations, axials, line))
 
-    together = 1
+    together = 4 if tables % 4 == 0 else 1
     field = pl.pallas_call(
         functools.partial(field_kernel, own, modes, together),
         in_specs=[whole()] * 5,
@@ -548,9 +540,8 @@
     dots, next_rows = pl.pallas_call(
         functools.partial(remainder_kernel, quarter, modes, mean_scale),
         in_specs=[whole()] * 3,
-        out_specs=[whole(), hbm()],
+        out_specs=[whole(), whole()],
         out_shape=[jax.ShapeDtypeStruct((2, vectors), F32), jax.ShapeDtypeStruct((rows // height, height, columns), F32)],
-        scratch_shapes=[pltpu.VMEM((rows // height, height, columns), F32), pltpu.SemaphoreType.DMA((rounded_up(full, 256) // 256,))],
         compiler_params=params(16),
         name="remainder",
     )(sums, blocks, image)

time: 59.7 us -> 57.1 us (0.956)
  Pallas kernels: 29.8 us -> 27.2 us
    pallas_call x1, Pallas kernels: 12.1 us -> 9.9 us  [shards(): pl.pallas_call(functools.partial(field_kernel, own, modes, together), in_...]
  transfers between devices with their start and end apart: 8 -> 8, of which waited for: 4 -> 4; matrix products, arithmetic and copies ran while one was open for 0% -> 0% of each run, Pallas kernels for 22% -> 23%
where the time goes in v15:
time: 57.1 us; the launch traced here: 56.8 us
  Pallas kernels  27.2 us (48%)
  blocking collectives  12.6 us (22%)
  starting transfers between devices  10.9 us (19%)
  waiting for transfers between devices  4.71 us (8%)
  between operations  1.37 us (2%)
    all_to_all x1, blocking collectives, shards(): lax.all_to_all(sums, ('blk', 'pair'), split_axis=0, concat_axis=0, tiled=...  12.6 us
    pallas_call x1, Pallas kernels, shards(): pl.pallas_call(functools.partial(field_kernel, own, modes, together), in_...  9.9 us
    pallas_call x1, Pallas kernels, shards(): pl.pallas_call(tables_kernel, in_specs=[hbm()] * 2, out_specs=[whole()] *...  8.74 us
    ppermute x2, starting transfers between devices, neighbours(): return (lax.ppermute(value, 'blk', up), lax.ppermute(value, 'blk', down))  5.85 us
    ppermute x6, starting transfers between devices, exchanged(): lax.ppermute(pieces[i], axis, [(p, p ^ i) for p in range(count)])  5.09 us
    ppermute x6, waiting for transfers between devices, exchanged(): lax.ppermute(pieces[i], axis, [(p, p ^ i) for p in range(count)])  4.31 us
    pallas_call x1, Pallas kernels, shards(): pl.pallas_call(functools.partial(gram_kernel, quarter, modes), in_specs=[...  3.35 us
    pallas_call x1, Pallas kernels, shards(): pl.pallas_call(functools.partial(remainder_kernel, quarter, modes, mean_s...  1.64 us
  transfers between devices with their start and end apart: 8, of which 4 were waited for; matrix products, arithmetic and copies ran while one was open for 0% of the time, Pallas kernels for 23%

profile of v15, /device:TPU:0, one launch (start us, length us, event | category | flops | bytes accessed | tf_op | source)
XLA Modules:
  0.0 56.8 jit_solution(7002627713957723178)
XLA Ops:
  1.3 1.3 %pack.1 = (bf16[2,2,16,512]{3,2,1,0:T(8,128)(2,1)S(1)}, bf16[2,2,16,512]{3,2,1,0:T(8,128)(2,1)S(1)}, bf16[2,2,16,512]{3,2,1,0:T(8,128)(2,1)S(1)}, bf16[2,2,16,512]{3,2,1,0:T(8,128)(2,1)S(1)}) custom-call(s32[3,1,128]{2,1,0:T(1,128)} %bitcast.19, s32[1]{0:T(128)S(6)} %copy.8.count_ref, f32[4,2040,128]{2,1,0:T(8,128)} %bitcast.14), custom_call_target="tpu_custom_call" | custom-call | tf_op jit(solution)/shard_map/pack/pallas_call | solution.py:441
  2.6 0.5 collective-permute-start
  3.1 2.6 %collective-permute-start.1 = (bf16[2,2,16,512]{3,2,1,0:T(8,128)(2,1)S(1)}, bf16[2,2,16,512]{3,2,1,0:T(8,128)(2,1)S(1)}, u32[]{:S(2)}, u32[]{:S(2)}) collective-permute-start(bf16[2,2,16,512]{3,2,1,0:T(8,128)(2,1)S(1)} %get-tuple-element.49), channel_id=1, source_target_pairs={{0,2},{1,3},{2,0},{3,1},{4,6},{5,7},{6,4},{7,5},{8,10},{9,11},{10,... | collective-permute-start | bytes 196616 | tf_op jit(solution)/shard_map/ppermute | solution.py:407
  5.7 0.1 collective-permute-start.2
  5.8 3.3 %gram.1 = (f32[8,8,8,128]{3,2,1,0:T(8,128)S(1)}, f32[4,2048,128]{2,1,0:T(8,128)S(1)}, f32[256,4,128]{2,1,0:T(4,128)S(1)}) custom-call(f32[4,2040,128]{2,1,0:T(8,128)} %bitcast.15, f32[255,4,128]{2,1,0:T(4,128)} %bitcast.18), custom_call_target="tpu_custom_call" | custom-call | tf_op jit(solution)/shard_map/gram/pallas_call | solution.py:460
  9.1 0.0 collective-permute-done.refs_1_
  9.1 0.0 collective-permute-done.1.refs_2_
  9.1 0.6 %collective-permute-done.2.refs_3_ = bf16[2,2,16,512]{3,2,1,0:T(8,128)(2,1)S(1)} collective-permute-done((bf16[2,2,16,512]{3,2,1,0:T(8,128)(2,1)S(1)}, bf16[2,2,16,512]{3,2,1,0:T(8,128)(2,1)S(1)}, u32[]{:S(2)}, u32[]{:S(2)}) %collective-permute-start.2) | collective-permute-done | bytes 65568 | tf_op jit(solution)/shard_map/ppermute | solution.py:407
  9.8 1.3 %collective-permute-start.4 = (bf16[4,2,2,16,512]{4,3,2,1,0:T(8,128)(2,1)S(1)}, bf16[4,2,2,16,512]{4,3,2,1,0:T(8,128)(2,1)S(1)}, u32[]{:S(2)}, u32[]{:S(2)}) collective-permute-start(bf16[4,2,2,16,512]{4,3,2,1,0:T(8,128)(2,1)S(1)} %join.1.own_ref), channel_id=1, source_target_pairs={{4,0},{8,4},{12,8},{16,12},{20,16},{24,20},{28,24},{5,1},{9,5},{13... | collective-permute-start | bytes 786440 | tf_op jit(solution)/shard_map/ppermute | solution.py:415
  11.1 4.6 %collective-permute-start.3 = (bf16[4,2,2,16,512]{4,3,2,1,0:T(8,128)(2,1)S(1)}, bf16[4,2,2,16,512]{4,3,2,1,0:T(8,128)(2,1)S(1)}, u32[]{:S(2)}, u32[]{:S(2)}) collective-permute-start(bf16[4,2,2,16,512]{4,3,2,1,0:T(8,128)(2,1)S(1)} %join.1.own_ref), channel_id=1, source_target_pairs={{0,4},{4,8},{8,12},{12,16},{16,20},{20,24},{24,28},{1,5},{5,9},{9,... | collective-permute-start | bytes 786440 | tf_op jit(solution)/shard_map/ppermute | solution.py:415
  15.6 0.8 %gram_end.1.gram_ref = f32[1,128]{1,0:T(1,128)S(1)} custom-call(f32[8,8,8,128]{3,2,1,0:T(8,128)S(1)} %get-tuple-element.61.products_ref, f32[4,2048,128]{2,1,0:T(8,128)S(1)} %get-tuple-element.45.blocks_ref), custom_call_target="tpu_custom_call" | custom-call | tf_op jit(solution)/shard_map/gram_end/pallas_call | solution.py:505
  16.4 8.7 %tables.1 = (bf16[8,512,512]{2,1,0:T(8,128)(2,1)S(1)}, bf16[8,1024,512]{2,1,0:T(8,128)(2,1)S(1)}) custom-call(bf16[8,510,2,510]{3,2,1,0:T(2,128)(2,1)} %bitcast.16, bf16[4080,510]{1,0:T(8,128)(2,1)} %bitcast.17), custom_call_target="tpu_custom_call" | custom-call | flops 2147483648 | bytes 25165824 | tf_op jit(solution)/shard_map/tables/pallas_call | solution.py:487
  25.2 0.0 collective-permute-done.4.above_ref
  25.2 0.4 collective-permute-done.3.below_ref
  25.6 9.9 %field.1 = (bf16[2,2,16,512]{3,2,1,0:T(8,128)(2,1)S(1)}, bf16[2,2,16,512]{3,2,1,0:T(8,128)(2,1)S(1)}, bf16[2,2,16,512]{3,2,1,0:T(8,128)(2,1)S(1)}, bf16[2,2,16,512]{3,2,1,0:T(8,128)(2,1)S(1)}) custom-call(bf16[8,512,512]{2,1,0:T(8,128)(2,1)S(1)} %get-tuple-element.63.rot_ref, bf16[8,1024,512]{2,1,0:T(8,128)(2,1)S(1)} %get-tuple-element.64.axial_ref, ...), custom_call_target="tpu_custom_call" | custom-call | tf_op jit(solution)/shard_map/field/pallas_call | solution.py:517
  35.5 0.1 collective-permute-start.5
  35.6 1.5 %collective-permute-start.6 = (bf16[2,2,16,512]{3,2,1,0:T(8,128)(2,1)S(1)}, bf16[2,2,16,512]{3,2,1,0:T(8,128)(2,1)S(1)}, u32[]{:S(2)}, u32[]{:S(2)}) collective-permute-start(bf16[2,2,16,512]{3,2,1,0:T(8,128)(2,1)S(1)} %get-tuple-element.70), channel_id=1, source_target_pairs={{0,2},{1,3},{2,0},{3,1},{4,6},{5,7},{6,4},{7,5},{8,10},{9,11},{10,... | collective-permute-start | bytes 196616 | tf_op jit(solution)/shard_map/ppermute | solution.py:407
  37.1 0.3 collective-permute-start.7
  37.4 0.0 collective-permute-done.5.rest_1_
  37.4 2.6 %collective-permute-done.6.rest_2_ = bf16[2,2,16,512]{3,2,1,0:T(8,128)(2,1)S(1)} collective-permute-done((bf16[2,2,16,512]{3,2,1,0:T(8,128)(2,1)S(1)}, bf16[2,2,16,512]{3,2,1,0:T(8,128)(2,1)S(1)}, u32[]{:S(2)}, u32[]{:S(2)}) %collective-permute-start.6) | collective-permute-done | bytes 65568 | tf_op jit(solution)/shard_map/ppermute | solution.py:407
  40.1 1.1 %collective-permute-done.7.rest_3_ = bf16[2,2,16,512]{3,2,1,0:T(8,128)(2,1)S(1)} collective-permute-done((bf16[2,2,16,512]{3,2,1,0:T(8,128)(2,1)S(1)}, bf16[2,2,16,512]{3,2,1,0:T(8,128)(2,1)S(1)}, u32[]{:S(2)}, u32[]{:S(2)}) %collective-permute-start.7) | collective-permute-done | bytes 65568 | tf_op jit(solution)/shard_map/ppermute | solution.py:407
  41.1 1.4 %image.1 = (f32[1024,128]{1,0:T(8,128)S(1)}, f32[32,1,128]{2,1,0:T(1,128)S(1)}) custom-call(f32[4,2048,128]{2,1,0:T(8,128)S(1)} %get-tuple-element.45.blocks_ref, f32[256,4,128]{2,1,0:T(4,128)S(1)} %get-tuple-element.46.mie_ref, f32[1,128]{1,0:T(1,128)S(1)} %gram_end.1.gram_ref, bf16[2,2,16,512]{3,2,1,0:T(8,128)(2,1)S(1)} %get-tuple-element.68.rest_0_, ...), custom_call_target="tpu_custom_call" | custom-call | tf_op jit(solution)/shard_map/image/pallas_call | solution.py:528
  42.6 12.6 %all_to_all.5.sums_ref = f32[32,1,128]{2,1,0:T(1,128)S(1)} all-to-all(f32[32,1,128]{2,1,0:T(1,128)S(1)} %get-tuple-element.72), channel_id=1, replica_groups=mesh['blk'=8,'pair'=4] {'blk','pair'}, dimensions={0} | all-to-all | bytes 32768 | tf_op jit(solution)/shard_map/all_to_all | solution.py:537
  55.2 1.6 %remainder.1 = (f32[2,8]{1,0:T(2,128)}, f32[255,4,128]{2,1,0:T(4,128)}) custom-call(f32[32,1,128]{2,1,0:T(1,128)S(1)} %all_to_all.5.sums_ref, f32[4,2048,128]{2,1,0:T(8,128)S(1)} %get-tuple-element.45.blocks_ref, f32[1024,128]{1,0:T(8,128)S(1)} %get-tuple-element.73.image_ref), custom_call_target="tpu_custom_call" | custom-call | tf_op jit(solution)/shard_map/remainder/pallas_call | solution.py:540
  (1 shorter events, 0.0 us)
Async XLA Ops:
  2.6 6.5 %collective-permute-start = (bf16[2,2,16,512]{3,2,1,0:T(8,128)(2,1)S(1)}, bf16[2,2,16,512]{3,2,1,0:T(8,128)(2,1)S(1)}, u32[]{:S(2)}, u32[]{:S(2)}) collective-permute-start(bf16[2,2,16,512]{3,2,1,0:T(8,128)(2,1)S(1)} %get-tuple-element.48), channel_id=1, source_target_pairs={{0,1},{1,0},{2,3},{3,2},{4,5},{5,4},{6,7},{7,6},{8,9},{9,8},{10,11... | collective-permute-start | bytes 196616 | tf_op jit(solution)/shard_map/ppermute | solution.py:407
  3.1 6.0 %collective-permute-start.1 = (bf16[2,2,16,512]{3,2,1,0:T(8,128)(2,1)S(1)}, bf16[2,2,16,512]{3,2,1,0:T(8,128)(2,1)S(1)}, u32[]{:S(2)}, u32[]{:S(2)}) collective-permute-start(bf16[2,2,16,512]{3,2,1,0:T(8,128)(2,1)S(1)} %get-tuple-element.49), channel_id=1, source_target_pairs={{0,2},{1,3},{2,0},{3,1},{4,6},{5,7},{6,4},{7,5},{8,10},{9,11},{10,... | collective-permute-start | bytes 196616 | tf_op jit(solution)/shard_map/ppermute | solution.py:407
  5.7 4.0 %collective-permute-start.2 = (bf16[2,2,16,512]{3,2,1,0:T(8,128)(2,1)S(1)}, bf16[2,2,16,512]{3,2,1,0:T(8,128)(2,1)S(1)}, u32[]{:S(2)}, u32[]{:S(2)}) collective-permute-start(bf16[2,2,16,512]{3,2,1,0:T(8,128)(2,1)S(1)} %get-tuple-element.50), channel_id=1, source_target_pairs={{0,3},{1,2},{2,1},{3,0},{4,7},{5,6},{6,5},{7,4},{8,11},{9,10},{10,... | collective-permute-start | bytes 196616 | tf_op jit(solution)/shard_map/ppermute | solution.py:407
  9.8 15.4 %collective-permute-start.4 = (bf16[4,2,2,16,512]{4,3,2,1,0:T(8,128)(2,1)S(1)}, bf16[4,2,2,16,512]{4,3,2,1,0:T(8,128)(2,1)S(1)}, u32[]{:S(2)}, u32[]{:S(2)}) collective-permute-start(bf16[4,2,2,16,512]{4,3,2,1,0:T(8,128)(2,1)S(1)} %join.1.own_ref), channel_id=1, source_target_pairs={{4,0},{8,4},{12,8},{16,12},{20,16},{24,20},{28,24},{5,1},{9,5},{13... | collective-permute-start | bytes 786440 | tf_op jit(solution)/shard_map/ppermute | solution.py:415
  11.1 14.5 %collective-permute-start.3 = (bf16[4,2,2,16,512]{4,3,2,1,0:T(8,128)(2,1)S(1)}, bf16[4,2,2,16,512]{4,3,2,1,0:T(8,128)(2,1)S(1)}, u32[]{:S(2)}, u32[]{:S(2)}) collective-permute-start(bf16[4,2,2,16,512]{4,3,2,1,0:T(8,128)(2,1)S(1)} %join.1.own_ref), channel_id=1, source_target_pairs={{0,4},{4,8},{8,12},{12,16},{16,20},{20,24},{24,28},{1,5},{5,9},{9,... | collective-permute-start | bytes 786440 | tf_op jit(solution)/shard_map/ppermute | solution.py:415
  35.5 1.9 %collective-permute-start.5 = (bf16[2,2,16,512]{3,2,1,0:T(8,128)(2,1)S(1)}, bf16[2,2,16,512]{3,2,1,0:T(8,128)(2,1)S(1)}, u32[]{:S(2)}, u32[]{:S(2)}) collective-permute-start(bf16[2,2,16,512]{3,2,1,0:T(8,128)(2,1)S(1)} %get-tuple-element.69), channel_id=1, source_target_pairs={{0,1},{1,0},{2,3},{3,2},{4,5},{5,4},{6,7},{7,6},{8,9},{9,8},{10,11... | collective-permute-start | bytes 196616 | tf_op jit(solution)/shard_map/ppermute | solution.py:407
  35.6 4.5 %collective-permute-start.6 = (bf16[2,2,16,512]{3,2,1,0:T(8,128)(2,1)S(1)}, bf16[2,2,16,512]{3,2,1,0:T(8,128)(2,1)S(1)}, u32[]{:S(2)}, u32[]{:S(2)}) collective-permute-start(bf16[2,2,16,512]{3,2,1,0:T(8,128)(2,1)S(1)} %get-tuple-element.70), channel_id=1, source_target_pairs={{0,2},{1,3},{2,0},{3,1},{4,6},{5,7},{6,4},{7,5},{8,10},{9,11},{10,... | collective-permute-start | bytes 196616 | tf_op jit(solution)/shard_map/ppermute | solution.py:407
  37.1 4.0 %collective-permute-start.7 = (bf16[2,2,16,512]{3,2,1,0:T(8,128)(2,1)S(1)}, bf16[2,2,16,512]{3,2,1,0:T(8,128)(2,1)S(1)}, u32[]{:S(2)}, u32[]{:S(2)}) collective-permute-start(bf16[2,2,16,512]{3,2,1,0:T(8,128)(2,1)S(1)} %get-tuple-element.71), channel_id=1, source_target_pairs={{0,3},{1,2},{2,1},{3,0},{4,7},{5,6},{6,5},{7,4},{8,11},{9,10},{10,... | collective-permute-start | bytes 196616 | tf_op jit(solution)/shard_map/ppermute | solution.py:407

commit v16 on v15

--- a/solution.py
+++ b/solution.py
@@ -207,7 +207,10 @@
         total_ref[...] += sum(dot_nn(value, rot_ref[g]) for g, value in zip(entries, moved))
         return carry
 
-    lax.fori_loop(0, tables // together, body, 0)
+    if together == tables:
+        body(0, 0)
+    else:
+        lax.fori_loop(0, tables // together, body, 0)
     row, source = iota((2 * group, 2 * group), 0), iota((2 * group, 2 * group), 1)
     sphere, c = lax.rem(row, part), lax.rem(lax.div(row, quarter * part), 2)
     owner = lax.div(row, 2 * quarter * part) ^ lax.axis_index("pair")
@@ -329,13 +332,13 @@
         last = (vectors - 1) % 2 * rows + first
         image = blocks_ref[(vectors - 1) // 2, last : last + chunk, :] - product
         image_ref[here, :] = image
-        turned = pltpu.roll(image, half, axis=1)
+        turned = pltpu.roll(product, half, axis=1)
         for k in range(vectors):
             start = k % 2 * rows + first
             values = blocks_ref[k // 2, start : start + chunk, :]
-            totals[2 * k] += folded(values * image)
+            totals[2 * k] += folded(values * product)
             totals[2 * k + 1] += folded(values * turned)
-        totals[2 * vectors] += folded(image * image)
+        totals[2 * vectors] += folded(product * product)
     lane = iota(gram_ref.shape, 1)
     line = gram_ref[...]
     left = iota((8, columns), 1) < half
@@ -363,21 +366,25 @@
         return line
 
     start = vectors * vectors
-    real = [lane_at(start + 2 * k) * mean_scale for k in range(vectors)]
-    imag = [lane_at(start + 2 * k + 1) * mean_scale for k in range(vectors)]
-    real_line, imag_line = on_lanes(real, lane), on_lanes(imag, lane)
-    dots_ref[0:1, :] = real_line[:, :vectors]
-    dots_ref[1:2, :] = imag_line[:, :vectors]
+    last = vectors - 1
+    taken_real = [lane_at(start + 2 * k) * mean_scale for k in range(vectors)]
+    taken_imag = [lane_at(start + 2 * k + 1) * mean_scale for k in range(vectors)]
+    real = [lane_at(k * vectors + last) * mean_scale - taken_real[k] for k in range(vectors)]
+    imag = [lane_at(last * vectors + k) * mean_scale - taken_imag[k] for k in range(last)] + [-taken_imag[last]]
+    dots_ref[0:1, :] = on_lanes(real, lane)[:, :vectors]
+    dots_ref[1:2, :] = on_lanes(imag, lane)[:, :vectors]
+    kept_real = [-value for value in real[:last]] + [1.0 - real[last]]
+    kept_imag = [-value for value in imag]
     first_index, last_index = lax.div(lane, vectors), lax.rem(lane, vectors)
-    real_first, real_last = on_lanes(real, first_index), on_lanes(real, last_index)
-    imag_first, imag_last = on_lanes(imag, first_index), on_lanes(imag, last_index)
+    real_first, real_last = on_lanes(kept_real, first_index), on_lanes(kept_real, last_index)
+    imag_first, imag_last = on_lanes(kept_imag, first_index), on_lanes(kept_imag, last_index)
     same = real_first * real_last + imag_first * imag_last
     cross = imag_last * real_first - real_last * imag_first
     often = jnp.where(first_index == last_index, 1.0, 2.0)
     spread = jnp.where(lane < start, total * often * jnp.where(first_index <= last_index, same, cross), 0.0)
     spread = jnp.sum(spread, axis=1, keepdims=True)
-    inside = jnp.sum(real_line * real_line + imag_line * imag_line, axis=1, keepdims=True)
-    norm_square = (lane_at(start + 2 * vectors) + spread) * mean_scale - 2.0 * inside
+    both = sum(kept_real[k] * taken_real[k] + kept_imag[k] * taken_imag[k] for k in range(vectors))
+    norm_square = (lane_at(start + 2 * vectors) + spread) * mean_scale - 2.0 * both
     scale = lax.rsqrt(norm_square)
     image_scale = jnp.broadcast_to(scale, (8, columns))
     reals = [jnp.broadcast_to(real[k] * scale, (8, columns)) for k in range(vectors)]
@@ -513,14 +520,14 @@
     )(products, blocks)
     below, above, rotations, axials, line = lax.optimization_barrier((below, above, rotations, axials, line))
 
-    together = 4 if tables % 4 == 0 else 1
+    together = tables
     field = pl.pallas_call(
         functools.partial(field_kernel, own, modes, together),
         in_specs=[whole()] * 5,
         out_specs=[whole()] * ways,
         out_shape=[jax.ShapeDtypeStruct((2, quarter, part, size), BF16)] * ways,
         scratch_shapes=[pltpu.VMEM((tables, 4 * group, size), BF16), pltpu.VMEM((2 * group, size), F32)],
-        compiler_params=params(20),
+        compiler_params=params(28),
         name="field",
     )(rotations, axials, below, own_pieces, above)
     field_pieces = exchanged(field, "pair")

time: 57.1 us -> 56.7 us (level)
  no operation moved by 1% of the time
where the time goes in v16:
time: 56.7 us; the launch traced here: 56.5 us
  Pallas kernels  26.8 us (47%)
  blocking collectives  12.6 us (22%)
  starting transfers between devices  11.1 us (20%)
  waiting for transfers between devices  4.51 us (8%)
  between operations  1.36 us (2%)
    all_to_all x1, blocking collectives, shards(): lax.all_to_all(sums, ('blk', 'pair'), split_axis=0, concat_axis=0, tiled=...  12.6 us
    pallas_call x1, Pallas kernels, shards(): pl.pallas_call(functools.partial(field_kernel, own, modes, together), in_...  9.51 us
    pallas_call x1, Pallas kernels, shards(): pl.pallas_call(tables_kernel, in_specs=[hbm()] * 2, out_specs=[whole()] *...  8.76 us
    ppermute x2, starting transfers between devices, neighbours(): return (lax.ppermute(value, 'blk', up), lax.ppermute(value, 'blk', down))  6.03 us
    ppermute x6, starting transfers between devices, exchanged(): lax.ppermute(pieces[i], axis, [(p, p ^ i) for p in range(count)])  5.09 us
    ppermute x6, waiting for transfers between devices, exchanged(): lax.ppermute(pieces[i], axis, [(p, p ^ i) for p in range(count)])  4.31 us
    pallas_call x1, Pallas kernels, shards(): pl.pallas_call(functools.partial(gram_kernel, quarter, modes), in_specs=[...  3.35 us
    pallas_call x1, Pallas kernels, shards(): pl.pallas_call(functools.partial(remainder_kernel, quarter, modes, mean_s...  1.65 us
  transfers between devices with their start and end apart: 8, of which 4 were waited for; matrix products, arithmetic and copies ran while one was open for 0% of the time, Pallas kernels for 23%

profile of v16, /device:TPU:0, one launch (start us, length us, event | category | flops | bytes accessed | tf_op | source)
XLA Modules:
  0.0 56.5 jit_solution(1594689821030329174)
XLA Ops:
  1.3 1.3 %pack.1 = (bf16[2,2,16,512]{3,2,1,0:T(8,128)(2,1)S(1)}, bf16[2,2,16,512]{3,2,1,0:T(8,128)(2,1)S(1)}, bf16[2,2,16,512]{3,2,1,0:T(8,128)(2,1)S(1)}, bf16[2,2,16,512]{3,2,1,0:T(8,128)(2,1)S(1)}) custom-call(s32[3,1,128]{2,1,0:T(1,128)} %bitcast.19, s32[1]{0:T(128)S(6)} %copy.8.count_ref, f32[4,2040,128]{2,1,0:T(8,128)} %bitcast.14), custom_call_target="tpu_custom_call" | custom-call | tf_op jit(solution)/shard_map/pack/pallas_call | solution.py:448
  2.6 0.5 collective-permute-start
  3.1 2.6 %collective-permute-start.1 = (bf16[2,2,16,512]{3,2,1,0:T(8,128)(2,1)S(1)}, bf16[2,2,16,512]{3,2,1,0:T(8,128)(2,1)S(1)}, u32[]{:S(2)}, u32[]{:S(2)}) collective-permute-start(bf16[2,2,16,512]{3,2,1,0:T(8,128)(2,1)S(1)} %get-tuple-element.49), channel_id=1, source_target_pairs={{0,2},{1,3},{2,0},{3,1},{4,6},{5,7},{6,4},{7,5},{8,10},{9,11},{10,... | collective-permute-start | bytes 196616 | tf_op jit(solution)/shard_map/ppermute | solution.py:414
  5.7 0.1 collective-permute-start.2
  5.8 3.3 %gram.1 = (f32[8,8,8,128]{3,2,1,0:T(8,128)S(1)}, f32[4,2048,128]{2,1,0:T(8,128)S(1)}, f32[256,4,128]{2,1,0:T(4,128)S(1)}) custom-call(f32[4,2040,128]{2,1,0:T(8,128)} %bitcast.15, f32[255,4,128]{2,1,0:T(4,128)} %bitcast.18), custom_call_target="tpu_custom_call" | custom-call | tf_op jit(solution)/shard_map/gram/pallas_call | solution.py:467
  9.1 0.0 collective-permute-done.refs_1_
  9.1 0.0 collective-permute-done.1.refs_2_
  9.1 0.6 %collective-permute-done.2.refs_3_ = bf16[2,2,16,512]{3,2,1,0:T(8,128)(2,1)S(1)} collective-permute-done((bf16[2,2,16,512]{3,2,1,0:T(8,128)(2,1)S(1)}, bf16[2,2,16,512]{3,2,1,0:T(8,128)(2,1)S(1)}, u32[]{:S(2)}, u32[]{:S(2)}) %collective-permute-start.2) | collective-permute-done | bytes 65568 | tf_op jit(solution)/shard_map/ppermute | solution.py:414
  9.8 1.3 %collective-permute-start.4 = (bf16[4,2,2,16,512]{4,3,2,1,0:T(8,128)(2,1)S(1)}, bf16[4,2,2,16,512]{4,3,2,1,0:T(8,128)(2,1)S(1)}, u32[]{:S(2)}, u32[]{:S(2)}) collective-permute-start(bf16[4,2,2,16,512]{4,3,2,1,0:T(8,128)(2,1)S(1)} %join.1.own_ref), channel_id=1, source_target_pairs={{4,0},{8,4},{12,8},{16,12},{20,16},{24,20},{28,24},{5,1},{9,5},{13... | collective-permute-start | bytes 786440 | tf_op jit(solution)/shard_map/ppermute | solution.py:422
  11.1 4.7 %collective-permute-start.3 = (bf16[4,2,2,16,512]{4,3,2,1,0:T(8,128)(2,1)S(1)}, bf16[4,2,2,16,512]{4,3,2,1,0:T(8,128)(2,1)S(1)}, u32[]{:S(2)}, u32[]{:S(2)}) collective-permute-start(bf16[4,2,2,16,512]{4,3,2,1,0:T(8,128)(2,1)S(1)} %join.1.own_ref), channel_id=1, source_target_pairs={{0,4},{4,8},{8,12},{12,16},{16,20},{20,24},{24,28},{1,5},{5,9},{9,... | collective-permute-start | bytes 786440 | tf_op jit(solution)/shard_map/ppermute | solution.py:422
  15.8 0.8 %gram_end.1.gram_ref = f32[1,128]{1,0:T(1,128)S(1)} custom-call(f32[8,8,8,128]{3,2,1,0:T(8,128)S(1)} %get-tuple-element.61.products_ref, f32[4,2048,128]{2,1,0:T(8,128)S(1)} %get-tuple-element.45.blocks_ref), custom_call_target="tpu_custom_call" | custom-call | tf_op jit(solution)/shard_map/gram_end/pallas_call | solution.py:512
  16.6 8.8 %tables.1 = (bf16[8,512,512]{2,1,0:T(8,128)(2,1)S(1)}, bf16[8,1024,512]{2,1,0:T(8,128)(2,1)S(1)}) custom-call(bf16[8,510,2,510]{3,2,1,0:T(2,128)(2,1)} %bitcast.16, bf16[4080,510]{1,0:T(8,128)(2,1)} %bitcast.17), custom_call_target="tpu_custom_call" | custom-call | flops 2147483648 | bytes 25165824 | tf_op jit(solution)/shard_map/tables/pallas_call | solution.py:494
  25.4 0.0 collective-permute-done.4.above_ref
  25.4 0.2 collective-permute-done.3.below_ref
  25.6 9.5 %field.1 = (bf16[2,2,16,512]{3,2,1,0:T(8,128)(2,1)S(1)}, bf16[2,2,16,512]{3,2,1,0:T(8,128)(2,1)S(1)}, bf16[2,2,16,512]{3,2,1,0:T(8,128)(2,1)S(1)}, bf16[2,2,16,512]{3,2,1,0:T(8,128)(2,1)S(1)}) custom-call(bf16[8,512,512]{2,1,0:T(8,128)(2,1)S(1)} %get-tuple-element.63.rot_ref, bf16[8,1024,512]{2,1,0:T(8,128)(2,1)S(1)} %get-tuple-element.64.axial_ref, ...), custom_call_target="tpu_custom_call" | custom-call | tf_op jit(solution)/shard_map/field/pallas_call | solution.py:524
  35.1 0.1 collective-permute-start.5
  35.2 1.5 %collective-permute-start.6 = (bf16[2,2,16,512]{3,2,1,0:T(8,128)(2,1)S(1)}, bf16[2,2,16,512]{3,2,1,0:T(8,128)(2,1)S(1)}, u32[]{:S(2)}, u32[]{:S(2)}) collective-permute-start(bf16[2,2,16,512]{3,2,1,0:T(8,128)(2,1)S(1)} %get-tuple-element.70), channel_id=1, source_target_pairs={{0,2},{1,3},{2,0},{3,1},{4,6},{5,7},{6,4},{7,5},{8,10},{9,11},{10,... | collective-permute-start | bytes 196616 | tf_op jit(solution)/shard_map/ppermute | solution.py:414
  36.7 0.3 collective-permute-start.7
  37.0 0.0 collective-permute-done.5.rest_1_
  37.0 2.6 %collective-permute-done.6.rest_2_ = bf16[2,2,16,512]{3,2,1,0:T(8,128)(2,1)S(1)} collective-permute-done((bf16[2,2,16,512]{3,2,1,0:T(8,128)(2,1)S(1)}, bf16[2,2,16,512]{3,2,1,0:T(8,128)(2,1)S(1)}, u32[]{:S(2)}, u32[]{:S(2)}) %collective-permute-start.6) | collective-permute-done | bytes 65568 | tf_op jit(solution)/shard_map/ppermute | solution.py:414
  39.7 1.1 %collective-permute-done.7.rest_3_ = bf16[2,2,16,512]{3,2,1,0:T(8,128)(2,1)S(1)} collective-permute-done((bf16[2,2,16,512]{3,2,1,0:T(8,128)(2,1)S(1)}, bf16[2,2,16,512]{3,2,1,0:T(8,128)(2,1)S(1)}, u32[]{:S(2)}, u32[]{:S(2)}) %collective-permute-start.7) | collective-permute-done | bytes 65568 | tf_op jit(solution)/shard_map/ppermute | solution.py:414
  40.7 1.4 %image.1 = (f32[1024,128]{1,0:T(8,128)S(1)}, f32[32,1,128]{2,1,0:T(1,128)S(1)}) custom-call(f32[4,2048,128]{2,1,0:T(8,128)S(1)} %get-tuple-element.45.blocks_ref, f32[256,4,128]{2,1,0:T(4,128)S(1)} %get-tuple-element.46.mie_ref, f32[1,128]{1,0:T(1,128)S(1)} %gram_end.1.gram_ref, bf16[2,2,16,512]{3,2,1,0:T(8,128)(2,1)S(1)} %get-tuple-element.68.rest_0_, ...), custom_call_target="tpu_custom_call" | custom-call | tf_op jit(solution)/shard_map/image/pallas_call | solution.py:535
  42.2 12.6 %all_to_all.5.sums_ref = f32[32,1,128]{2,1,0:T(1,128)S(1)} all-to-all(f32[32,1,128]{2,1,0:T(1,128)S(1)} %get-tuple-element.72), channel_id=1, replica_groups=mesh['blk'=8,'pair'=4] {'blk','pair'}, dimensions={0} | all-to-all | bytes 32768 | tf_op jit(solution)/shard_map/all_to_all | solution.py:544
  54.8 1.7 %remainder.1 = (f32[2,8]{1,0:T(2,128)}, f32[255,4,128]{2,1,0:T(4,128)}) custom-call(f32[32,1,128]{2,1,0:T(1,128)S(1)} %all_to_all.5.sums_ref, f32[4,2048,128]{2,1,0:T(8,128)S(1)} %get-tuple-element.45.blocks_ref, f32[1024,128]{1,0:T(8,128)S(1)} %get-tuple-element.73.image_ref), custom_call_target="tpu_custom_call" | custom-call | tf_op jit(solution)/shard_map/remainder/pallas_call | solution.py:547
  (1 shorter events, 0.0 us)
Async XLA Ops:
  2.6 6.5 %collective-permute-start = (bf16[2,2,16,512]{3,2,1,0:T(8,128)(2,1)S(1)}, bf16[2,2,16,512]{3,2,1,0:T(8,128)(2,1)S(1)}, u32[]{:S(2)}, u32[]{:S(2)}) collective-permute-start(bf16[2,2,16,512]{3,2,1,0:T(8,128)(2,1)S(1)} %get-tuple-element.48), channel_id=1, source_target_pairs={{0,1},{1,0},{2,3},{3,2},{4,5},{5,4},{6,7},{7,6},{8,9},{9,8},{10,11... | collective-permute-start | bytes 196616 | tf_op jit(solution)/shard_map/ppermute | solution.py:414
  3.1 6.0 %collective-permute-start.1 = (bf16[2,2,16,512]{3,2,1,0:T(8,128)(2,1)S(1)}, bf16[2,2,16,512]{3,2,1,0:T(8,128)(2,1)S(1)}, u32[]{:S(2)}, u32[]{:S(2)}) collective-permute-start(bf16[2,2,16,512]{3,2,1,0:T(8,128)(2,1)S(1)} %get-tuple-element.49), channel_id=1, source_target_pairs={{0,2},{1,3},{2,0},{3,1},{4,6},{5,7},{6,4},{7,5},{8,10},{9,11},{10,... | collective-permute-start | bytes 196616 | tf_op jit(solution)/shard_map/ppermute | solution.py:414
  5.7 4.0 %collective-permute-start.2 = (bf16[2,2,16,512]{3,2,1,0:T(8,128)(2,1)S(1)}, bf16[2,2,16,512]{3,2,1,0:T(8,128)(2,1)S(1)}, u32[]{:S(2)}, u32[]{:S(2)}) collective-permute-start(bf16[2,2,16,512]{3,2,1,0:T(8,128)(2,1)S(1)} %get-tuple-element.50), channel_id=1, source_target_pairs={{0,3},{1,2},{2,1},{3,0},{4,7},{5,6},{6,5},{7,4},{8,11},{9,10},{10,... | collective-permute-start | bytes 196616 | tf_op jit(solution)/shard_map/ppermute | solution.py:414
  9.8 15.6 %collective-permute-start.4 = (bf16[4,2,2,16,512]{4,3,2,1,0:T(8,128)(2,1)S(1)}, bf16[4,2,2,16,512]{4,3,2,1,0:T(8,128)(2,1)S(1)}, u32[]{:S(2)}, u32[]{:S(2)}) collective-permute-start(bf16[4,2,2,16,512]{4,3,2,1,0:T(8,128)(2,1)S(1)} %join.1.own_ref), channel_id=1, source_target_pairs={{4,0},{8,4},{12,8},{16,12},{20,16},{24,20},{28,24},{5,1},{9,5},{13... | collective-permute-start | bytes 786440 | tf_op jit(solution)/shard_map/ppermute | solution.py:422
  11.1 14.5 %collective-permute-start.3 = (bf16[4,2,2,16,512]{4,3,2,1,0:T(8,128)(2,1)S(1)}, bf16[4,2,2,16,512]{4,3,2,1,0:T(8,128)(2,1)S(1)}, u32[]{:S(2)}, u32[]{:S(2)}) collective-permute-start(bf16[4,2,2,16,512]{4,3,2,1,0:T(8,128)(2,1)S(1)} %join.1.own_ref), channel_id=1, source_target_pairs={{0,4},{4,8},{8,12},{12,16},{16,20},{20,24},{24,28},{1,5},{5,9},{9,... | collective-permute-start | bytes 786440 | tf_op jit(solution)/shard_map/ppermute | solution.py:422
  35.1 1.9 %collective-permute-start.5 = (bf16[2,2,16,512]{3,2,1,0:T(8,128)(2,1)S(1)}, bf16[2,2,16,512]{3,2,1,0:T(8,128)(2,1)S(1)}, u32[]{:S(2)}, u32[]{:S(2)}) collective-permute-start(bf16[2,2,16,512]{3,2,1,0:T(8,128)(2,1)S(1)} %get-tuple-element.69), channel_id=1, source_target_pairs={{0,1},{1,0},{2,3},{3,2},{4,5},{5,4},{6,7},{7,6},{8,9},{9,8},{10,11... | collective-permute-start | bytes 196616 | tf_op jit(solution)/shard_map/ppermute | solution.py:414
  35.2 4.5 %collective-permute-start.6 = (bf16[2,2,16,512]{3,2,1,0:T(8,128)(2,1)S(1)}, bf16[2,2,16,512]{3,2,1,0:T(8,128)(2,1)S(1)}, u32[]{:S(2)}, u32[]{:S(2)}) collective-permute-start(bf16[2,2,16,512]{3,2,1,0:T(8,128)(2,1)S(1)} %get-tuple-element.70), channel_id=1, source_target_pairs={{0,2},{1,3},{2,0},{3,1},{4,6},{5,7},{6,4},{7,5},{8,10},{9,11},{10,... | collective-permute-start | bytes 196616 | tf_op jit(solution)/shard_map/ppermute | solution.py:414
  36.7 4.0 %collective-permute-start.7 = (bf16[2,2,16,512]{3,2,1,0:T(8,128)(2,1)S(1)}, bf16[2,2,16,512]{3,2,1,0:T(8,128)(2,1)S(1)}, u32[]{:S(2)}, u32[]{:S(2)}) collective-permute-start(bf16[2,2,16,512]{3,2,1,0:T(8,128)(2,1)S(1)} %get-tuple-element.71), channel_id=1, source_target_pairs={{0,3},{1,2},{2,1},{3,0},{4,7},{5,6},{6,5},{7,4},{8,11},{9,10},{10,... | collective-permute-start | bytes 196616 | tf_op jit(solution)/shard_map/ppermute | solution.py:414

commit v17 on v16

--- a/solution.py
+++ b/solution.py
@@ -88,27 +88,48 @@
         out_ref[lax.axis_index("pair") ^ i] = ref[...]
 
 
-def tables_kernel(axial_ref, rot_ref, rot_out_ref, axial_out_ref, axials_ref, rots_ref, sems):
-    tables, size, _ = rot_out_ref.shape
+def rotations_kernel(rot_ref, out_ref, rots_ref, sems):
+    tables, size, _ = out_ref.shape
+    listed, modes = rot_ref.shape
+    chunk = 256
+    copies = []
+    for i, first in enumerate(range(0, listed, 4 * chunk)):
+        here = pl.ds(first, min(4 * chunk, listed - first))
+        copies.append(pltpu.make_async_copy(rot_ref.at[here], rots_ref.at[here], sems.at[i]))
+        copies[-1].start()
+    out_row, in_row = iota((chunk, chunk), 0), iota((chunk, chunk), 1)
+    share = chunk // tables
+    entries = (in_row == tables * lax.rem(out_row, share) + lax.div(out_row, share)).astype(F32).astype(BF16)
+    out_ref[:, :, size - 128 : size] = jnp.zeros((tables, size, 128), BF16)
+    rots_ref[listed:, :] = jnp.zeros((rots_ref.shape[0] - listed, modes), BF16)
+
+    def pick(i, carry):
+        rows = rots_ref[pl.ds(pl.multiple_of(i * chunk, chunk), chunk), :]
+        sorted_rows = dot_nn(entries, rows).astype(BF16)
+        for g in range(tables):
+            here = pl.ds(pl.multiple_of(i * share, share), share)
+            out_ref[g, here, 0:modes] = sorted_rows[g * share : (g + 1) * share]
+        return carry
+
+    for i, copy in enumerate(copies):
+        copy.wait()
+        lax.fori_loop(4 * i, min(4 * (i + 1), rots_ref.shape[0] // chunk), pick, 0)
+
+
+def axials_kernel(axial_ref, out_ref, axials_ref, sems):
+    tables, double, size = out_ref.shape
     modes = axial_ref.shape[1]
-    listed = rot_ref.shape[0]
 
     def fetch(g):
         return pltpu.make_async_copy(axial_ref.at[g], axials_ref.at[g], sems.at[g])
 
     for g in range(tables):
         fetch(g).start()
-    rot_copy = pltpu.make_async_copy(rot_ref, rots_ref.at[pl.ds(0, listed)], sems.at[tables])
-    rot_copy.start()
     chunk = 256
     out_row, in_row = iota((chunk, chunk), 0), iota((chunk, chunk), 1)
     each = chunk // 2
     halves = (in_row == 2 * lax.rem(out_row, each) + lax.div(out_row, each)).astype(F32).astype(BF16)
-    share = chunk // tables
-    entries = (in_row == tables * lax.rem(out_row, share) + lax.div(out_row, share)).astype(F32).astype(BF16)
-    for ref in (rot_out_ref, axial_out_ref):
-        ref[:, :, size - 128 : size] = jnp.zeros((tables, ref.shape[1], 128), BF16)
-    rots_ref[listed:, :] = jnp.zeros((rots_ref.shape[0] - listed, modes), BF16)
+    out_ref[:, :, size - 128 : size] = jnp.zeros((tables, double, 128), BF16)
 
     def split(g, carry):
         fetch(g).wait()
@@ -117,21 +138,10 @@
             rows = axials_ref[g, first : first + count].reshape(2 * count, modes)
             sorted_rows = dot_nn(halves[:, : 2 * count], rows).astype(BF16)
             for c in range(2):
-                axial_out_ref[g, c * size + first : c * size + first + each, 0:modes] = sorted_rows[c * each : (c + 1) * each]
+                out_ref[g, c * size + first : c * size + first + each, 0:modes] = sorted_rows[c * each : (c + 1) * each]
         return carry
 
     lax.fori_loop(0, tables, split, 0)
-    rot_copy.wait()
-
-    def pick(i, carry):
-        rows = rots_ref[pl.ds(pl.multiple_of(i * chunk, chunk), chunk), :]
-        sorted_rows = dot_nn(entries, rows).astype(BF16)
-        for g in range(tables):
-            here = pl.ds(pl.multiple_of(i * share, share), share)
-            rot_out_ref[g, here, 0:modes] = sorted_rows[g * share : (g + 1) * share]
-        return carry
-
-    lax.fori_loop(0, rots_ref.shape[0] // chunk, pick, 0)
 
 
 def swapped(value):
@@ -415,11 +425,9 @@
     return received
 
 
-def neighbours(value):
-    count = lax.axis_size("blk")
-    up = [(i, i + 1) for i in range(count - 1)]
-    down = [(j, i) for i, j in up]
-    return lax.ppermute(value, "blk", up), lax.ppermute(value, "blk", down)
+def from_neighbour(value, up):
+    pairs = [(i, i + 1) for i in range(lax.axis_size("blk") - 1)]
+    return lax.ppermute(value, "blk", pairs if up else [(j, i) for i, j in pairs])
 
 
 def shards(basis, mie_coeffs, rot_table, axial_table, pair_table, pair_count):
@@ -489,26 +497,8 @@
         compiler_params=params(4),
         name="join",
     )(*received)
-    below, above = neighbours(own_pieces)
-
-    rotations, axials = pl.pallas_call(
-        tables_kernel,
-        in_specs=[hbm()] * 2,
-        out_specs=[whole()] * 2,
-        out_shape=[
-            jax.ShapeDtypeStruct((tables, size, size), BF16),
-            jax.ShapeDtypeStruct((tables, 2 * size, size), BF16),
-        ],
-        scratch_shapes=[
-            pltpu.VMEM(axial_rows.shape, BF16),
-            pltpu.VMEM((tables * size, modes), BF16),
-            pltpu.SemaphoreType.DMA((tables + 1,)),
-        ],
-        compiler_params=params(20),
-        cost_estimate=pl.CostEstimate(flops=tables * 8 * 256 * 256 * size, bytes_accessed=6 * tables * size * size * 2, transcendentals=0),
-        name="tables",
-    )(axial_rows, rot_rows)
-    own_pieces, products = lax.optimization_barrier((own_pieces, products))
+    own_pieces, products, rot_rows = lax.optimization_barrier((own_pieces, products, rot_rows))
+    above = from_neighbour(own_pieces, False)
     line = pl.pallas_call(
         functools.partial(gram_end_kernel, quarter, modes),
         in_specs=[whole()] * 2,
@@ -518,7 +508,31 @@
         compiler_params=params(4),
         name="gram_end",
     )(products, blocks)
-    below, above, rotations, axials, line = lax.optimization_barrier((below, above, rotations, axials, line))
+    rotations = pl.pallas_call(
+        rotations_kernel,
+        in_specs=[hbm()],
+        out_specs=whole(),
+        out_shape=jax.ShapeDtypeStruct((tables, size, size), BF16),
+        scratch_shapes=[
+            pltpu.VMEM((tables * size, modes), BF16),
+            pltpu.SemaphoreType.DMA((rounded_up(modes * tables, 1024) // 1024,)),
+        ],
+        compiler_params=params(8),
+        name="rotations",
+    )(rot_rows)
+    own_pieces, line, rotations, axial_rows = lax.optimization_barrier((own_pieces, line, rotations, axial_rows))
+    below = from_neighbour(own_pieces, True)
+    axials = pl.pallas_call(
+        axials_kernel,
+        in_specs=[hbm()],
+        out_specs=whole(),
+        out_shape=jax.ShapeDtypeStruct((tables, 2 * size, size), BF16),
+        scratch_shapes=[pltpu.VMEM(axial_rows.shape, BF16), pltpu.SemaphoreType.DMA((tables,))],
+        compiler_params=params(16),
+        cost_estimate=pl.CostEstimate(flops=tables * 8 * 256 * 256 * size, bytes_accessed=4 * tables * size * size * 2, transcendentals=0),
+        name="axials",
+    )(axial_rows)
+    below, above, axials = lax.optimization_barrier((below, above, axials))
 
     together = tables
     field = pl.pallas_call(

time: 56.7 us -> 60 us (1.058)
  blocking collectives: 12.6 us -> 14.4 us
  Pallas kernels: 26.8 us -> 28.1 us
    all_to_all x1, blocking collectives: 12.6 us -> 14.4 us  [shards(): lax.all_to_all(sums, ('blk', 'pair'), split_axis=0, concat_axis=0, tiled=...]
    pallas_call x1 -> x2, Pallas kernels: 8.76 us -> 9.97 us  [the longest x1 5.02 us: shards(): pl.pallas_call(rotations_kernel, in_specs=[hbm()], out_specs=whole(), out...]
  transfers between devices with their start and end apart: 8 -> 8, of which waited for: 4 -> 4; matrix products, arithmetic and copies ran while one was open for 0% -> 0% of each run, Pallas kernels for 23% -> 24%
where the time goes in v17:
time: 60 us; the launch traced here: 59.7 us
  Pallas kernels  28.1 us (47%)
  blocking collectives  14.4 us (24%)
  starting transfers between devices  11.1 us (18%)
  waiting for transfers between devices  4.8 us (8%)
  between operations  1.38 us (2%)
    all_to_all x1, blocking collectives, shards(): lax.all_to_all(sums, ('blk', 'pair'), split_axis=0, concat_axis=0, tiled=...  14.4 us
    pallas_call x1, Pallas kernels, shards(): pl.pallas_call(functools.partial(field_kernel, own, modes, together), in_...  9.51 us
    ppermute x2, starting transfers between devices, from_neighbour(): lax.ppermute(value, 'blk', pairs if up else [(j, i) for i, j in pairs])  5.97 us
    ppermute x6, starting transfers between devices, exchanged(): lax.ppermute(pieces[i], axis, [(p, p ^ i) for p in range(count)])  5.08 us
    pallas_call x1, Pallas kernels, shards(): pl.pallas_call(rotations_kernel, in_specs=[hbm()], out_specs=whole(), out...  5.02 us
    pallas_call x1, Pallas kernels, shards(): pl.pallas_call(axials_kernel, in_specs=[hbm()], out_specs=whole(), out_sh...  4.95 us
    ppermute x6, waiting for transfers between devices, exchanged(): lax.ppermute(pieces[i], axis, [(p, p ^ i) for p in range(count)])  4.36 us
    pallas_call x1, Pallas kernels, shards(): pl.pallas_call(functools.partial(gram_kernel, quarter, modes), in_specs=[...  3.35 us
  transfers between devices with their start and end apart: 8, of which 4 were waited for; matrix products, arithmetic and copies ran while one was open for 0% of the time, Pallas kernels for 24%

profile of v17, /device:TPU:0, one launch (start us, length us, event | category | flops | bytes accessed | tf_op | source)
XLA Modules:
  0.0 59.7 jit_solution(8106228426152005005)
XLA Ops:
  1.3 1.3 %pack.1 = (bf16[2,2,16,512]{3,2,1,0:T(8,128)(2,1)S(1)}, bf16[2,2,16,512]{3,2,1,0:T(8,128)(2,1)S(1)}, bf16[2,2,16,512]{3,2,1,0:T(8,128)(2,1)S(1)}, bf16[2,2,16,512]{3,2,1,0:T(8,128)(2,1)S(1)}) custom-call(s32[3,1,128]{2,1,0:T(1,128)} %bitcast.19, s32[1]{0:T(128)S(6)} %copy.8.count_ref, f32[4,2040,128]{2,1,0:T(8,128)} %bitcast.14), custom_call_target="tpu_custom_call" | custom-call | tf_op jit(solution)/shard_map/pack/pallas_call | solution.py:456
  2.6 0.5 collective-permute-start
  3.1 2.6 %collective-permute-start.1 = (bf16[2,2,16,512]{3,2,1,0:T(8,128)(2,1)S(1)}, bf16[2,2,16,512]{3,2,1,0:T(8,128)(2,1)S(1)}, u32[]{:S(2)}, u32[]{:S(2)}) collective-permute-start(bf16[2,2,16,512]{3,2,1,0:T(8,128)(2,1)S(1)} %get-tuple-element.50), channel_id=1, source_target_pairs={{0,2},{1,3},{2,0},{3,1},{4,6},{5,7},{6,4},{7,5},{8,10},{9,11},{10,... | collective-permute-start | bytes 196616 | tf_op jit(solution)/shard_map/ppermute | solution.py:424
  5.7 0.1 collective-permute-start.2
  5.8 3.3 %gram.1 = (f32[8,8,8,128]{3,2,1,0:T(8,128)S(1)}, f32[4,2048,128]{2,1,0:T(8,128)S(1)}, f32[256,4,128]{2,1,0:T(4,128)S(1)}) custom-call(f32[4,2040,128]{2,1,0:T(8,128)} %bitcast.15, f32[255,4,128]{2,1,0:T(4,128)} %bitcast.18), custom_call_target="tpu_custom_call" | custom-call | tf_op jit(solution)/shard_map/gram/pallas_call | solution.py:475
  9.1 0.0 collective-permute-done.refs_1_
  9.1 0.0 collective-permute-done.1.refs_2_
  9.1 0.6 %collective-permute-done.2.refs_3_ = bf16[2,2,16,512]{3,2,1,0:T(8,128)(2,1)S(1)} collective-permute-done((bf16[2,2,16,512]{3,2,1,0:T(8,128)(2,1)S(1)}, bf16[2,2,16,512]{3,2,1,0:T(8,128)(2,1)S(1)}, u32[]{:S(2)}, u32[]{:S(2)}) %collective-permute-start.2) | collective-permute-done | bytes 65568 | tf_op jit(solution)/shard_map/ppermute | solution.py:424
  9.8 1.3 %collective-permute-start.4 = (bf16[4,2,2,16,512]{4,3,2,1,0:T(8,128)(2,1)S(1)}, bf16[4,2,2,16,512]{4,3,2,1,0:T(8,128)(2,1)S(1)}, u32[]{:S(2)}, u32[]{:S(2)}) collective-permute-start(bf16[4,2,2,16,512]{4,3,2,1,0:T(8,128)(2,1)S(1)} %join.1.own_ref), channel_id=1, source_target_pairs={{4,0},{8,4},{12,8},{16,12},{20,16},{24,20},{28,24},{5,1},{9,5},{13... | collective-permute-start | bytes 786440 | tf_op jit(solution)/shard_map/ppermute | solution.py:430
  11.1 5.0 %rotations.1.rot_ref = bf16[8,512,512]{2,1,0:T(8,128)(2,1)S(1)} custom-call(bf16[4080,510]{1,0:T(8,128)(2,1)} %bitcast.17), custom_call_target="tpu_custom_call" | custom-call | tf_op jit(solution)/shard_map/rotations/pallas_call | solution.py:511
  16.1 0.8 %gram_end.1.gram_ref = f32[1,128]{1,0:T(1,128)S(1)} custom-call(f32[8,8,8,128]{3,2,1,0:T(8,128)S(1)} %get-tuple-element.60.products_ref, f32[4,2048,128]{2,1,0:T(8,128)S(1)} %get-tuple-element.46.blocks_ref), custom_call_target="tpu_custom_call" | custom-call | tf_op jit(solution)/shard_map/gram_end/pallas_call | solution.py:502
  16.9 4.7 %collective-permute-start.3 = (bf16[4,2,2,16,512]{4,3,2,1,0:T(8,128)(2,1)S(1)}, bf16[4,2,2,16,512]{4,3,2,1,0:T(8,128)(2,1)S(1)}, u32[]{:S(2)}, u32[]{:S(2)}) collective-permute-start(bf16[4,2,2,16,512]{4,3,2,1,0:T(8,128)(2,1)S(1)} %join.1.own_ref), channel_id=1, source_target_pairs={{0,4},{4,8},{8,12},{12,16},{16,20},{20,24},{24,28},{1,5},{5,9},{9,... | collective-permute-start | bytes 786440 | tf_op jit(solution)/shard_map/ppermute | solution.py:430
  21.6 4.9 %axials.1.axial_ref = bf16[8,1024,512]{2,1,0:T(8,128)(2,1)S(1)} custom-call(bf16[8,510,2,510]{3,2,1,0:T(2,128)(2,1)} %bitcast.16), custom_call_target="tpu_custom_call" | custom-call | flops 2147483648 | bytes 16777216 | tf_op jit(solution)/shard_map/axials/pallas_call | solution.py:525
  26.5 0.0 collective-permute-done.4.above_ref
  26.5 0.4 collective-permute-done.3.below_ref
  27.0 9.5 %field.1 = (bf16[2,2,16,512]{3,2,1,0:T(8,128)(2,1)S(1)}, bf16[2,2,16,512]{3,2,1,0:T(8,128)(2,1)S(1)}, bf16[2,2,16,512]{3,2,1,0:T(8,128)(2,1)S(1)}, bf16[2,2,16,512]{3,2,1,0:T(8,128)(2,1)S(1)}) custom-call(bf16[8,512,512]{2,1,0:T(8,128)(2,1)S(1)} %rotations.1.rot_ref, bf16[8,1024,512]{2,1,0:T(8,128)(2,1)S(1)} %axials.1.axial_ref, ...), custom_call_target="tpu_custom_call" | custom-call | tf_op jit(solution)/shard_map/field/pallas_call | solution.py:538
  36.5 0.1 collective-permute-start.5
  36.6 1.6 %collective-permute-start.6 = (bf16[2,2,16,512]{3,2,1,0:T(8,128)(2,1)S(1)}, bf16[2,2,16,512]{3,2,1,0:T(8,128)(2,1)S(1)}, u32[]{:S(2)}, u32[]{:S(2)}) collective-permute-start(bf16[2,2,16,512]{3,2,1,0:T(8,128)(2,1)S(1)} %get-tuple-element.72), channel_id=1, source_target_pairs={{0,2},{1,3},{2,0},{3,1},{4,6},{5,7},{6,4},{7,5},{8,10},{9,11},{10,... | collective-permute-start | bytes 196616 | tf_op jit(solution)/shard_map/ppermute | solution.py:424
  38.1 0.3 collective-permute-start.7
  38.4 0.0 collective-permute-done.5.rest_1_
  38.4 2.6 %collective-permute-done.6.rest_2_ = bf16[2,2,16,512]{3,2,1,0:T(8,128)(2,1)S(1)} collective-permute-done((bf16[2,2,16,512]{3,2,1,0:T(8,128)(2,1)S(1)}, bf16[2,2,16,512]{3,2,1,0:T(8,128)(2,1)S(1)}, u32[]{:S(2)}, u32[]{:S(2)}) %collective-permute-start.6) | collective-permute-done | bytes 65568 | tf_op jit(solution)/shard_map/ppermute | solution.py:424
  41.1 1.1 %collective-permute-done.7.rest_3_ = bf16[2,2,16,512]{3,2,1,0:T(8,128)(2,1)S(1)} collective-permute-done((bf16[2,2,16,512]{3,2,1,0:T(8,128)(2,1)S(1)}, bf16[2,2,16,512]{3,2,1,0:T(8,128)(2,1)S(1)}, u32[]{:S(2)}, u32[]{:S(2)}) %collective-permute-start.7) | collective-permute-done | bytes 65568 | tf_op jit(solution)/shard_map/ppermute | solution.py:424
  42.2 1.4 %image.1 = (f32[1024,128]{1,0:T(8,128)S(1)}, f32[32,1,128]{2,1,0:T(1,128)S(1)}) custom-call(f32[4,2048,128]{2,1,0:T(8,128)S(1)} %get-tuple-element.46.blocks_ref, f32[256,4,128]{2,1,0:T(4,128)S(1)} %get-tuple-element.47.mie_ref, f32[1,128]{1,0:T(1,128)S(1)} %gram_end.1.gram_ref, bf16[2,2,16,512]{3,2,1,0:T(8,128)(2,1)S(1)} %get-tuple-element.70.rest_0_, ...), custom_call_target="tpu_custom_call" | custom-call | tf_op jit(solution)/shard_map/image/pallas_call | solution.py:549
  43.6 14.4 %all_to_all.5.sums_ref = f32[32,1,128]{2,1,0:T(1,128)S(1)} all-to-all(f32[32,1,128]{2,1,0:T(1,128)S(1)} %get-tuple-element.74), channel_id=1, replica_groups=mesh['blk'=8,'pair'=4] {'blk','pair'}, dimensions={0} | all-to-all | bytes 32768 | tf_op jit(solution)/shard_map/all_to_all | solution.py:558
  58.1 1.7 %remainder.1 = (f32[2,8]{1,0:T(2,128)}, f32[255,4,128]{2,1,0:T(4,128)}) custom-call(f32[32,1,128]{2,1,0:T(1,128)S(1)} %all_to_all.5.sums_ref, f32[4,2048,128]{2,1,0:T(8,128)S(1)} %get-tuple-element.46.blocks_ref, f32[1024,128]{1,0:T(8,128)S(1)} %get-tuple-element.75.image_ref), custom_call_target="tpu_custom_call" | custom-call | tf_op jit(solution)/shard_map/remainder/pallas_call | solution.py:561
  (1 shorter events, 0.0 us)
Async XLA Ops:
  2.6 6.5 %collective-permute-start = (bf16[2,2,16,512]{3,2,1,0:T(8,128)(2,1)S(1)}, bf16[2,2,16,512]{3,2,1,0:T(8,128)(2,1)S(1)}, u32[]{:S(2)}, u32[]{:S(2)}) collective-permute-start(bf16[2,2,16,512]{3,2,1,0:T(8,128)(2,1)S(1)} %get-tuple-element.49), channel_id=1, source_target_pairs={{0,1},{1,0},{2,3},{3,2},{4,5},{5,4},{6,7},{7,6},{8,9},{9,8},{10,11... | collective-permute-start | bytes 196616 | tf_op jit(solution)/shard_map/ppermute | solution.py:424
  3.1 6.0 %collective-permute-start.1 = (bf16[2,2,16,512]{3,2,1,0:T(8,128)(2,1)S(1)}, bf16[2,2,16,512]{3,2,1,0:T(8,128)(2,1)S(1)}, u32[]{:S(2)}, u32[]{:S(2)}) collective-permute-start(bf16[2,2,16,512]{3,2,1,0:T(8,128)(2,1)S(1)} %get-tuple-element.50), channel_id=1, source_target_pairs={{0,2},{1,3},{2,0},{3,1},{4,6},{5,7},{6,4},{7,5},{8,10},{9,11},{10,... | collective-permute-start | bytes 196616 | tf_op jit(solution)/shard_map/ppermute | solution.py:424
  5.7 4.0 %collective-permute-start.2 = (bf16[2,2,16,512]{3,2,1,0:T(8,128)(2,1)S(1)}, bf16[2,2,16,512]{3,2,1,0:T(8,128)(2,1)S(1)}, u32[]{:S(2)}, u32[]{:S(2)}) collective-permute-start(bf16[2,2,16,512]{3,2,1,0:T(8,128)(2,1)S(1)} %get-tuple-element.51), channel_id=1, source_target_pairs={{0,3},{1,2},{2,1},{3,0},{4,7},{5,6},{6,5},{7,4},{8,11},{9,10},{10,... | collective-permute-start | bytes 196616 | tf_op jit(solution)/shard_map/ppermute | solution.py:424
  9.8 16.8 %collective-permute-start.4 = (bf16[4,2,2,16,512]{4,3,2,1,0:T(8,128)(2,1)S(1)}, bf16[4,2,2,16,512]{4,3,2,1,0:T(8,128)(2,1)S(1)}, u32[]{:S(2)}, u32[]{:S(2)}) collective-permute-start(bf16[4,2,2,16,512]{4,3,2,1,0:T(8,128)(2,1)S(1)} %join.1.own_ref), channel_id=1, source_target_pairs={{4,0},{8,4},{12,8},{16,12},{20,16},{24,20},{28,24},{5,1},{9,5},{13... | collective-permute-start | bytes 786440 | tf_op jit(solution)/shard_map/ppermute | solution.py:430
  16.9 10.1 %collective-permute-start.3 = (bf16[4,2,2,16,512]{4,3,2,1,0:T(8,128)(2,1)S(1)}, bf16[4,2,2,16,512]{4,3,2,1,0:T(8,128)(2,1)S(1)}, u32[]{:S(2)}, u32[]{:S(2)}) collective-permute-start(bf16[4,2,2,16,512]{4,3,2,1,0:T(8,128)(2,1)S(1)} %join.1.own_ref), channel_id=1, source_target_pairs={{0,4},{4,8},{8,12},{12,16},{16,20},{20,24},{24,28},{1,5},{5,9},{9,... | collective-permute-start | bytes 786440 | tf_op jit(solution)/shard_map/ppermute | solution.py:430
  36.5 1.9 %collective-permute-start.5 = (bf16[2,2,16,512]{3,2,1,0:T(8,128)(2,1)S(1)}, bf16[2,2,16,512]{3,2,1,0:T(8,128)(2,1)S(1)}, u32[]{:S(2)}, u32[]{:S(2)}) collective-permute-start(bf16[2,2,16,512]{3,2,1,0:T(8,128)(2,1)S(1)} %get-tuple-element.71), channel_id=1, source_target_pairs={{0,1},{1,0},{2,3},{3,2},{4,5},{5,4},{6,7},{7,6},{8,9},{9,8},{10,11... | collective-permute-start | bytes 196616 | tf_op jit(solution)/shard_map/ppermute | solution.py:424
  36.6 4.5 %collective-permute-start.6 = (bf16[2,2,16,512]{3,2,1,0:T(8,128)(2,1)S(1)}, bf16[2,2,16,512]{3,2,1,0:T(8,128)(2,1)S(1)}, u32[]{:S(2)}, u32[]{:S(2)}) collective-permute-start(bf16[2,2,16,512]{3,2,1,0:T(8,128)(2,1)S(1)} %get-tuple-element.72), channel_id=1, source_target_pairs={{0,2},{1,3},{2,0},{3,1},{4,6},{5,7},{6,4},{7,5},{8,10},{9,11},{10,... | collective-permute-start | bytes 196616 | tf_op jit(solution)/shard_map/ppermute | solution.py:424
  38.1 4.0 %collective-permute-start.7 = (bf16[2,2,16,512]{3,2,1,0:T(8,128)(2,1)S(1)}, bf16[2,2,16,512]{3,2,1,0:T(8,128)(2,1)S(1)}, u32[]{:S(2)}, u32[]{:S(2)}) collective-permute-start(bf16[2,2,16,512]{3,2,1,0:T(8,128)(2,1)S(1)} %get-tuple-element.73), channel_id=1, source_target_pairs={{0,3},{1,2},{2,1},{3,0},{4,7},{5,6},{6,5},{7,4},{8,11},{9,10},{10,... | collective-permute-start | bytes 196616 | tf_op jit(solution)/shard_map/ppermute | solution.py:424

commit v18 on v17

--- a/solution.py
+++ b/solution.py
@@ -103,17 +103,14 @@
     out_ref[:, :, size - 128 : size] = jnp.zeros((tables, size, 128), BF16)
     rots_ref[listed:, :] = jnp.zeros((rots_ref.shape[0] - listed, modes), BF16)
 
-    def pick(i, carry):
-        rows = rots_ref[pl.ds(pl.multiple_of(i * chunk, chunk), chunk), :]
-        sorted_rows = dot_nn(entries, rows).astype(BF16)
-        for g in range(tables):
-            here = pl.ds(pl.multiple_of(i * share, share), share)
-            out_ref[g, here, 0:modes] = sorted_rows[g * share : (g + 1) * share]
-        return carry
-
     for i, copy in enumerate(copies):
         copy.wait()
-        lax.fori_loop(4 * i, min(4 * (i + 1), rots_ref.shape[0] // chunk), pick, 0)
+        chunks = range(4 * i, min(4 * (i + 1), rots_ref.shape[0] // chunk))
+        rows = [rots_ref[q * chunk : (q + 1) * chunk, :] for q in chunks]
+        results = [dot_nn(entries, value).astype(BF16) for value in rows]
+        for q, result in zip(chunks, results):
+            for g in range(tables):
+                out_ref[g, q * share : (q + 1) * share, 0:modes] = result[g * share : (g + 1) * share]
 
 
 def axials_kernel(axial_ref, out_ref, axials_ref, sems):
@@ -131,17 +128,24 @@
     halves = (in_row == 2 * lax.rem(out_row, each) + lax.div(out_row, each)).astype(F32).astype(BF16)
     out_ref[:, :, size - 128 : size] = jnp.zeros((tables, double, 128), BF16)
 
-    def split(g, carry):
-        fetch(g).wait()
-        for first in range(0, modes, each):
+    together = 2 if tables % 2 == 0 else 1
+
+    def split(step, carry):
+        entries = [step * together + i for i in range(together)]
+        for g in entries:
+            fetch(g).wait()
+        places = [(g, first) for g in entries for first in range(0, modes, each)]
+        results = []
+        for g, first in places:
             count = min(each, modes - first)
             rows = axials_ref[g, first : first + count].reshape(2 * count, modes)
-            sorted_rows = dot_nn(halves[:, : 2 * count], rows).astype(BF16)
+            results.append(dot_nn(halves[:, : 2 * count], rows).astype(BF16))
+        for (g, first), result in zip(places, results):
             for c in range(2):
-                out_ref[g, c * size + first : c * size + first + each, 0:modes] = sorted_rows[c * each : (c + 1) * each]
+                out_ref[g, c * size + first : c * size + first + each, 0:modes] = result[c * each : (c + 1) * each]
         return carry
 
-    lax.fori_loop(0, tables, split, 0)
+    lax.fori_loop(0, tables // together, split, 0)
 
 
 def swapped(value):

time: 60 us -> 58 us (0.967)
  Pallas kernels: 28.1 us -> 25.7 us
  waiting for transfers between devices: 4.8 us -> 5.67 us
    pallas_call x1, Pallas kernels: 5.02 us -> 3.02 us  [shards(): pl.pallas_call(rotations_kernel, in_specs=[hbm()], out_specs=whole(), out...]
    ppermute x2, waiting for transfers between devices: 0.44 us -> 1.36 us  [from_neighbour(): lax.ppermute(value, 'blk', pairs if up else [(j, i) for i, j in pairs])]
  transfers between devices with their start and end apart: 8 -> 8, of which waited for: 4 -> 4; matrix products, arithmetic and copies ran while one was open for 0% -> 0% of each run, Pallas kernels for 24% -> 20%
where the time goes in v18:
time: 58 us; the launch traced here: 57.8 us
  Pallas kernels  25.7 us (44%)
  blocking collectives  13.9 us (24%)
  starting transfers between devices  11.1 us (19%)
  waiting for transfers between devices  5.67 us (10%)
  between operations  1.38 us (2%)
    all_to_all x1, blocking collectives, shards(): lax.all_to_all(sums, ('blk', 'pair'), split_axis=0, concat_axis=0, tiled=...  13.9 us
    pallas_call x1, Pallas kernels, shards(): pl.pallas_call(functools.partial(field_kernel, own, modes, together), in_...  9.51 us
    ppermute x2, starting transfers between devices, from_neighbour(): lax.ppermute(value, 'blk', pairs if up else [(j, i) for i, j in pairs])  6.03 us
    ppermute x6, starting transfers between devices, exchanged(): lax.ppermute(pieces[i], axis, [(p, p ^ i) for p in range(count)])  5.08 us
    pallas_call x1, Pallas kernels, shards(): pl.pallas_call(axials_kernel, in_specs=[hbm()], out_specs=whole(), out_sh...  4.57 us
    ppermute x6, waiting for transfers between devices, exchanged(): lax.ppermute(pieces[i], axis, [(p, p ^ i) for p in range(count)])  4.31 us
    pallas_call x1, Pallas kernels, shards(): pl.pallas_call(functools.partial(gram_kernel, quarter, modes), in_specs=[...  3.35 us
    pallas_call x1, Pallas kernels, shards(): pl.pallas_call(rotations_kernel, in_specs=[hbm()], out_specs=whole(), out...  3.02 us
  transfers between devices with their start and end apart: 8, of which 4 were waited for; matrix products, arithmetic and copies ran while one was open for 0% of the time, Pallas kernels for 20%

profile of v18, /device:TPU:0, one launch (start us, length us, event | category | flops | bytes accessed | tf_op | source)
XLA Modules:
  0.0 57.8 jit_solution(5238662240624719884)
XLA Ops:
  1.3 1.3 %pack.1 = (bf16[2,2,16,512]{3,2,1,0:T(8,128)(2,1)S(1)}, bf16[2,2,16,512]{3,2,1,0:T(8,128)(2,1)S(1)}, bf16[2,2,16,512]{3,2,1,0:T(8,128)(2,1)S(1)}, bf16[2,2,16,512]{3,2,1,0:T(8,128)(2,1)S(1)}) custom-call(s32[3,1,128]{2,1,0:T(1,128)} %bitcast.19, s32[1]{0:T(128)S(6)} %copy.8.count_ref, f32[4,2040,128]{2,1,0:T(8,128)} %bitcast.14), custom_call_target="tpu_custom_call" | custom-call | tf_op jit(solution)/shard_map/pack/pallas_call | solution.py:460
  2.6 0.5 collective-permute-start
  3.1 2.6 %collective-permute-start.1 = (bf16[2,2,16,512]{3,2,1,0:T(8,128)(2,1)S(1)}, bf16[2,2,16,512]{3,2,1,0:T(8,128)(2,1)S(1)}, u32[]{:S(2)}, u32[]{:S(2)}) collective-permute-start(bf16[2,2,16,512]{3,2,1,0:T(8,128)(2,1)S(1)} %get-tuple-element.50), channel_id=1, source_target_pairs={{0,2},{1,3},{2,0},{3,1},{4,6},{5,7},{6,4},{7,5},{8,10},{9,11},{10,... | collective-permute-start | bytes 196616 | tf_op jit(solution)/shard_map/ppermute | solution.py:428
  5.7 0.1 collective-permute-start.2
  5.8 3.3 %gram.1 = (f32[8,8,8,128]{3,2,1,0:T(8,128)S(1)}, f32[4,2048,128]{2,1,0:T(8,128)S(1)}, f32[256,4,128]{2,1,0:T(4,128)S(1)}) custom-call(f32[4,2040,128]{2,1,0:T(8,128)} %bitcast.15, f32[255,4,128]{2,1,0:T(4,128)} %bitcast.18), custom_call_target="tpu_custom_call" | custom-call | tf_op jit(solution)/shard_map/gram/pallas_call | solution.py:479
  9.1 0.0 collective-permute-done.refs_1_
  9.1 0.0 collective-permute-done.1.refs_2_
  9.1 0.6 %collective-permute-done.2.refs_3_ = bf16[2,2,16,512]{3,2,1,0:T(8,128)(2,1)S(1)} collective-permute-done((bf16[2,2,16,512]{3,2,1,0:T(8,128)(2,1)S(1)}, bf16[2,2,16,512]{3,2,1,0:T(8,128)(2,1)S(1)}, u32[]{:S(2)}, u32[]{:S(2)}) %collective-permute-start.2) | collective-permute-done | bytes 65568 | tf_op jit(solution)/shard_map/ppermute | solution.py:428
  9.8 1.3 %collective-permute-start.4 = (bf16[4,2,2,16,512]{4,3,2,1,0:T(8,128)(2,1)S(1)}, bf16[4,2,2,16,512]{4,3,2,1,0:T(8,128)(2,1)S(1)}, u32[]{:S(2)}, u32[]{:S(2)}) collective-permute-start(bf16[4,2,2,16,512]{4,3,2,1,0:T(8,128)(2,1)S(1)} %join.1.own_ref), channel_id=1, source_target_pairs={{4,0},{8,4},{12,8},{16,12},{20,16},{24,20},{28,24},{5,1},{9,5},{13... | collective-permute-start | bytes 786440 | tf_op jit(solution)/shard_map/ppermute | solution.py:434
  11.1 3.0 %rotations.1.rot_ref = bf16[8,512,512]{2,1,0:T(8,128)(2,1)S(1)} custom-call(bf16[4080,510]{1,0:T(8,128)(2,1)} %bitcast.17), custom_call_target="tpu_custom_call" | custom-call | tf_op jit(solution)/shard_map/rotations/pallas_call | solution.py:515
  14.1 0.8 %gram_end.1.gram_ref = f32[1,128]{1,0:T(1,128)S(1)} custom-call(f32[8,8,8,128]{3,2,1,0:T(8,128)S(1)} %get-tuple-element.60.products_ref, f32[4,2048,128]{2,1,0:T(8,128)S(1)} %get-tuple-element.46.blocks_ref), custom_call_target="tpu_custom_call" | custom-call | tf_op jit(solution)/shard_map/gram_end/pallas_call | solution.py:506
  14.9 4.7 %collective-permute-start.3 = (bf16[4,2,2,16,512]{4,3,2,1,0:T(8,128)(2,1)S(1)}, bf16[4,2,2,16,512]{4,3,2,1,0:T(8,128)(2,1)S(1)}, u32[]{:S(2)}, u32[]{:S(2)}) collective-permute-start(bf16[4,2,2,16,512]{4,3,2,1,0:T(8,128)(2,1)S(1)} %join.1.own_ref), channel_id=1, source_target_pairs={{0,4},{4,8},{8,12},{12,16},{16,20},{20,24},{24,28},{1,5},{5,9},{9,... | collective-permute-start | bytes 786440 | tf_op jit(solution)/shard_map/ppermute | solution.py:434
  19.6 4.6 %axials.1.axial_ref = bf16[8,1024,512]{2,1,0:T(8,128)(2,1)S(1)} custom-call(bf16[8,510,2,510]{3,2,1,0:T(2,128)(2,1)} %bitcast.16), custom_call_target="tpu_custom_call" | custom-call | flops 2147483648 | bytes 16777216 | tf_op jit(solution)/shard_map/axials/pallas_call | solution.py:529
  24.2 0.0 collective-permute-done.4.above_ref
  24.2 1.4 %collective-permute-done.3.below_ref = bf16[4,2,2,16,512]{4,3,2,1,0:T(8,128)(2,1)S(1)} collective-permute-done((bf16[4,2,2,16,512]{4,3,2,1,0:T(8,128)(2,1)S(1)}, bf16[4,2,2,16,512]{4,3,2,1,0:T(8,128)(2,1)S(1)}, u32[]{:S(2)}, u32[]{:S(2)}) %collective-permute-start.3) | collective-permute-done | bytes 262176 | tf_op jit(solution)/shard_map/ppermute | solution.py:434
  25.6 9.5 %field.1 = (bf16[2,2,16,512]{3,2,1,0:T(8,128)(2,1)S(1)}, bf16[2,2,16,512]{3,2,1,0:T(8,128)(2,1)S(1)}, bf16[2,2,16,512]{3,2,1,0:T(8,128)(2,1)S(1)}, bf16[2,2,16,512]{3,2,1,0:T(8,128)(2,1)S(1)}) custom-call(bf16[8,512,512]{2,1,0:T(8,128)(2,1)S(1)} %rotations.1.rot_ref, bf16[8,1024,512]{2,1,0:T(8,128)(2,1)S(1)} %axials.1.axial_ref, ...), custom_call_target="tpu_custom_call" | custom-call | tf_op jit(solution)/shard_map/field/pallas_call | solution.py:542
  35.1 0.1 collective-permute-start.5
  35.2 1.5 %collective-permute-start.6 = (bf16[2,2,16,512]{3,2,1,0:T(8,128)(2,1)S(1)}, bf16[2,2,16,512]{3,2,1,0:T(8,128)(2,1)S(1)}, u32[]{:S(2)}, u32[]{:S(2)}) collective-permute-start(bf16[2,2,16,512]{3,2,1,0:T(8,128)(2,1)S(1)} %get-tuple-element.72), channel_id=1, source_target_pairs={{0,2},{1,3},{2,0},{3,1},{4,6},{5,7},{6,4},{7,5},{8,10},{9,11},{10,... | collective-permute-start | bytes 196616 | tf_op jit(solution)/shard_map/ppermute | solution.py:428
  36.7 0.3 collective-permute-start.7
  37.0 0.0 collective-permute-done.5.rest_1_
  37.0 2.6 %collective-permute-done.6.rest_2_ = bf16[2,2,16,512]{3,2,1,0:T(8,128)(2,1)S(1)} collective-permute-done((bf16[2,2,16,512]{3,2,1,0:T(8,128)(2,1)S(1)}, bf16[2,2,16,512]{3,2,1,0:T(8,128)(2,1)S(1)}, u32[]{:S(2)}, u32[]{:S(2)}) %collective-permute-start.6) | collective-permute-done | bytes 65568 | tf_op jit(solution)/shard_map/ppermute | solution.py:428
  39.7 1.1 %collective-permute-done.7.rest_3_ = bf16[2,2,16,512]{3,2,1,0:T(8,128)(2,1)S(1)} collective-permute-done((bf16[2,2,16,512]{3,2,1,0:T(8,128)(2,1)S(1)}, bf16[2,2,16,512]{3,2,1,0:T(8,128)(2,1)S(1)}, u32[]{:S(2)}, u32[]{:S(2)}) %collective-permute-start.7) | collective-permute-done | bytes 65568 | tf_op jit(solution)/shard_map/ppermute | solution.py:428
  40.7 1.4 %image.1 = (f32[1024,128]{1,0:T(8,128)S(1)}, f32[32,1,128]{2,1,0:T(1,128)S(1)}) custom-call(f32[4,2048,128]{2,1,0:T(8,128)S(1)} %get-tuple-element.46.blocks_ref, f32[256,4,128]{2,1,0:T(4,128)S(1)} %get-tuple-element.47.mie_ref, f32[1,128]{1,0:T(1,128)S(1)} %gram_end.1.gram_ref, bf16[2,2,16,512]{3,2,1,0:T(8,128)(2,1)S(1)} %get-tuple-element.70.rest_0_, ...), custom_call_target="tpu_custom_call" | custom-call | tf_op jit(solution)/shard_map/image/pallas_call | solution.py:553
  42.2 13.9 %all_to_all.5.sums_ref = f32[32,1,128]{2,1,0:T(1,128)S(1)} all-to-all(f32[32,1,128]{2,1,0:T(1,128)S(1)} %get-tuple-element.74), channel_id=1, replica_groups=mesh['blk'=8,'pair'=4] {'blk','pair'}, dimensions={0} | all-to-all | bytes 32768 | tf_op jit(solution)/shard_map/all_to_all | solution.py:562
  56.1 1.7 %remainder.1 = (f32[2,8]{1,0:T(2,128)}, f32[255,4,128]{2,1,0:T(4,128)}) custom-call(f32[32,1,128]{2,1,0:T(1,128)S(1)} %all_to_all.5.sums_ref, f32[4,2048,128]{2,1,0:T(8,128)S(1)} %get-tuple-element.46.blocks_ref, f32[1024,128]{1,0:T(8,128)S(1)} %get-tuple-element.75.image_ref), custom_call_target="tpu_custom_call" | custom-call | tf_op jit(solution)/shard_map/remainder/pallas_call | solution.py:565
  (1 shorter events, 0.0 us)
Async XLA Ops:
  2.6 6.5 %collective-permute-start = (bf16[2,2,16,512]{3,2,1,0:T(8,128)(2,1)S(1)}, bf16[2,2,16,512]{3,2,1,0:T(8,128)(2,1)S(1)}, u32[]{:S(2)}, u32[]{:S(2)}) collective-permute-start(bf16[2,2,16,512]{3,2,1,0:T(8,128)(2,1)S(1)} %get-tuple-element.49), channel_id=1, source_target_pairs={{0,1},{1,0},{2,3},{3,2},{4,5},{5,4},{6,7},{7,6},{8,9},{9,8},{10,11... | collective-permute-start | bytes 196616 | tf_op jit(solution)/shard_map/ppermute | solution.py:428
  3.1 6.0 %collective-permute-start.1 = (bf16[2,2,16,512]{3,2,1,0:T(8,128)(2,1)S(1)}, bf16[2,2,16,512]{3,2,1,0:T(8,128)(2,1)S(1)}, u32[]{:S(2)}, u32[]{:S(2)}) collective-permute-start(bf16[2,2,16,512]{3,2,1,0:T(8,128)(2,1)S(1)} %get-tuple-element.50), channel_id=1, source_target_pairs={{0,2},{1,3},{2,0},{3,1},{4,6},{5,7},{6,4},{7,5},{8,10},{9,11},{10,... | collective-permute-start | bytes 196616 | tf_op jit(solution)/shard_map/ppermute | solution.py:428
  5.7 4.0 %collective-permute-start.2 = (bf16[2,2,16,512]{3,2,1,0:T(8,128)(2,1)S(1)}, bf16[2,2,16,512]{3,2,1,0:T(8,128)(2,1)S(1)}, u32[]{:S(2)}, u32[]{:S(2)}) collective-permute-start(bf16[2,2,16,512]{3,2,1,0:T(8,128)(2,1)S(1)} %get-tuple-element.51), channel_id=1, source_target_pairs={{0,3},{1,2},{2,1},{3,0},{4,7},{5,6},{6,5},{7,4},{8,11},{9,10},{10,... | collective-permute-start | bytes 196616 | tf_op jit(solution)/shard_map/ppermute | solution.py:428
  9.8 14.5 %collective-permute-start.4 = (bf16[4,2,2,16,512]{4,3,2,1,0:T(8,128)(2,1)S(1)}, bf16[4,2,2,16,512]{4,3,2,1,0:T(8,128)(2,1)S(1)}, u32[]{:S(2)}, u32[]{:S(2)}) collective-permute-start(bf16[4,2,2,16,512]{4,3,2,1,0:T(8,128)(2,1)S(1)} %join.1.own_ref), channel_id=1, source_target_pairs={{4,0},{8,4},{12,8},{16,12},{20,16},{24,20},{28,24},{5,1},{9,5},{13... | collective-permute-start | bytes 786440 | tf_op jit(solution)/shard_map/ppermute | solution.py:434
  14.9 10.7 %collective-permute-start.3 = (bf16[4,2,2,16,512]{4,3,2,1,0:T(8,128)(2,1)S(1)}, bf16[4,2,2,16,512]{4,3,2,1,0:T(8,128)(2,1)S(1)}, u32[]{:S(2)}, u32[]{:S(2)}) collective-permute-start(bf16[4,2,2,16,512]{4,3,2,1,0:T(8,128)(2,1)S(1)} %join.1.own_ref), channel_id=1, source_target_pairs={{0,4},{4,8},{8,12},{12,16},{16,20},{20,24},{24,28},{1,5},{5,9},{9,... | collective-permute-start | bytes 786440 | tf_op jit(solution)/shard_map/ppermute | solution.py:434
  35.1 1.9 %collective-permute-start.5 = (bf16[2,2,16,512]{3,2,1,0:T(8,128)(2,1)S(1)}, bf16[2,2,16,512]{3,2,1,0:T(8,128)(2,1)S(1)}, u32[]{:S(2)}, u32[]{:S(2)}) collective-permute-start(bf16[2,2,16,512]{3,2,1,0:T(8,128)(2,1)S(1)} %get-tuple-element.71), channel_id=1, source_target_pairs={{0,1},{1,0},{2,3},{3,2},{4,5},{5,4},{6,7},{7,6},{8,9},{9,8},{10,11... | collective-permute-start | bytes 196616 | tf_op jit(solution)/shard_map/ppermute | solution.py:428
  35.2 4.5 %collective-permute-start.6 = (bf16[2,2,16,512]{3,2,1,0:T(8,128)(2,1)S(1)}, bf16[2,2,16,512]{3,2,1,0:T(8,128)(2,1)S(1)}, u32[]{:S(2)}, u32[]{:S(2)}) collective-permute-start(bf16[2,2,16,512]{3,2,1,0:T(8,128)(2,1)S(1)} %get-tuple-element.72), channel_id=1, source_target_pairs={{0,2},{1,3},{2,0},{3,1},{4,6},{5,7},{6,4},{7,5},{8,10},{9,11},{10,... | collective-permute-start | bytes 196616 | tf_op jit(solution)/shard_map/ppermute | solution.py:428
  36.7 4.0 %collective-permute-start.7 = (bf16[2,2,16,512]{3,2,1,0:T(8,128)(2,1)S(1)}, bf16[2,2,16,512]{3,2,1,0:T(8,128)(2,1)S(1)}, u32[]{:S(2)}, u32[]{:S(2)}) collective-permute-start(bf16[2,2,16,512]{3,2,1,0:T(8,128)(2,1)S(1)} %get-tuple-element.73), channel_id=1, source_target_pairs={{0,3},{1,2},{2,1},{3,0},{4,7},{5,6},{6,5},{7,4},{8,11},{9,10},{10,... | collective-permute-start | bytes 196616 | tf_op jit(solution)/shard_map/ppermute | solution.py:428

commit v19 on v16

--- a/solution.py
+++ b/solution.py
@@ -88,50 +88,60 @@
         out_ref[lax.axis_index("pair") ^ i] = ref[...]
 
 
-def tables_kernel(axial_ref, rot_ref, rot_out_ref, axial_out_ref, axials_ref, rots_ref, sems):
+def tables_kernel(
+    quarter, modes, rot_ref, axial_ref, products_ref, blocks_ref, rot_out_ref, axial_out_ref, line_ref, rots_ref, axials_ref, totals_ref, sems,
+):
     tables, size, _ = rot_out_ref.shape
-    modes = axial_ref.shape[1]
     listed = rot_ref.shape[0]
+    chunk = 256
+    rot_copies = []
+    for i, first in enumerate(range(0, listed, 4 * chunk)):
+        here = pl.ds(first, min(4 * chunk, listed - first))
+        rot_copies.append(pltpu.make_async_copy(rot_ref.at[here], rots_ref.at[here], sems.at[tables + i]))
+        rot_copies[-1].start()
 
     def fetch(g):
         return pltpu.make_async_copy(axial_ref.at[g], axials_ref.at[g], sems.at[g])
 
     for g in range(tables):
         fetch(g).start()
-    rot_copy = pltpu.make_async_copy(rot_ref, rots_ref.at[pl.ds(0, listed)], sems.at[tables])
-    rot_copy.start()
-    chunk = 256
-    out_row, in_row = iota((chunk, chunk), 0), iota((chunk, chunk), 1)
-    each = chunk // 2
-    halves = (in_row == 2 * lax.rem(out_row, each) + lax.div(out_row, each)).astype(F32).astype(BF16)
-    share = chunk // tables
-    entries = (in_row == tables * lax.rem(out_row, share) + lax.div(out_row, share)).astype(F32).astype(BF16)
     for ref in (rot_out_ref, axial_out_ref):
         ref[:, :, size - 128 : size] = jnp.zeros((tables, ref.shape[1], 128), BF16)
     rots_ref[listed:, :] = jnp.zeros((rots_ref.shape[0] - listed, modes), BF16)
-
-    def split(g, carry):
-        fetch(g).wait()
-        for first in range(0, modes, each):
+    gram_end(quarter * modes, products_ref, blocks_ref, line_ref, totals_ref)
+
+    out_row, in_row = iota((chunk, chunk), 0), iota((chunk, chunk), 1)
+    share = chunk // tables
+    entries = (in_row == tables * lax.rem(out_row, share) + lax.div(out_row, share)).astype(F32).astype(BF16)
+    for i, copy in enumerate(rot_copies):
+        copy.wait()
+        chunks = range(4 * i, min(4 * (i + 1), rots_ref.shape[0] // chunk))
+        rows = [rots_ref[q * chunk : (q + 1) * chunk, :] for q in chunks]
+        results = [dot_nn(entries, value).astype(BF16) for value in rows]
+        for q, result in zip(chunks, results):
+            for g in range(tables):
+                rot_out_ref[g, q * share : (q + 1) * share, 0:modes] = result[g * share : (g + 1) * share]
+
+    each = chunk // 2
+    halves = (in_row == 2 * lax.rem(out_row, each) + lax.div(out_row, each)).astype(F32).astype(BF16)
+    together = 2 if tables % 2 == 0 else 1
+
+    def split(step, carry):
+        members = [step * together + i for i in range(together)]
+        for g in members:
+            fetch(g).wait()
+        places = [(g, first) for g in members for first in range(0, modes, each)]
+        results = []
+        for g, first in places:
             count = min(each, modes - first)
             rows = axials_ref[g, first : first + count].reshape(2 * count, modes)
-            sorted_rows = dot_nn(halves[:, : 2 * count], rows).astype(BF16)
+            results.append(dot_nn(halves[:, : 2 * count], rows).astype(BF16))
+        for (g, first), result in zip(places, results):
             for c in range(2):
-                axial_out_ref[g, c * size + first : c * size + first + each, 0:modes] = sorted_rows[c * each : (c + 1) * each]
+                axial_out_ref[g, c * size + first : c * size + first + each, 0:modes] = result[c * each : (c + 1) * each]
         return carry
 
-    lax.fori_loop(0, tables, split, 0)
-    rot_copy.wait()
-
-    def pick(i, carry):
-        rows = rots_ref[pl.ds(pl.multiple_of(i * chunk, chunk), chunk), :]
-        sorted_rows = dot_nn(entries, rows).astype(BF16)
-        for g in range(tables):
-            here = pl.ds(pl.multiple_of(i * share, share), share)
-            rot_out_ref[g, here, 0:modes] = sorted_rows[g * share : (g + 1) * share]
-        return carry
-
-    lax.fori_loop(0, rots_ref.shape[0] // chunk, pick, 0)
+    lax.fori_loop(0, tables // together, split, 0)
 
 
 def swapped(value):
@@ -292,8 +302,7 @@
     mie_copy.wait()
 
 
-def gram_end_kernel(quarter, modes, products_ref, blocks_ref, line_ref, totals_ref):
-    rows = quarter * modes
+def gram_end(rows, products_ref, blocks_ref, line_ref, totals_ref):
     parts, chunk = 4, 32
     totals_ref[...] = products_ref[...]
     for first in range(rounded_up(rows, 8 * parts) // parts * (parts - 1), rows, chunk):
@@ -490,34 +499,26 @@
         name="join",
     )(*received)
     below, above = neighbours(own_pieces)
-
-    rotations, axials = pl.pallas_call(
-        tables_kernel,
-        in_specs=[hbm()] * 2,
-        out_specs=[whole()] * 2,
+    own_pieces, products, rot_rows, axial_rows = lax.optimization_barrier((own_pieces, products, rot_rows, axial_rows))
+    rotations, axials, line = pl.pallas_call(
+        functools.partial(tables_kernel, quarter, modes),
+        in_specs=[hbm()] * 2 + [whole()] * 2,
+        out_specs=[whole()] * 3,
         out_shape=[
             jax.ShapeDtypeStruct((tables, size, size), BF16),
             jax.ShapeDtypeStruct((tables, 2 * size, size), BF16),
+            jax.ShapeDtypeStruct((1, 128), F32),
         ],
         scratch_shapes=[
+            pltpu.VMEM((tables * size, modes), BF16),
             pltpu.VMEM(axial_rows.shape, BF16),
-            pltpu.VMEM((tables * size, modes), BF16),
-            pltpu.SemaphoreType.DMA((tables + 1,)),
+            pltpu.VMEM((vectors, vectors, 8, columns), F32),
+            pltpu.SemaphoreType.DMA((tables + rounded_up(modes * tables, 1024) // 1024,)),
         ],
         compiler_params=params(20),
         cost_estimate=pl.CostEstimate(flops=tables * 8 * 256 * 256 * size, bytes_accessed=6 * tables * size * size * 2, transcendentals=0),
         name="tables",
-    )(axial_rows, rot_rows)
-    own_pieces, products = lax.optimization_barrier((own_pieces, products))
-    line = pl.pallas_call(
-        functools.partial(gram_end_kernel, quarter, modes),
-        in_specs=[whole()] * 2,
-        out_specs=whole(),
-        out_shape=jax.ShapeDtypeStruct((1, 128), F32),
-        scratch_shapes=[pltpu.VMEM((vectors, vectors, 8, columns), F32)],
-        compiler_params=params(4),
-        name="gram_end",
-    )(products, blocks)
+    )(rot_rows, axial_rows, products, blocks)
     below, above, rotations, axials, line = lax.optimization_barrier((below, above, rotations, axials, line))
 
     together = tables

time: 56.7 us -> 56.8 us (level)
  waiting for transfers between devices: 4.51 us -> 7.17 us
  Pallas kernels: 26.8 us -> 24.3 us
    ppermute x2, waiting for transfers between devices: 0.2 us -> 2.97 us  [neighbours(): return (lax.ppermute(value, 'blk', up), lax.ppermute(value, 'blk', down))]
    pallas_call x2 -> x1, Pallas kernels: 9.56 us -> 6.78 us  [shards(): pl.pallas_call(functools.partial(tables_kernel, quarter, modes), in_specs...]
  transfers between devices with their start and end apart: 8 -> 8, of which waited for: 4 -> 4; matrix products, arithmetic and copies ran while one was open for 0% -> 0% of each run, Pallas kernels for 23% -> 18%
where the time goes in v19:
time: 56.8 us; the launch traced here: 56.6 us
  Pallas kernels  24.3 us (43%)
  blocking collectives  12.6 us (22%)
  starting transfers between devices  11.1 us (20%)
  waiting for transfers between devices  7.17 us (13%)
  between operations  1.37 us (2%)
    all_to_all x1, blocking collectives, shards(): lax.all_to_all(sums, ('blk', 'pair'), split_axis=0, concat_axis=0, tiled=...  12.6 us
    pallas_call x1, Pallas kernels, shards(): pl.pallas_call(functools.partial(field_kernel, own, modes, together), in_...  9.53 us
    pallas_call x1, Pallas kernels, shards(): pl.pallas_call(functools.partial(tables_kernel, quarter, modes), in_specs...  6.78 us
    ppermute x2, starting transfers between devices, neighbours(): return (lax.ppermute(value, 'blk', up), lax.ppermute(value, 'blk', down))  6.03 us
    ppermute x6, starting transfers between devices, exchanged(): lax.ppermute(pieces[i], axis, [(p, p ^ i) for p in range(count)])  5.09 us
    ppermute x6, waiting for transfers between devices, exchanged(): lax.ppermute(pieces[i], axis, [(p, p ^ i) for p in range(count)])  4.2 us
    pallas_call x1, Pallas kernels, shards(): pl.pallas_call(functools.partial(gram_kernel, quarter, modes), in_specs=[...  3.46 us
    ppermute x2, waiting for transfers between devices, neighbours(): return (lax.ppermute(value, 'blk', up), lax.ppermute(value, 'blk', down))  2.97 us
  transfers between devices with their start and end apart: 8, of which 4 were waited for; matrix products, arithmetic and copies ran while one was open for 0% of the time, Pallas kernels for 18%

profile of v19, /device:TPU:0, one launch (start us, length us, event | category | flops | bytes accessed | tf_op | source)
XLA Modules:
  0.0 56.6 jit_solution(15978853364766187591)
XLA Ops:
  1.3 1.3 %pack.1 = (bf16[2,2,16,512]{3,2,1,0:T(8,128)(2,1)S(1)}, bf16[2,2,16,512]{3,2,1,0:T(8,128)(2,1)S(1)}, bf16[2,2,16,512]{3,2,1,0:T(8,128)(2,1)S(1)}, bf16[2,2,16,512]{3,2,1,0:T(8,128)(2,1)S(1)}) custom-call(s32[3,1,128]{2,1,0:T(1,128)} %bitcast.19, s32[1]{0:T(128)S(6)} %copy.8.count_ref, f32[4,2040,128]{2,1,0:T(8,128)} %bitcast.14), custom_call_target="tpu_custom_call" | custom-call | tf_op jit(solution)/shard_map/pack/pallas_call | solution.py:457
  2.6 0.5 collective-permute-start
  3.1 2.6 %collective-permute-start.1 = (bf16[2,2,16,512]{3,2,1,0:T(8,128)(2,1)S(1)}, bf16[2,2,16,512]{3,2,1,0:T(8,128)(2,1)S(1)}, u32[]{:S(2)}, u32[]{:S(2)}) collective-permute-start(bf16[2,2,16,512]{3,2,1,0:T(8,128)(2,1)S(1)} %get-tuple-element.52), channel_id=1, source_target_pairs={{0,2},{1,3},{2,0},{3,1},{4,6},{5,7},{6,4},{7,5},{8,10},{9,11},{10,... | collective-permute-start | bytes 196616 | tf_op jit(solution)/shard_map/ppermute | solution.py:423
  5.7 0.1 collective-permute-start.2
  5.7 3.5 %gram.1 = (f32[8,8,8,128]{3,2,1,0:T(8,128)S(1)}, f32[4,2048,128]{2,1,0:T(8,128)S(1)}, f32[256,4,128]{2,1,0:T(4,128)S(1)}) custom-call(f32[4,2040,128]{2,1,0:T(8,128)} %bitcast.15, f32[255,4,128]{2,1,0:T(4,128)} %bitcast.18), custom_call_target="tpu_custom_call" | custom-call | tf_op jit(solution)/shard_map/gram/pallas_call | solution.py:476
  9.2 0.0 collective-permute-done.refs_1_
  9.2 0.0 collective-permute-done.1.refs_2_
  9.2 0.5 collective-permute-done.2.refs_3_
  9.8 1.3 %collective-permute-start.4 = (bf16[4,2,2,16,512]{4,3,2,1,0:T(8,128)(2,1)S(1)}, bf16[4,2,2,16,512]{4,3,2,1,0:T(8,128)(2,1)S(1)}, u32[]{:S(2)}, u32[]{:S(2)}) collective-permute-start(bf16[4,2,2,16,512]{4,3,2,1,0:T(8,128)(2,1)S(1)} %join.1.own_ref), channel_id=1, source_target_pairs={{4,0},{8,4},{12,8},{16,12},{20,16},{24,20},{28,24},{5,1},{9,5},{13... | collective-permute-start | bytes 786440 | tf_op jit(solution)/shard_map/ppermute | solution.py:431
  11.1 4.7 %collective-permute-start.3 = (bf16[4,2,2,16,512]{4,3,2,1,0:T(8,128)(2,1)S(1)}, bf16[4,2,2,16,512]{4,3,2,1,0:T(8,128)(2,1)S(1)}, u32[]{:S(2)}, u32[]{:S(2)}) collective-permute-start(bf16[4,2,2,16,512]{4,3,2,1,0:T(8,128)(2,1)S(1)} %join.1.own_ref), channel_id=1, source_target_pairs={{0,4},{4,8},{8,12},{12,16},{16,20},{20,24},{24,28},{1,5},{5,9},{9,... | collective-permute-start | bytes 786440 | tf_op jit(solution)/shard_map/ppermute | solution.py:431
  15.8 6.8 %tables.1 = (bf16[8,512,512]{2,1,0:T(8,128)(2,1)S(1)}, bf16[8,1024,512]{2,1,0:T(8,128)(2,1)S(1)}, f32[1,128]{1,0:T(1,128)S(1)}) custom-call(bf16[4080,510]{1,0:T(8,128)(2,1)} %bitcast.17, bf16[8,510,2,510]{3,2,1,0:T(2,128)(2,1)} %bitcast.16, f32[8,8,8,128]{3,2,1,0:T(8,128)S(1)} %get-tuple-element.64.products_ref, ...), custom_call_target="tpu_custom_call" | custom-call | flops 2147483648 | bytes 25165824 | tf_op jit(solution)/shard_map/tables/pallas_call | solution.py:503
  22.6 0.0 collective-permute-done.4.above_ref
  22.6 3.0 %collective-permute-done.3.below_ref = bf16[4,2,2,16,512]{4,3,2,1,0:T(8,128)(2,1)S(1)} collective-permute-done((bf16[4,2,2,16,512]{4,3,2,1,0:T(8,128)(2,1)S(1)}, bf16[4,2,2,16,512]{4,3,2,1,0:T(8,128)(2,1)S(1)}, u32[]{:S(2)}, u32[]{:S(2)}) %collective-permute-start.3) | collective-permute-done | bytes 262176 | tf_op jit(solution)/shard_map/ppermute | solution.py:431
  25.6 9.5 %field.1 = (bf16[2,2,16,512]{3,2,1,0:T(8,128)(2,1)S(1)}, bf16[2,2,16,512]{3,2,1,0:T(8,128)(2,1)S(1)}, bf16[2,2,16,512]{3,2,1,0:T(8,128)(2,1)S(1)}, bf16[2,2,16,512]{3,2,1,0:T(8,128)(2,1)S(1)}) custom-call(bf16[8,512,512]{2,1,0:T(8,128)(2,1)S(1)} %get-tuple-element.69.rot_ref, bf16[8,1024,512]{2,1,0:T(8,128)(2,1)S(1)} %get-tuple-element.70.axial_ref, ...), custom_call_target="tpu_custom_call" | custom-call | tf_op jit(solution)/shard_map/field/pallas_call | solution.py:525
  35.1 0.1 collective-permute-start.5
  35.2 1.5 %collective-permute-start.6 = (bf16[2,2,16,512]{3,2,1,0:T(8,128)(2,1)S(1)}, bf16[2,2,16,512]{3,2,1,0:T(8,128)(2,1)S(1)}, u32[]{:S(2)}, u32[]{:S(2)}) collective-permute-start(bf16[2,2,16,512]{3,2,1,0:T(8,128)(2,1)S(1)} %get-tuple-element.76), channel_id=1, source_target_pairs={{0,2},{1,3},{2,0},{3,1},{4,6},{5,7},{6,4},{7,5},{8,10},{9,11},{10,... | collective-permute-start | bytes 196616 | tf_op jit(solution)/shard_map/ppermute | solution.py:423
  36.7 0.3 collective-permute-start.7
  37.1 0.0 collective-permute-done.5.rest_1_
  37.1 2.6 %collective-permute-done.6.rest_2_ = bf16[2,2,16,512]{3,2,1,0:T(8,128)(2,1)S(1)} collective-permute-done((bf16[2,2,16,512]{3,2,1,0:T(8,128)(2,1)S(1)}, bf16[2,2,16,512]{3,2,1,0:T(8,128)(2,1)S(1)}, u32[]{:S(2)}, u32[]{:S(2)}) %collective-permute-start.6) | collective-permute-done | bytes 65568 | tf_op jit(solution)/shard_map/ppermute | solution.py:423
  39.7 1.1 %collective-permute-done.7.rest_3_ = bf16[2,2,16,512]{3,2,1,0:T(8,128)(2,1)S(1)} collective-permute-done((bf16[2,2,16,512]{3,2,1,0:T(8,128)(2,1)S(1)}, bf16[2,2,16,512]{3,2,1,0:T(8,128)(2,1)S(1)}, u32[]{:S(2)}, u32[]{:S(2)}) %collective-permute-start.7) | collective-permute-done | bytes 65568 | tf_op jit(solution)/shard_map/ppermute | solution.py:423
  40.8 1.5 %image.1 = (f32[1024,128]{1,0:T(8,128)S(1)}, f32[32,1,128]{2,1,0:T(1,128)S(1)}) custom-call(f32[4,2048,128]{2,1,0:T(8,128)S(1)} %get-tuple-element.48.blocks_ref, f32[256,4,128]{2,1,0:T(4,128)S(1)} %get-tuple-element.49.mie_ref, f32[1,128]{1,0:T(1,128)S(1)} %get-tuple-element.68.gram_ref, bf16[2,2,16,512]{3,2,1,0:T(8,128)(2,1)S(1)} %get-tuple-element.74.rest_0_, ...), custom_call_target="tpu_custom_call" | custom-call | tf_op jit(solution)/shard_map/image/pallas_call | solution.py:536
  42.2 12.6 %all_to_all.5.sums_ref = f32[32,1,128]{2,1,0:T(1,128)S(1)} all-to-all(f32[32,1,128]{2,1,0:T(1,128)S(1)} %get-tuple-element.78), channel_id=1, replica_groups=mesh['blk'=8,'pair'=4] {'blk','pair'}, dimensions={0} | all-to-all | bytes 32768 | tf_op jit(solution)/shard_map/all_to_all | solution.py:545
  54.8 1.7 %remainder.1 = (f32[2,8]{1,0:T(2,128)}, f32[255,4,128]{2,1,0:T(4,128)}) custom-call(f32[32,1,128]{2,1,0:T(1,128)S(1)} %all_to_all.5.sums_ref, f32[4,2048,128]{2,1,0:T(8,128)S(1)} %get-tuple-element.48.blocks_ref, f32[1024,128]{1,0:T(8,128)S(1)} %get-tuple-element.79.image_ref), custom_call_target="tpu_custom_call" | custom-call | tf_op jit(solution)/shard_map/remainder/pallas_call | solution.py:548
  (1 shorter events, 0.0 us)
Async XLA Ops:
  2.6 6.6 %collective-permute-start = (bf16[2,2,16,512]{3,2,1,0:T(8,128)(2,1)S(1)}, bf16[2,2,16,512]{3,2,1,0:T(8,128)(2,1)S(1)}, u32[]{:S(2)}, u32[]{:S(2)}) collective-permute-start(bf16[2,2,16,512]{3,2,1,0:T(8,128)(2,1)S(1)} %get-tuple-element.51), channel_id=1, source_target_pairs={{0,1},{1,0},{2,3},{3,2},{4,5},{5,4},{6,7},{7,6},{8,9},{9,8},{10,11... | collective-permute-start | bytes 196616 | tf_op jit(solution)/shard_map/ppermute | solution.py:423
  3.1 6.1 %collective-permute-start.1 = (bf16[2,2,16,512]{3,2,1,0:T(8,128)(2,1)S(1)}, bf16[2,2,16,512]{3,2,1,0:T(8,128)(2,1)S(1)}, u32[]{:S(2)}, u32[]{:S(2)}) collective-permute-start(bf16[2,2,16,512]{3,2,1,0:T(8,128)(2,1)S(1)} %get-tuple-element.52), channel_id=1, source_target_pairs={{0,2},{1,3},{2,0},{3,1},{4,6},{5,7},{6,4},{7,5},{8,10},{9,11},{10,... | collective-permute-start | bytes 196616 | tf_op jit(solution)/shard_map/ppermute | solution.py:423
  5.7 4.0 %collective-permute-start.2 = (bf16[2,2,16,512]{3,2,1,0:T(8,128)(2,1)S(1)}, bf16[2,2,16,512]{3,2,1,0:T(8,128)(2,1)S(1)}, u32[]{:S(2)}, u32[]{:S(2)}) collective-permute-start(bf16[2,2,16,512]{3,2,1,0:T(8,128)(2,1)S(1)} %get-tuple-element.53), channel_id=1, source_target_pairs={{0,3},{1,2},{2,1},{3,0},{4,7},{5,6},{6,5},{7,4},{8,11},{9,10},{10,... | collective-permute-start | bytes 196616 | tf_op jit(solution)/shard_map/ppermute | solution.py:423
  9.8 12.8 %collective-permute-start.4 = (bf16[4,2,2,16,512]{4,3,2,1,0:T(8,128)(2,1)S(1)}, bf16[4,2,2,16,512]{4,3,2,1,0:T(8,128)(2,1)S(1)}, u32[]{:S(2)}, u32[]{:S(2)}) collective-permute-start(bf16[4,2,2,16,512]{4,3,2,1,0:T(8,128)(2,1)S(1)} %join.1.own_ref), channel_id=1, source_target_pairs={{4,0},{8,4},{12,8},{16,12},{20,16},{24,20},{28,24},{5,1},{9,5},{13... | collective-permute-start | bytes 786440 | tf_op jit(solution)/shard_map/ppermute | solution.py:431
  11.1 14.5 %collective-permute-start.3 = (bf16[4,2,2,16,512]{4,3,2,1,0:T(8,128)(2,1)S(1)}, bf16[4,2,2,16,512]{4,3,2,1,0:T(8,128)(2,1)S(1)}, u32[]{:S(2)}, u32[]{:S(2)}) collective-permute-start(bf16[4,2,2,16,512]{4,3,2,1,0:T(8,128)(2,1)S(1)} %join.1.own_ref), channel_id=1, source_target_pairs={{0,4},{4,8},{8,12},{12,16},{16,20},{20,24},{24,28},{1,5},{5,9},{9,... | collective-permute-start | bytes 786440 | tf_op jit(solution)/shard_map/ppermute | solution.py:431
  35.1 1.9 %collective-permute-start.5 = (bf16[2,2,16,512]{3,2,1,0:T(8,128)(2,1)S(1)}, bf16[2,2,16,512]{3,2,1,0:T(8,128)(2,1)S(1)}, u32[]{:S(2)}, u32[]{:S(2)}) collective-permute-start(bf16[2,2,16,512]{3,2,1,0:T(8,128)(2,1)S(1)} %get-tuple-element.75), channel_id=1, source_target_pairs={{0,1},{1,0},{2,3},{3,2},{4,5},{5,4},{6,7},{7,6},{8,9},{9,8},{10,11... | collective-permute-start | bytes 196616 | tf_op jit(solution)/shard_map/ppermute | solution.py:423
  35.2 4.5 %collective-permute-start.6 = (bf16[2,2,16,512]{3,2,1,0:T(8,128)(2,1)S(1)}, bf16[2,2,16,512]{3,2,1,0:T(8,128)(2,1)S(1)}, u32[]{:S(2)}, u32[]{:S(2)}) collective-permute-start(bf16[2,2,16,512]{3,2,1,0:T(8,128)(2,1)S(1)} %get-tuple-element.76), channel_id=1, source_target_pairs={{0,2},{1,3},{2,0},{3,1},{4,6},{5,7},{6,4},{7,5},{8,10},{9,11},{10,... | collective-permute-start | bytes 196616 | tf_op jit(solution)/shard_map/ppermute | solution.py:423
  36.7 4.0 %collective-permute-start.7 = (bf16[2,2,16,512]{3,2,1,0:T(8,128)(2,1)S(1)}, bf16[2,2,16,512]{3,2,1,0:T(8,128)(2,1)S(1)}, u32[]{:S(2)}, u32[]{:S(2)}) collective-permute-start(bf16[2,2,16,512]{3,2,1,0:T(8,128)(2,1)S(1)} %get-tuple-element.77), channel_id=1, source_target_pairs={{0,3},{1,2},{2,1},{3,0},{4,7},{5,6},{6,5},{7,4},{8,11},{9,10},{10,... | collective-permute-start | bytes 196616 | tf_op jit(solution)/shard_map/ppermute | solution.py:423

commit v20 on v18

--- a/solution.py
+++ b/solution.py
@@ -83,26 +83,26 @@
 
 
 def join_kernel(*refs):
-    out_ref = refs[-1]
-    for i, ref in enumerate(refs[:-1]):
-        out_ref[lax.axis_index("pair") ^ i] = ref[...]
-
-
-def rotations_kernel(rot_ref, out_ref, rots_ref, sems):
+    for i, ref in enumerate(refs[:-2]):
+        for c, out_ref in enumerate(refs[-2:]):
+            out_ref[lax.axis_index("pair") ^ i] = ref[c]
+
+
+def rotations_kernel(quarter, modes, rot_ref, products_ref, blocks_ref, out_ref, line_ref, rots_ref, totals_ref, sems):
     tables, size, _ = out_ref.shape
-    listed, modes = rot_ref.shape
+    listed = rot_ref.shape[0]
     chunk = 256
     copies = []
     for i, first in enumerate(range(0, listed, 4 * chunk)):
         here = pl.ds(first, min(4 * chunk, listed - first))
         copies.append(pltpu.make_async_copy(rot_ref.at[here], rots_ref.at[here], sems.at[i]))
         copies[-1].start()
+    out_ref[:, :, size - 128 : size] = jnp.zeros((tables, size, 128), BF16)
+    rots_ref[listed:, :] = jnp.zeros((rots_ref.shape[0] - listed, modes), BF16)
+    gram_end(quarter * modes, products_ref, blocks_ref, line_ref, totals_ref)
     out_row, in_row = iota((chunk, chunk), 0), iota((chunk, chunk), 1)
     share = chunk // tables
     entries = (in_row == tables * lax.rem(out_row, share) + lax.div(out_row, share)).astype(F32).astype(BF16)
-    out_ref[:, :, size - 128 : size] = jnp.zeros((tables, size, 128), BF16)
-    rots_ref[listed:, :] = jnp.zeros((rots_ref.shape[0] - listed, modes), BF16)
-
     for i, copy in enumerate(copies):
         copy.wait()
         chunks = range(4 * i, min(4 * (i + 1), rots_ref.shape[0] // chunk))
@@ -122,19 +122,18 @@
 
     for g in range(tables):
         fetch(g).start()
+    out_ref[:, :, size - 128 : size] = jnp.zeros((tables, double, 128), BF16)
     chunk = 256
     out_row, in_row = iota((chunk, chunk), 0), iota((chunk, chunk), 1)
     each = chunk // 2
     halves = (in_row == 2 * lax.rem(out_row, each) + lax.div(out_row, each)).astype(F32).astype(BF16)
-    out_ref[:, :, size - 128 : size] = jnp.zeros((tables, double, 128), BF16)
-
     together = 2 if tables % 2 == 0 else 1
 
     def split(step, carry):
-        entries = [step * together + i for i in range(together)]
-        for g in entries:
+        members = [step * together + i for i in range(together)]
+        for g in members:
             fetch(g).wait()
-        places = [(g, first) for g in entries for first in range(0, modes, each)]
+        places = [(g, first) for g in members for first in range(0, modes, each)]
         results = []
         for g, first in places:
             count = min(each, modes - first)
@@ -154,24 +153,28 @@
 
 
 def pair_counts(own, tables, lane, refs):
-    ways, parts, octets, height, size = refs[0].shape
+    ways, octets, height, size = refs[0][0].shape
     group = ways * octets * height
     wanted = iota((tables * own, group), 0) + own
 
     def one_hot(hit):
         return jnp.where(hit, 1.0, 0.0).astype(BF16)
 
+    even = lax.rem(lax.axis_index("blk"), 2) == 0
+    windows = (jnp.where(even, 2, 0), 1, jnp.where(even, 0, 2))
     forward, backward = None, []
-    for window, ref in enumerate(refs):
-        values = ref[:, :, :, :, size - 128 : size].reshape(2 * group, 128).astype(F32)
+    for order, (window, halves) in enumerate(zip(windows, refs)):
+        values = jnp.stack([ref[:, :, :, size - 128 : size] for ref in halves], axis=1).reshape(2 * group, 128).astype(F32)
         marks_column, sources_column = (values[h * group : (h + 1) * group, lane : lane + 1].astype(jnp.int32) for h in range(2))
         marks, sources = (jnp.transpose(values[h * group : (h + 1) * group])[lane : lane + 1].astype(jnp.int32) for h in range(2))
-        if window == 1:
+        if order == 1:
+            turned = (2 - lax.div(sources_column, own)) * own + lax.rem(sources_column, own)
+            sources_column = jnp.where(even, turned, sources_column)
             forward = dot_nn(one_hot(marks == wanted), one_hot(sources_column == iota((group, 3 * own), 1)))
         block = sources - (2 - window) * own
         inside = (block >= 0) & (block < own) & (marks >= own)
         hits = one_hot(jnp.where(inside, lax.div(marks, own) * own + block, -1) == wanted)
-        place = lax.rem(marks_column, own) + window * own
+        place = lax.rem(marks_column, own) + order * own
         backward.append(dot_nn(hits, one_hot(place == iota((group, 3 * own), 1))))
     return jnp.concatenate([forward, sum(backward)], axis=0).astype(BF16)
 
@@ -181,12 +184,12 @@
 
 
 def field_kernel(
-    own, modes, together, rot_ref, axial_ref, below_ref, own_ref, above_ref, *rest
+    own, modes, together, rot_ref, axial_ref, near0, near1, own0, own1, far0, far1, *rest
 ):
     outs, (sums_ref, total_ref) = rest[:-2], rest[-2:]
     tables, _, size = rot_ref.shape
-    refs = (below_ref, own_ref, above_ref)
-    ways, _, octets, height, _ = own_ref.shape
+    refs = ((near0, near1), (own0, own1), (far0, far1))
+    ways, octets, height, _ = own0.shape
     quarter = own // ways
     each = height // quarter
     part = octets * each
@@ -199,7 +202,7 @@
     kinds = 2 * tables * own
     for c in range(2):
         for o in range(octets):
-            blocks = jnp.concatenate([ref[:, c, o].reshape(ways * height, size) for ref in refs], axis=0)
+            blocks = jnp.concatenate([halves[c][:, o].reshape(ways * height, size) for halves in refs], axis=0)
             for i in range(0, each, 2):
                 results = dot_nn(chosen[i * kinds : (i + 2) * kinds], blocks)
                 for kind in range(2 * tables):
@@ -306,8 +309,7 @@
     mie_copy.wait()
 
 
-def gram_end_kernel(quarter, modes, products_ref, blocks_ref, line_ref, totals_ref):
-    rows = quarter * modes
+def gram_end(rows, products_ref, blocks_ref, line_ref, totals_ref):
     parts, chunk = 4, 32
     totals_ref[...] = products_ref[...]
     for first in range(rounded_up(rows, 8 * parts) // parts * (parts - 1), rows, chunk):
@@ -429,9 +431,15 @@
     return received
 
 
-def from_neighbour(value, up):
-    pairs = [(i, i + 1) for i in range(lax.axis_size("blk") - 1)]
-    return lax.ppermute(value, "blk", pairs if up else [(j, i) for i, j in pairs])
+def from_near(value):
+    count = lax.axis_size("blk")
+    return lax.ppermute(value, "blk", [(i, i ^ 1) for i in range(count) if i ^ 1 < count])
+
+
+def from_far(value):
+    count = lax.axis_size("blk")
+    steps = [(i, i - 2 if i % 2 else i + 2) for i in range(count)]
+    return lax.ppermute(value, "blk", [(i, j) for i, j in steps if 0 <= j < count])
 
 
 def shards(basis, mie_coeffs, rot_table, axial_table, pair_table, pair_count):
@@ -493,39 +501,34 @@
         name="gram",
     )(basis_rows, mie_rows)
     *received, products, rot_rows, axial_rows = lax.optimization_barrier((*received, products, rot_rows, axial_rows))
-    own_pieces = pl.pallas_call(
+    half = jax.ShapeDtypeStruct((ways, *piece.shape[1:]), BF16)
+    own0, own1 = pl.pallas_call(
         join_kernel,
         in_specs=[whole()] * ways,
-        out_specs=whole(),
-        out_shape=jax.ShapeDtypeStruct((ways, *piece.shape), BF16),
+        out_specs=[whole()] * 2,
+        out_shape=[half] * 2,
         compiler_params=params(4),
         name="join",
     )(*received)
-    own_pieces, products, rot_rows = lax.optimization_barrier((own_pieces, products, rot_rows))
-    above = from_neighbour(own_pieces, False)
-    line = pl.pallas_call(
-        functools.partial(gram_end_kernel, quarter, modes),
-        in_specs=[whole()] * 2,
-        out_specs=whole(),
-        out_shape=jax.ShapeDtypeStruct((1, 128), F32),
-        scratch_shapes=[pltpu.VMEM((vectors, vectors, 8, columns), F32)],
-        compiler_params=params(4),
-        name="gram_end",
-    )(products, blocks)
-    rotations = pl.pallas_call(
-        rotations_kernel,
-        in_specs=[hbm()],
-        out_specs=whole(),
-        out_shape=jax.ShapeDtypeStruct((tables, size, size), BF16),
+    near0, near1 = from_near(own0), from_near(own1)
+    own0, own1, products, rot_rows = lax.optimization_barrier((own0, own1, products, rot_rows))
+    rotations, line = pl.pallas_call(
+        functools.partial(rotations_kernel, quarter, modes),
+        in_specs=[hbm()] + [whole()] * 2,
+        out_specs=[whole()] * 2,
+        out_shape=[jax.ShapeDtypeStruct((tables, size, size), BF16), jax.ShapeDtypeStruct((1, 128), F32)],
         scratch_shapes=[
             pltpu.VMEM((tables * size, modes), BF16),
+            pltpu.VMEM((vectors, vectors, 8, columns), F32),
             pltpu.SemaphoreType.DMA((rounded_up(modes * tables, 1024) // 1024,)),
         ],
-        compiler_params=params(8),
+        compiler_params=params(12),
         name="rotations",
-    )(rot_rows)
-    own_pieces, line, rotations, axial_rows = lax.optimization_barrier((own_pieces, line, rotations, axial_rows))
-    below = from_neighbour(own_pieces, True)
+    )(rot_rows, products, blocks)
+    near0, rotations, line = lax.optimization_barrier((near0, rotations, line))
+    far0 = from_far(near0)
+    near1, rotations, axial_rows = lax.optimization_barrier((near1, rotations, axial_rows))
+    far1 = from_far(near1)
     axials = pl.pallas_call(
         axials_kernel,
         in_specs=[hbm()],
@@ -536,18 +539,18 @@
         cost_estimate=pl.CostEstimate(flops=tables * 8 * 256 * 256 * size, bytes_accessed=4 * tables * size * size * 2, transcendentals=0),
         name="axials",
     )(axial_rows)
-    below, above, axials = lax.optimization_barrier((below, above, axials))
+    far0, far1, axials = lax.optimization_barrier((far0, far1, axials))
 
     together = tables
     field = pl.pallas_call(
         functools.partial(field_kernel, own, modes, together),
-        in_specs=[whole()] * 5,
+        in_specs=[whole()] * 8,
         out_specs=[whole()] * ways,
         out_shape=[jax.ShapeDtypeStruct((2, quarter, part, size), BF16)] * ways,
         scratch_shapes=[pltpu.VMEM((tables, 4 * group, size), BF16), pltpu.VMEM((2 * group, size), F32)],
         compiler_params=params(28),
         name="field",
-    )(rotations, axials, below, own_pieces, above)
+    )(rotations, axials, near0, near1, own0, own1, far0, far1)
     field_pieces = exchanged(field, "pair")
 
     image, sums = pl.pallas_call(

time: 58 us -> 58.9 us (1.016)
  blocking collectives: 13.9 us -> 10.4 us
  starting transfers between devices: 11.1 us -> 14.3 us
  waiting for transfers between devices: 5.67 us -> 6.77 us
    all_to_all x1, blocking collectives: 13.9 us -> 10.4 us  [shards(): lax.all_to_all(sums, ('blk', 'pair'), split_axis=0, concat_axis=0, tiled=...]
    ppermute x2 -> x4, starting transfers between devices: 6.03 us -> 9.23 us  [the longest x2 7.14 us: from_far(): lax.ppermute(value, 'blk', [(i, j) for i, j in steps if 0 <= j < count])]
    ppermute x2 -> x4, waiting for transfers between devices: 1.36 us -> 2.57 us  [the longest x2 2.57 us: from_near(): lax.ppermute(value, 'blk', [(i, i ^ 1) for i in range(count) if i ^ 1 < c...]
    pallas_call x3 -> x2, Pallas kernels: 3.85 us -> 3.8 us  [the longest x1 3.77 us: shards(): pl.pallas_call(functools.partial(rotations_kernel, quarter, modes), in_sp...]
  transfers between devices with their start and end apart: 8 -> 10, of which waited for: 4 -> 5; matrix products, arithmetic and copies ran while one was open for 0% -> 0% of each run, Pallas kernels for 20% -> 20%
where the time goes in v20:
time: 58.9 us; the launch traced here: 58.7 us
  Pallas kernels  25.8 us (44%)
  starting transfers between devices  14.3 us (24%)
  blocking collectives  10.4 us (18%)
  waiting for transfers between devices  6.77 us (11%)
  between operations  1.39 us (2%)
    all_to_all x1, blocking collectives, shards(): lax.all_to_all(sums, ('blk', 'pair'), split_axis=0, concat_axis=0, tiled=...  10.4 us
    pallas_call x1, Pallas kernels, shards(): pl.pallas_call(functools.partial(field_kernel, own, modes, together), in_...  9.55 us
    ppermute x2, starting transfers between devices, from_far(): lax.ppermute(value, 'blk', [(i, j) for i, j in steps if 0 <= j < count])  7.14 us
    ppermute x6, starting transfers between devices, exchanged(): lax.ppermute(pieces[i], axis, [(p, p ^ i) for p in range(count)])  5.08 us
    pallas_call x1, Pallas kernels, shards(): pl.pallas_call(axials_kernel, in_specs=[hbm()], out_specs=whole(), out_sh...  4.57 us
    ppermute x6, waiting for transfers between devices, exchanged(): lax.ppermute(pieces[i], axis, [(p, p ^ i) for p in range(count)])  4.2 us
    pallas_call x1, Pallas kernels, shards(): pl.pallas_call(functools.partial(rotations_kernel, quarter, modes), in_sp...  3.77 us
    pallas_call x1, Pallas kernels, shards(): pl.pallas_call(functools.partial(gram_kernel, quarter, modes), in_specs=[...  3.46 us
  transfers between devices with their start and end apart: 10, of which 5 were waited for; matrix products, arithmetic and copies ran while one was open for 0% of the time, Pallas kernels for 20%

profile of v20, /device:TPU:0, one launch (start us, length us, event | category | flops | bytes accessed | tf_op | source)
XLA Modules:
  0.0 58.7 jit_solution(3659488103868311115)
XLA Ops:
  1.3 1.3 %pack.1 = (bf16[2,2,16,512]{3,2,1,0:T(8,128)(2,1)S(1)}, bf16[2,2,16,512]{3,2,1,0:T(8,128)(2,1)S(1)}, bf16[2,2,16,512]{3,2,1,0:T(8,128)(2,1)S(1)}, bf16[2,2,16,512]{3,2,1,0:T(8,128)(2,1)S(1)}) custom-call(s32[3,1,128]{2,1,0:T(1,128)} %bitcast.19, s32[1]{0:T(128)S(6)} %copy.8.count_ref, f32[4,2040,128]{2,1,0:T(8,128)} %bitcast.14), custom_call_target="tpu_custom_call" | custom-call | tf_op jit(solution)/shard_map/pack/pallas_call | solution.py:468
  2.6 0.5 collective-permute-start
  3.1 2.6 %collective-permute-start.1 = (bf16[2,2,16,512]{3,2,1,0:T(8,128)(2,1)S(1)}, bf16[2,2,16,512]{3,2,1,0:T(8,128)(2,1)S(1)}, u32[]{:S(2)}, u32[]{:S(2)}) collective-permute-start(bf16[2,2,16,512]{3,2,1,0:T(8,128)(2,1)S(1)} %get-tuple-element.57), channel_id=1, source_target_pairs={{0,2},{1,3},{2,0},{3,1},{4,6},{5,7},{6,4},{7,5},{8,10},{9,11},{10,... | collective-permute-start | bytes 196616 | tf_op jit(solution)/shard_map/ppermute | solution.py:430
  5.7 0.1 collective-permute-start.2
  5.8 3.5 %gram.1 = (f32[8,8,8,128]{3,2,1,0:T(8,128)S(1)}, f32[4,2048,128]{2,1,0:T(8,128)S(1)}, f32[256,4,128]{2,1,0:T(4,128)S(1)}) custom-call(f32[4,2040,128]{2,1,0:T(8,128)} %bitcast.15, f32[255,4,128]{2,1,0:T(4,128)} %bitcast.18), custom_call_target="tpu_custom_call" | custom-call | tf_op jit(solution)/shard_map/gram/pallas_call | solution.py:487
  9.2 0.0 collective-permute-done.refs_1_
  9.2 0.0 collective-permute-done.1.refs_2_
  9.2 0.5 collective-permute-done.2.refs_3_
  9.8 1.6 %collective-permute-start.3 = (bf16[4,2,16,512]{3,2,1,0:T(8,128)(2,1)S(1)}, bf16[4,2,16,512]{3,2,1,0:T(8,128)(2,1)S(1)}, u32[]{:S(2)}, u32[]{:S(2)}) collective-permute-start(bf16[4,2,16,512]{3,2,1,0:T(8,128)(2,1)S(1)} %get-tuple-element.80.own0), channel_id=1, source_target_pairs={{0,4},{4,0},{8,12},{12,8},{16,20},{20,16},{24,28},{28,24},{1,5},{5... | collective-permute-start | bytes 393224 | tf_op jit(solution)/shard_map/ppermute | solution.py:436
  11.4 0.5 collective-permute-start.4
  11.8 3.8 %rotations.1 = (bf16[8,512,512]{2,1,0:T(8,128)(2,1)S(1)}, f32[1,128]{1,0:T(1,128)S(1)}) custom-call(bf16[4080,510]{1,0:T(8,128)(2,1)} %bitcast.17, f32[8,8,8,128]{3,2,1,0:T(8,128)S(1)} %get-tuple-element.69.products_ref, f32[4,2048,128]{2,1,0:T(8,128)S(1)} %get-tuple-element.53.blocks_ref), custom_call_target="tpu_custom_call" | custom-call | tf_op jit(solution)/shard_map/rotations/pallas_call | solution.py:515
  15.6 0.5 collective-permute-done.3.near0
  16.2 2.0 %collective-permute-done.4.near1 = bf16[4,2,16,512]{3,2,1,0:T(8,128)(2,1)S(1)} collective-permute-done((bf16[4,2,16,512]{3,2,1,0:T(8,128)(2,1)S(1)}, bf16[4,2,16,512]{3,2,1,0:T(8,128)(2,1)S(1)}, u32[]{:S(2)}, u32[]{:S(2)}) %collective-permute-start.4) | collective-permute-done | bytes 131104 | tf_op jit(solution)/shard_map/ppermute | solution.py:436
  18.2 3.5 %collective-permute-start.6 = (bf16[4,2,16,512]{3,2,1,0:T(8,128)(2,1)S(1)}, bf16[4,2,16,512]{3,2,1,0:T(8,128)(2,1)S(1)}, u32[]{:S(2)}, u32[]{:S(2)}) collective-permute-start(bf16[4,2,16,512]{3,2,1,0:T(8,128)(2,1)S(1)} %collective-permute-done.4.near1), channel_id=1, source_target_pairs={{0,8},{8,16},{12,4},{16,24},{20,12},{28,20},{1,9},{9,17},{13,5},{1... | collective-permute-start | bytes 393224 | tf_op jit(solution)/shard_map/ppermute | solution.py:442
  21.7 3.7 %collective-permute-start.5 = (bf16[4,2,16,512]{3,2,1,0:T(8,128)(2,1)S(1)}, bf16[4,2,16,512]{3,2,1,0:T(8,128)(2,1)S(1)}, u32[]{:S(2)}, u32[]{:S(2)}) collective-permute-start(bf16[4,2,16,512]{3,2,1,0:T(8,128)(2,1)S(1)} %collective-permute-done.3.near0), channel_id=1, source_target_pairs={{0,8},{8,16},{12,4},{16,24},{20,12},{28,20},{1,9},{9,17},{13,5},{1... | collective-permute-start | bytes 393224 | tf_op jit(solution)/shard_map/ppermute | solution.py:442
  25.4 4.6 %axials.1.axial_ref = bf16[8,1024,512]{2,1,0:T(8,128)(2,1)S(1)} custom-call(bf16[8,510,2,510]{3,2,1,0:T(2,128)(2,1)} %bitcast.16), custom_call_target="tpu_custom_call" | custom-call | flops 2147483648 | bytes 16777216 | tf_op jit(solution)/shard_map/axials/pallas_call | solution.py:532
  29.9 0.0 collective-permute-done.6.far1
  29.9 0.0 collective-permute-done.5.far0
  30.0 9.5 %field.1 = (bf16[2,2,16,512]{3,2,1,0:T(8,128)(2,1)S(1)}, bf16[2,2,16,512]{3,2,1,0:T(8,128)(2,1)S(1)}, bf16[2,2,16,512]{3,2,1,0:T(8,128)(2,1)S(1)}, bf16[2,2,16,512]{3,2,1,0:T(8,128)(2,1)S(1)}) custom-call(bf16[8,512,512]{2,1,0:T(8,128)(2,1)S(1)} %get-tuple-element.75.rot_ref, bf16[8,1024,512]{2,1,0:T(8,128)(2,1)S(1)} %axials.1.axial_ref, ...), custom_call_target="tpu_custom_call" | custom-call | tf_op jit(solution)/shard_map/field/pallas_call | solution.py:545
  39.5 0.1 collective-permute-start.7
  39.6 1.5 %collective-permute-start.8 = (bf16[2,2,16,512]{3,2,1,0:T(8,128)(2,1)S(1)}, bf16[2,2,16,512]{3,2,1,0:T(8,128)(2,1)S(1)}, u32[]{:S(2)}, u32[]{:S(2)}) collective-permute-start(bf16[2,2,16,512]{3,2,1,0:T(8,128)(2,1)S(1)} %get-tuple-element.86), channel_id=1, source_target_pairs={{0,2},{1,3},{2,0},{3,1},{4,6},{5,7},{6,4},{7,5},{8,10},{9,11},{10,... | collective-permute-start | bytes 196616 | tf_op jit(solution)/shard_map/ppermute | solution.py:430
  41.1 0.3 collective-permute-start.9
  41.5 0.0 collective-permute-done.7.rest_1_
  41.5 2.7 %collective-permute-done.8.rest_2_ = bf16[2,2,16,512]{3,2,1,0:T(8,128)(2,1)S(1)} collective-permute-done((bf16[2,2,16,512]{3,2,1,0:T(8,128)(2,1)S(1)}, bf16[2,2,16,512]{3,2,1,0:T(8,128)(2,1)S(1)}, u32[]{:S(2)}, u32[]{:S(2)}) %collective-permute-start.8) | collective-permute-done | bytes 65568 | tf_op jit(solution)/shard_map/ppermute | solution.py:430
  44.1 1.0 %collective-permute-done.9.rest_3_ = bf16[2,2,16,512]{3,2,1,0:T(8,128)(2,1)S(1)} collective-permute-done((bf16[2,2,16,512]{3,2,1,0:T(8,128)(2,1)S(1)}, bf16[2,2,16,512]{3,2,1,0:T(8,128)(2,1)S(1)}, u32[]{:S(2)}, u32[]{:S(2)}) %collective-permute-start.9) | collective-permute-done | bytes 65568 | tf_op jit(solution)/shard_map/ppermute | solution.py:430
  45.2 1.4 %image.1 = (f32[1024,128]{1,0:T(8,128)S(1)}, f32[32,1,128]{2,1,0:T(1,128)S(1)}) custom-call(f32[4,2048,128]{2,1,0:T(8,128)S(1)} %get-tuple-element.53.blocks_ref, f32[256,4,128]{2,1,0:T(4,128)S(1)} %get-tuple-element.54.mie_ref, f32[1,128]{1,0:T(1,128)S(1)} %get-tuple-element.72.gram_ref, bf16[2,2,16,512]{3,2,1,0:T(8,128)(2,1)S(1)} %get-tuple-element.84.rest_0_, ...), custom_call_target="tpu_custom_call" | custom-call | tf_op jit(solution)/shard_map/image/pallas_call | solution.py:556
  46.6 10.4 %all_to_all.5.sums_ref = f32[32,1,128]{2,1,0:T(1,128)S(1)} all-to-all(f32[32,1,128]{2,1,0:T(1,128)S(1)} %get-tuple-element.88), channel_id=1, replica_groups=mesh['blk'=8,'pair'=4] {'blk','pair'}, dimensions={0} | all-to-all | bytes 32768 | tf_op jit(solution)/shard_map/all_to_all | solution.py:565
  57.0 1.7 %remainder.1 = (f32[2,8]{1,0:T(2,128)}, f32[255,4,128]{2,1,0:T(4,128)}) custom-call(f32[32,1,128]{2,1,0:T(1,128)S(1)} %all_to_all.5.sums_ref, f32[4,2048,128]{2,1,0:T(8,128)S(1)} %get-tuple-element.53.blocks_ref, f32[1024,128]{1,0:T(8,128)S(1)} %get-tuple-element.89.image_ref), custom_call_target="tpu_custom_call" | custom-call | tf_op jit(solution)/shard_map/remainder/pallas_call | solution.py:568
  (1 shorter events, 0.0 us)
Async XLA Ops:
  2.6 6.6 %collective-permute-start = (bf16[2,2,16,512]{3,2,1,0:T(8,128)(2,1)S(1)}, bf16[2,2,16,512]{3,2,1,0:T(8,128)(2,1)S(1)}, u32[]{:S(2)}, u32[]{:S(2)}) collective-permute-start(bf16[2,2,16,512]{3,2,1,0:T(8,128)(2,1)S(1)} %get-tuple-element.56), channel_id=1, source_target_pairs={{0,1},{1,0},{2,3},{3,2},{4,5},{5,4},{6,7},{7,6},{8,9},{9,8},{10,11... | collective-permute-start | bytes 196616 | tf_op jit(solution)/shard_map/ppermute | solution.py:430
  3.1 6.1 %collective-permute-start.1 = (bf16[2,2,16,512]{3,2,1,0:T(8,128)(2,1)S(1)}, bf16[2,2,16,512]{3,2,1,0:T(8,128)(2,1)S(1)}, u32[]{:S(2)}, u32[]{:S(2)}) collective-permute-start(bf16[2,2,16,512]{3,2,1,0:T(8,128)(2,1)S(1)} %get-tuple-element.57), channel_id=1, source_target_pairs={{0,2},{1,3},{2,0},{3,1},{4,6},{5,7},{6,4},{7,5},{8,10},{9,11},{10,... | collective-permute-start | bytes 196616 | tf_op jit(solution)/shard_map/ppermute | solution.py:430
  5.7 4.0 %collective-permute-start.2 = (bf16[2,2,16,512]{3,2,1,0:T(8,128)(2,1)S(1)}, bf16[2,2,16,512]{3,2,1,0:T(8,128)(2,1)S(1)}, u32[]{:S(2)}, u32[]{:S(2)}) collective-permute-start(bf16[2,2,16,512]{3,2,1,0:T(8,128)(2,1)S(1)} %get-tuple-element.58), channel_id=1, source_target_pairs={{0,3},{1,2},{2,1},{3,0},{4,7},{5,6},{6,5},{7,4},{8,11},{9,10},{10,... | collective-permute-start | bytes 196616 | tf_op jit(solution)/shard_map/ppermute | solution.py:430
  9.8 6.4 %collective-permute-start.3 = (bf16[4,2,16,512]{3,2,1,0:T(8,128)(2,1)S(1)}, bf16[4,2,16,512]{3,2,1,0:T(8,128)(2,1)S(1)}, u32[]{:S(2)}, u32[]{:S(2)}) collective-permute-start(bf16[4,2,16,512]{3,2,1,0:T(8,128)(2,1)S(1)} %get-tuple-element.80.own0), channel_id=1, source_target_pairs={{0,4},{4,0},{8,12},{12,8},{16,20},{20,16},{24,28},{28,24},{1,5},{5... | collective-permute-start | bytes 393224 | tf_op jit(solution)/shard_map/ppermute | solution.py:436
  11.4 6.8 %collective-permute-start.4 = (bf16[4,2,16,512]{3,2,1,0:T(8,128)(2,1)S(1)}, bf16[4,2,16,512]{3,2,1,0:T(8,128)(2,1)S(1)}, u32[]{:S(2)}, u32[]{:S(2)}) collective-permute-start(bf16[4,2,16,512]{3,2,1,0:T(8,128)(2,1)S(1)} %get-tuple-element.81.own1), channel_id=1, source_target_pairs={{0,4},{4,0},{8,12},{12,8},{16,20},{20,16},{24,28},{28,24},{1,5},{5... | collective-permute-start | bytes 393224 | tf_op jit(solution)/shard_map/ppermute | solution.py:436
  18.2 11.7 %collective-permute-start.6 = (bf16[4,2,16,512]{3,2,1,0:T(8,128)(2,1)S(1)}, bf16[4,2,16,512]{3,2,1,0:T(8,128)(2,1)S(1)}, u32[]{:S(2)}, u32[]{:S(2)}) collective-permute-start(bf16[4,2,16,512]{3,2,1,0:T(8,128)(2,1)S(1)} %collective-permute-done.4.near1), channel_id=1, source_target_pairs={{0,8},{8,16},{12,4},{16,24},{20,12},{28,20},{1,9},{9,17},{13,5},{1... | collective-permute-start | bytes 393224 | tf_op jit(solution)/shard_map/ppermute | solution.py:442
  21.7 8.3 %collective-permute-start.5 = (bf16[4,2,16,512]{3,2,1,0:T(8,128)(2,1)S(1)}, bf16[4,2,16,512]{3,2,1,0:T(8,128)(2,1)S(1)}, u32[]{:S(2)}, u32[]{:S(2)}) collective-permute-start(bf16[4,2,16,512]{3,2,1,0:T(8,128)(2,1)S(1)} %collective-permute-done.3.near0), channel_id=1, source_target_pairs={{0,8},{8,16},{12,4},{16,24},{20,12},{28,20},{1,9},{9,17},{13,5},{1... | collective-permute-start | bytes 393224 | tf_op jit(solution)/shard_map/ppermute | solution.py:442
  39.5 1.9 %collective-permute-start.7 = (bf16[2,2,16,512]{3,2,1,0:T(8,128)(2,1)S(1)}, bf16[2,2,16,512]{3,2,1,0:T(8,128)(2,1)S(1)}, u32[]{:S(2)}, u32[]{:S(2)}) collective-permute-start(bf16[2,2,16,512]{3,2,1,0:T(8,128)(2,1)S(1)} %get-tuple-element.85), channel_id=1, source_target_pairs={{0,1},{1,0},{2,3},{3,2},{4,5},{5,4},{6,7},{7,6},{8,9},{9,8},{10,11... | collective-permute-start | bytes 196616 | tf_op jit(solution)/shard_map/ppermute | solution.py:430
  39.6 4.5 %collective-permute-start.8 = (bf16[2,2,16,512]{3,2,1,0:T(8,128)(2,1)S(1)}, bf16[2,2,16,512]{3,2,1,0:T(8,128)(2,1)S(1)}, u32[]{:S(2)}, u32[]{:S(2)}) collective-permute-start(bf16[2,2,16,512]{3,2,1,0:T(8,128)(2,1)S(1)} %get-tuple-element.86), channel_id=1, source_target_pairs={{0,2},{1,3},{2,0},{3,1},{4,6},{5,7},{6,4},{7,5},{8,10},{9,11},{10,... | collective-permute-start | bytes 196616 | tf_op jit(solution)/shard_map/ppermute | solution.py:430
  41.1 4.1 %collective-permute-start.9 = (bf16[2,2,16,512]{3,2,1,0:T(8,128)(2,1)S(1)}, bf16[2,2,16,512]{3,2,1,0:T(8,128)(2,1)S(1)}, u32[]{:S(2)}, u32[]{:S(2)}) collective-permute-start(bf16[2,2,16,512]{3,2,1,0:T(8,128)(2,1)S(1)} %get-tuple-element.87), channel_id=1, source_target_pairs={{0,3},{1,2},{2,1},{3,0},{4,7},{5,6},{6,5},{7,4},{8,11},{9,10},{10,... | collective-permute-start | bytes 196616 | tf_op jit(solution)/shard_map/ppermute | solution.py:430

commit v21 on v19

--- a/solution.py
+++ b/solution.py
@@ -296,7 +296,7 @@
     for q in range(parts):
         for copy in copies[2 * blocks * q : 2 * blocks * (q + 1)]:
             copy.wait()
-        if q < parts - 1:
+        if q < parts - 2:
             for first in range(step * q, step * (q + 1), chunk):
                 add_products(blocks_ref, products_ref, rows, first, chunk)
     mie_copy.wait()
@@ -305,7 +305,7 @@
 def gram_end(rows, products_ref, blocks_ref, line_ref, totals_ref):
     parts, chunk = 4, 32
     totals_ref[...] = products_ref[...]
-    for first in range(rounded_up(rows, 8 * parts) // parts * (parts - 1), rows, chunk):
+    for first in range(rounded_up(rows, 8 * parts) // parts * (parts - 2), rows, chunk):
         add_products(blocks_ref, totals_ref, rows, first, chunk)
     line_ref[...] = products_line(totals_ref)
 

time: 56.8 us -> 56.8 us (level)
    pallas_call x1, Pallas kernels: 6.78 us -> 7.48 us  [shards(): pl.pallas_call(functools.partial(tables_kernel, quarter, modes), in_specs...]
    pallas_call x1, Pallas kernels: 3.46 us -> 2.85 us  [shards(): pl.pallas_call(functools.partial(gram_kernel, quarter, modes), in_specs=[...]
    ppermute x6, waiting for transfers between devices: 4.2 us -> 4.81 us  [exchanged(): lax.ppermute(pieces[i], axis, [(p, p ^ i) for p in range(count)])]
where the time goes in v21:
time: 56.8 us; the launch traced here: 56.6 us
  Pallas kernels  24.4 us (43%)
  blocking collectives  12.6 us (22%)
  starting transfers between devices  10.9 us (19%)
  waiting for transfers between devices  7.27 us (13%)
  between operations  1.37 us (2%)
    all_to_all x1, blocking collectives, shards(): lax.all_to_all(sums, ('blk', 'pair'), split_axis=0, concat_axis=0, tiled=...  12.6 us
    pallas_call x1, Pallas kernels, shards(): pl.pallas_call(functools.partial(field_kernel, own, modes, together), in_...  9.53 us
    pallas_call x1, Pallas kernels, shards(): pl.pallas_call(functools.partial(tables_kernel, quarter, modes), in_specs...  7.48 us
    ppermute x2, starting transfers between devices, neighbours(): return (lax.ppermute(value, 'blk', up), lax.ppermute(value, 'blk', down))  5.85 us
    ppermute x6, starting transfers between devices, exchanged(): lax.ppermute(pieces[i], axis, [(p, p ^ i) for p in range(count)])  5.09 us
    ppermute x6, waiting for transfers between devices, exchanged(): lax.ppermute(pieces[i], axis, [(p, p ^ i) for p in range(count)])  4.81 us
    pallas_call x1, Pallas kernels, shards(): pl.pallas_call(functools.partial(gram_kernel, quarter, modes), in_specs=[...  2.85 us
    ppermute x2, waiting for transfers between devices, neighbours(): return (lax.ppermute(value, 'blk', up), lax.ppermute(value, 'blk', down))  2.46 us
  transfers between devices with their start and end apart: 8, of which 4 were waited for; matrix products, arithmetic and copies ran while one was open for 0% of the time, Pallas kernels for 18%

profile of v21, /device:TPU:0, one launch (start us, length us, event | category | flops | bytes accessed | tf_op | source)
XLA Modules:
  0.0 56.6 jit_solution(4392802587729478141)
XLA Ops:
  1.3 1.3 %pack.1 = (bf16[2,2,16,512]{3,2,1,0:T(8,128)(2,1)S(1)}, bf16[2,2,16,512]{3,2,1,0:T(8,128)(2,1)S(1)}, bf16[2,2,16,512]{3,2,1,0:T(8,128)(2,1)S(1)}, bf16[2,2,16,512]{3,2,1,0:T(8,128)(2,1)S(1)}) custom-call(s32[3,1,128]{2,1,0:T(1,128)} %bitcast.19, s32[1]{0:T(128)S(6)} %copy.8.count_ref, f32[4,2040,128]{2,1,0:T(8,128)} %bitcast.14), custom_call_target="tpu_custom_call" | custom-call | tf_op jit(solution)/shard_map/pack/pallas_call | solution.py:457
  2.6 0.5 collective-permute-start
  3.1 2.6 %collective-permute-start.1 = (bf16[2,2,16,512]{3,2,1,0:T(8,128)(2,1)S(1)}, bf16[2,2,16,512]{3,2,1,0:T(8,128)(2,1)S(1)}, u32[]{:S(2)}, u32[]{:S(2)}) collective-permute-start(bf16[2,2,16,512]{3,2,1,0:T(8,128)(2,1)S(1)} %get-tuple-element.52), channel_id=1, source_target_pairs={{0,2},{1,3},{2,0},{3,1},{4,6},{5,7},{6,4},{7,5},{8,10},{9,11},{10,... | collective-permute-start | bytes 196616 | tf_op jit(solution)/shard_map/ppermute | solution.py:423
  5.7 0.1 collective-permute-start.2
  5.7 2.8 %gram.1 = (f32[8,8,8,128]{3,2,1,0:T(8,128)S(1)}, f32[4,2048,128]{2,1,0:T(8,128)S(1)}, f32[256,4,128]{2,1,0:T(4,128)S(1)}) custom-call(f32[4,2040,128]{2,1,0:T(8,128)} %bitcast.15, f32[255,4,128]{2,1,0:T(4,128)} %bitcast.18), custom_call_target="tpu_custom_call" | custom-call | tf_op jit(solution)/shard_map/gram/pallas_call | solution.py:476
  8.6 0.0 collective-permute-done.refs_1_
  8.6 0.0 collective-permute-done.1.refs_2_
  8.6 1.1 %collective-permute-done.2.refs_3_ = bf16[2,2,16,512]{3,2,1,0:T(8,128)(2,1)S(1)} collective-permute-done((bf16[2,2,16,512]{3,2,1,0:T(8,128)(2,1)S(1)}, bf16[2,2,16,512]{3,2,1,0:T(8,128)(2,1)S(1)}, u32[]{:S(2)}, u32[]{:S(2)}) %collective-permute-start.2) | collective-permute-done | bytes 65568 | tf_op jit(solution)/shard_map/ppermute | solution.py:423
  9.8 1.3 %collective-permute-start.4 = (bf16[4,2,2,16,512]{4,3,2,1,0:T(8,128)(2,1)S(1)}, bf16[4,2,2,16,512]{4,3,2,1,0:T(8,128)(2,1)S(1)}, u32[]{:S(2)}, u32[]{:S(2)}) collective-permute-start(bf16[4,2,2,16,512]{4,3,2,1,0:T(8,128)(2,1)S(1)} %join.1.own_ref), channel_id=1, source_target_pairs={{4,0},{8,4},{12,8},{16,12},{20,16},{24,20},{28,24},{5,1},{9,5},{13... | collective-permute-start | bytes 786440 | tf_op jit(solution)/shard_map/ppermute | solution.py:431
  11.1 4.6 %collective-permute-start.3 = (bf16[4,2,2,16,512]{4,3,2,1,0:T(8,128)(2,1)S(1)}, bf16[4,2,2,16,512]{4,3,2,1,0:T(8,128)(2,1)S(1)}, u32[]{:S(2)}, u32[]{:S(2)}) collective-permute-start(bf16[4,2,2,16,512]{4,3,2,1,0:T(8,128)(2,1)S(1)} %join.1.own_ref), channel_id=1, source_target_pairs={{0,4},{4,8},{8,12},{12,16},{16,20},{20,24},{24,28},{1,5},{5,9},{9,... | collective-permute-start | bytes 786440 | tf_op jit(solution)/shard_map/ppermute | solution.py:431
  15.6 7.5 %tables.1 = (bf16[8,512,512]{2,1,0:T(8,128)(2,1)S(1)}, bf16[8,1024,512]{2,1,0:T(8,128)(2,1)S(1)}, f32[1,128]{1,0:T(1,128)S(1)}) custom-call(bf16[4080,510]{1,0:T(8,128)(2,1)} %bitcast.17, bf16[8,510,2,510]{3,2,1,0:T(2,128)(2,1)} %bitcast.16, f32[8,8,8,128]{3,2,1,0:T(8,128)S(1)} %get-tuple-element.64.products_ref, ...), custom_call_target="tpu_custom_call" | custom-call | flops 2147483648 | bytes 25165824 | tf_op jit(solution)/shard_map/tables/pallas_call | solution.py:503
  23.1 0.0 collective-permute-done.4.above_ref
  23.1 2.5 %collective-permute-done.3.below_ref = bf16[4,2,2,16,512]{4,3,2,1,0:T(8,128)(2,1)S(1)} collective-permute-done((bf16[4,2,2,16,512]{4,3,2,1,0:T(8,128)(2,1)S(1)}, bf16[4,2,2,16,512]{4,3,2,1,0:T(8,128)(2,1)S(1)}, u32[]{:S(2)}, u32[]{:S(2)}) %collective-permute-start.3) | collective-permute-done | bytes 262176 | tf_op jit(solution)/shard_map/ppermute | solution.py:431
  25.6 9.5 %field.1 = (bf16[2,2,16,512]{3,2,1,0:T(8,128)(2,1)S(1)}, bf16[2,2,16,512]{3,2,1,0:T(8,128)(2,1)S(1)}, bf16[2,2,16,512]{3,2,1,0:T(8,128)(2,1)S(1)}, bf16[2,2,16,512]{3,2,1,0:T(8,128)(2,1)S(1)}) custom-call(bf16[8,512,512]{2,1,0:T(8,128)(2,1)S(1)} %get-tuple-element.69.rot_ref, bf16[8,1024,512]{2,1,0:T(8,128)(2,1)S(1)} %get-tuple-element.70.axial_ref, ...), custom_call_target="tpu_custom_call" | custom-call | tf_op jit(solution)/shard_map/field/pallas_call | solution.py:525
  35.1 0.1 collective-permute-start.5
  35.2 1.5 %collective-permute-start.6 = (bf16[2,2,16,512]{3,2,1,0:T(8,128)(2,1)S(1)}, bf16[2,2,16,512]{3,2,1,0:T(8,128)(2,1)S(1)}, u32[]{:S(2)}, u32[]{:S(2)}) collective-permute-start(bf16[2,2,16,512]{3,2,1,0:T(8,128)(2,1)S(1)} %get-tuple-element.76), channel_id=1, source_target_pairs={{0,2},{1,3},{2,0},{3,1},{4,6},{5,7},{6,4},{7,5},{8,10},{9,11},{10,... | collective-permute-start | bytes 196616 | tf_op jit(solution)/shard_map/ppermute | solution.py:423
  36.7 0.3 collective-permute-start.7
  37.1 0.0 collective-permute-done.5.rest_1_
  37.1 2.6 %collective-permute-done.6.rest_2_ = bf16[2,2,16,512]{3,2,1,0:T(8,128)(2,1)S(1)} collective-permute-done((bf16[2,2,16,512]{3,2,1,0:T(8,128)(2,1)S(1)}, bf16[2,2,16,512]{3,2,1,0:T(8,128)(2,1)S(1)}, u32[]{:S(2)}, u32[]{:S(2)}) %collective-permute-start.6) | collective-permute-done | bytes 65568 | tf_op jit(solution)/shard_map/ppermute | solution.py:423
  39.7 1.1 %collective-permute-done.7.rest_3_ = bf16[2,2,16,512]{3,2,1,0:T(8,128)(2,1)S(1)} collective-permute-done((bf16[2,2,16,512]{3,2,1,0:T(8,128)(2,1)S(1)}, bf16[2,2,16,512]{3,2,1,0:T(8,128)(2,1)S(1)}, u32[]{:S(2)}, u32[]{:S(2)}) %collective-permute-start.7) | collective-permute-done | bytes 65568 | tf_op jit(solution)/shard_map/ppermute | solution.py:423
  40.8 1.5 %image.1 = (f32[1024,128]{1,0:T(8,128)S(1)}, f32[32,1,128]{2,1,0:T(1,128)S(1)}) custom-call(f32[4,2048,128]{2,1,0:T(8,128)S(1)} %get-tuple-element.48.blocks_ref, f32[256,4,128]{2,1,0:T(4,128)S(1)} %get-tuple-element.49.mie_ref, f32[1,128]{1,0:T(1,128)S(1)} %get-tuple-element.68.gram_ref, bf16[2,2,16,512]{3,2,1,0:T(8,128)(2,1)S(1)} %get-tuple-element.74.rest_0_, ...), custom_call_target="tpu_custom_call" | custom-call | tf_op jit(solution)/shard_map/image/pallas_call | solution.py:536
  42.2 12.6 %all_to_all.5.sums_ref = f32[32,1,128]{2,1,0:T(1,128)S(1)} all-to-all(f32[32,1,128]{2,1,0:T(1,128)S(1)} %get-tuple-element.78), channel_id=1, replica_groups=mesh['blk'=8,'pair'=4] {'blk','pair'}, dimensions={0} | all-to-all | bytes 32768 | tf_op jit(solution)/shard_map/all_to_all | solution.py:545
  54.8 1.7 %remainder.1 = (f32[2,8]{1,0:T(2,128)}, f32[255,4,128]{2,1,0:T(4,128)}) custom-call(f32[32,1,128]{2,1,0:T(1,128)S(1)} %all_to_all.5.sums_ref, f32[4,2048,128]{2,1,0:T(8,128)S(1)} %get-tuple-element.48.blocks_ref, f32[1024,128]{1,0:T(8,128)S(1)} %get-tuple-element.79.image_ref), custom_call_target="tpu_custom_call" | custom-call | tf_op jit(solution)/shard_map/remainder/pallas_call | solution.py:548
  (1 shorter events, 0.0 us)
Async XLA Ops:
  2.6 6.0 %collective-permute-start = (bf16[2,2,16,512]{3,2,1,0:T(8,128)(2,1)S(1)}, bf16[2,2,16,512]{3,2,1,0:T(8,128)(2,1)S(1)}, u32[]{:S(2)}, u32[]{:S(2)}) collective-permute-start(bf16[2,2,16,512]{3,2,1,0:T(8,128)(2,1)S(1)} %get-tuple-element.51), channel_id=1, source_target_pairs={{0,1},{1,0},{2,3},{3,2},{4,5},{5,4},{6,7},{7,6},{8,9},{9,8},{10,11... | collective-permute-start | bytes 196616 | tf_op jit(solution)/shard_map/ppermute | solution.py:423
  3.1 5.5 %collective-permute-start.1 = (bf16[2,2,16,512]{3,2,1,0:T(8,128)(2,1)S(1)}, bf16[2,2,16,512]{3,2,1,0:T(8,128)(2,1)S(1)}, u32[]{:S(2)}, u32[]{:S(2)}) collective-permute-start(bf16[2,2,16,512]{3,2,1,0:T(8,128)(2,1)S(1)} %get-tuple-element.52), channel_id=1, source_target_pairs={{0,2},{1,3},{2,0},{3,1},{4,6},{5,7},{6,4},{7,5},{8,10},{9,11},{10,... | collective-permute-start | bytes 196616 | tf_op jit(solution)/shard_map/ppermute | solution.py:423
  5.7 4.0 %collective-permute-start.2 = (bf16[2,2,16,512]{3,2,1,0:T(8,128)(2,1)S(1)}, bf16[2,2,16,512]{3,2,1,0:T(8,128)(2,1)S(1)}, u32[]{:S(2)}, u32[]{:S(2)}) collective-permute-start(bf16[2,2,16,512]{3,2,1,0:T(8,128)(2,1)S(1)} %get-tuple-element.53), channel_id=1, source_target_pairs={{0,3},{1,2},{2,1},{3,0},{4,7},{5,6},{6,5},{7,4},{8,11},{9,10},{10,... | collective-permute-start | bytes 196616 | tf_op jit(solution)/shard_map/ppermute | solution.py:423
  9.8 13.4 %collective-permute-start.4 = (bf16[4,2,2,16,512]{4,3,2,1,0:T(8,128)(2,1)S(1)}, bf16[4,2,2,16,512]{4,3,2,1,0:T(8,128)(2,1)S(1)}, u32[]{:S(2)}, u32[]{:S(2)}) collective-permute-start(bf16[4,2,2,16,512]{4,3,2,1,0:T(8,128)(2,1)S(1)} %join.1.own_ref), channel_id=1, source_target_pairs={{4,0},{8,4},{12,8},{16,12},{20,16},{24,20},{28,24},{5,1},{9,5},{13... | collective-permute-start | bytes 786440 | tf_op jit(solution)/shard_map/ppermute | solution.py:431
  11.1 14.5 %collective-permute-start.3 = (bf16[4,2,2,16,512]{4,3,2,1,0:T(8,128)(2,1)S(1)}, bf16[4,2,2,16,512]{4,3,2,1,0:T(8,128)(2,1)S(1)}, u32[]{:S(2)}, u32[]{:S(2)}) collective-permute-start(bf16[4,2,2,16,512]{4,3,2,1,0:T(8,128)(2,1)S(1)} %join.1.own_ref), channel_id=1, source_target_pairs={{0,4},{4,8},{8,12},{12,16},{16,20},{20,24},{24,28},{1,5},{5,9},{9,... | collective-permute-start | bytes 786440 | tf_op jit(solution)/shard_map/ppermute | solution.py:431
  35.1 1.9 %collective-permute-start.5 = (bf16[2,2,16,512]{3,2,1,0:T(8,128)(2,1)S(1)}, bf16[2,2,16,512]{3,2,1,0:T(8,128)(2,1)S(1)}, u32[]{:S(2)}, u32[]{:S(2)}) collective-permute-start(bf16[2,2,16,512]{3,2,1,0:T(8,128)(2,1)S(1)} %get-tuple-element.75), channel_id=1, source_target_pairs={{0,1},{1,0},{2,3},{3,2},{4,5},{5,4},{6,7},{7,6},{8,9},{9,8},{10,11... | collective-permute-start | bytes 196616 | tf_op jit(solution)/shard_map/ppermute | solution.py:423
  35.2 4.5 %collective-permute-start.6 = (bf16[2,2,16,512]{3,2,1,0:T(8,128)(2,1)S(1)}, bf16[2,2,16,512]{3,2,1,0:T(8,128)(2,1)S(1)}, u32[]{:S(2)}, u32[]{:S(2)}) collective-permute-start(bf16[2,2,16,512]{3,2,1,0:T(8,128)(2,1)S(1)} %get-tuple-element.76), channel_id=1, source_target_pairs={{0,2},{1,3},{2,0},{3,1},{4,6},{5,7},{6,4},{7,5},{8,10},{9,11},{10,... | collective-permute-start | bytes 196616 | tf_op jit(solution)/shard_map/ppermute | solution.py:423
  36.7 4.0 %collective-permute-start.7 = (bf16[2,2,16,512]{3,2,1,0:T(8,128)(2,1)S(1)}, bf16[2,2,16,512]{3,2,1,0:T(8,128)(2,1)S(1)}, u32[]{:S(2)}, u32[]{:S(2)}) collective-permute-start(bf16[2,2,16,512]{3,2,1,0:T(8,128)(2,1)S(1)} %get-tuple-element.77), channel_id=1, source_target_pairs={{0,3},{1,2},{2,1},{3,0},{4,7},{5,6},{6,5},{7,4},{8,11},{9,10},{10,... | collective-permute-start | bytes 196616 | tf_op jit(solution)/shard_map/ppermute | solution.py:423

commit v22 on v19

--- a/solution.py
+++ b/solution.py
@@ -428,7 +428,8 @@
     count = lax.axis_size("blk")
     up = [(i, i + 1) for i in range(count - 1)]
     down = [(j, i) for i, j in up]
-    return lax.ppermute(value, "blk", up), lax.ppermute(value, "blk", down)
+    above = lax.ppermute(value, "blk", down)
+    return lax.ppermute(value, "blk", up), above
 
 
 def shards(basis, mie_coeffs, rot_table, axial_table, pair_table, pair_count):
@@ -519,7 +520,7 @@
         cost_estimate=pl.CostEstimate(flops=tables * 8 * 256 * 256 * size, bytes_accessed=6 * tables * size * size * 2, transcendentals=0),
         name="tables",
     )(rot_rows, axial_rows, products, blocks)
-    below, above, rotations, axials, line = lax.optimization_barrier((below, above, rotations, axials, line))
+    above, below, rotations, axials, line = lax.optimization_barrier((above, below, rotations, axials, line))
 
     together = tables
     field = pl.pallas_call(

time: 56.8 us -> 56.9 us (level)
  starting transfers between devices: 11.1 us -> 10 us
  blocking collectives: 12.6 us -> 13.6 us
    ppermute x2, starting transfers between devices: 6.03 us -> 4.91 us  [the longest x1 3.44 us: neighbours(): return (lax.ppermute(value, 'blk', up), above)]
    all_to_all x1, blocking collectives: 12.6 us -> 13.6 us  [shards(): lax.all_to_all(sums, ('blk', 'pair'), split_axis=0, concat_axis=0, tiled=...]
where the time goes in v22:
time: 56.9 us; the launch traced here: 56.6 us
  Pallas kernels  24.3 us (43%)
  blocking collectives  13.6 us (24%)
  starting transfers between devices  10 us (18%)
  waiting for transfers between devices  7.4 us (13%)
  between operations  1.36 us (2%)
    all_to_all x1, blocking collectives, shards(): lax.all_to_all(sums, ('blk', 'pair'), split_axis=0, concat_axis=0, tiled=...  13.6 us
    pallas_call x1, Pallas kernels, shards(): pl.pallas_call(functools.partial(field_kernel, own, modes, together), in_...  9.53 us
    pallas_call x1, Pallas kernels, shards(): pl.pallas_call(functools.partial(tables_kernel, quarter, modes), in_specs...  6.8 us
    ppermute x6, starting transfers between devices, exchanged(): lax.ppermute(pieces[i], axis, [(p, p ^ i) for p in range(count)])  5.08 us
    ppermute x6, waiting for transfers between devices, exchanged(): lax.ppermute(pieces[i], axis, [(p, p ^ i) for p in range(count)])  4.2 us
    pallas_call x1, Pallas kernels, shards(): pl.pallas_call(functools.partial(gram_kernel, quarter, modes), in_specs=[...  3.46 us
    ppermute x1, starting transfers between devices, neighbours(): return (lax.ppermute(value, 'blk', up), above)  3.44 us
    ppermute x1, waiting for transfers between devices, neighbours(): return (lax.ppermute(value, 'blk', up), above)  3.2 us
  transfers between devices with their start and end apart: 8, of which 4 were waited for; matrix products, arithmetic and copies ran while one was open for 0% of the time, Pallas kernels for 18%

profile of v22, /device:TPU:0, one launch (start us, length us, event | category | flops | bytes accessed | tf_op | source)
XLA Modules:
  0.0 56.6 jit_solution(17746288012042807564)
XLA Ops:
  1.3 1.3 %pack.1 = (bf16[2,2,16,512]{3,2,1,0:T(8,128)(2,1)S(1)}, bf16[2,2,16,512]{3,2,1,0:T(8,128)(2,1)S(1)}, bf16[2,2,16,512]{3,2,1,0:T(8,128)(2,1)S(1)}, bf16[2,2,16,512]{3,2,1,0:T(8,128)(2,1)S(1)}) custom-call(s32[3,1,128]{2,1,0:T(1,128)} %bitcast.19, s32[1]{0:T(128)S(6)} %copy.8.count_ref, f32[4,2040,128]{2,1,0:T(8,128)} %bitcast.14), custom_call_target="tpu_custom_call" | custom-call | tf_op jit(solution)/shard_map/pack/pallas_call | solution.py:458
  2.6 0.5 collective-permute-start
  3.1 2.6 %collective-permute-start.1 = (bf16[2,2,16,512]{3,2,1,0:T(8,128)(2,1)S(1)}, bf16[2,2,16,512]{3,2,1,0:T(8,128)(2,1)S(1)}, u32[]{:S(2)}, u32[]{:S(2)}) collective-permute-start(bf16[2,2,16,512]{3,2,1,0:T(8,128)(2,1)S(1)} %get-tuple-element.52), channel_id=1, source_target_pairs={{0,2},{1,3},{2,0},{3,1},{4,6},{5,7},{6,4},{7,5},{8,10},{9,11},{10,... | collective-permute-start | bytes 196616 | tf_op jit(solution)/shard_map/ppermute | solution.py:423
  5.7 0.1 collective-permute-start.2
  5.7 3.5 %gram.1 = (f32[8,8,8,128]{3,2,1,0:T(8,128)S(1)}, f32[4,2048,128]{2,1,0:T(8,128)S(1)}, f32[256,4,128]{2,1,0:T(4,128)S(1)}) custom-call(f32[4,2040,128]{2,1,0:T(8,128)} %bitcast.15, f32[255,4,128]{2,1,0:T(4,128)} %bitcast.18), custom_call_target="tpu_custom_call" | custom-call | tf_op jit(solution)/shard_map/gram/pallas_call | solution.py:477
  9.2 0.0 collective-permute-done.refs_1_
  9.2 0.0 collective-permute-done.1.refs_2_
  9.2 0.5 collective-permute-done.2.refs_3_
  9.8 3.4 %collective-permute-start.4 = (bf16[4,2,2,16,512]{4,3,2,1,0:T(8,128)(2,1)S(1)}, bf16[4,2,2,16,512]{4,3,2,1,0:T(8,128)(2,1)S(1)}, u32[]{:S(2)}, u32[]{:S(2)}) collective-permute-start(bf16[4,2,2,16,512]{4,3,2,1,0:T(8,128)(2,1)S(1)} %join.1.own_ref), channel_id=1, source_target_pairs={{0,4},{4,8},{8,12},{12,16},{16,20},{20,24},{24,28},{1,5},{5,9},{9,... | collective-permute-start | bytes 786440 | tf_op jit(solution)/shard_map/ppermute | solution.py:432
  13.2 1.5 %collective-permute-start.3 = (bf16[4,2,2,16,512]{4,3,2,1,0:T(8,128)(2,1)S(1)}, bf16[4,2,2,16,512]{4,3,2,1,0:T(8,128)(2,1)S(1)}, u32[]{:S(2)}, u32[]{:S(2)}) collective-permute-start(bf16[4,2,2,16,512]{4,3,2,1,0:T(8,128)(2,1)S(1)} %join.1.own_ref), channel_id=1, source_target_pairs={{4,0},{8,4},{12,8},{16,12},{20,16},{24,20},{28,24},{5,1},{9,5},{13... | collective-permute-start | bytes 786440 | tf_op jit(solution)/shard_map/ppermute | solution.py:431
  14.7 6.8 %tables.1 = (bf16[8,512,512]{2,1,0:T(8,128)(2,1)S(1)}, bf16[8,1024,512]{2,1,0:T(8,128)(2,1)S(1)}, f32[1,128]{1,0:T(1,128)S(1)}) custom-call(bf16[4080,510]{1,0:T(8,128)(2,1)} %bitcast.17, bf16[8,510,2,510]{3,2,1,0:T(2,128)(2,1)} %bitcast.16, f32[8,8,8,128]{3,2,1,0:T(8,128)S(1)} %get-tuple-element.64.products_ref, ...), custom_call_target="tpu_custom_call" | custom-call | flops 2147483648 | bytes 25165824 | tf_op jit(solution)/shard_map/tables/pallas_call | solution.py:504
  21.5 3.2 %collective-permute-done.4.below_ref = bf16[4,2,2,16,512]{4,3,2,1,0:T(8,128)(2,1)S(1)} collective-permute-done((bf16[4,2,2,16,512]{4,3,2,1,0:T(8,128)(2,1)S(1)}, bf16[4,2,2,16,512]{4,3,2,1,0:T(8,128)(2,1)S(1)}, u32[]{:S(2)}, u32[]{:S(2)}) %collective-permute-start.4) | collective-permute-done | bytes 262176 | tf_op jit(solution)/shard_map/ppermute | solution.py:432
  24.7 0.0 collective-permute-done.3.above_ref
  24.7 9.5 %field.1 = (bf16[2,2,16,512]{3,2,1,0:T(8,128)(2,1)S(1)}, bf16[2,2,16,512]{3,2,1,0:T(8,128)(2,1)S(1)}, bf16[2,2,16,512]{3,2,1,0:T(8,128)(2,1)S(1)}, bf16[2,2,16,512]{3,2,1,0:T(8,128)(2,1)S(1)}) custom-call(bf16[8,512,512]{2,1,0:T(8,128)(2,1)S(1)} %get-tuple-element.69.rot_ref, bf16[8,1024,512]{2,1,0:T(8,128)(2,1)S(1)} %get-tuple-element.70.axial_ref, ...), custom_call_target="tpu_custom_call" | custom-call | tf_op jit(solution)/shard_map/field/pallas_call | solution.py:526
  34.2 0.1 collective-permute-start.5
  34.3 1.5 %collective-permute-start.6 = (bf16[2,2,16,512]{3,2,1,0:T(8,128)(2,1)S(1)}, bf16[2,2,16,512]{3,2,1,0:T(8,128)(2,1)S(1)}, u32[]{:S(2)}, u32[]{:S(2)}) collective-permute-start(bf16[2,2,16,512]{3,2,1,0:T(8,128)(2,1)S(1)} %get-tuple-element.76), channel_id=1, source_target_pairs={{0,2},{1,3},{2,0},{3,1},{4,6},{5,7},{6,4},{7,5},{8,10},{9,11},{10,... | collective-permute-start | bytes 196616 | tf_op jit(solution)/shard_map/ppermute | solution.py:423
  35.8 0.3 collective-permute-start.7
  36.2 0.0 collective-permute-done.5.rest_1_
  36.2 2.6 %collective-permute-done.6.rest_2_ = bf16[2,2,16,512]{3,2,1,0:T(8,128)(2,1)S(1)} collective-permute-done((bf16[2,2,16,512]{3,2,1,0:T(8,128)(2,1)S(1)}, bf16[2,2,16,512]{3,2,1,0:T(8,128)(2,1)S(1)}, u32[]{:S(2)}, u32[]{:S(2)}) %collective-permute-start.6) | collective-permute-done | bytes 65568 | tf_op jit(solution)/shard_map/ppermute | solution.py:423
  38.8 1.1 %collective-permute-done.7.rest_3_ = bf16[2,2,16,512]{3,2,1,0:T(8,128)(2,1)S(1)} collective-permute-done((bf16[2,2,16,512]{3,2,1,0:T(8,128)(2,1)S(1)}, bf16[2,2,16,512]{3,2,1,0:T(8,128)(2,1)S(1)}, u32[]{:S(2)}, u32[]{:S(2)}) %collective-permute-start.7) | collective-permute-done | bytes 65568 | tf_op jit(solution)/shard_map/ppermute | solution.py:423
  39.9 1.5 %image.1 = (f32[1024,128]{1,0:T(8,128)S(1)}, f32[32,1,128]{2,1,0:T(1,128)S(1)}) custom-call(f32[4,2048,128]{2,1,0:T(8,128)S(1)} %get-tuple-element.48.blocks_ref, f32[256,4,128]{2,1,0:T(4,128)S(1)} %get-tuple-element.49.mie_ref, f32[1,128]{1,0:T(1,128)S(1)} %get-tuple-element.68.gram_ref, bf16[2,2,16,512]{3,2,1,0:T(8,128)(2,1)S(1)} %get-tuple-element.74.rest_0_, ...), custom_call_target="tpu_custom_call" | custom-call | tf_op jit(solution)/shard_map/image/pallas_call | solution.py:537
  41.3 13.6 %all_to_all.5.sums_ref = f32[32,1,128]{2,1,0:T(1,128)S(1)} all-to-all(f32[32,1,128]{2,1,0:T(1,128)S(1)} %get-tuple-element.78), channel_id=1, replica_groups=mesh['blk'=8,'pair'=4] {'blk','pair'}, dimensions={0} | all-to-all | bytes 32768 | tf_op jit(solution)/shard_map/all_to_all | solution.py:546
  54.9 1.7 %remainder.1 = (f32[2,8]{1,0:T(2,128)}, f32[255,4,128]{2,1,0:T(4,128)}) custom-call(f32[32,1,128]{2,1,0:T(1,128)S(1)} %all_to_all.5.sums_ref, f32[4,2048,128]{2,1,0:T(8,128)S(1)} %get-tuple-element.48.blocks_ref, f32[1024,128]{1,0:T(8,128)S(1)} %get-tuple-element.79.image_ref), custom_call_target="tpu_custom_call" | custom-call | tf_op jit(solution)/shard_map/remainder/pallas_call | solution.py:549
  (1 shorter events, 0.0 us)
Async XLA Ops:
  2.6 6.6 %collective-permute-start = (bf16[2,2,16,512]{3,2,1,0:T(8,128)(2,1)S(1)}, bf16[2,2,16,512]{3,2,1,0:T(8,128)(2,1)S(1)}, u32[]{:S(2)}, u32[]{:S(2)}) collective-permute-start(bf16[2,2,16,512]{3,2,1,0:T(8,128)(2,1)S(1)} %get-tuple-element.51), channel_id=1, source_target_pairs={{0,1},{1,0},{2,3},{3,2},{4,5},{5,4},{6,7},{7,6},{8,9},{9,8},{10,11... | collective-permute-start | bytes 196616 | tf_op jit(solution)/shard_map/ppermute | solution.py:423
  3.1 6.1 %collective-permute-start.1 = (bf16[2,2,16,512]{3,2,1,0:T(8,128)(2,1)S(1)}, bf16[2,2,16,512]{3,2,1,0:T(8,128)(2,1)S(1)}, u32[]{:S(2)}, u32[]{:S(2)}) collective-permute-start(bf16[2,2,16,512]{3,2,1,0:T(8,128)(2,1)S(1)} %get-tuple-element.52), channel_id=1, source_target_pairs={{0,2},{1,3},{2,0},{3,1},{4,6},{5,7},{6,4},{7,5},{8,10},{9,11},{10,... | collective-permute-start | bytes 196616 | tf_op jit(solution)/shard_map/ppermute | solution.py:423
  5.7 4.0 %collective-permute-start.2 = (bf16[2,2,16,512]{3,2,1,0:T(8,128)(2,1)S(1)}, bf16[2,2,16,512]{3,2,1,0:T(8,128)(2,1)S(1)}, u32[]{:S(2)}, u32[]{:S(2)}) collective-permute-start(bf16[2,2,16,512]{3,2,1,0:T(8,128)(2,1)S(1)} %get-tuple-element.53), channel_id=1, source_target_pairs={{0,3},{1,2},{2,1},{3,0},{4,7},{5,6},{6,5},{7,4},{8,11},{9,10},{10,... | collective-permute-start | bytes 196616 | tf_op jit(solution)/shard_map/ppermute | solution.py:423
  9.8 14.9 %collective-permute-start.4 = (bf16[4,2,2,16,512]{4,3,2,1,0:T(8,128)(2,1)S(1)}, bf16[4,2,2,16,512]{4,3,2,1,0:T(8,128)(2,1)S(1)}, u32[]{:S(2)}, u32[]{:S(2)}) collective-permute-start(bf16[4,2,2,16,512]{4,3,2,1,0:T(8,128)(2,1)S(1)} %join.1.own_ref), channel_id=1, source_target_pairs={{0,4},{4,8},{8,12},{12,16},{16,20},{20,24},{24,28},{1,5},{5,9},{9,... | collective-permute-start | bytes 786440 | tf_op jit(solution)/shard_map/ppermute | solution.py:432
  13.2 11.5 %collective-permute-start.3 = (bf16[4,2,2,16,512]{4,3,2,1,0:T(8,128)(2,1)S(1)}, bf16[4,2,2,16,512]{4,3,2,1,0:T(8,128)(2,1)S(1)}, u32[]{:S(2)}, u32[]{:S(2)}) collective-permute-start(bf16[4,2,2,16,512]{4,3,2,1,0:T(8,128)(2,1)S(1)} %join.1.own_ref), channel_id=1, source_target_pairs={{4,0},{8,4},{12,8},{16,12},{20,16},{24,20},{28,24},{5,1},{9,5},{13... | collective-permute-start | bytes 786440 | tf_op jit(solution)/shard_map/ppermute | solution.py:431
  34.2 1.9 %collective-permute-start.5 = (bf16[2,2,16,512]{3,2,1,0:T(8,128)(2,1)S(1)}, bf16[2,2,16,512]{3,2,1,0:T(8,128)(2,1)S(1)}, u32[]{:S(2)}, u32[]{:S(2)}) collective-permute-start(bf16[2,2,16,512]{3,2,1,0:T(8,128)(2,1)S(1)} %get-tuple-element.75), channel_id=1, source_target_pairs={{0,1},{1,0},{2,3},{3,2},{4,5},{5,4},{6,7},{7,6},{8,9},{9,8},{10,11... | collective-permute-start | bytes 196616 | tf_op jit(solution)/shard_map/ppermute | solution.py:423
  34.3 4.5 %collective-permute-start.6 = (bf16[2,2,16,512]{3,2,1,0:T(8,128)(2,1)S(1)}, bf16[2,2,16,512]{3,2,1,0:T(8,128)(2,1)S(1)}, u32[]{:S(2)}, u32[]{:S(2)}) collective-permute-start(bf16[2,2,16,512]{3,2,1,0:T(8,128)(2,1)S(1)} %get-tuple-element.76), channel_id=1, source_target_pairs={{0,2},{1,3},{2,0},{3,1},{4,6},{5,7},{6,4},{7,5},{8,10},{9,11},{10,... | collective-permute-start | bytes 196616 | tf_op jit(solution)/shard_map/ppermute | solution.py:423
  35.8 4.0 %collective-permute-start.7 = (bf16[2,2,16,512]{3,2,1,0:T(8,128)(2,1)S(1)}, bf16[2,2,16,512]{3,2,1,0:T(8,128)(2,1)S(1)}, u32[]{:S(2)}, u32[]{:S(2)}) collective-permute-start(bf16[2,2,16,512]{3,2,1,0:T(8,128)(2,1)S(1)} %get-tuple-element.77), channel_id=1, source_target_pairs={{0,3},{1,2},{2,1},{3,0},{4,7},{5,6},{6,5},{7,4},{8,11},{9,10},{10,... | collective-permute-start | bytes 196616 | tf_op jit(solution)/shard_map/ppermute | solution.py:423
